TPU v7x, 32 devices: a whole 2x2x4 slice. The times are simulated.
32 devices in a mesh: edge: 8 (over z, x), feat: 4 (over y, core).
Axes of the slice: x: 2, y: 2, z: 4, core: 2. Of those that a mesh axis runs over, the one named last changes fastest.
Arguments:
- features: bfloat16 [4096, 2048], P('edge', 'feat'), may hold values from -6 to 6
- tiles: bfloat16 [384, 128, 128], P('edge'), may hold values from -0.109375 to 0.109375
- tile_slot: int32 [768], P('edge'), may hold values from 0 to 31, as said below
- tile_col: int32 [768], P('edge'), may hold values from 0 to 3, as said below
- tile_id: int32 [768], P('edge'), may hold values from 0 to 47
- touched: int32 [8, 8, 4], replicated, may hold values from 0 to 3, as said below
- weight: bfloat16 [2048, 2048], P(None, 'feat'), may hold values from -0.125 to 0.125
- readers: int32 [128], P('edge'), may hold values from 0 to 31, as said below
Outputs:
- hidden: bfloat16 [4096, 2048], P('edge', 'feat')
- ghosts: bfloat16 [16384, 2048], P('edge', 'feat')
Inputs may be any that keep to these rules, and one draw needn't show every extreme that they name: For each sender and owner, the 4 entries of touched are distinct block numbers below 4. Within one device's 96 listed products, the pairs (tile_slot, tile_col) are all distinct. Within one device's 96 listed products, the pairs (tile_slot, tile_col) are all distinct. `readers`: one device's 16 entries are distinct, and at most 2 of them lie in the row blocks of any one index of edge; every device's list has some index of edge with exactly 2.
All inputs are finite; a program needn't handle non-finite values.
Results may differ from a plain program's by a relative error of at most 0.0049.
Values may be sent and summed in bfloat16 or wider, within the bound.
No kernel may reach another device: no remote copies, remote signals or barrier semaphores. Data moves between devices by JAX's collectives and lax.ppermute only.
A program may use at most 128 MiB of HBM per device.

v0:
```python
import math

import jax
import jax.numpy as jnp
from jax import lax
from jax.sharding import PartitionSpec as P


def local(features, tiles, tile_slot, tile_col, tile_id, touched, weight, readers):
    edge_count = lax.axis_size("edge")
    my_index = lax.axis_index("edge")
    row_count, width = features.shape
    block_size = tiles.shape[1]
    local_blocks = row_count // block_size
    slot_cap = touched.shape[2]
    slot_total = edge_count * slot_cap
    inputs = features.reshape(local_blocks, block_size, width)
    tile_count = tile_slot.shape[0]
    per_step = math.gcd(tile_count, 64)

    def add_group(turn, partial_value):
        first_pos = turn * per_step
        slots = lax.dynamic_slice_in_dim(tile_slot, first_pos, per_step)
        columns = lax.dynamic_slice_in_dim(tile_col, first_pos, per_step)
        chosen = lax.dynamic_slice_in_dim(tile_id, first_pos, per_step)
        product = jnp.einsum(
            "gij,gjc->gic", tiles[chosen], inputs[columns], preferred_element_type=jnp.float32
        )
        return partial_value.at[slots].add(product)

    partial_value = lax.fori_loop(
        0,
        tile_count // per_step,
        add_group,
        jnp.zeros((slot_total, block_size, width), jnp.float32),
    )
    outgoing = partial_value.reshape(edge_count, slot_cap, block_size, width)
    incoming = lax.all_to_all(outgoing, "edge", split_axis=0, concat_axis=0, tiled=True)
    senders = lax.dynamic_index_in_dim(touched, my_index, 1, keepdims=False)
    summed = (
        jnp.zeros((local_blocks, block_size, width), jnp.float32)
        .at[senders.reshape(-1)]
        .add(incoming.reshape(-1, block_size, width))
    )
    aggregated = summed.reshape(row_count, width).astype(jnp.bfloat16)
    mixed = jnp.dot(
        lax.all_gather(aggregated, "feat", axis=1, tiled=True),
        weight,
        preferred_element_type=jnp.float32,
    )
    hidden = jnp.maximum(mixed, 0.0).astype(jnp.bfloat16)
    read_count = readers.shape[0]
    piece_blocks = lax.all_gather(hidden, "edge", axis=0, tiled=True).reshape(-1, block_size, width)
    numbers = jnp.arange(piece_blocks.shape[0], dtype=jnp.int32)
    selector = (readers[:, None] == numbers[None, :]).astype(jnp.bfloat16)
    gathered = jnp.einsum("rn,nic->ric", selector, piece_blocks, preferred_element_type=jnp.float32)
    return (hidden, gathered.reshape(read_count * block_size, width).astype(jnp.bfloat16))


def solution(mesh):
    in_specs = (
        P("edge", "feat"),
        P("edge", None, None),
        P("edge"),
        P("edge"),
        P("edge"),
        P(),
        P(None, "feat"),
        P("edge"),
    )
    out_specs = (P("edge", "feat"), P("edge", "feat"))
    return jax.shard_map(local, mesh=mesh, in_specs=in_specs, out_specs=out_specs, check_vma=False)
```

profile of v0, /device:TPU:0, one launch (start us, length us, event | category | flops | bytes accessed | tf_op | source)
XLA Modules:
  0.0 430.9 jit_solution(17408373667327433448)
XLA Ops:
  7.2 4.3 %broadcast_in_dim.31 = f32[32,128,512]{2,1,0:T(8,128)} broadcast(f32[]{:T(128)} %constant.56.clone.1), dimensions={} | broadcast | bytes 8388612 | tf_op jit(solution)/shard_map/broadcast_in_dim | solution.py:35
  11.5 94.8 %while.13 = (s32[]{:T(128)}, f32[32,128,512]{2,1,0:T(8,128)}, s32[96]{0:T(128)S(1)}, s32[96]{0:T(128)S(1)}, bf16[48,128,128]{2,1,0:T(8,128)(2,1)}, /*index=5*/s3...) while((s32[]{:T(128)}, f32[32,128,512]{2,1,0:T(8,128)}, ...), condition=%wide.region_2.0_spmd, body=%wide.region_0.0_spmd.sunk | while | flops 538970432 | bytes 49292832 | solution.py:31
  11.6 2.8 gather_fusion.1
  14.4 3.1 gather_fusion
  17.5 7.0 %fusion.20 = f32[32,128,512]{2,1,0:T(8,128)} fusion(bf16[32,128,128]{2,1,0:T(8,128)(2,1)} %gather_fusion, bf16[32,128,512]{2,1,0:T(8,128)(2,1)} %gather_fusion.1), kind=kOutput, calls=%fused_computation.20.clone.1 | convolution fusion | flops 536870912 | bytes 13631488 | tf_op jit(solution)/shard_map/while/body/eval_jaxpr/gij,gjc->gic/dot_general | solution.py:26
  24.5 18.7 %scatter_fusion = f32[32,128,512]{2,1,0:T(8,128)} fusion(f32[32,128,512]{2,1,0:T(8,128)} %get-tuple-element.202, s32[32]{0:T(128)S(1)} %compare_select_fusion.6, f32[32,128,512]{2,1,0:T(8,128)} %fusion.20), kind=kCustom, calls=%fused_computation.2.clone.1 | custom fusion | flops 2097152 | bytes 25165952 | tf_op jit(solution)/shard_map/while/body/eval_jaxpr/scatter-add | solution.py:29
  43.3 2.7 gather_fusion.1
  46.1 3.1 gather_fusion
  49.1 7.0 %fusion.20 = f32[32,128,512]{2,1,0:T(8,128)} fusion(bf16[32,128,128]{2,1,0:T(8,128)(2,1)} %gather_fusion, bf16[32,128,512]{2,1,0:T(8,128)(2,1)} %gather_fusion.1), kind=kOutput, calls=%fused_computation.20.clone.1 | convolution fusion | flops 536870912 | bytes 13631488 | tf_op jit(solution)/shard_map/while/body/eval_jaxpr/gij,gjc->gic/dot_general | solution.py:26
  56.2 18.5 %scatter_fusion = f32[32,128,512]{2,1,0:T(8,128)} fusion(f32[32,128,512]{2,1,0:T(8,128)} %get-tuple-element.202, s32[32]{0:T(128)S(1)} %compare_select_fusion.6, f32[32,128,512]{2,1,0:T(8,128)} %fusion.20), kind=kCustom, calls=%fused_computation.2.clone.1 | custom fusion | flops 2097152 | bytes 25165952 | tf_op jit(solution)/shard_map/while/body/eval_jaxpr/scatter-add | solution.py:29
  74.8 2.7 gather_fusion.1
  77.5 3.1 gather_fusion
  80.6 7.0 %fusion.20 = f32[32,128,512]{2,1,0:T(8,128)} fusion(bf16[32,128,128]{2,1,0:T(8,128)(2,1)} %gather_fusion, bf16[32,128,512]{2,1,0:T(8,128)(2,1)} %gather_fusion.1), kind=kOutput, calls=%fused_computation.20.clone.1 | convolution fusion | flops 536870912 | bytes 13631488 | tf_op jit(solution)/shard_map/while/body/eval_jaxpr/gij,gjc->gic/dot_general | solution.py:26
  87.7 18.7 %scatter_fusion = f32[32,128,512]{2,1,0:T(8,128)} fusion(f32[32,128,512]{2,1,0:T(8,128)} %get-tuple-element.202, s32[32]{0:T(128)S(1)} %compare_select_fusion.6, f32[32,128,512]{2,1,0:T(8,128)} %fusion.20), kind=kCustom, calls=%fused_computation.2.clone.1 | custom fusion | flops 2097152 | bytes 25165952 | tf_op jit(solution)/shard_map/while/body/eval_jaxpr/scatter-add | solution.py:29
  106.4 7.2 %all-to-all-start = ((f32[8,4,128,512]{3,2,1,0:T(8,128)}), f32[8,4,128,512]{3,2,1,0:T(8,128)}, u32[]{:S(2)}, u32[]{:S(2)}) async-start(f32[8,4,128,512]{3,2,1,0:T(8,128)} %bitcast.20), calls=%async_computation | async-start | bytes 16777216 | tf_op jit(solution)/shard_map/all_to_all | solution.py:38
  114.0 182.7 %all-to-all-done = f32[8,4,128,512]{3,2,1,0:T(8,128)} async-done(((f32[8,4,128,512]{3,2,1,0:T(8,128)}), f32[8,4,128,512]{3,2,1,0:T(8,128)}, u32[]{:S(2)}, u32[]{:S(2)}) %all-to-all-start) | async-done | bytes 8388640 | tf_op jit(solution)/shard_map/all_to_all | solution.py:38
  296.8 1.1 broadcast_in_dim.30
  297.9 17.5 %scatter_fusion.1 = f32[4,128,512]{2,1,0:T(8,128)} fusion(f32[4,128,512]{2,1,0:T(8,128)} %broadcast_in_dim.30, s32[32]{0:T(128)S(1)} %fusion.9, f32[32,128,512]{2,1,0:T(8,128)} %bitcast.3), kind=kCustom, calls=%fused_computation.3 | custom fusion | flops 2097152 | bytes 25165952 | tf_op jit(solution)/shard_map/scatter-add | solution.py:43
  315.4 2.1 convert_element_type.16
  317.5 21.8 %all-gather.3.cloned.1.call-done = bf16[512,2048]{1,0:T(8,128)(2,1)} async-done(((bf16[512,512]{1,0:T(8,128)(2,1)}), bf16[512,2048]{1,0:T(8,128)(2,1)}) %all-gather.3.cloned.1.call-update) | async-done | bytes 2097168 | tf_op jit(solution)/shard_map/all_gather | solution.py:47
  339.3 3.6 fusion.5
  343.0 73.5 %all-gather.5.cloned.1.call-done = bf16[4096,512]{1,0:T(8,128)(2,1)} async-done(((bf16[512,512]{1,0:T(8,128)(2,1)}), bf16[4096,512]{1,0:T(8,128)(2,1)}) %all-gather.5.cloned.1.call-update) | async-done | bytes 4194320 | tf_op jit(solution)/shard_map/all_gather | solution.py:53
  416.5 5.1 %fusion.2 = bf16[16,128,512]{2,0,1:T(8,128)(2,1)S(1)} fusion(bf16[32,128,512]{2,1,0:T(8,128)(2,1)} %bitcast.21, s32[16]{0:T(128)S(1)} %copy-done.5), kind=kOutput, calls=%fused_computation.11 | convolution fusion | flops 68157952 | bytes 6291520 | tf_op jit(solution)/shard_map/rn,nic->ric/dot_general | solution.py:56
  421.6 2.5 copy.12
  (33 shorter events, 1.0 us)
Async XLA Ops:
  7.2 332.2 %copy-start = (bf16[2048,512]{1,0:T(8,128)(2,1)S(1)}, bf16[2048,512]{1,0:T(8,128)(2,1)}, u32[]{:S(2)}) copy-start(bf16[2048,512]{1,0:T(8,128)(2,1)} %param.16) | copy-start | bytes 6291460
  7.2 4.4 %copy-start.1 = (bf16[512,512]{1,0:T(8,128)(2,1)S(1)}, bf16[512,512]{1,0:T(8,128)(2,1)}, u32[]{:S(2)}) copy-start(bf16[512,512]{1,0:T(8,128)(2,1)} %param.10) | copy-start | bytes 1572868
  7.2 4.3 %copy-start.3 = (s32[96]{0:T(128)S(1)}, s32[96]{0:T(128)}, u32[]{:S(2)}) copy-start(s32[96]{0:T(128)} %param.14) | copy-start | bytes 1156
  7.2 4.3 %copy-start.4 = (s32[96]{0:T(128)S(1)}, s32[96]{0:T(128)}, u32[]{:S(2)}) copy-start(s32[96]{0:T(128)} %param.13) | copy-start | bytes 1156
  7.2 4.3 %copy-start.6 = (s32[96]{0:T(128)S(1)}, s32[96]{0:T(128)}, u32[]{:S(2)}) copy-start(s32[96]{0:T(128)} %param.12) | copy-start | bytes 1156
  106.4 7.3 %copy-start.2 = (s32[8,8,4]{1,2,0:T(4,128)S(1)}, s32[8,8,4]{1,2,0:T(4,128)}, u32[]{:S(2)}) copy-start(s32[8,8,4]{1,2,0:T(4,128)} %param.15) | copy-start | bytes 3076
  106.4 190.4 %all-to-all-start = ((f32[8,4,128,512]{3,2,1,0:T(8,128)}), f32[8,4,128,512]{3,2,1,0:T(8,128)}, u32[]{:S(2)}, u32[]{:S(2)}) async-start(f32[8,4,128,512]{3,2,1,0:T(8,128)} %bitcast.20), calls=%async_computation | async-start | bytes 16777216 | tf_op jit(solution)/shard_map/all_to_all | solution.py:38
  113.6 225.7 %all-gather.3.cloned.1.call-start = ((), (), s32[]{:S(2)}) async-start(), calls=%async_computation.1 | async-start | bytes 2621440 | tf_op jit(solution)/shard_map/all_gather | solution.py:47
  317.5 99.1 %copy-start.5 = (s32[16]{0:T(128)S(1)}, s32[16]{0:T(128)}, u32[]{:S(2)}) copy-start(s32[16]{0:T(128)} %param.17) | copy-start | bytes 196
  317.5 99.0 %all-gather.5.cloned.1.call-start = ((), (), s32[]{:S(2)}) async-start(), calls=%async_computation.2 | async-start | bytes 4718592 | tf_op jit(solution)/shard_map/all_gather | solution.py:53
Sparse Core Ops, SparseCore 0:
  317.6 21.6 all-gather.2
  343.1 73.3 all-gather.4
where the time goes:
time: 432 us; the launch traced here: 431 us
  waiting for transfers between devices  278 us (64%)
  other arithmetic  76 us (18%)
  matrix products  29.7 us (7%)
  local copies, waits for them, and re-layouts  25.7 us (6%)
  between operations  14.1 us (3%)
  starting transfers between devices  7.31 us (2%)
    all_to_all x1, waiting for transfers between devices, local(): lax.all_to_all(outgoing, 'edge', split_axis=0, concat_axis=0, tiled=True)  183 us
    all_gather x1, waiting for transfers between devices, local(): lax.all_gather(hidden, 'edge', axis=0, tiled=True)  73.5 us
    scatter-add x3, other arithmetic, add_group(): return partial_value.at[slots].add(product)  55.9 us
    all_gather x1, waiting for transfers between devices, local(): lax.all_gather(aggregated, 'feat', axis=1, tiled=True)  21.8 us
    dot_general x3, matrix products, add_group(): jnp.einsum('gij,gjc->gic', tiles[chosen], inputs[columns], preferred_elem...  21 us
    scatter-add x1, other arithmetic, local(): summed = jnp.zeros((local_blocks, block_size, width), jnp.float32).at[sen...  17.5 us
    gather x3, local copies, waits for them, and re-layouts, add_group(): tiles[chosen]  9.17 us
  transfers between devices with their start and end apart: 3, of which 3 were waited for; matrix products, arithmetic and copies ran while one was open for 0% of the time, Pallas kernels for 0%

commit v1 on v0

v1 whole, which is shorter than its diff:
```python
import jax
import jax.numpy as jnp
from jax import lax
from jax.experimental import pallas as pl
from jax.experimental.pallas import tpu as pltpu
from jax.sharding import PartitionSpec as P

PARTS = 4
READ_CAP = 2
VMEM_BYTES = 40 * 1024 * 1024

SMEM = pl.BlockSpec(memory_space=pltpu.SMEM)
VMEM = pl.BlockSpec(memory_space=pltpu.VMEM)
ANY = pl.BlockSpec(memory_space=pl.ANY)


def reversed_bits(value, bits):
    result = value & 1
    for i in range(1, bits):
        result = (result << 1) | ((value >> i) & 1)
    return result


def partial_sums(me, slot, col, tile_id, touched, tiles, features, first, count, parts):
    block = tiles.shape[1]
    blocks = features.shape[0] // block
    width = features.shape[1]
    rows = block // parts
    products = slot.shape[0]
    edges, cap = touched.shape[1], touched.shape[2]
    bits = edges.bit_length() - 1
    square = blocks * blocks

    def body(me_ref, slot_ref, col_ref, id_ref, touched_ref, tiles_hbm, x_hbm, *refs):
        outs = refs[:parts]
        table, tiles_ref, x_ref, lhs, sems = refs[parts:]
        load_tiles = pltpu.make_async_copy(tiles_hbm, tiles_ref, sems.at[0])
        load_x = pltpu.make_async_copy(x_hbm, x_ref, sems.at[1])
        load_tiles.start()
        load_x.start()

        def clear(i, carry):
            table[i] = 0
            return carry

        lax.fori_loop(0, edges * square, clear, 0, unroll=8)

        def enter(k, carry):
            owner, entry = slot_ref[k] // cap, slot_ref[k] % cap
            target = touched_ref[owner * cap + entry]
            place = reversed_bits(owner ^ me_ref[0], bits)
            table[(place * blocks + target) * blocks + col_ref[k]] = id_ref[k] + 1
            return carry

        lax.fori_loop(0, products, enter, 0, unroll=4)
        load_tiles.wait()
        load_x.wait()

        def one_owner(i, carry):
            base = (first + i) * square
            for b in range(blocks):
                for c in range(blocks):
                    entry = table[base + b * blocks + c]
                    tile = tiles_ref[jnp.maximum(entry - 1, 0)]
                    tile = jnp.where(entry > 0, tile, jnp.zeros_like(tile))
                    for part in range(parts):
                        lhs[pl.ds((part * blocks + b) * rows, rows), pl.ds(c * block, block)] = tile[
                            part * rows : (part + 1) * rows
                        ]
            total = jnp.dot(lhs[...], x_ref[...], preferred_element_type=jnp.float32)
            total = total.astype(jnp.bfloat16).reshape(parts, blocks, rows, width)
            for part in range(parts):
                outs[part][i] = total[part]
            return carry

        lax.fori_loop(0, count, one_owner, 0)

    return pl.pallas_call(
        body,
        out_shape=[jax.ShapeDtypeStruct((count, blocks, rows, width), jnp.bfloat16)] * parts,
        in_specs=[SMEM] * 5 + [ANY] * 2,
        out_specs=[VMEM] * parts,
        scratch_shapes=[
            pltpu.SMEM((edges * square,), jnp.int32),
            pltpu.VMEM(tiles.shape, jnp.bfloat16),
            pltpu.VMEM(features.shape, jnp.bfloat16),
            pltpu.VMEM((blocks * block, blocks * block), jnp.bfloat16),
            pltpu.SemaphoreType.DMA((2,)),
        ],
        compiler_params=pltpu.CompilerParams(vmem_limit_bytes=VMEM_BYTES),
        cost_estimate=pl.CostEstimate(
            flops=2 * count * (blocks * block) ** 2 * width,
            bytes_accessed=2 * (tiles.size + features.size + count * blocks * block * width),
            transcendentals=0,
        ),
    )(me, slot, col, tile_id, touched[me[0]].reshape(-1), tiles, features)


def mix(mine, pieces, weight):
    blocks, rows, depth = pieces[0].shape
    width = weight.shape[1]

    def body(mine_ref, w_ref, *refs):
        out_ref = refs[-1]
        total = jnp.zeros((blocks * rows, width), jnp.float32)
        for j, piece in enumerate(refs[:-1]):
            at = pl.multiple_of((mine_ref[0] ^ j) * depth, depth)
            total += jnp.dot(
                piece[...].reshape(blocks * rows, depth),
                w_ref[pl.ds(at, depth)],
                preferred_element_type=jnp.float32,
            )
        out_ref[...] = jnp.maximum(total, 0.0).astype(jnp.bfloat16).reshape(out_ref.shape)

    return pl.pallas_call(
        body,
        out_shape=jax.ShapeDtypeStruct((blocks, rows, width), jnp.bfloat16),
        in_specs=[SMEM] + [VMEM] * (1 + len(pieces)),
        out_specs=VMEM,
        compiler_params=pltpu.CompilerParams(vmem_limit_bytes=VMEM_BYTES),
        cost_estimate=pl.CostEstimate(
            flops=2 * len(pieces) * pieces[0].size * width,
            bytes_accessed=2 * (len(pieces) * pieces[0].size + weight.size + blocks * rows * width),
            transcendentals=0,
        ),
    )(mine, weight, *pieces)


def pick(choice, near):
    count = choice.shape[0]

    def body(choice_ref, *refs):
        for i in range(count):
            refs[-1][i] = refs[i // READ_CAP][choice_ref[i]]

    return pl.pallas_call(
        body,
        out_shape=jax.ShapeDtypeStruct((count, *near[0].shape[1:]), near[0].dtype),
        in_specs=[SMEM] + [VMEM] * len(near),
        out_specs=VMEM,
        compiler_params=pltpu.CompilerParams(vmem_limit_bytes=VMEM_BYTES),
        cost_estimate=pl.CostEstimate(flops=0, bytes_accessed=4 * count * near[0][0].size, transcendentals=0),
    )(choice, *near)


def lay_out(place, near, far, ghosts, part, block):
    count = place.shape[0]
    blocks, rows, width = near[0].shape
    near_count = len(near) * blocks

    def body(place_ref, *refs):
        sources, far_ref = refs[: len(near)], refs[len(near)]
        out_ref, sems = refs[-2:]

        def target(r):
            return out_ref.at[r, pl.ds(part * rows, rows)]

        for r in range(count):
            spot = place_ref[r]
            for i, source in enumerate(sources):

                @pl.when(spot // blocks == i)
                def _():
                    pltpu.make_async_copy(source.at[spot % blocks], target(r), sems.at[r]).start()

            @pl.when(spot >= near_count)
            def _():
                pltpu.make_async_copy(far_ref.at[spot - near_count], target(r), sems.at[r]).start()

        for r in range(count):
            pltpu.make_async_copy(far_ref.at[0], target(r), sems.at[r]).wait()

    earlier = [] if ghosts is None else [ghosts]
    return pl.pallas_call(
        body,
        out_shape=jax.ShapeDtypeStruct((count, block, width), jnp.bfloat16),
        in_specs=[SMEM] + [VMEM] * (len(near) + 1) + [ANY] * len(earlier),
        out_specs=ANY,
        scratch_shapes=[pltpu.SemaphoreType.DMA((count,))],
        input_output_aliases={len(near) + 2: 0} if earlier else {},
        compiler_params=pltpu.CompilerParams(vmem_limit_bytes=VMEM_BYTES),
        cost_estimate=pl.CostEstimate(flops=0, bytes_accessed=4 * count * rows * width, transcendentals=0),
    )(place, *near, far, *earlier)


def local(features, tiles, tile_slot, tile_col, tile_id, touched, weight, readers):
    edges, feats = lax.axis_size("edge"), lax.axis_size("feat")
    half = edges // 2
    me, mine = lax.axis_index("edge"), lax.axis_index("feat")
    block = tiles.shape[1]
    blocks = features.shape[0] // block
    width = features.shape[1]
    parts = PARTS

    def flip(value, bit, axis="edge"):
        return lax.ppermute(value, axis, [(d, d ^ bit) for d in range(lax.axis_size(axis))])

    def spread(value, size, lowest, axis):
        held = {0: value}
        bit = size // 2
        while bit >= lowest:
            held.update({j | bit: flip(held[j], bit, axis) for j in list(held)})
            bit //= 2
        return [held[j] for j in sorted(held)]

    order = jnp.arange(readers.shape[0], dtype=jnp.int32)

    def ranks(listed):
        same = (listed[:, None] // blocks) == (listed[None, :] // blocks)
        return jnp.sum((same & (order[None, :] < order[:, None])).astype(jnp.int32), axis=1)

    other = flip(readers, 1)
    entries = jnp.arange(half * READ_CAP, dtype=jnp.int32)
    wanted = lax.bitwise_xor(2 * (entries // READ_CAP), me)
    hit = ((other // blocks)[None, :] == wanted[:, None]) & (ranks(other)[None, :] == (entries % READ_CAP)[:, None])
    choice = jnp.sum(jnp.where(hit, (other % blocks)[None, :], 0), axis=1)
    peer = lax.bitwise_xor(readers // blocks, me)
    place = jnp.where(
        peer % 2 == 0,
        (peer // 2) * blocks + readers % blocks,
        half * blocks + (peer // 2) * READ_CAP + ranks(readers),
    )

    products = (me.reshape(1), tile_slot, tile_col, tile_id, touched, tiles, features)
    away = partial_sums(*products, half, half, parts)
    kept = partial_sums(*products, 0, half, parts)
    hidden, ghosts = [], None
    for part in range(parts):
        total = kept[part].astype(jnp.float32) + flip(away[part], 1).astype(jnp.float32)
        bit = 2
        while bit < edges:
            left = total.shape[0] // 2
            total = total[:left] + flip(total[left:].astype(jnp.bfloat16), bit).astype(jnp.float32)
            bit *= 2
        pieces = spread(total[0].astype(jnp.bfloat16), feats, 1, "feat")
        mixed = mix(mine.reshape(1), pieces, weight)
        hidden.append(mixed)
        near = spread(mixed, edges, 2, "edge")
        far = flip(pick(choice, near), 1)
        ghosts = lay_out(place, near, far, ghosts, part, block)
    return (
        jnp.concatenate(hidden, axis=1).reshape(blocks * block, width),
        ghosts.reshape(-1, width),
    )


def solution(mesh):
    in_specs = (
        P("edge", "feat"),
        P("edge", None, None),
        P("edge"),
        P("edge"),
        P("edge"),
        P(),
        P(None, "feat"),
        P("edge"),
    )
    out_specs = (P("edge", "feat"), P("edge", "feat"))
    return jax.shard_map(local, mesh=mesh, in_specs=in_specs, out_specs=out_specs, check_vma=False)
```

time: 432 us -> 154 us (0.36)
  waiting for transfers between devices: 278 us -> 76.5 us
  other arithmetic: 76 us -> 6.65 us
  starting transfers between devices: 7.31 us -> 44.9 us
  matrix products: 29.7 us -> 0 us
  local copies, waits for them, and re-layouts: 25.7 us -> 5.52 us
  Pallas kernels: 0 us -> 18.7 us
  between operations: 14.1 us -> 1.04 us
    all_to_all x1 -> x0, waiting for transfers between devices: 183 us -> none  [local(): lax.all_to_all(outgoing, 'edge', split_axis=0, concat_axis=0, tiled=True)]
    all_gather x2 -> x0, waiting for transfers between devices: 95.3 us -> none  [the longest x1 73.5 us: local(): lax.all_gather(hidden, 'edge', axis=0, tiled=True)]
    ppermute x0 -> x41, waiting for transfers between devices: none -> 76.5 us  [flip(): lax.ppermute(value, axis, [(d, d ^ bit) for d in range(lax.axis_size(axis...]
    scatter-add x4 -> x0, other arithmetic: 73.4 us -> none  [the longest x3 55.9 us: add_group(): return partial_value.at[slots].add(product)]
    ppermute x0 -> x41, starting transfers between devices: none -> 44.9 us  [flip(): lax.ppermute(value, axis, [(d, d ^ bit) for d in range(lax.axis_size(axis...]
    dot_general x5 -> x0, matrix products: 29.7 us -> none  [the longest x3 21 us: add_group(): jnp.einsum('gij,gjc->gic', tiles[chosen], inputs[columns], preferred_elem...]
    pallas_call x0 -> x14, Pallas kernels: none -> 18.7 us  [the longest x2 8.64 us: partial_sums(): pl.pallas_call(body, out_shape=[jax.ShapeDtypeStruct((count, blocks, rows...]
    gather x6 -> x0, local copies, waits for them, and re-layouts: 17.4 us -> none  [the longest x3 9.17 us: add_group(): tiles[chosen]]
  transfers between devices with their start and end apart: 3 -> 41, of which waited for: 3 -> 20; matrix products, arithmetic and copies ran while one was open for 0% -> 4% of each run, Pallas kernels for 0% -> 8%
where the time goes in v1:
time: 154 us; the launch traced here: 153 us
  waiting for transfers between devices  76.5 us (50%)
  starting transfers between devices  44.9 us (29%)
  Pallas kernels  18.7 us (12%)
  other arithmetic  6.65 us (4%)
  local copies, waits for them, and re-layouts  5.52 us (4%)
    ppermute x41, waiting for transfers between devices, flip(): lax.ppermute(value, axis, [(d, d ^ bit) for d in range(lax.axis_size(axis...  76.5 us
    ppermute x41, starting transfers between devices, flip(): lax.ppermute(value, axis, [(d, d ^ bit) for d in range(lax.axis_size(axis...  44.9 us
    pallas_call x2, Pallas kernels, partial_sums(): pl.pallas_call(body, out_shape=[jax.ShapeDtypeStruct((count, blocks, rows...  8.64 us
    pallas_call x4, Pallas kernels, lay_out(): pl.pallas_call(body, out_shape=jax.ShapeDtypeStruct((count, block, width)...  6 us
    unnamed x16, local copies, waits for them, and re-layouts  5.14 us
    add x4, other arithmetic, local(): kept[part].astype(jnp.float32) + flip(away[part], 1).astype(jnp.float32)  4.79 us
  transfers between devices with their start and end apart: 41, of which 20 were waited for; matrix products, arithmetic and copies ran while one was open for 4% of the time, Pallas kernels for 8%

profile of v1, /device:TPU:0, one launch (start us, length us, event | category | flops | bytes accessed | tf_op | source)
XLA Modules:
  0.0 153.3 jit_solution(9946134773592133153)
XLA Ops:
  5.9 4.8 %shard_map.96 = (bf16[4,4,32,512]{3,2,1,0:T(8,128)(2,1)}, bf16[4,4,32,512]{3,2,1,0:T(8,128)(2,1)}, bf16[4,4,32,512]{3,2,1,0:T(8,128)(2,1)S(1)}, bf16[4,4,32,512]{3,2,1,0:T(8,128)(2,1)S(1)}) custom-call(s32[1]{0:T(128)} %bitcast.1.me_ref, s32[96]{0:T(128)S(1)} %copy-done.4, s32[96]{0:T(128)S(1)} %copy-done.5, s32[96]{0:T(128)S(1)} %copy-done.6, ...), custom_call_target="tpu_custom_call" | custom-call | flops 1073741824 | bytes 4194304 | tf_op jit(solution)/shard_map/pallas_call | solution.py:78
  10.7 3.0 %collective-permute-start = (bf16[4,4,32,512]{3,2,1,0:T(8,128)(2,1)}, bf16[4,4,32,512]{3,2,1,0:T(8,128)(2,1)}, u32[]{:S(2)}, u32[]{:S(2)}) collective-permute-start(bf16[4,4,32,512]{3,2,1,0:T(8,128)(2,1)} %get-tuple-element.11), channel_id=1, source_target_pairs={{0,4},{4,0},{8,12},{12,8},{16,20},{20,16},{24,28},{28,24},{1,5},{5... | collective-permute-start | bytes 1572872 | tf_op jit(solution)/shard_map/ppermute | solution.py:196
  15.8 3.9 %shard_map.95 = (bf16[4,4,32,512]{3,2,1,0:T(8,128)(2,1)S(1)}, bf16[4,4,32,512]{3,2,1,0:T(8,128)(2,1)S(1)}, bf16[4,4,32,512]{3,2,1,0:T(8,128)(2,1)S(1)}, bf16[4,4,32,512]{3,2,1,0:T(8,128)(2,1)S(1)}) custom-call(s32[1]{0:T(128)} %bitcast.1.me_ref, s32[96]{0:T(128)S(1)} %copy-done.4, s32[96]{0:T(128)S(1)} %copy-done.5, s32[96]{0:T(128)S(1)} %copy-done.6, ...), custom_call_target="tpu_custom_call" | custom-call | flops 1073741824 | bytes 4194304 | tf_op jit(solution)/shard_map/pallas_call | solution.py:78
  19.8 7.0 %collective-permute-done = bf16[4,4,32,512]{3,2,1,0:T(8,128)(2,1)} collective-permute-done((bf16[4,4,32,512]{3,2,1,0:T(8,128)(2,1)}, bf16[4,4,32,512]{3,2,1,0:T(8,128)(2,1)}, u32[]{:S(2)}, u32[]{:S(2)}) %collective-permute-start) | collective-permute-done | bytes 524320 | tf_op jit(solution)/shard_map/ppermute | solution.py:196
  28.0 2.2 %collective-permute-start.1 = (bf16[2,4,32,512]{3,2,1,0:T(8,128)(2,1)S(1)}, bf16[2,4,32,512]{3,2,1,0:T(8,128)(2,1)S(1)}, u32[]{:S(2)}, u32[]{:S(2)}) collective-permute-start(bf16[2,4,32,512]{3,2,1,0:T(8,128)(2,1)S(1)} %slice.123), channel_id=1, source_target_pairs={{0,8},{4,12},{8,0},{12,4},{16,24},{20,28},{24,16},{28,20},{1,9},{5... | collective-permute-start | bytes 786440 | tf_op jit(solution)/shard_map/ppermute | solution.py:196
  30.2 7.8 %collective-permute-done.6 = bf16[4,4,32,512]{3,2,1,0:T(8,128)(2,1)} collective-permute-done((bf16[4,4,32,512]{3,2,1,0:T(8,128)(2,1)}, bf16[4,4,32,512]{3,2,1,0:T(8,128)(2,1)}, u32[]{:S(2)}, u32[]{:S(2)}) %collective-permute-start.6) | collective-permute-done | bytes 524320 | tf_op jit(solution)/shard_map/ppermute | solution.py:196
  39.3 2.2 %collective-permute-start.7 = (bf16[2,4,32,512]{3,2,1,0:T(8,128)(2,1)S(1)}, bf16[2,4,32,512]{3,2,1,0:T(8,128)(2,1)S(1)}, u32[]{:S(2)}, u32[]{:S(2)}) collective-permute-start(bf16[2,4,32,512]{3,2,1,0:T(8,128)(2,1)S(1)} %slice.122), channel_id=1, source_target_pairs={{0,8},{4,12},{8,0},{12,4},{16,24},{20,28},{24,16},{28,20},{1,9},{5... | collective-permute-start | bytes 786440 | tf_op jit(solution)/shard_map/ppermute | solution.py:196
  41.5 7.8 %collective-permute-done.12 = bf16[4,4,32,512]{3,2,1,0:T(8,128)(2,1)} collective-permute-done((bf16[4,4,32,512]{3,2,1,0:T(8,128)(2,1)S(1)}, bf16[4,4,32,512]{3,2,1,0:T(8,128)(2,1)}, u32[]{:S(2)}, u32[]{:S(2)}) %collective-permute-start.12) | collective-permute-done | bytes 524320 | tf_op jit(solution)/shard_map/ppermute | solution.py:196
  50.5 2.2 %collective-permute-start.13 = (bf16[2,4,32,512]{3,2,1,0:T(8,128)(2,1)S(1)}, bf16[2,4,32,512]{3,2,1,0:T(8,128)(2,1)S(1)}, u32[]{:S(2)}, u32[]{:S(2)}) collective-permute-start(bf16[2,4,32,512]{3,2,1,0:T(8,128)(2,1)S(1)} %slice.121), channel_id=1, source_target_pairs={{0,8},{4,12},{8,0},{12,4},{16,24},{20,28},{24,16},{28,20},{1,9},{5... | collective-permute-start | bytes 786440 | tf_op jit(solution)/shard_map/ppermute | solution.py:196
  52.7 7.0 %collective-permute-done.18 = bf16[4,4,32,512]{3,2,1,0:T(8,128)(2,1)} collective-permute-done((bf16[4,4,32,512]{3,2,1,0:T(8,128)(2,1)S(1)}, bf16[4,4,32,512]{3,2,1,0:T(8,128)(2,1)}, u32[]{:S(2)}, u32[]{:S(2)}) %collective-permute-start.18) | collective-permute-done | bytes 524320 | tf_op jit(solution)/shard_map/ppermute | solution.py:196
  62.9 2.7 %collective-permute-start.2 = (bf16[1,4,32,512]{3,2,1,0:T(8,128)(2,1)S(1)}, bf16[1,4,32,512]{3,2,1,0:T(8,128)(2,1)S(1)}, u32[]{:S(2)}, u32[]{:S(2)}) collective-permute-start(bf16[1,4,32,512]{3,2,1,0:T(8,128)(2,1)S(1)} %slice.127), channel_id=1, source_target_pairs={{0,16},{4,20},{8,24},{12,28},{16,0},{20,4},{24,8},{28,12},{1,17},{... | collective-permute-start | bytes 393224 | tf_op jit(solution)/shard_map/ppermute | solution.py:196
  66.2 2.7 %collective-permute-start.14 = (bf16[1,4,32,512]{3,2,1,0:T(8,128)(2,1)S(1)}, bf16[1,4,32,512]{3,2,1,0:T(8,128)(2,1)S(1)}, u32[]{:S(2)}, u32[]{:S(2)}) collective-permute-start(bf16[1,4,32,512]{3,2,1,0:T(8,128)(2,1)S(1)} %slice.125), channel_id=1, source_target_pairs={{0,16},{4,20},{8,24},{12,28},{16,0},{20,4},{24,8},{28,12},{1,17},{... | collective-permute-start | bytes 393224 | tf_op jit(solution)/shard_map/ppermute | solution.py:196
  68.9 4.1 %collective-permute-done.19 = bf16[2,4,32,512]{3,2,1,0:T(8,128)(2,1)S(1)} collective-permute-done((bf16[2,4,32,512]{3,2,1,0:T(8,128)(2,1)S(1)}, bf16[2,4,32,512]{3,2,1,0:T(8,128)(2,1)S(1)}, u32[]{:S(2)}, u32[]{:S(2)}) %collective-permute-start.19) | collective-permute-done | bytes 262176 | tf_op jit(solution)/shard_map/ppermute | solution.py:196
  76.1 8.0 %collective-permute-done.8 = bf16[1,4,32,512]{3,2,1,0:T(8,128)(2,1)S(1)} collective-permute-done((bf16[1,4,32,512]{3,2,1,0:T(8,128)(2,1)S(1)}, bf16[1,4,32,512]{3,2,1,0:T(8,128)(2,1)S(1)}, u32[]{:S(2)}, u32[]{:S(2)}) %collective-permute-start.8) | collective-permute-done | bytes 131104 | tf_op jit(solution)/shard_map/ppermute | solution.py:196
  93.7 2.6 %collective-permute-done.22.refs_2_ = bf16[4,32,512]{2,1,0:T(8,128)(2,1)S(1)} collective-permute-done((bf16[4,32,512]{2,1,0:T(8,128)(2,1)S(1)}, bf16[4,32,512]{2,1,0:T(8,128)(2,1)S(1)}, u32[]{:S(2)}, u32[]{:S(2)}) %collective-permute-start.22) | collective-permute-done | bytes 131104 | tf_op jit(solution)/shard_map/ppermute | solution.py:196
  96.3 2.2 %collective-permute-start.37 = (bf16[4,32,512]{2,1,0:T(8,128)(2,1)S(1)}, bf16[4,32,512]{2,1,0:T(8,128)(2,1)S(1)}, u32[]{:S(2)}, u32[]{:S(2)}) collective-permute-start(bf16[4,32,512]{2,1,0:T(8,128)(2,1)S(1)} %shard_map.97.refs_0_), channel_id=1, source_target_pairs={{0,8},{4,12},{8,0},{12,4},{16,24},{20,28},{24,16},{28,20},{1,9},{5... | collective-permute-start | bytes 393224 | tf_op jit(solution)/shard_map/ppermute | solution.py:196
  108.0 8.4 %collective-permute-done.34.refs_2_ = bf16[4,32,512]{2,1,0:T(8,128)(2,1)S(1)} collective-permute-done((bf16[4,32,512]{2,1,0:T(8,128)(2,1)S(1)}, bf16[4,32,512]{2,1,0:T(8,128)(2,1)S(1)}, u32[]{:S(2)}, u32[]{:S(2)}) %collective-permute-start.34) | collective-permute-done | bytes 131104 | tf_op jit(solution)/shard_map/ppermute | solution.py:196
  119.3 2.7 %collective-permute-done.25.refs_2_ = bf16[4,32,512]{2,1,0:T(8,128)(2,1)S(1)} collective-permute-done((bf16[4,32,512]{2,1,0:T(8,128)(2,1)S(1)}, bf16[4,32,512]{2,1,0:T(8,128)(2,1)S(1)}, u32[]{:S(2)}, u32[]{:S(2)}) %collective-permute-start.25) | collective-permute-done | bytes 131104 | tf_op jit(solution)/shard_map/ppermute | solution.py:196
  124.9 5.5 %collective-permute-done.35.refs_3_ = bf16[4,32,512]{2,1,0:T(8,128)(2,1)S(1)} collective-permute-done((bf16[4,32,512]{2,1,0:T(8,128)(2,1)S(1)}, bf16[4,32,512]{2,1,0:T(8,128)(2,1)S(1)}, u32[]{:S(2)}, u32[]{:S(2)}) %collective-permute-start.35) | collective-permute-done | bytes 131104 | tf_op jit(solution)/shard_map/ppermute | solution.py:196
  131.0 2.1 %collective-permute-start.36 = (bf16[8,32,512]{2,1,0:T(8,128)(2,1)S(1)}, bf16[8,32,512]{2,1,0:T(8,128)(2,1)S(1)}, u32[]{:S(2)}, u32[]{:S(2)}) collective-permute-start(bf16[8,32,512]{2,1,0:T(8,128)(2,1)S(1)} %shard_map.103), channel_id=1, source_target_pairs={{0,4},{4,0},{8,12},{12,8},{16,20},{20,16},{24,28},{28,24},{1,5},{5... | collective-permute-start | bytes 786440 | tf_op jit(solution)/shard_map/ppermute | solution.py:196
  134.4 2.1 %collective-permute-start.28 = (bf16[8,32,512]{2,1,0:T(8,128)(2,1)S(1)}, bf16[8,32,512]{2,1,0:T(8,128)(2,1)S(1)}, u32[]{:S(2)}, u32[]{:S(2)}) collective-permute-start(bf16[8,32,512]{2,1,0:T(8,128)(2,1)S(1)} %shard_map.101), channel_id=1, source_target_pairs={{0,4},{4,0},{8,12},{12,8},{16,20},{20,16},{24,28},{28,24},{1,5},{5... | collective-permute-start | bytes 786440 | tf_op jit(solution)/shard_map/ppermute | solution.py:196
  137.3 2.4 %collective-permute-done.40.refs_4_ = bf16[8,32,512]{2,1,0:T(8,128)(2,1)S(1)} collective-permute-done((bf16[8,32,512]{2,1,0:T(8,128)(2,1)S(1)}, bf16[8,32,512]{2,1,0:T(8,128)(2,1)S(1)}, u32[]{:S(2)}, u32[]{:S(2)}) %collective-permute-start.40) | collective-permute-done | bytes 262176 | tf_op jit(solution)/shard_map/ppermute | solution.py:196
  141.2 4.1 %collective-permute-done.36.refs_4_ = bf16[8,32,512]{2,1,0:T(8,128)(2,1)S(1)} collective-permute-done((bf16[8,32,512]{2,1,0:T(8,128)(2,1)S(1)}, bf16[8,32,512]{2,1,0:T(8,128)(2,1)S(1)}, u32[]{:S(2)}, u32[]{:S(2)}) %collective-permute-start.36) | collective-permute-done | bytes 262176 | tf_op jit(solution)/shard_map/ppermute | solution.py:196
  146.8 2.2 %collective-permute-done.32.refs_4_ = bf16[8,32,512]{2,1,0:T(8,128)(2,1)S(1)} collective-permute-done((bf16[8,32,512]{2,1,0:T(8,128)(2,1)S(1)}, bf16[8,32,512]{2,1,0:T(8,128)(2,1)S(1)}, u32[]{:S(2)}, u32[]{:S(2)}) %collective-permute-start.32) | collective-permute-done | bytes 262176 | tf_op jit(solution)/shard_map/ppermute | solution.py:196
  (119 shorter events, 52.9 us)
Async XLA Ops:
  10.7 16.1 %collective-permute-start = (bf16[4,4,32,512]{3,2,1,0:T(8,128)(2,1)}, bf16[4,4,32,512]{3,2,1,0:T(8,128)(2,1)}, u32[]{:S(2)}, u32[]{:S(2)}) collective-permute-start(bf16[4,4,32,512]{3,2,1,0:T(8,128)(2,1)} %get-tuple-element.11), channel_id=1, source_target_pairs={{0,4},{4,0},{8,12},{12,8},{16,20},{20,16},{24,28},{28,24},{1,5},{5... | collective-permute-start | bytes 1572872 | tf_op jit(solution)/shard_map/ppermute | solution.py:196
  13.7 24.3 %collective-permute-start.6 = (bf16[4,4,32,512]{3,2,1,0:T(8,128)(2,1)}, bf16[4,4,32,512]{3,2,1,0:T(8,128)(2,1)}, u32[]{:S(2)}, u32[]{:S(2)}) collective-permute-start(bf16[4,4,32,512]{3,2,1,0:T(8,128)(2,1)} %get-tuple-element.13), channel_id=1, source_target_pairs={{0,4},{4,0},{8,12},{12,8},{16,20},{20,16},{24,28},{28,24},{1,5},{5... | collective-permute-start | bytes 1572872 | tf_op jit(solution)/shard_map/ppermute | solution.py:196
  13.8 35.5 %collective-permute-start.12 = (bf16[4,4,32,512]{3,2,1,0:T(8,128)(2,1)S(1)}, bf16[4,4,32,512]{3,2,1,0:T(8,128)(2,1)}, u32[]{:S(2)}, u32[]{:S(2)}) collective-permute-start(bf16[4,4,32,512]{3,2,1,0:T(8,128)(2,1)S(1)} %get-tuple-element.15), channel_id=1, source_target_pairs={{0,4},{4,0},{8,12},{12,8},{16,20},{20,16},{24,28},{28,24},{1,5},{5... | collective-permute-start | bytes 1572872 | tf_op jit(solution)/shard_map/ppermute | solution.py:196
  15.7 43.9 %collective-permute-start.18 = (bf16[4,4,32,512]{3,2,1,0:T(8,128)(2,1)S(1)}, bf16[4,4,32,512]{3,2,1,0:T(8,128)(2,1)}, u32[]{:S(2)}, u32[]{:S(2)}) collective-permute-start(bf16[4,4,32,512]{3,2,1,0:T(8,128)(2,1)S(1)} %get-tuple-element.17), channel_id=1, source_target_pairs={{0,4},{4,0},{8,12},{12,8},{16,20},{20,16},{24,28},{28,24},{1,5},{5... | collective-permute-start | bytes 1572872 | tf_op jit(solution)/shard_map/ppermute | solution.py:196
  28.0 34.8 %collective-permute-start.1 = (bf16[2,4,32,512]{3,2,1,0:T(8,128)(2,1)S(1)}, bf16[2,4,32,512]{3,2,1,0:T(8,128)(2,1)S(1)}, u32[]{:S(2)}, u32[]{:S(2)}) collective-permute-start(bf16[2,4,32,512]{3,2,1,0:T(8,128)(2,1)S(1)} %slice.123), channel_id=1, source_target_pairs={{0,8},{4,12},{8,0},{12,4},{16,24},{20,28},{24,16},{28,20},{1,9},{5... | collective-permute-start | bytes 786440 | tf_op jit(solution)/shard_map/ppermute | solution.py:196
  39.3 26.3 %collective-permute-start.7 = (bf16[2,4,32,512]{3,2,1,0:T(8,128)(2,1)S(1)}, bf16[2,4,32,512]{3,2,1,0:T(8,128)(2,1)S(1)}, u32[]{:S(2)}, u32[]{:S(2)}) collective-permute-start(bf16[2,4,32,512]{3,2,1,0:T(8,128)(2,1)S(1)} %slice.122), channel_id=1, source_target_pairs={{0,8},{4,12},{8,0},{12,4},{16,24},{20,28},{24,16},{28,20},{1,9},{5... | collective-permute-start | bytes 786440 | tf_op jit(solution)/shard_map/ppermute | solution.py:196
  50.5 15.6 %collective-permute-start.13 = (bf16[2,4,32,512]{3,2,1,0:T(8,128)(2,1)S(1)}, bf16[2,4,32,512]{3,2,1,0:T(8,128)(2,1)S(1)}, u32[]{:S(2)}, u32[]{:S(2)}) collective-permute-start(bf16[2,4,32,512]{3,2,1,0:T(8,128)(2,1)S(1)} %slice.121), channel_id=1, source_target_pairs={{0,8},{4,12},{8,0},{12,4},{16,24},{20,28},{24,16},{28,20},{1,9},{5... | collective-permute-start | bytes 786440 | tf_op jit(solution)/shard_map/ppermute | solution.py:196
  60.9 12.1 %collective-permute-start.19 = (bf16[2,4,32,512]{3,2,1,0:T(8,128)(2,1)S(1)}, bf16[2,4,32,512]{3,2,1,0:T(8,128)(2,1)S(1)}, u32[]{:S(2)}, u32[]{:S(2)}) collective-permute-start(bf16[2,4,32,512]{3,2,1,0:T(8,128)(2,1)S(1)} %slice.120), channel_id=1, source_target_pairs={{0,8},{4,12},{8,0},{12,4},{16,24},{20,28},{24,16},{28,20},{1,9},{5... | collective-permute-start | bytes 786440 | tf_op jit(solution)/shard_map/ppermute | solution.py:196
  65.7 18.4 %collective-permute-start.8 = (bf16[1,4,32,512]{3,2,1,0:T(8,128)(2,1)S(1)}, bf16[1,4,32,512]{3,2,1,0:T(8,128)(2,1)S(1)}, u32[]{:S(2)}, u32[]{:S(2)}) collective-permute-start(bf16[1,4,32,512]{3,2,1,0:T(8,128)(2,1)S(1)} %slice.126), channel_id=1, source_target_pairs={{0,16},{4,20},{8,24},{12,28},{16,0},{20,4},{24,8},{28,12},{1,17},{... | collective-permute-start | bytes 393224 | tf_op jit(solution)/shard_map/ppermute | solution.py:196
  66.2 20.7 %collective-permute-start.14 = (bf16[1,4,32,512]{3,2,1,0:T(8,128)(2,1)S(1)}, bf16[1,4,32,512]{3,2,1,0:T(8,128)(2,1)S(1)}, u32[]{:S(2)}, u32[]{:S(2)}) collective-permute-start(bf16[1,4,32,512]{3,2,1,0:T(8,128)(2,1)S(1)} %slice.125), channel_id=1, source_target_pairs={{0,16},{4,20},{8,24},{12,28},{16,0},{20,4},{24,8},{28,12},{1,17},{... | collective-permute-start | bytes 393224 | tf_op jit(solution)/shard_map/ppermute | solution.py:196
  73.1 15.4 %collective-permute-start.20 = (bf16[1,4,32,512]{3,2,1,0:T(8,128)(2,1)S(1)}, bf16[1,4,32,512]{3,2,1,0:T(8,128)(2,1)S(1)}, u32[]{:S(2)}, u32[]{:S(2)}) collective-permute-start(bf16[1,4,32,512]{3,2,1,0:T(8,128)(2,1)S(1)} %slice.124), channel_id=1, source_target_pairs={{0,16},{4,20},{8,24},{12,28},{16,0},{20,4},{24,8},{28,12},{1,17},{... | collective-permute-start | bytes 393224 | tf_op jit(solution)/shard_map/ppermute | solution.py:196
  74.5 15.5 %collective-permute-start.4 = (bf16[4,32,512]{2,1,0:T(8,128)(2,1)S(1)}, bf16[4,32,512]{2,1,0:T(8,128)(2,1)S(1)}, u32[]{:S(2)}, u32[]{:S(2)}) collective-permute-start(bf16[4,32,512]{2,1,0:T(8,128)(2,1)S(1)} %fusion.4.refs_0_), channel_id=1, source_target_pairs={{0,2},{1,3},{2,0},{3,1},{4,6},{5,7},{6,4},{7,5},{8,10},{9,11},{10,... | collective-permute-start | bytes 393224 | tf_op jit(solution)/shard_map/ppermute | solution.py:196
  76.1 14.0 %collective-permute-start.3 = (bf16[4,32,512]{2,1,0:T(8,128)(2,1)S(1)}, bf16[4,32,512]{2,1,0:T(8,128)(2,1)S(1)}, u32[]{:S(2)}, u32[]{:S(2)}) collective-permute-start(bf16[4,32,512]{2,1,0:T(8,128)(2,1)S(1)} %fusion.4.refs_0_), channel_id=1, source_target_pairs={{0,1},{1,0},{2,3},{3,2},{4,5},{5,4},{6,7},{7,6},{8,9},{9,8},{10,11... | collective-permute-start | bytes 393224 | tf_op jit(solution)/shard_map/ppermute | solution.py:196
  101.0 15.3 %collective-permute-start.34 = (bf16[4,32,512]{2,1,0:T(8,128)(2,1)S(1)}, bf16[4,32,512]{2,1,0:T(8,128)(2,1)S(1)}, u32[]{:S(2)}, u32[]{:S(2)}) collective-permute-start(bf16[4,32,512]{2,1,0:T(8,128)(2,1)S(1)} %shard_map.98.refs_0_), channel_id=1, source_target_pairs={{0,16},{4,20},{8,24},{12,28},{16,0},{20,4},{24,8},{28,12},{1,17},{... | collective-permute-start | bytes 393224 | tf_op jit(solution)/shard_map/ppermute | solution.py:196
  101.8 14.5 %collective-permute-start.33 = (bf16[4,32,512]{2,1,0:T(8,128)(2,1)S(1)}, bf16[4,32,512]{2,1,0:T(8,128)(2,1)S(1)}, u32[]{:S(2)}, u32[]{:S(2)}) collective-permute-start(bf16[4,32,512]{2,1,0:T(8,128)(2,1)S(1)} %shard_map.98.refs_0_), channel_id=1, source_target_pairs={{0,8},{4,12},{8,0},{12,4},{16,24},{20,28},{24,16},{28,20},{1,9},{5... | collective-permute-start | bytes 393224 | tf_op jit(solution)/shard_map/ppermute | solution.py:196
  104.3 15.0 %collective-permute-start.30 = (bf16[4,32,512]{2,1,0:T(8,128)(2,1)S(1)}, bf16[4,32,512]{2,1,0:T(8,128)(2,1)S(1)}, u32[]{:S(2)}, u32[]{:S(2)}) collective-permute-start(bf16[4,32,512]{2,1,0:T(8,128)(2,1)S(1)} %shard_map.99.refs_0_), channel_id=1, source_target_pairs={{0,16},{4,20},{8,24},{12,28},{16,0},{20,4},{24,8},{28,12},{1,17},{... | collective-permute-start | bytes 393224 | tf_op jit(solution)/shard_map/ppermute | solution.py:196
  105.2 16.8 %collective-permute-start.25 = (bf16[4,32,512]{2,1,0:T(8,128)(2,1)S(1)}, bf16[4,32,512]{2,1,0:T(8,128)(2,1)S(1)}, u32[]{:S(2)}, u32[]{:S(2)}) collective-permute-start(bf16[4,32,512]{2,1,0:T(8,128)(2,1)S(1)} %shard_map.100.refs_0_), channel_id=1, source_target_pairs={{0,16},{4,20},{8,24},{12,28},{16,0},{20,4},{24,8},{28,12},{1,17},{... | collective-permute-start | bytes 393224 | tf_op jit(solution)/shard_map/ppermute | solution.py:196
  107.3 14.7 %collective-permute-start.39 = (bf16[4,32,512]{2,1,0:T(8,128)(2,1)S(1)}, bf16[4,32,512]{2,1,0:T(8,128)(2,1)S(1)}, u32[]{:S(2)}, u32[]{:S(2)}) collective-permute-start(bf16[4,32,512]{2,1,0:T(8,128)(2,1)S(1)} %collective-permute-done.38.refs_2_), channel_id=1, source_target_pairs={{0,8},{4,12},{8,0},{12,4},{16,24},{20,28},{24,16},{28,20},{1,9},{5... | collective-permute-start | bytes 393224 | tf_op jit(solution)/shard_map/ppermute | solution.py:196
  116.3 14.7 %collective-permute-start.29 = (bf16[4,32,512]{2,1,0:T(8,128)(2,1)S(1)}, bf16[4,32,512]{2,1,0:T(8,128)(2,1)S(1)}, u32[]{:S(2)}, u32[]{:S(2)}) collective-permute-start(bf16[4,32,512]{2,1,0:T(8,128)(2,1)S(1)} %shard_map.99.refs_0_), channel_id=1, source_target_pairs={{0,8},{4,12},{8,0},{12,4},{16,24},{20,28},{24,16},{28,20},{1,9},{5... | collective-permute-start | bytes 393224 | tf_op jit(solution)/shard_map/ppermute | solution.py:196
  116.3 17.5 %collective-permute-start.24 = (bf16[4,32,512]{2,1,0:T(8,128)(2,1)S(1)}, bf16[4,32,512]{2,1,0:T(8,128)(2,1)S(1)}, u32[]{:S(2)}, u32[]{:S(2)}) collective-permute-start(bf16[4,32,512]{2,1,0:T(8,128)(2,1)S(1)} %shard_map.100.refs_0_), channel_id=1, source_target_pairs={{0,8},{4,12},{8,0},{12,4},{16,24},{20,28},{24,16},{28,20},{1,9},{5... | collective-permute-start | bytes 393224 | tf_op jit(solution)/shard_map/ppermute | solution.py:196
  122.0 11.8 %collective-permute-start.26 = (bf16[4,32,512]{2,1,0:T(8,128)(2,1)S(1)}, bf16[4,32,512]{2,1,0:T(8,128)(2,1)S(1)}, u32[]{:S(2)}, u32[]{:S(2)}) collective-permute-start(bf16[4,32,512]{2,1,0:T(8,128)(2,1)S(1)} %collective-permute-done.25.refs_2_), channel_id=1, source_target_pairs={{0,8},{4,12},{8,0},{12,4},{16,24},{20,28},{24,16},{28,20},{1,9},{5... | collective-permute-start | bytes 393224 | tf_op jit(solution)/shard_map/ppermute | solution.py:196
  131.0 14.3 %collective-permute-start.36 = (bf16[8,32,512]{2,1,0:T(8,128)(2,1)S(1)}, bf16[8,32,512]{2,1,0:T(8,128)(2,1)S(1)}, u32[]{:S(2)}, u32[]{:S(2)}) collective-permute-start(bf16[8,32,512]{2,1,0:T(8,128)(2,1)S(1)} %shard_map.103), channel_id=1, source_target_pairs={{0,4},{4,0},{8,12},{12,8},{16,20},{20,16},{24,28},{28,24},{1,5},{5... | collective-permute-start | bytes 786440 | tf_op jit(solution)/shard_map/ppermute | solution.py:196
  133.7 15.3 %collective-permute-start.32 = (bf16[8,32,512]{2,1,0:T(8,128)(2,1)S(1)}, bf16[8,32,512]{2,1,0:T(8,128)(2,1)S(1)}, u32[]{:S(2)}, u32[]{:S(2)}) collective-permute-start(bf16[8,32,512]{2,1,0:T(8,128)(2,1)S(1)} %shard_map.102), channel_id=1, source_target_pairs={{0,4},{4,0},{8,12},{12,8},{16,20},{20,16},{24,28},{28,24},{1,5},{5... | collective-permute-start | bytes 786440 | tf_op jit(solution)/shard_map/ppermute | solution.py:196
  134.4 17.4 %collective-permute-start.28 = (bf16[8,32,512]{2,1,0:T(8,128)(2,1)S(1)}, bf16[8,32,512]{2,1,0:T(8,128)(2,1)S(1)}, u32[]{:S(2)}, u32[]{:S(2)}) collective-permute-start(bf16[8,32,512]{2,1,0:T(8,128)(2,1)S(1)} %shard_map.101), channel_id=1, source_target_pairs={{0,4},{4,0},{8,12},{12,8},{16,20},{20,16},{24,28},{28,24},{1,5},{5... | collective-permute-start | bytes 786440 | tf_op jit(solution)/shard_map/ppermute | solution.py:196
  (25 other events, 162.7 us)

commit v2 on v1

v2 whole, which is shorter than its diff:
```python
import jax
import jax.numpy as jnp
from jax import lax
from jax.experimental import pallas as pl
from jax.experimental.pallas import tpu as pltpu
from jax.sharding import PartitionSpec as P

SHARES = (1, 2, 2, 2, 1)
READ_CAP = 2
VMEM_BYTES = 40 * 1024 * 1024
UNIT_TIME, STEP_TIME, LATENCY = 10.5, 0.7, 1.5

SMEM = pl.BlockSpec(memory_space=pltpu.SMEM)
VMEM = pl.BlockSpec(memory_space=pltpu.VMEM)
ANY = pl.BlockSpec(memory_space=pl.ANY)
TOKEN = jax.ShapeDtypeStruct((8, 128), jnp.float32)


def call(body, out_shape, in_specs, out_specs, operands, scratch=(), aliases=None, flops=0):
    moved = sum(a.size * a.dtype.itemsize for a in [*operands, *out_shape])
    return pl.pallas_call(
        body,
        out_shape=out_shape,
        in_specs=in_specs,
        out_specs=out_specs,
        scratch_shapes=list(scratch),
        input_output_aliases=aliases or {},
        compiler_params=pltpu.CompilerParams(vmem_limit_bytes=VMEM_BYTES),
        cost_estimate=pl.CostEstimate(flops=flops, bytes_accessed=moved, transcendentals=0),
    )(*operands)


def split(value, size):
    if size & (size - 1) == 0:
        return value >> (size.bit_length() - 1), value & (size - 1)
    return lax.div(value, size), lax.rem(value, size)


def reversed_bits(value, bits):
    result = value & 1
    for i in range(1, bits):
        result = (result << 1) | ((value >> i) & 1)
    return result


def multiply_owner(table, base, tiles, inputs, lhs, outs, index, spans, row_base, blocks, block):
    for b in range(blocks):
        for c in range(blocks):
            entry = table[base + b * blocks + c]
            tile = tiles[jnp.maximum(entry - 1, 0)]
            tile = jnp.where(entry > 0, tile, jnp.zeros_like(tile))
            at = 0
            for first, rows in spans:
                lhs[pl.ds(at + b * rows, rows), pl.ds(c * block, block)] = tile[first - row_base : first - row_base + rows]
                at += blocks * rows
    total = jnp.dot(lhs[...], inputs[...], preferred_element_type=jnp.float32).astype(jnp.bfloat16)
    at = 0
    for out, (first, rows) in zip(outs, spans):
        out[index] = total[at : at + blocks * rows].reshape(blocks, rows, total.shape[1])
        at += blocks * rows


def first_part(me, slot, col, tile_id, touched, tiles, features, first, count, span):
    block = tiles.shape[1]
    blocks = features.shape[0] // block
    width = features.shape[1]
    edges, cap = touched.shape[1], touched.shape[2]
    bits = edges.bit_length() - 1
    products = slot.shape[0]
    start, rows = span
    square = blocks * blocks

    def body(me_ref, slot_ref, col_ref, id_ref, touched_ref, tiles_hbm, x_hbm, table, out, x_out, tiles_ref, lhs, bases, sems):
        load_tiles = pltpu.make_async_copy(tiles_hbm.at[:, pl.ds(start, rows)], tiles_ref, sems.at[0])
        load_x = pltpu.make_async_copy(x_hbm, x_out, sems.at[1])
        load_tiles.start()
        load_x.start()

        def clear(i, carry):
            table[i] = 0
            return carry

        lax.fori_loop(0, edges * square, clear, 0, unroll=16)

        def place_slot(k, carry):
            owner, entry = split(k, cap)
            place = reversed_bits(owner ^ me_ref[0], bits)
            bases[k] = (place * blocks + touched_ref[k]) * blocks
            return carry

        lax.fori_loop(0, edges * cap, place_slot, 0, unroll=8)

        def enter(k, carry):
            table[bases[slot_ref[k]] + col_ref[k]] = id_ref[k] + 1
            return carry

        lax.fori_loop(0, products, enter, 0, unroll=8)
        load_tiles.wait()
        load_x.wait()

        def one_owner(i, carry):
            multiply_owner(
                table, (first + i) * square, tiles_ref, x_out, lhs, [out], i, [span], start, blocks, block
            )
            return carry

        lax.fori_loop(0, count, one_owner, 0)

    return call(
        body,
        [
            jax.ShapeDtypeStruct((edges * square,), jnp.int32),
            jax.ShapeDtypeStruct((count, blocks, rows, width), jnp.bfloat16),
            jax.ShapeDtypeStruct(features.shape, jnp.bfloat16),
        ],
        [SMEM] * 5 + [ANY] * 2,
        [SMEM, VMEM, VMEM],
        (me, slot, col, tile_id, touched[me[0]].reshape(-1), tiles, features),
        [
            pltpu.VMEM((tiles.shape[0], rows, block), jnp.bfloat16),
            pltpu.VMEM((blocks * rows, blocks * block), jnp.bfloat16),
            pltpu.SMEM((edges * cap,), jnp.int32),
            pltpu.SemaphoreType.DMA((2,)),
        ],
        flops=2 * count * blocks * rows * blocks * block * width,
    )


def other_parts(table, tiles, inputs, first, count, spans):
    block = tiles.shape[1]
    blocks = inputs.shape[0] // block
    width = inputs.shape[1]
    total_rows = sum(rows for _, rows in spans)

    def body(table_ref, tiles_hbm, x_ref, *refs):
        outs = refs[: len(spans)]
        tiles_ref, lhs, sem = refs[len(spans) :]
        load = pltpu.make_async_copy(tiles_hbm, tiles_ref, sem.at[0])
        load.start()
        load.wait()

        def one_owner(i, carry):
            base = (first + i) * blocks * blocks
            multiply_owner(table_ref, base, tiles_ref, x_ref, lhs, outs, i, spans, 0, blocks, block)
            return carry

        lax.fori_loop(0, count, one_owner, 0)

    return call(
        body,
        [jax.ShapeDtypeStruct((count, blocks, rows, width), jnp.bfloat16) for _, rows in spans],
        [SMEM, ANY, VMEM],
        [VMEM] * len(spans),
        (table, tiles, inputs),
        [
            pltpu.VMEM(tiles.shape, jnp.bfloat16),
            pltpu.VMEM((blocks * total_rows, blocks * block), jnp.bfloat16),
            pltpu.SemaphoreType.DMA((1,)),
        ],
        flops=2 * count * blocks * total_rows * blocks * block * width,
    )


def combine(token, total, got):
    count = total.shape[0]
    left = count // 2

    def body(token_ref, total_ref, got_ref, *outs):
        value = total_ref[...].astype(jnp.float32) + got_ref[...].astype(jnp.float32)
        if left:
            outs[0][...] = value[:left]
            outs[1][...] = value[left:].astype(jnp.bfloat16)
        else:
            outs[0][...] = value[0].astype(jnp.bfloat16)
        outs[-1][...] = token_ref[...]

    shape = total.shape[1:]
    if left:
        out_shape = [
            jax.ShapeDtypeStruct((left, *shape), jnp.float32),
            jax.ShapeDtypeStruct((count - left, *shape), jnp.bfloat16),
        ]
    else:
        out_shape = [jax.ShapeDtypeStruct(shape, jnp.bfloat16)]
    out_shape.append(TOKEN)
    return call(body, out_shape, [VMEM] * 3, [VMEM] * len(out_shape), (token, total, got))


def relay(token, values):
    def body(token_ref, *refs):
        for source, target in zip(refs[: len(values)], refs[len(values) :]):
            target[...] = source[...]
        refs[-1][...] = token_ref[...]

    out_shape = [jax.ShapeDtypeStruct(v.shape, v.dtype) for v in values] + [TOKEN]
    *copies, token = call(body, out_shape, [VMEM] * (1 + len(values)), [VMEM] * len(out_shape), (token, *values))
    return copies, token


def mix(token, mine, pieces, weight):
    blocks, rows, depth = pieces[0].shape
    width = weight.shape[1]

    def body(token_ref, mine_ref, w_ref, *refs):
        out_ref, token_out = refs[-2:]
        total = jnp.zeros((blocks * rows, width), jnp.float32)
        for j, piece in enumerate(refs[:-2]):
            at = pl.multiple_of((mine_ref[0] ^ j) * depth, depth)
            total += jnp.dot(
                piece[...].reshape(blocks * rows, depth),
                w_ref[pl.ds(at, depth)],
                preferred_element_type=jnp.float32,
            )
        out_ref[...] = jnp.maximum(total, 0.0).astype(jnp.bfloat16).reshape(out_ref.shape)
        token_out[...] = token_ref[...]

    return call(
        body,
        [jax.ShapeDtypeStruct((blocks, rows, width), jnp.bfloat16), TOKEN],
        [VMEM, SMEM] + [VMEM] * (1 + len(pieces)),
        [VMEM] * 2,
        (token, mine, weight, *pieces),
        flops=2 * len(pieces) * pieces[0].size * width,
    )


def pick(token, choice, near):
    count = choice.shape[0]

    def body(token_ref, choice_ref, *refs):
        for i in range(count):
            refs[-2][i] = refs[i // READ_CAP][choice_ref[i]]
        refs[-1][...] = token_ref[...]

    return call(
        body,
        [jax.ShapeDtypeStruct((count, *near[0].shape[1:]), near[0].dtype), TOKEN],
        [VMEM, SMEM] + [VMEM] * len(near),
        [VMEM] * 2,
        (token, choice, *near),
    )


def lay_out(token, place, near, far, outputs, span, block):
    count = place.shape[0]
    blocks, _, width = near[0].shape
    start, rows = span
    near_count = len(near) * blocks

    def body(token_ref, place_ref, *refs):
        sources, far_ref = refs[: len(near)], refs[len(near)]
        hidden_ref, ghost_ref, token_out, sems = refs[-4:]

        def target(r):
            return ghost_ref.at[r, pl.ds(start, rows)]

        own = pltpu.make_async_copy(sources[0], hidden_ref.at[:, pl.ds(start, rows)], sems.at[count])
        own.start()
        for r in range(count):
            spot = place_ref[r]
            which, within = split(spot, blocks)
            for i, source in enumerate(sources):

                @pl.when(which == i)
                def _():
                    pltpu.make_async_copy(source.at[within], target(r), sems.at[r]).start()

            @pl.when(spot >= near_count)
            def _():
                pltpu.make_async_copy(far_ref.at[spot - near_count], target(r), sems.at[r]).start()

        token_out[...] = token_ref[...]
        own.wait()
        for r in range(count):
            pltpu.make_async_copy(far_ref.at[0], target(r), sems.at[r]).wait()

    operands = (token, place, *near, far, *outputs)
    return call(
        body,
        [
            jax.ShapeDtypeStruct((blocks, block, width), jnp.bfloat16),
            jax.ShapeDtypeStruct((count, block, width), jnp.bfloat16),
            TOKEN,
        ],
        [VMEM, SMEM] + [VMEM] * (len(near) + 1) + [ANY] * len(outputs),
        [ANY, ANY, VMEM],
        operands,
        [pltpu.SemaphoreType.DMA((count + 1,))],
        aliases={len(operands) - 2: 0, len(operands) - 1: 1} if outputs else None,
    )


def local(features, tiles, tile_slot, tile_col, tile_id, touched, weight, readers):
    edges, feats = lax.axis_size("edge"), lax.axis_size("feat")
    half = edges // 2
    me, mine = lax.axis_index("edge"), lax.axis_index("feat")
    block = tiles.shape[1]
    blocks = features.shape[0] // block
    width = features.shape[1]

    def flip(value, bit, axis="edge"):
        return lax.ppermute(value, axis, [(d, d ^ bit) for d in range(lax.axis_size(axis))])

    order = jnp.arange(readers.shape[0], dtype=jnp.int32)

    def ranks(listed):
        same = (listed[:, None] // blocks) == (listed[None, :] // blocks)
        return jnp.sum((same & (order[None, :] < order[:, None])).astype(jnp.int32), axis=1)

    other = flip(readers, 1)
    entries = jnp.arange(half * READ_CAP, dtype=jnp.int32)
    wanted = lax.bitwise_xor(2 * (entries // READ_CAP), me)
    hit = ((other // blocks)[None, :] == wanted[:, None]) & (ranks(other)[None, :] == (entries % READ_CAP)[:, None])
    choice = jnp.sum(jnp.where(hit, (other % blocks)[None, :], 0), axis=1)
    peer = lax.bitwise_xor(readers // blocks, me)
    place = jnp.where(
        peer % 2 == 0,
        (peer // 2) * blocks + readers % blocks,
        half * blocks + (peer // 2) * READ_CAP + ranks(readers),
    )

    unit = block // sum(SHARES)
    spans = [(sum(SHARES[:i]) * unit, share * unit) for i, share in enumerate(SHARES)]
    table, early, inputs = first_part(
        me.reshape(1), tile_slot, tile_col, tile_id, touched, tiles, features, half, half, spans[0]
    )
    away = [early, *other_parts(table, tiles, inputs, half, half, spans[1:])]
    kept = other_parts(table, tiles, inputs, 0, half, spans)

    state = {"token": jnp.zeros(TOKEN.shape, TOKEN.dtype), "outputs": ()}

    def chained(function, *operands):
        *results, state["token"] = function(state["token"], *operands)
        return results

    def spread(value, size, lowest, axis, link, share):
        bits = [1 << i for i in reversed(range(size.bit_length() - 1)) if 1 << i >= lowest]
        held, sources = {0: value}, {0: value}
        while sources:
            fresh = {}
            for j, source in sources.items():
                for bit in bits:
                    if j == 0 or bit < (j & -j):
                        fresh[j | bit] = flip(source, bit, axis)
            held.update(fresh)
            yield link, share * len(fresh)
            onward = [j for j in fresh if any(bit < (j & -j) for bit in bits)]
            if not onward:
                break
            copies, state["token"] = relay(state["token"], [fresh[j] for j in onward])
            sources = dict(zip(onward, copies))
        return [held[j] for j in sorted(held)]

    def one_part(part):
        share = spans[part][1] / block
        got = flip(away[part], 1)
        yield "low", share * half
        total, sent = chained(combine, kept[part], got)
        bit = 2
        while bit < edges:
            got = flip(sent, bit)
            yield "high", share * 2
            total, *sent = chained(combine, total, got)
            sent = sent[0] if sent else None
            bit *= 2
        pieces = yield from spread(total, feats, 1, "feat", "feat", share / 2)
        (mixed,) = chained(mix, mine.reshape(1), pieces, weight)
        near = yield from spread(mixed, edges, 2, "edge", "high", share)
        (picked,) = chained(pick, choice, near)
        far = flip(picked, 1)
        yield "low", share * 2
        state["outputs"] = chained(lay_out, place, near, far, state["outputs"], spans[part], block)

    now, free, waiting = 0.0, {"low": 0.0, "high": 0.0, "feat": 0.0}, []

    def advance(part, steps):
        nonlocal now
        link, units = next(steps, (None, 0))
        if link is not None:
            now += STEP_TIME
            free[link] = max(free[link], now) + units * UNIT_TIME
            waiting.append((free[link] + LATENCY, part, steps))

    for part in range(len(spans)):
        advance(part, one_part(part))
    while waiting:
        ready, part, steps = min(waiting, key=lambda item: item[:2])
        waiting = [item for item in waiting if item[1] != part]
        now = max(now, ready)
        advance(part, steps)
    hidden, ghosts = state["outputs"]
    return hidden.reshape(blocks * block, width), ghosts.reshape(-1, width)


def solution(mesh):
    in_specs = (
        P("edge", "feat"),
        P("edge", None, None),
        P("edge"),
        P("edge"),
        P("edge"),
        P(),
        P(None, "feat"),
        P("edge"),
    )
    out_specs = (P("edge", "feat"), P("edge", "feat"))
    return jax.shard_map(local, mesh=mesh, in_specs=in_specs, out_specs=out_specs, check_vma=False)
```

time: 154 us -> 158 us (1.026)
  Pallas kernels: 18.7 us -> 25.1 us
  other arithmetic: 6.65 us -> 1.13 us
  starting transfers between devices: 44.9 us -> 49.8 us
  waiting for transfers between devices: 76.5 us -> 73.2 us
  local copies, waits for them, and re-layouts: 5.52 us -> 7.36 us
    pallas_call x14 -> x43, Pallas kernels: 18.7 us -> 25.1 us  [call(): pl.pallas_call(body, out_shape=out_shape, in_specs=in_specs, out_specs=ou...]
    add x8 -> x0, other arithmetic: 5.11 us -> none  [the longest x4 4.79 us: local(): kept[part].astype(jnp.float32) + flip(away[part], 1).astype(jnp.float32)]
    ppermute x41 -> x51, starting transfers between devices: 44.9 us -> 49.8 us  [flip(): lax.ppermute(value, axis, [(d, d ^ bit) for d in range(lax.axis_size(axis...]
    ppermute x41 -> x51, waiting for transfers between devices: 76.5 us -> 73.2 us  [flip(): lax.ppermute(value, axis, [(d, d ^ bit) for d in range(lax.axis_size(axis...]
    unnamed x16 -> x38, local copies, waits for them, and re-layouts: 5.14 us -> 7.19 us
  transfers between devices with their start and end apart: 41 -> 51, of which waited for: 20 -> 23; matrix products, arithmetic and copies ran while one was open for 4% -> 1% of each run, Pallas kernels for 8% -> 11%
where the time goes in v2:
time: 158 us
  waiting for transfers between devices  73.2 us (46%)
  starting transfers between devices  49.8 us (32%)
  Pallas kernels  25.1 us (16%)
  local copies, waits for them, and re-layouts  7.36 us (5%)
    ppermute x51, waiting for transfers between devices, flip(): lax.ppermute(value, axis, [(d, d ^ bit) for d in range(lax.axis_size(axis...  73.2 us
    ppermute x51, starting transfers between devices, flip(): lax.ppermute(value, axis, [(d, d ^ bit) for d in range(lax.axis_size(axis...  49.8 us
    pallas_call x43, Pallas kernels, call(): pl.pallas_call(body, out_shape=out_shape, in_specs=in_specs, out_specs=ou...  25.1 us
    unnamed x38, local copies, waits for them, and re-layouts  7.19 us
  transfers between devices with their start and end apart: 51, of which 23 were waited for; matrix products, arithmetic and copies ran while one was open for 1% of the time, Pallas kernels for 11%

profile of v2, /device:TPU:0, one launch (start us, length us, event | category | flops | bytes accessed | tf_op | source)
XLA Modules:
  0.0 157.7 jit_solution(15545802444952195902)
XLA Ops:
  5.9 2.6 %shard_map.95 = (s32[128]{0:T(128)S(1)}, bf16[4,4,16,512]{3,2,1,0:T(8,128)(2,1)S(1)}, bf16[512,512]{1,0:T(8,128)(2,1)S(1)}) custom-call(s32[1]{0:T(128)} %bitcast.me_ref, s32[96]{0:T(128)S(1)} %copy-done.11, s32[96]{0:T(128)S(1)} %copy-done.12, s32[96]{0:T(128)S(1)} %copy-done.13, s32[32]{0:T(128)S(1)} %reshape_squeeze.3.touched_ref, ...), custom_call_target="tpu_custom_call" | custom-call | flops 134217728 | bytes 2885380 | tf_op jit(solution)/shard_map/pallas_call | solution.py:21
  8.5 3.3 %shard_map.100 = (bf16[4,4,32,512]{3,2,1,0:T(8,128)(2,1)S(1)}, bf16[4,4,32,512]{3,2,1,0:T(8,128)(2,1)}, bf16[4,4,32,512]{3,2,1,0:T(8,128)(2,1)}, bf16[4,4,16,512]{3,2,1,0:T(8,128)(2,1)S(1)}) custom-call(s32[128]{0:T(128)S(1)} %get-tuple-element.108.table_ref, bf16[48,128,128]{2,1,0:T(8,128)(2,1)S(1)} %copy-done.3, bf16[512,512]{1,0:T(8,128)(2,1)S(1)} %get-tuple-element.109.x_ref), custom_call_target="tpu_custom_call" | custom-call | flops 939524096 | bytes 3932672 | tf_op jit(solution)/shard_map/pallas_call | solution.py:21
  12.5 2.9 %collective-permute-start.3 = (bf16[4,4,32,512]{3,2,1,0:T(8,128)(2,1)S(1)}, bf16[4,4,32,512]{3,2,1,0:T(8,128)(2,1)S(1)}, u32[]{:S(2)}, u32[]{:S(2)}) collective-permute-start(bf16[4,4,32,512]{3,2,1,0:T(8,128)(2,1)S(1)} %get-tuple-element.120), channel_id=1, source_target_pairs={{0,4},{4,0},{8,12},{12,8},{16,20},{20,16},{24,28},{28,24},{1,5},{5... | collective-permute-start | bytes 1572872 | tf_op jit(solution)/shard_map/ppermute | solution.py:302
  15.5 2.5 %shard_map.96 = (bf16[4,4,16,512]{3,2,1,0:T(8,128)(2,1)S(1)}, bf16[4,4,32,512]{3,2,1,0:T(8,128)(2,1)S(1)}, bf16[4,4,32,512]{3,2,1,0:T(8,128)(2,1)S(1)}, bf16[4,4...) custom-call(s32[128]{0:T(128)S(1)} %get-tuple-element.108.table_ref, bf16[48,128,128]{2,1,0:T(8,128)(2,1)S(1)} %copy-done.3, ...), custom_call_target="tpu_custom_call" | custom-call | flops 1073741824 | bytes 4194816 | tf_op jit(solution)/shard_map/pallas_call | solution.py:21
  18.0 15.0 %collective-permute-done.got_ref = bf16[4,4,16,512]{3,2,1,0:T(8,128)(2,1)S(1)} collective-permute-done((bf16[4,4,16,512]{3,2,1,0:T(8,128)(2,1)S(1)}, bf16[4,4,16,512]{3,2,1,0:T(8,128)(2,1)S(1)}, u32[]{:S(2)}, u32[]{:S(2)}) %collective-permute-start) | collective-permute-done | bytes 262176 | tf_op jit(solution)/shard_map/ppermute | solution.py:302
  34.9 3.1 %collective-permute-done.1.got_ref = bf16[2,4,16,512]{3,2,1,0:T(8,128)(2,1)S(1)} collective-permute-done((bf16[2,4,16,512]{3,2,1,0:T(8,128)(2,1)S(1)}, bf16[2,4,16,512]{3,2,1,0:T(8,128)(2,1)S(1)}, u32[]{:S(2)}, u32[]{:S(2)}) %collective-permute-start.1) | collective-permute-done | bytes 131104 | tf_op jit(solution)/shard_map/ppermute | solution.py:302
  38.1 2.9 %collective-permute-start.2 = (bf16[1,4,16,512]{3,2,1,0:T(8,128)(2,1)S(1)}, bf16[1,4,16,512]{3,2,1,0:T(8,128)(2,1)S(1)}, u32[]{:S(2)}, u32[]{:S(2)}) collective-permute-start(bf16[1,4,16,512]{3,2,1,0:T(8,128)(2,1)S(1)} %get-tuple-element.117), channel_id=1, source_target_pairs={{0,16},{4,20},{8,24},{12,28},{16,0},{20,4},{24,8},{28,12},{1,17},{... | collective-permute-start | bytes 196616 | tf_op jit(solution)/shard_map/ppermute | solution.py:302
  52.0 3.2 %collective-permute-start.8 = (bf16[4,16,512]{2,1,0:T(8,128)(2,1)S(1)}, bf16[4,16,512]{2,1,0:T(8,128)(2,1)S(1)}, u32[]{:S(2)}, u32[]{:S(2)}) collective-permute-start(bf16[4,16,512]{2,1,0:T(8,128)(2,1)S(1)} %get-tuple-element.129.refs_0_), channel_id=1, source_target_pairs={{0,16},{4,20},{8,24},{12,28},{16,0},{20,4},{24,8},{28,12},{1,17},{... | collective-permute-start | bytes 196616 | tf_op jit(solution)/shard_map/ppermute | solution.py:302
  56.0 7.9 %collective-permute-done.11 = s32[16]{0:T(128)S(1)} collective-permute-done((s32[16]{0:T(128)}, s32[16]{0:T(128)S(1)}, u32[]{:S(2)}, u32[]{:S(2)}) %collective-permute-start.11) | collective-permute-done | bytes 96 | tf_op jit(solution)/shard_map/ppermute | solution.py:302
  71.0 3.0 %collective-permute-done.13.refs_3_ = bf16[4,16,512]{2,1,0:T(8,128)(2,1)S(1)} collective-permute-done((bf16[4,16,512]{2,1,0:T(8,128)(2,1)S(1)}, bf16[4,16,512]{2,1,0:T(8,128)(2,1)S(1)}, u32[]{:S(2)}, u32[]{:S(2)}) %collective-permute-start.13) | collective-permute-done | bytes 65568 | tf_op jit(solution)/shard_map/ppermute | solution.py:302
  81.8 2.3 %collective-permute-done.20.got_ref = bf16[2,4,32,512]{3,2,1,0:T(8,128)(2,1)S(1)} collective-permute-done((bf16[2,4,32,512]{3,2,1,0:T(8,128)(2,1)S(1)}, bf16[2,4,32,512]{3,2,1,0:T(8,128)(2,1)S(1)}, u32[]{:S(2)}, u32[]{:S(2)}) %collective-permute-start.20) | collective-permute-done | bytes 262176 | tf_op jit(solution)/shard_map/ppermute | solution.py:302
  85.7 3.3 %collective-permute-done.22.got_ref = bf16[1,4,32,512]{3,2,1,0:T(8,128)(2,1)S(1)} collective-permute-done((bf16[1,4,32,512]{3,2,1,0:T(8,128)(2,1)S(1)}, bf16[1,4,32,512]{3,2,1,0:T(8,128)(2,1)S(1)}, u32[]{:S(2)}, u32[]{:S(2)}) %collective-permute-start.22) | collective-permute-done | bytes 131104 | tf_op jit(solution)/shard_map/ppermute | solution.py:302
  90.0 2.2 %collective-permute-start.25 = (bf16[2,4,16,512]{3,2,1,0:T(8,128)(2,1)S(1)}, bf16[2,4,16,512]{3,2,1,0:T(8,128)(2,1)S(1)}, u32[]{:S(2)}, u32[]{:S(2)}) collective-permute-start(bf16[2,4,16,512]{3,2,1,0:T(8,128)(2,1)S(1)} %get-tuple-element.165), channel_id=1, source_target_pairs={{0,8},{4,12},{8,0},{12,4},{16,24},{20,28},{24,16},{28,20},{1,9},{5... | collective-permute-start | bytes 393224 | tf_op jit(solution)/shard_map/ppermute | solution.py:302
  92.1 2.1 %collective-permute-done.23.refs_0_.refs_2_ = bf16[4,32,512]{2,1,0:T(8,128)(2,1)S(1)} collective-permute-done((bf16[4,32,512]{2,1,0:T(8,128)(2,1)S(1)}, bf16[4,32,512]{2,1,0:T(8,128)(2,1)S(1)}, u32[]{:S(2)}, u32[]{:S(2)}) %collective-permute-start.23) | collective-permute-done | bytes 131104 | tf_op jit(solution)/shard_map/ppermute | solution.py:302
  94.4 6.1 %collective-permute-done.24.refs_0_.refs_2_ = bf16[4,32,512]{2,1,0:T(8,128)(2,1)S(1)} collective-permute-done((bf16[4,32,512]{2,1,0:T(8,128)(2,1)S(1)}, bf16[4,32,512]{2,1,0:T(8,128)(2,1)S(1)}, u32[]{:S(2)}, u32[]{:S(2)}) %collective-permute-start.24) | collective-permute-done | bytes 131104 | tf_op jit(solution)/shard_map/ppermute | solution.py:302
  100.5 2.1 %collective-permute-start.30 = (bf16[4,32,512]{2,1,0:T(8,128)(2,1)S(1)}, bf16[4,32,512]{2,1,0:T(8,128)(2,1)S(1)}, u32[]{:S(2)}, u32[]{:S(2)}) collective-permute-start(bf16[4,32,512]{2,1,0:T(8,128)(2,1)S(1)} %get-tuple-element.172), channel_id=1, source_target_pairs={{0,8},{4,12},{8,0},{12,4},{16,24},{20,28},{24,16},{28,20},{1,9},{5... | collective-permute-start | bytes 393224 | tf_op jit(solution)/shard_map/ppermute | solution.py:302
  104.2 2.6 %collective-permute-done.29.refs_1_ = bf16[4,32,512]{2,1,0:T(8,128)(2,1)S(1)} collective-permute-done((bf16[4,32,512]{2,1,0:T(8,128)(2,1)S(1)}, bf16[4,32,512]{2,1,0:T(8,128)(2,1)S(1)}, u32[]{:S(2)}, u32[]{:S(2)}) %collective-permute-start.29) | collective-permute-done | bytes 131104 | tf_op jit(solution)/shard_map/ppermute | solution.py:302
  111.1 2.6 %collective-permute-start.37 = (bf16[4,32,512]{2,1,0:T(8,128)(2,1)S(1)}, bf16[4,32,512]{2,1,0:T(8,128)(2,1)S(1)}, u32[]{:S(2)}, u32[]{:S(2)}) collective-permute-start(bf16[4,32,512]{2,1,0:T(8,128)(2,1)S(1)} %get-tuple-element.187.refs_0_), channel_id=1, source_target_pairs={{0,16},{4,20},{8,24},{12,28},{16,0},{20,4},{24,8},{28,12},{1,17},{... | collective-permute-start | bytes 393224 | tf_op jit(solution)/shard_map/ppermute | solution.py:302
  113.7 6.0 %collective-permute-done.32.got_ref = bf16[1,4,16,512]{3,2,1,0:T(8,128)(2,1)S(1)} collective-permute-done((bf16[1,4,16,512]{3,2,1,0:T(8,128)(2,1)S(1)}, bf16[1,4,16,512]{3,2,1,0:T(8,128)(2,1)S(1)}, u32[]{:S(2)}, u32[]{:S(2)}) %collective-permute-start.32) | collective-permute-done | bytes 65568 | tf_op jit(solution)/shard_map/ppermute | solution.py:302
  120.6 3.4 %collective-permute-done.35.refs_0_.refs_2_ = bf16[4,16,512]{2,1,0:T(8,128)(2,1)S(1)} collective-permute-done((bf16[4,16,512]{2,1,0:T(8,128)(2,1)S(1)}, bf16[4,16,512]{2,1,0:T(8,128)(2,1)S(1)}, u32[]{:S(2)}, u32[]{:S(2)}) %collective-permute-start.35) | collective-permute-done | bytes 65568 | tf_op jit(solution)/shard_map/ppermute | solution.py:302
  125.7 2.1 %collective-permute-start.44 = (bf16[4,32,512]{2,1,0:T(8,128)(2,1)S(1)}, bf16[4,32,512]{2,1,0:T(8,128)(2,1)S(1)}, u32[]{:S(2)}, u32[]{:S(2)}) collective-permute-start(bf16[4,32,512]{2,1,0:T(8,128)(2,1)S(1)} %get-tuple-element.191.refs_0_), channel_id=1, source_target_pairs={{0,8},{4,12},{8,0},{12,4},{16,24},{20,28},{24,16},{28,20},{1,9},{5... | collective-permute-start | bytes 393224 | tf_op jit(solution)/shard_map/ppermute | solution.py:302
  131.4 7.0 %collective-permute-done.42.refs_3_ = bf16[4,32,512]{2,1,0:T(8,128)(2,1)S(1)} collective-permute-done((bf16[4,32,512]{2,1,0:T(8,128)(2,1)S(1)}, bf16[4,32,512]{2,1,0:T(8,128)(2,1)S(1)}, u32[]{:S(2)}, u32[]{:S(2)}) %collective-permute-start.42) | collective-permute-done | bytes 131104 | tf_op jit(solution)/shard_map/ppermute | solution.py:302
  144.4 2.5 %collective-permute-done.46.refs_1_ = bf16[4,16,512]{2,1,0:T(8,128)(2,1)S(1)} collective-permute-done((bf16[4,16,512]{2,1,0:T(8,128)(2,1)S(1)}, bf16[4,16,512]{2,1,0:T(8,128)(2,1)S(1)}, u32[]{:S(2)}, u32[]{:S(2)}) %collective-permute-start.46) | collective-permute-done | bytes 65568 | tf_op jit(solution)/shard_map/ppermute | solution.py:302
  151.2 2.7 %collective-permute-done.49.refs_4_ = bf16[8,32,512]{2,1,0:T(8,128)(2,1)S(1)} collective-permute-done((bf16[8,32,512]{2,1,0:T(8,128)(2,1)S(1)}, bf16[8,32,512]{2,1,0:T(8,128)(2,1)S(1)}, u32[]{:S(2)}, u32[]{:S(2)}) %collective-permute-start.49) | collective-permute-done | bytes 262176 | tf_op jit(solution)/shard_map/ppermute | solution.py:302
  (170 shorter events, 63.2 us)
Async XLA Ops:
  12.5 32.7 %collective-permute-start.3 = (bf16[4,4,32,512]{3,2,1,0:T(8,128)(2,1)S(1)}, bf16[4,4,32,512]{3,2,1,0:T(8,128)(2,1)S(1)}, u32[]{:S(2)}, u32[]{:S(2)}) collective-permute-start(bf16[4,4,32,512]{3,2,1,0:T(8,128)(2,1)S(1)} %get-tuple-element.120), channel_id=1, source_target_pairs={{0,4},{4,0},{8,12},{12,8},{16,20},{20,16},{24,28},{28,24},{1,5},{5... | collective-permute-start | bytes 1572872 | tf_op jit(solution)/shard_map/ppermute | solution.py:302
  15.5 17.5 %collective-permute-start = (bf16[4,4,16,512]{3,2,1,0:T(8,128)(2,1)S(1)}, bf16[4,4,16,512]{3,2,1,0:T(8,128)(2,1)S(1)}, u32[]{:S(2)}, u32[]{:S(2)}) collective-permute-start(bf16[4,4,16,512]{3,2,1,0:T(8,128)(2,1)S(1)} %get-tuple-element.111), channel_id=1, source_target_pairs={{0,4},{4,0},{8,12},{12,8},{16,20},{20,16},{24,28},{28,24},{1,5},{5... | collective-permute-start | bytes 786440 | tf_op jit(solution)/shard_map/ppermute | solution.py:302
  41.0 24.6 %collective-permute-start.9 = (bf16[4,4,32,512]{3,2,1,0:T(8,128)(2,1)}, bf16[4,4,32,512]{3,2,1,0:T(8,128)(2,1)}, u32[]{:S(2)}, u32[]{:S(2)}) collective-permute-start(bf16[4,4,32,512]{3,2,1,0:T(8,128)(2,1)} %get-tuple-element.132), channel_id=1, source_target_pairs={{0,4},{4,0},{8,12},{12,8},{16,20},{20,16},{24,28},{28,24},{1,5},{5... | collective-permute-start | bytes 1572872 | tf_op jit(solution)/shard_map/ppermute | solution.py:302
  42.5 33.5 %collective-permute-start.15 = (bf16[4,4,32,512]{3,2,1,0:T(8,128)(2,1)}, bf16[4,4,32,512]{3,2,1,0:T(8,128)(2,1)}, u32[]{:S(2)}, u32[]{:S(2)}) collective-permute-start(bf16[4,4,32,512]{3,2,1,0:T(8,128)(2,1)} %get-tuple-element.142), channel_id=1, source_target_pairs={{0,4},{4,0},{8,12},{12,8},{16,20},{20,16},{24,28},{28,24},{1,5},{5... | collective-permute-start | bytes 1572872 | tf_op jit(solution)/shard_map/ppermute | solution.py:302
  50.0 14.0 %collective-permute-start.11 = (s32[16]{0:T(128)}, s32[16]{0:T(128)S(1)}, u32[]{:S(2)}, u32[]{:S(2)}) collective-permute-start(s32[16]{0:T(128)} %param.15), channel_id=1, source_target_pairs={{0,4},{4,0},{8,12},{12,8},{16,20},{20,16},{24,28},{28,24},{1,5},{5... | collective-permute-start | bytes 200 | tf_op jit(solution)/shard_map/ppermute | solution.py:302
  52.0 13.6 %collective-permute-start.8 = (bf16[4,16,512]{2,1,0:T(8,128)(2,1)S(1)}, bf16[4,16,512]{2,1,0:T(8,128)(2,1)S(1)}, u32[]{:S(2)}, u32[]{:S(2)}) collective-permute-start(bf16[4,16,512]{2,1,0:T(8,128)(2,1)S(1)} %get-tuple-element.129.refs_0_), channel_id=1, source_target_pairs={{0,16},{4,20},{8,24},{12,28},{16,0},{20,4},{24,8},{28,12},{1,17},{... | collective-permute-start | bytes 196616 | tf_op jit(solution)/shard_map/ppermute | solution.py:302
  55.3 12.1 %collective-permute-start.10 = (bf16[1,4,32,512]{3,2,1,0:T(8,128)(2,1)S(1)}, bf16[1,4,32,512]{3,2,1,0:T(8,128)(2,1)S(1)}, u32[]{:S(2)}, u32[]{:S(2)}) collective-permute-start(bf16[1,4,32,512]{3,2,1,0:T(8,128)(2,1)S(1)} %get-tuple-element.135), channel_id=1, source_target_pairs={{0,16},{4,20},{8,24},{12,28},{16,0},{20,4},{24,8},{28,12},{1,17},{... | collective-permute-start | bytes 393224 | tf_op jit(solution)/shard_map/ppermute | solution.py:302
  66.8 12.4 %collective-permute-start.16 = (bf16[2,4,32,512]{3,2,1,0:T(8,128)(2,1)S(1)}, bf16[2,4,32,512]{3,2,1,0:T(8,128)(2,1)S(1)}, u32[]{:S(2)}, u32[]{:S(2)}) collective-permute-start(bf16[2,4,32,512]{3,2,1,0:T(8,128)(2,1)S(1)} %get-tuple-element.145), channel_id=1, source_target_pairs={{0,8},{4,12},{8,0},{12,4},{16,24},{20,28},{24,16},{28,20},{1,9},{5... | collective-permute-start | bytes 786440 | tf_op jit(solution)/shard_map/ppermute | solution.py:302
  79.3 9.7 %collective-permute-start.22 = (bf16[1,4,32,512]{3,2,1,0:T(8,128)(2,1)S(1)}, bf16[1,4,32,512]{3,2,1,0:T(8,128)(2,1)S(1)}, u32[]{:S(2)}, u32[]{:S(2)}) collective-permute-start(bf16[1,4,32,512]{3,2,1,0:T(8,128)(2,1)S(1)} %get-tuple-element.158), channel_id=1, source_target_pairs={{0,16},{4,20},{8,24},{12,28},{16,0},{20,4},{24,8},{28,12},{1,17},{... | collective-permute-start | bytes 393224 | tf_op jit(solution)/shard_map/ppermute | solution.py:302
  89.9 10.5 %collective-permute-start.24 = (bf16[4,32,512]{2,1,0:T(8,128)(2,1)S(1)}, bf16[4,32,512]{2,1,0:T(8,128)(2,1)S(1)}, u32[]{:S(2)}, u32[]{:S(2)}) collective-permute-start(bf16[4,32,512]{2,1,0:T(8,128)(2,1)S(1)} %get-tuple-element.162.refs_0_), channel_id=1, source_target_pairs={{0,16},{4,20},{8,24},{12,28},{16,0},{20,4},{24,8},{28,12},{1,17},{... | collective-permute-start | bytes 393224 | tf_op jit(solution)/shard_map/ppermute | solution.py:302
  90.0 10.5 %collective-permute-start.25 = (bf16[2,4,16,512]{3,2,1,0:T(8,128)(2,1)S(1)}, bf16[2,4,16,512]{3,2,1,0:T(8,128)(2,1)S(1)}, u32[]{:S(2)}, u32[]{:S(2)}) collective-permute-start(bf16[2,4,16,512]{3,2,1,0:T(8,128)(2,1)S(1)} %get-tuple-element.165), channel_id=1, source_target_pairs={{0,8},{4,12},{8,0},{12,4},{16,24},{20,28},{24,16},{28,20},{1,9},{5... | collective-permute-start | bytes 393224 | tf_op jit(solution)/shard_map/ppermute | solution.py:302
  92.1 10.5 %collective-permute-start.26 = (bf16[4,32,512]{2,1,0:T(8,128)(2,1)S(1)}, bf16[4,32,512]{2,1,0:T(8,128)(2,1)S(1)}, u32[]{:S(2)}, u32[]{:S(2)}) collective-permute-start(bf16[4,32,512]{2,1,0:T(8,128)(2,1)S(1)} %get-tuple-element.160.refs_0_), channel_id=1, source_target_pairs={{0,1},{1,0},{2,3},{3,2},{4,5},{5,4},{6,7},{7,6},{8,9},{9,8},{10,11... | collective-permute-start | bytes 393224 | tf_op jit(solution)/shard_map/ppermute | solution.py:302
  94.3 8.9 %collective-permute-start.28 = (bf16[1,4,32,512]{3,2,1,0:T(8,128)(2,1)S(1)}, bf16[1,4,32,512]{3,2,1,0:T(8,128)(2,1)S(1)}, u32[]{:S(2)}, u32[]{:S(2)}) collective-permute-start(bf16[1,4,32,512]{3,2,1,0:T(8,128)(2,1)S(1)} %get-tuple-element.170), channel_id=1, source_target_pairs={{0,16},{4,20},{8,24},{12,28},{16,0},{20,4},{24,8},{28,12},{1,17},{... | collective-permute-start | bytes 393224 | tf_op jit(solution)/shard_map/ppermute | solution.py:302
  104.2 15.8 %collective-permute-start.33 = (bf16[4,32,512]{2,1,0:T(8,128)(2,1)S(1)}, bf16[4,32,512]{2,1,0:T(8,128)(2,1)S(1)}, u32[]{:S(2)}, u32[]{:S(2)}) collective-permute-start(bf16[4,32,512]{2,1,0:T(8,128)(2,1)S(1)} %get-tuple-element.174.refs_0_), channel_id=1, source_target_pairs={{0,1},{1,0},{2,3},{3,2},{4,5},{5,4},{6,7},{7,6},{8,9},{9,8},{10,11... | collective-permute-start | bytes 393224 | tf_op jit(solution)/shard_map/ppermute | solution.py:302
  109.4 10.7 %collective-permute-start.34 = (bf16[4,32,512]{2,1,0:T(8,128)(2,1)S(1)}, bf16[4,32,512]{2,1,0:T(8,128)(2,1)S(1)}, u32[]{:S(2)}, u32[]{:S(2)}) collective-permute-start(bf16[4,32,512]{2,1,0:T(8,128)(2,1)S(1)} %get-tuple-element.179), channel_id=1, source_target_pairs={{0,1},{1,0},{2,3},{3,2},{4,5},{5,4},{6,7},{7,6},{8,9},{9,8},{10,11... | collective-permute-start | bytes 393224 | tf_op jit(solution)/shard_map/ppermute | solution.py:302
  109.4 14.7 %collective-permute-start.36 = (bf16[8,32,512]{2,1,0:T(8,128)(2,1)S(1)}, bf16[8,32,512]{2,1,0:T(8,128)(2,1)S(1)}, u32[]{:S(2)}, u32[]{:S(2)}) collective-permute-start(bf16[8,32,512]{2,1,0:T(8,128)(2,1)S(1)} %get-tuple-element.183), channel_id=1, source_target_pairs={{0,4},{4,0},{8,12},{12,8},{16,20},{20,16},{24,28},{28,24},{1,5},{5... | collective-permute-start | bytes 786440 | tf_op jit(solution)/shard_map/ppermute | solution.py:302
  110.8 8.9 %collective-permute-start.32 = (bf16[1,4,16,512]{3,2,1,0:T(8,128)(2,1)S(1)}, bf16[1,4,16,512]{3,2,1,0:T(8,128)(2,1)S(1)}, u32[]{:S(2)}, u32[]{:S(2)}) collective-permute-start(bf16[1,4,16,512]{3,2,1,0:T(8,128)(2,1)S(1)} %get-tuple-element.177), channel_id=1, source_target_pairs={{0,16},{4,20},{8,24},{12,28},{16,0},{20,4},{24,8},{28,12},{1,17},{... | collective-permute-start | bytes 196616 | tf_op jit(solution)/shard_map/ppermute | solution.py:302
  111.1 14.6 %collective-permute-start.37 = (bf16[4,32,512]{2,1,0:T(8,128)(2,1)S(1)}, bf16[4,32,512]{2,1,0:T(8,128)(2,1)S(1)}, u32[]{:S(2)}, u32[]{:S(2)}) collective-permute-start(bf16[4,32,512]{2,1,0:T(8,128)(2,1)S(1)} %get-tuple-element.187.refs_0_), channel_id=1, source_target_pairs={{0,16},{4,20},{8,24},{12,28},{16,0},{20,4},{24,8},{28,12},{1,17},{... | collective-permute-start | bytes 393224 | tf_op jit(solution)/shard_map/ppermute | solution.py:302
  125.7 13.9 %collective-permute-start.44 = (bf16[4,32,512]{2,1,0:T(8,128)(2,1)S(1)}, bf16[4,32,512]{2,1,0:T(8,128)(2,1)S(1)}, u32[]{:S(2)}, u32[]{:S(2)}) collective-permute-start(bf16[4,32,512]{2,1,0:T(8,128)(2,1)S(1)} %get-tuple-element.191.refs_0_), channel_id=1, source_target_pairs={{0,8},{4,12},{8,0},{12,4},{16,24},{20,28},{24,16},{28,20},{1,9},{5... | collective-permute-start | bytes 393224 | tf_op jit(solution)/shard_map/ppermute | solution.py:302
  127.8 10.6 %collective-permute-start.42 = (bf16[4,32,512]{2,1,0:T(8,128)(2,1)S(1)}, bf16[4,32,512]{2,1,0:T(8,128)(2,1)S(1)}, u32[]{:S(2)}, u32[]{:S(2)}) collective-permute-start(bf16[4,32,512]{2,1,0:T(8,128)(2,1)S(1)} %get-tuple-element.193), channel_id=1, source_target_pairs={{0,8},{4,12},{8,0},{12,4},{16,24},{20,28},{24,16},{28,20},{1,9},{5... | collective-permute-start | bytes 393224 | tf_op jit(solution)/shard_map/ppermute | solution.py:302
  128.6 12.5 %collective-permute-start.45 = (bf16[4,32,512]{2,1,0:T(8,128)(2,1)S(1)}, bf16[4,32,512]{2,1,0:T(8,128)(2,1)S(1)}, u32[]{:S(2)}, u32[]{:S(2)}) collective-permute-start(bf16[4,32,512]{2,1,0:T(8,128)(2,1)S(1)} %get-tuple-element.197), channel_id=1, source_target_pairs={{0,8},{4,12},{8,0},{12,4},{16,24},{20,28},{24,16},{28,20},{1,9},{5... | collective-permute-start | bytes 393224 | tf_op jit(solution)/shard_map/ppermute | solution.py:302
  130.5 9.1 %collective-permute-start.43 = (bf16[4,16,512]{2,1,0:T(8,128)(2,1)S(1)}, bf16[4,16,512]{2,1,0:T(8,128)(2,1)S(1)}, u32[]{:S(2)}, u32[]{:S(2)}) collective-permute-start(bf16[4,16,512]{2,1,0:T(8,128)(2,1)S(1)} %get-tuple-element.195.refs_0_), channel_id=1, source_target_pairs={{0,16},{4,20},{8,24},{12,28},{16,0},{20,4},{24,8},{28,12},{1,17},{... | collective-permute-start | bytes 196616 | tf_op jit(solution)/shard_map/ppermute | solution.py:302
  139.0 10.7 %collective-permute-start.48 = (bf16[8,32,512]{2,1,0:T(8,128)(2,1)S(1)}, bf16[8,32,512]{2,1,0:T(8,128)(2,1)S(1)}, u32[]{:S(2)}, u32[]{:S(2)}) collective-permute-start(bf16[8,32,512]{2,1,0:T(8,128)(2,1)S(1)} %get-tuple-element.201), channel_id=1, source_target_pairs={{0,4},{4,0},{8,12},{12,8},{16,20},{20,16},{24,28},{28,24},{1,5},{5... | collective-permute-start | bytes 786440 | tf_op jit(solution)/shard_map/ppermute | solution.py:302
  141.7 12.1 %collective-permute-start.49 = (bf16[8,32,512]{2,1,0:T(8,128)(2,1)S(1)}, bf16[8,32,512]{2,1,0:T(8,128)(2,1)S(1)}, u32[]{:S(2)}, u32[]{:S(2)}) collective-permute-start(bf16[8,32,512]{2,1,0:T(8,128)(2,1)S(1)} %get-tuple-element.205), channel_id=1, source_target_pairs={{0,4},{4,0},{8,12},{12,8},{16,20},{20,16},{24,28},{28,24},{1,5},{5... | collective-permute-start | bytes 786440 | tf_op jit(solution)/shard_map/ppermute | solution.py:302
  (46 other events, 385.5 us)

commit v3 on v0

v3 whole, which is shorter than its diff:
```python
import jax
import jax.numpy as jnp
from jax import lax
from jax.experimental import pallas as pl
from jax.experimental.pallas import tpu as pltpu
from jax.sharding import PartitionSpec as P

SHARES = (2, 2, 2, 1, 1)
READ_CAP = 2
VMEM_BYTES = 12 * 1024 * 1024

SMEM = pl.BlockSpec(memory_space=pltpu.SMEM)
VMEM = pl.BlockSpec(memory_space=pltpu.VMEM)
HBM = pl.BlockSpec(memory_space=pltpu.HBM)


def call(body, out_shape, in_specs, out_specs, operands, scratch=(), aliases=None, limit=VMEM_BYTES):
    return pl.pallas_call(
        body,
        out_shape=out_shape,
        in_specs=in_specs,
        out_specs=out_specs,
        scratch_shapes=list(scratch),
        input_output_aliases=aliases or {},
        compiler_params=pltpu.CompilerParams(vmem_limit_bytes=limit),
        cost_estimate=pl.CostEstimate(flops=0, bytes_accessed=1, transcendentals=0),
    )(*operands)


class Task:
    def __init__(self, body, operands, out_shape, specs=None):
        self.body, self.operands, self.out_shape = body, operands, out_shape
        self.specs = specs or [VMEM] * len(operands)


def joint(tasks):
    def body(*refs):
        ins = refs[: sum(len(t.operands) for t in tasks)]
        outs = refs[len(ins) :]
        for t in tasks:
            t.body(ins[: len(t.operands)], outs[: len(t.out_shape)])
            ins, outs = ins[len(t.operands) :], outs[len(t.out_shape) :]

    out_shape = [s for t in tasks for s in t.out_shape]
    results = call(
        body,
        out_shape,
        [s for t in tasks for s in t.specs],
        [VMEM] * len(out_shape),
        [a for t in tasks for a in t.operands],
    )
    grouped = []
    for t in tasks:
        grouped.append(results[: len(t.out_shape)])
        results = results[len(t.out_shape) :]
    return grouped


def split(value, size):
    if size & (size - 1) == 0:
        return value >> (size.bit_length() - 1), value & (size - 1)
    return lax.div(value, size), lax.rem(value, size)


def reversed_bits(value, bits):
    result = value & 1
    for i in range(1, bits):
        result = (result << 1) | ((value >> i) & 1)
    return result


def lay_tiles(table, base, tiles, lhs, spans, row_base, blocks, block, at=0):
    for b in range(blocks):
        for c in range(blocks):
            entry = table[base + b * blocks + c]
            tile = tiles[jnp.maximum(entry - 1, 0)]
            tile = jnp.where(entry > 0, tile, jnp.zeros_like(tile))
            top = at
            for first, rows in spans:
                lhs[pl.ds(top + b * rows, rows), pl.ds(c * block, block)] = tile[first - row_base : first - row_base + rows]
                top = top + blocks * rows


def first_part(me, slot, col, tile_id, touched, tiles, features, after, first, count, span):
    block = tiles.shape[1]
    blocks = features.shape[0] // block
    width = features.shape[1]
    edges, cap = touched.shape[1], touched.shape[2]
    bits = edges.bit_length() - 1
    products = slot.shape[0]
    start, rows = span
    square = blocks * blocks

    def body(me_ref, slot_hbm, col_hbm, id_hbm, touched_ref, tiles_hbm, x_hbm, after_ref, *refs):
        table, low, high, x_out, *scratch = refs
        slot_ref, col_ref, id_ref, tiles_ref, lhs, bases, sems = scratch
        loads = [
            pltpu.make_async_copy(slot_hbm, slot_ref, sems.at[0]),
            pltpu.make_async_copy(col_hbm, col_ref, sems.at[1]),
            pltpu.make_async_copy(id_hbm, id_ref, sems.at[2]),
            pltpu.make_async_copy(x_hbm, x_out, sems.at[3]),
            pltpu.make_async_copy(tiles_hbm.at[:, pl.ds(start, rows)], tiles_ref, sems.at[4]),
        ]
        for load in loads:
            load.start()

        def clear(i, carry):
            table[i] = 0
            return carry

        lax.fori_loop(0, edges * square, clear, 0, unroll=16)

        def place_slot(k, carry):
            owner, _ = split(k, cap)
            place = reversed_bits(owner ^ me_ref[0], bits)
            bases[k] = (place * blocks + touched_ref[k]) * blocks
            return carry

        lax.fori_loop(0, edges * cap, place_slot, 0, unroll=8)
        for load in loads[:3]:
            load.wait()

        def enter(k, carry):
            table[bases[slot_ref[k]] + col_ref[k]] = id_ref[k] + 1
            return carry

        lax.fori_loop(0, products, enter, 0, unroll=8)
        for load in loads[3:]:
            load.wait()

        def one_owner(i, carry):
            at = pl.multiple_of(i * blocks * rows, blocks * rows)
            lay_tiles(table, (first + i) * square, tiles_ref, lhs, [span], start, blocks, block, at)
            return carry

        lax.fori_loop(0, count, one_owner, 0)
        half = count // 2 * blocks * rows
        for out, at in ((high, half), (low, 0)):
            total = jnp.dot(lhs[pl.ds(at, half)], x_out[...], preferred_element_type=jnp.float32)
            out[...] = total.astype(jnp.bfloat16).reshape(out.shape)

    part = jax.ShapeDtypeStruct((count // 2, blocks, rows, width), jnp.bfloat16)
    return call(
        body,
        [
            jax.ShapeDtypeStruct((edges * square,), jnp.int32),
            part,
            part,
            jax.ShapeDtypeStruct(features.shape, jnp.bfloat16),
        ],
        [SMEM, HBM, HBM, HBM, SMEM, HBM, HBM, SMEM],
        [SMEM, VMEM, VMEM, VMEM],
        (me, slot, col, tile_id, touched[me[0]].reshape(-1), tiles, features, after),
        [
            pltpu.SMEM((products,), jnp.int32),
            pltpu.SMEM((products,), jnp.int32),
            pltpu.SMEM((products,), jnp.int32),
            pltpu.VMEM((tiles.shape[0], rows, block), jnp.bfloat16),
            pltpu.VMEM((count * blocks * rows, blocks * block), jnp.bfloat16),
            pltpu.SMEM((edges * cap,), jnp.int32),
            pltpu.SemaphoreType.DMA((5,)),
        ],
        limit=62 * 1024 * 1024,
    )


def other_parts(table, tiles, inputs, first, count, spans):
    block = tiles.shape[1]
    blocks = inputs.shape[0] // block
    width = inputs.shape[1]
    total_rows = sum(rows for _, rows in spans)
    half = count // 2

    def body(table_ref, tiles_hbm, x_ref, *refs):
        outs = refs[: 2 * len(spans)]
        tiles_ref, lhs, sem = refs[2 * len(spans) :]
        load = pltpu.make_async_copy(tiles_hbm, tiles_ref, sem.at[0])
        load.start()
        load.wait()

        def one_owner(side):
            def step(i, carry):
                base = (first + side * half + i) * blocks * blocks
                lay_tiles(table_ref, base, tiles_ref, lhs, spans, 0, blocks, block)
                total = jnp.dot(lhs[...], x_ref[...], preferred_element_type=jnp.float32).astype(jnp.bfloat16)
                at = 0
                for n, (_, rows) in enumerate(spans):
                    outs[2 * n + side][i] = total[at : at + blocks * rows].reshape(blocks, rows, width)
                    at += blocks * rows
                return carry

            return step

        for side in (1, 0):
            lax.fori_loop(0, half, one_owner(side), 0)

    results = call(
        body,
        [
            jax.ShapeDtypeStruct((half, blocks, rows, width), jnp.bfloat16)
            for _, rows in spans
            for side in range(2)
        ],
        [SMEM, HBM, VMEM],
        [VMEM] * (2 * len(spans)),
        (table, tiles, inputs),
        [
            pltpu.VMEM(tiles.shape, jnp.bfloat16),
            pltpu.VMEM((blocks * total_rows, blocks * block), jnp.bfloat16),
            pltpu.SemaphoreType.DMA((1,)),
        ],
    )
    return [(results[2 * n], results[2 * n + 1]) for n in range(len(spans))]


def add_and_send(total, got):
    def body(ins, outs):
        outs[0][...] = (ins[0][...].astype(jnp.float32) + ins[1][...].astype(jnp.float32)).astype(jnp.bfloat16)

    return Task(body, [total, got], [jax.ShapeDtypeStruct(got.shape, jnp.bfloat16)])


def add_and_halve(terms):
    count, *shape = terms[0].shape
    left = count // 2

    def body(ins, outs):
        value = ins[0][...].astype(jnp.float32)
        for term in ins[1:]:
            value = value + term[...].astype(jnp.float32)
        if left:
            outs[0][...] = value[:left]
            outs[1][...] = value[left:].astype(jnp.bfloat16)
        else:
            outs[0][...] = value[0].astype(jnp.bfloat16)

    if left:
        out_shape = [
            jax.ShapeDtypeStruct((left, *shape), jnp.float32),
            jax.ShapeDtypeStruct((count - left, *shape), jnp.bfloat16),
        ]
    else:
        out_shape = [jax.ShapeDtypeStruct(tuple(shape), jnp.bfloat16)]
    return Task(body, terms, out_shape)


def mix_and_pick(me, mine, choice, weight, pieces, edges):
    blocks, rows, depth = pieces[0].shape
    width = weight.shape[1]

    def body(ins, outs):
        me_ref, mine_ref, choice_ref, w_ref, *piece_refs = ins
        out_ref, picked_ref = outs
        total = jnp.zeros((blocks * rows, width), jnp.float32)
        for j, piece in enumerate(piece_refs):
            at = pl.multiple_of((mine_ref[0] ^ j) * depth, depth)
            total += jnp.dot(
                piece[...].reshape(blocks * rows, depth),
                w_ref[pl.ds(at, depth)],
                preferred_element_type=jnp.float32,
            )
        out_ref[...] = jnp.maximum(total, 0.0).astype(jnp.bfloat16).reshape(out_ref.shape)
        for p in range(edges):
            for j in range(READ_CAP):
                picked_ref[me_ref[0] ^ p, j] = out_ref[choice_ref[p * READ_CAP + j]]

    return Task(
        body,
        [me, mine, choice, weight, *pieces],
        [
            jax.ShapeDtypeStruct((blocks, rows, width), jnp.bfloat16),
            jax.ShapeDtypeStruct((edges, READ_CAP, rows, width), jnp.bfloat16),
        ],
        [SMEM] * 3 + [VMEM] * (1 + len(pieces)),
    )


def wait_for(token):
    return Task(lambda ins, outs: None, [token], [])


def lay_out(entry, mixed, got, outputs, count, span, block):
    blocks, _, width = mixed.shape
    edges = got.shape[0]
    start, rows = span
    slots = edges * READ_CAP

    def body(entry_ref, mixed_ref, got_ref, *refs):
        hidden_ref, ghost_ref, token, sems = refs[-4:]
        token[...] = jnp.zeros_like(token)
        own = pltpu.make_async_copy(mixed_ref, hidden_ref.at[:, pl.ds(start, rows)], sems.at[slots])
        own.start()

        def each(act):
            for o in range(edges):
                for j in range(READ_CAP):
                    r = entry_ref[o * READ_CAP + j]

                    @pl.when(r >= 0)
                    def _():
                        target = ghost_ref.at[r, pl.ds(start, rows)]
                        act(pltpu.make_async_copy(got_ref.at[o, j], target, sems.at[o * READ_CAP + j]))

        each(lambda copy: copy.start())
        own.wait()
        each(lambda copy: copy.wait())

    operands = (entry, mixed, got, *outputs)
    return call(
        body,
        [
            jax.ShapeDtypeStruct((blocks, block, width), jnp.bfloat16),
            jax.ShapeDtypeStruct((count, block, width), jnp.bfloat16),
            jax.ShapeDtypeStruct((8, 128), jnp.float32),
        ],
        [SMEM] + [VMEM] * 2 + [HBM] * len(outputs),
        [HBM, HBM, VMEM],
        operands,
        [pltpu.SemaphoreType.DMA((slots + 1,))],
        aliases={3: 0, 4: 1} if outputs else None,
    )


def local(features, tiles, tile_slot, tile_col, tile_id, touched, weight, readers):
    edges, feats = lax.axis_size("edge"), lax.axis_size("feat")
    half = edges // 2
    me, mine = lax.axis_index("edge"), lax.axis_index("feat")
    block = tiles.shape[1]
    blocks = features.shape[0] // block
    width = features.shape[1]
    unit = block // sum(SHARES)
    spans = [(sum(SHARES[:i]) * unit, share * unit) for i, share in enumerate(SHARES)]

    def flip(value, bit, axis="edge"):
        return lax.ppermute(value, axis, [(d, d ^ bit) for d in range(lax.axis_size(axis))])

    neighbour = flip(readers, 1)
    lists, bit = jnp.stack([readers, neighbour]), 2
    while bit < edges:
        lists = jnp.concatenate([lists, flip(lists, bit)])
        bit *= 2
    count = readers.shape[0]
    order = jnp.arange(count, dtype=jnp.int32)
    position = jnp.arange(READ_CAP, dtype=jnp.int32)
    earlier = order[None, :] < order[:, None]
    asked = lists // blocks == me
    rank = jnp.sum((asked[:, None, :] & earlier[None]).astype(jnp.int32), axis=2)
    chosen = asked[:, None, :] & (rank[:, None, :] == position[None, :, None])
    choice = jnp.sum(jnp.where(chosen, (lists % blocks)[:, None, :], 0), axis=2).reshape(-1)
    owner = readers // blocks
    rank = jnp.sum(((owner[:, None] == owner[None, :]) & earlier).astype(jnp.int32), axis=1)
    place = jnp.arange(edges * READ_CAP, dtype=jnp.int32)
    found = (owner * READ_CAP + rank)[None, :] == place[:, None]
    entry = jnp.sum(jnp.where(found, order[None, :] + 1, 0), axis=1) - 1
    me, mine = me.reshape(1), mine.reshape(1)

    table, low, high, inputs = first_part(
        me, tile_slot, tile_col, tile_id, touched, tiles, features, neighbour, half, half, spans[0]
    )
    away = [(low, high)] + other_parts(table, tiles, inputs, half, half, spans[1:])
    kept = other_parts(table, tiles, inputs, 0, half, spans)
    outputs = ()

    def one_part(part):
        nonlocal outputs
        first = flip(away[part][1], 1)
        (sent,) = yield add_and_send(kept[part][1], first)
        second, got = flip(away[part][0], 1), flip(sent, 2)
        terms, bit = [kept[part][0], second, got], 2
        while True:
            total, *sent = yield add_and_halve(terms)
            if not sent:
                break
            bit *= 2
            terms = [total, flip(sent[0], bit)]
        pieces = [total] + [flip(total, j, "feat") for j in range(1, feats)]
        mixed, picked = yield mix_and_pick(me, mine, choice, weight, pieces, edges)
        got = lax.all_to_all(picked, "edge", split_axis=0, concat_axis=0)
        *outputs, token = lay_out(entry, mixed, got, outputs, count, spans[part], block)
        tokens[step + 2] = token

    tokens = {}
    ways, tasks, part = {}, {}, 0
    step = 0
    while part < len(spans) or tasks:
        if step % 2 == 0 and part < len(spans):
            ways[part] = one_part(part)
            tasks[part] = next(ways[part])
            part += 1
        ready = sorted(tasks)
        waits = [wait_for(tokens[step])] if step in tokens else []
        results = joint([tasks[n] for n in ready] + waits)
        tasks = {}
        for n, result in zip(ready, results):
            try:
                tasks[n] = ways[n].send(result)
            except StopIteration:
                pass
        step += 1
    hidden, ghosts = outputs
    return hidden.reshape(blocks * block, width), ghosts.reshape(-1, width)


def solution(mesh):
    in_specs = (
        P("edge", "feat"),
        P("edge", None, None),
        P("edge"),
        P("edge"),
        P("edge"),
        P(),
        P(None, "feat"),
        P("edge"),
    )
    out_specs = (P("edge", "feat"), P("edge", "feat"))
    return jax.shard_map(local, mesh=mesh, in_specs=in_specs, out_specs=out_specs, check_vma=False)
```

time: 432 us -> 195 us (0.45)
  waiting for transfers between devices: 278 us -> 74.6 us
  other arithmetic: 76 us -> 0.74 us
  starting transfers between devices: 7.31 us -> 64.5 us
  matrix products: 29.7 us -> 0 us
  Pallas kernels: 0 us -> 25.4 us
  blocking collectives: 0 us -> 13.3 us
  between operations: 14.1 us -> 1.02 us
  local copies, waits for them, and re-layouts: 25.7 us -> 14.7 us
    all_to_all x1 -> x4, waiting for transfers between devices: 183 us -> 0.01 us  [one_part(): got = lax.all_to_all(picked, 'edge', split_axis=0, concat_axis=0)]
    all_gather x2 -> x0, waiting for transfers between devices: 95.3 us -> none  [the longest x1 73.5 us: local(): lax.all_gather(hidden, 'edge', axis=0, tiled=True)]
    ppermute x0 -> x38, waiting for transfers between devices: none -> 74.6 us  [flip(): lax.ppermute(value, axis, [(d, d ^ bit) for d in range(lax.axis_size(axis...]
    scatter-add x4 -> x0, other arithmetic: 73.4 us -> none  [the longest x3 55.9 us: add_group(): return partial_value.at[slots].add(product)]
    ppermute x0 -> x38, starting transfers between devices: none -> 44.4 us  [flip(): lax.ppermute(value, axis, [(d, d ^ bit) for d in range(lax.axis_size(axis...]
    dot_general x5 -> x0, matrix products: 29.7 us -> none  [the longest x3 21 us: add_group(): jnp.einsum('gij,gjc->gic', tiles[chosen], inputs[columns], preferred_elem...]
    pallas_call x0 -> x20, Pallas kernels: none -> 25.4 us  [call(): pl.pallas_call(body, out_shape=out_shape, in_specs=in_specs, out_specs=ou...]
    gather x6 -> x0, local copies, waits for them, and re-layouts: 17.4 us -> none  [the longest x3 9.17 us: add_group(): tiles[chosen]]
  transfers between devices with their start and end apart: 3 -> 42, of which waited for: 3 -> 24; matrix products, arithmetic and copies ran while one was open for 0% -> 1% of each run, Pallas kernels for 0% -> 6%
where the time goes in v3:
time: 195 us; the launch traced here: 194 us
  waiting for transfers between devices  74.6 us (38%)
  starting transfers between devices  64.5 us (33%)
  Pallas kernels  25.4 us (13%)
  local copies, waits for them, and re-layouts  14.7 us (8%)
  blocking collectives  13.3 us (7%)
    ppermute x38, waiting for transfers between devices, flip(): lax.ppermute(value, axis, [(d, d ^ bit) for d in range(lax.axis_size(axis...  74.6 us
    ppermute x38, starting transfers between devices, flip(): lax.ppermute(value, axis, [(d, d ^ bit) for d in range(lax.axis_size(axis...  44.4 us
    pallas_call x20, Pallas kernels, call(): pl.pallas_call(body, out_shape=out_shape, in_specs=in_specs, out_specs=ou...  25.4 us
    all_to_all x4, starting transfers between devices, one_part(): got = lax.all_to_all(picked, 'edge', split_axis=0, concat_axis=0)  20.1 us
    unnamed x62, local copies, waits for them, and re-layouts  13.9 us
    all_to_all x1, blocking collectives, one_part(): got = lax.all_to_all(picked, 'edge', split_axis=0, concat_axis=0)  13.3 us
  transfers between devices with their start and end apart: 42, of which 24 were waited for; matrix products, arithmetic and copies ran while one was open for 1% of the time, Pallas kernels for 6%

profile of v3, /device:TPU:0, one launch (start us, length us, event | category | flops | bytes accessed | tf_op | source)
XLA Modules:
  0.0 194.2 jit_solution(9668812472391075247)
XLA Ops:
  0.7 3.0 %collective-permute-start = (s32[16]{0:T(128)}, s32[16]{0:T(128)S(1)}, u32[]{:S(2)}, u32[]{:S(2)}) collective-permute-start(s32[16]{0:T(128)} %param.15), channel_id=1, source_target_pairs={{0,4},{4,0},{8,12},{12,8},{16,20},{20,16},{24,28},{28,24},{1,5},{5... | collective-permute-start | bytes 200 | tf_op jit(solution)/shard_map/ppermute | solution.py:335
  5.9 3.4 %shard_map.95 = (s32[128]{0:T(128)}, bf16[2,4,32,512]{3,2,1,0:T(8,128)(2,1)}, bf16[2,4,32,512]{3,2,1,0:T(8,128)(2,1)}, bf16[512,512]{1,0:T(8,128)(2,1)}) custom-call(s32[1]{0:T(128)} %bitcast.me_ref.refs_0_, s32[96]{0:T(128)} %slot_hbm.1, s32[96]{0:T(128)} %col_hbm.1, s32[96]{0:T(128)} %id_hbm.1, s32[32]{0:T(128)} %reshape_squeeze.3.touched_ref, ...), custom_call_target="tpu_custom_call" | custom-call | bytes 1 | tf_op jit(solution)/shard_map/pallas_call | solution.py:18
  13.2 2.5 %shard_map.96 = (bf16[2,4,32,512]{3,2,1,0:T(8,128)(2,1)S(1)}, bf16[2,4,32,512]{3,2,1,0:T(8,128)(2,1)S(1)}, bf16[2,4,32,512]{3,2,1,0:T(8,128)(2,1)S(1)}, bf16[2,4...) custom-call(s32[128]{0:T(128)S(1)} %copy-done.14, ...), custom_call_target="tpu_custom_call" | custom-call | bytes 1 | tf_op jit(solution)/shard_map/pallas_call | solution.py:18
  15.7 3.1 %collective-permute-done.4.refs_1_ = bf16[2,4,32,512]{3,2,1,0:T(8,128)(2,1)S(1)} collective-permute-done((bf16[2,4,32,512]{3,2,1,0:T(8,128)(2,1)}, bf16[2,4,32,512]{3,2,1,0:T(8,128)(2,1)S(1)}, u32[]{:S(2)}, u32[]{:S(2)}) %collective-permute-start.4) | collective-permute-done | bytes 262176 | tf_op jit(solution)/shard_map/ppermute | solution.py:335
  21.1 2.7 %shard_map.99 = (bf16[2,4,32,512]{3,2,1,0:T(8,128)(2,1)S(1)}, bf16[2,4,32,512]{3,2,1,0:T(8,128)(2,1)}, bf16[2,4,32,512]{3,2,1,0:T(8,128)(2,1)S(1)}, bf16[2,4,32,...) custom-call(s32[128]{0:T(128)S(1)} %copy-done.14, ...), custom_call_target="tpu_custom_call" | custom-call | bytes 1 | tf_op jit(solution)/shard_map/pallas_call | solution.py:18
  28.6 2.7 %collective-permute-start.6 = (bf16[1,4,32,512]{3,2,1,0:T(8,128)(2,1)S(1)}, bf16[1,4,32,512]{3,2,1,0:T(8,128)(2,1)S(1)}, u32[]{:S(2)}, u32[]{:S(2)}) collective-permute-start(bf16[1,4,32,512]{3,2,1,0:T(8,128)(2,1)S(1)} %get-tuple-element.73), channel_id=1, source_target_pairs={{0,16},{4,20},{8,24},{12,28},{16,0},{20,4},{24,8},{28,12},{1,17},{... | collective-permute-start | bytes 393224 | tf_op jit(solution)/shard_map/ppermute | solution.py:335
  31.6 2.7 %collective-permute-start.2 = (s32[4,16]{1,0:T(4,128)S(1)}, s32[4,16]{1,0:T(4,128)S(1)}, u32[]{:S(2)}, u32[]{:S(2)}) collective-permute-start(s32[4,16]{1,0:T(4,128)S(1)} %pad_add_fusion.1), channel_id=1, source_target_pairs={{0,16},{4,20},{8,24},{12,28},{16,0},{20,4},{24,8},{28,12},{1,17},{... | collective-permute-start | bytes 776 | tf_op jit(solution)/shard_map/ppermute | solution.py:335
  40.8 2.9 %collective-permute-done.10.refs_7_ = bf16[4,32,512]{2,1,0:T(8,128)(2,1)S(1)} collective-permute-done((bf16[4,32,512]{2,1,0:T(8,128)(2,1)S(1)}, bf16[4,32,512]{2,1,0:T(8,128)(2,1)S(1)}, u32[]{:S(2)}, u32[]{:S(2)}) %collective-permute-start.10) | collective-permute-done | bytes 131104 | tf_op jit(solution)/shard_map/ppermute | solution.py:335
  43.7 2.9 %collective-permute-done.9.refs_6_ = bf16[4,32,512]{2,1,0:T(8,128)(2,1)S(1)} collective-permute-done((bf16[4,32,512]{2,1,0:T(8,128)(2,1)S(1)}, bf16[4,32,512]{2,1,0:T(8,128)(2,1)S(1)}, u32[]{:S(2)}, u32[]{:S(2)}) %collective-permute-start.9) | collective-permute-done | bytes 131104 | tf_op jit(solution)/shard_map/ppermute | solution.py:335
  51.0 3.9 %all-to-all-start = ((bf16[8,2,32,512]{3,2,1,0:T(8,128)(2,1)}), bf16[8,2,32,512]{3,2,1,0:T(8,128)(2,1)S(1)}, u32[]{:S(2)}, u32[]{:S(2)}) async-start(bf16[8,2,32,512]{3,2,1,0:T(8,128)(2,1)} %get-tuple-element.89), calls=%async_computation | async-start | bytes 1048576 | tf_op jit(solution)/shard_map/all_to_all | solution.py:378
  57.2 2.4 %collective-permute-start.13 = (bf16[1,4,32,512]{3,2,1,0:T(8,128)(2,1)S(1)}, bf16[1,4,32,512]{3,2,1,0:T(8,128)(2,1)S(1)}, u32[]{:S(2)}, u32[]{:S(2)}) collective-permute-start(bf16[1,4,32,512]{3,2,1,0:T(8,128)(2,1)S(1)} %get-tuple-element.81), channel_id=1, source_target_pairs={{0,16},{4,20},{8,24},{12,28},{16,0},{20,4},{24,8},{28,12},{1,17},{... | collective-permute-start | bytes 393224 | tf_op jit(solution)/shard_map/ppermute | solution.py:335
  60.3 9.7 %collective-permute-done.14.refs_3_ = bf16[2,4,32,512]{3,2,1,0:T(8,128)(2,1)S(1)} collective-permute-done((bf16[2,4,32,512]{3,2,1,0:T(8,128)(2,1)S(1)}, bf16[2,4,32,512]{3,2,1,0:T(8,128)(2,1)S(1)}, u32[]{:S(2)}, u32[]{:S(2)}) %collective-permute-start.14) | collective-permute-done | bytes 262176 | tf_op jit(solution)/shard_map/ppermute | solution.py:335
  70.0 5.3 %collective-permute-done.13.refs_1_ = bf16[1,4,32,512]{3,2,1,0:T(8,128)(2,1)S(1)} collective-permute-done((bf16[1,4,32,512]{3,2,1,0:T(8,128)(2,1)S(1)}, bf16[1,4,32,512]{3,2,1,0:T(8,128)(2,1)S(1)}, u32[]{:S(2)}, u32[]{:S(2)}) %collective-permute-start.13) | collective-permute-done | bytes 131104 | tf_op jit(solution)/shard_map/ppermute | solution.py:335
  79.0 2.4 %collective-permute-done.17.refs_7_ = bf16[4,32,512]{2,1,0:T(8,128)(2,1)S(1)} collective-permute-done((bf16[4,32,512]{2,1,0:T(8,128)(2,1)S(1)}, bf16[4,32,512]{2,1,0:T(8,128)(2,1)S(1)}, u32[]{:S(2)}, u32[]{:S(2)}) %collective-permute-start.17) | collective-permute-done | bytes 131104 | tf_op jit(solution)/shard_map/ppermute | solution.py:335
  86.0 5.8 %all-to-all-start.1 = ((bf16[8,2,32,512]{3,2,1,0:T(8,128)(2,1)}), bf16[8,2,32,512]{3,2,1,0:T(8,128)(2,1)S(1)}, u32[]{:S(2)}, u32[]{:S(2)}) async-start(bf16[8,2,32,512]{3,2,1,0:T(8,128)(2,1)} %get-tuple-element.100), calls=%async_computation.1 | async-start | bytes 1048576 | tf_op jit(solution)/shard_map/all_to_all | solution.py:378
  96.8 6.5 %collective-permute-done.21.refs_3_ = bf16[2,4,16,512]{3,2,1,0:T(8,128)(2,1)S(1)} collective-permute-done((bf16[2,4,16,512]{3,2,1,0:T(8,128)(2,1)S(1)}, bf16[2,4,16,512]{3,2,1,0:T(8,128)(2,1)S(1)}, u32[]{:S(2)}, u32[]{:S(2)}) %collective-permute-start.21) | collective-permute-done | bytes 131104 | tf_op jit(solution)/shard_map/ppermute | solution.py:335
  103.3 8.9 %collective-permute-done.20.refs_1_ = bf16[1,4,32,512]{3,2,1,0:T(8,128)(2,1)S(1)} collective-permute-done((bf16[1,4,32,512]{3,2,1,0:T(8,128)(2,1)S(1)}, bf16[1,4,32,512]{3,2,1,0:T(8,128)(2,1)S(1)}, u32[]{:S(2)}, u32[]{:S(2)}) %collective-permute-start.20) | collective-permute-done | bytes 131104 | tf_op jit(solution)/shard_map/ppermute | solution.py:335
  122.7 5.7 %all-to-all-start.2 = ((bf16[8,2,32,512]{3,2,1,0:T(8,128)(2,1)}), bf16[8,2,32,512]{3,2,1,0:T(8,128)(2,1)S(1)}, u32[]{:S(2)}, u32[]{:S(2)}) async-start(bf16[8,2,32,512]{3,2,1,0:T(8,128)(2,1)} %get-tuple-element.113), calls=%async_computation.2 | async-start | bytes 1048576 | tf_op jit(solution)/shard_map/all_to_all | solution.py:378
  133.3 6.6 %collective-permute-done.28.refs_3_ = bf16[2,4,16,512]{3,2,1,0:T(8,128)(2,1)S(1)} collective-permute-done((bf16[2,4,16,512]{3,2,1,0:T(8,128)(2,1)S(1)}, bf16[2,4,16,512]{3,2,1,0:T(8,128)(2,1)S(1)}, u32[]{:S(2)}, u32[]{:S(2)}) %collective-permute-start.28) | collective-permute-done | bytes 131104 | tf_op jit(solution)/shard_map/ppermute | solution.py:335
  139.9 6.1 %collective-permute-done.27.refs_1_ = bf16[1,4,16,512]{3,2,1,0:T(8,128)(2,1)S(1)} collective-permute-done((bf16[1,4,16,512]{3,2,1,0:T(8,128)(2,1)S(1)}, bf16[1,4,16,512]{3,2,1,0:T(8,128)(2,1)S(1)}, u32[]{:S(2)}, u32[]{:S(2)}) %collective-permute-start.27) | collective-permute-done | bytes 65568 | tf_op jit(solution)/shard_map/ppermute | solution.py:335
  154.5 4.8 %all-to-all-start.3 = ((bf16[8,2,16,512]{3,2,1,0:T(8,128)(2,1)}), bf16[8,2,16,512]{3,2,1,0:T(8,128)(2,1)S(1)}, u32[]{:S(2)}, u32[]{:S(2)}) async-start(bf16[8,2,16,512]{3,2,1,0:T(8,128)(2,1)} %get-tuple-element.120), calls=%async_computation.3 | async-start | bytes 524288 | tf_op jit(solution)/shard_map/all_to_all | solution.py:378
  159.3 2.9 %collective-permute-start.34 = (bf16[1,4,16,512]{3,2,1,0:T(8,128)(2,1)S(1)}, bf16[1,4,16,512]{3,2,1,0:T(8,128)(2,1)S(1)}, u32[]{:S(2)}, u32[]{:S(2)}) collective-permute-start(bf16[1,4,16,512]{3,2,1,0:T(8,128)(2,1)S(1)} %get-tuple-element.118), channel_id=1, source_target_pairs={{0,16},{4,20},{8,24},{12,28},{16,0},{20,4},{24,8},{28,12},{1,17},{... | collective-permute-start | bytes 196616 | tf_op jit(solution)/shard_map/ppermute | solution.py:335
  162.2 9.0 %collective-permute-done.34.refs_1_ = bf16[1,4,16,512]{3,2,1,0:T(8,128)(2,1)S(1)} collective-permute-done((bf16[1,4,16,512]{3,2,1,0:T(8,128)(2,1)S(1)}, bf16[1,4,16,512]{3,2,1,0:T(8,128)(2,1)S(1)}, u32[]{:S(2)}, u32[]{:S(2)}) %collective-permute-start.34) | collective-permute-done | bytes 65568 | tf_op jit(solution)/shard_map/ppermute | solution.py:335
  179.0 13.3 %all_to_all.25.got_ref = bf16[8,2,16,512]{3,2,1,0:T(8,128)(2,1)S(1)} all-to-all(bf16[8,2,16,512]{3,2,1,0:T(8,128)(2,1)S(1)} %get-tuple-element.125), channel_id=1, replica_groups=mesh['edge'=8,'feat'=4] {'edge'}, dimensions={0} | all-to-all | bytes 524288 | tf_op jit(solution)/shard_map/all_to_all | solution.py:378
  (161 shorter events, 74.3 us)
Async XLA Ops:
  9.3 9.5 %collective-permute-start.4 = (bf16[2,4,32,512]{3,2,1,0:T(8,128)(2,1)}, bf16[2,4,32,512]{3,2,1,0:T(8,128)(2,1)S(1)}, u32[]{:S(2)}, u32[]{:S(2)}) collective-permute-start(bf16[2,4,32,512]{3,2,1,0:T(8,128)(2,1)} %get-tuple-element.71), channel_id=1, source_target_pairs={{0,4},{4,0},{8,12},{12,8},{16,20},{20,16},{24,28},{28,24},{1,5},{5... | collective-permute-start | bytes 786440 | tf_op jit(solution)/shard_map/ppermute | solution.py:335
  11.4 17.1 %collective-permute-start.3 = (bf16[2,4,32,512]{3,2,1,0:T(8,128)(2,1)}, bf16[2,4,32,512]{3,2,1,0:T(8,128)(2,1)S(1)}, u32[]{:S(2)}, u32[]{:S(2)}) collective-permute-start(bf16[2,4,32,512]{3,2,1,0:T(8,128)(2,1)} %get-tuple-element.69), channel_id=1, source_target_pairs={{0,4},{4,0},{8,12},{12,8},{16,20},{20,16},{24,28},{28,24},{1,5},{5... | collective-permute-start | bytes 786440 | tf_op jit(solution)/shard_map/ppermute | solution.py:335
  18.9 9.6 %collective-permute-start.5 = (bf16[2,4,32,512]{3,2,1,0:T(8,128)(2,1)S(1)}, bf16[2,4,32,512]{3,2,1,0:T(8,128)(2,1)S(1)}, u32[]{:S(2)}, u32[]{:S(2)}) collective-permute-start(bf16[2,4,32,512]{3,2,1,0:T(8,128)(2,1)S(1)} %shard_map.97), channel_id=1, source_target_pairs={{0,8},{4,12},{8,0},{12,4},{16,24},{20,28},{24,16},{28,20},{1,9},{5... | collective-permute-start | bytes 786440 | tf_op jit(solution)/shard_map/ppermute | solution.py:335
  26.4 9.8 %collective-permute-start.7 = (bf16[2,4,32,512]{3,2,1,0:T(8,128)(2,1)}, bf16[2,4,32,512]{3,2,1,0:T(8,128)(2,1)S(1)}, u32[]{:S(2)}, u32[]{:S(2)}) collective-permute-start(bf16[2,4,32,512]{3,2,1,0:T(8,128)(2,1)} %get-tuple-element.75), channel_id=1, source_target_pairs={{0,4},{4,0},{8,12},{12,8},{16,20},{20,16},{24,28},{28,24},{1,5},{5... | collective-permute-start | bytes 786440 | tf_op jit(solution)/shard_map/ppermute | solution.py:335
  28.6 7.6 %collective-permute-start.6 = (bf16[1,4,32,512]{3,2,1,0:T(8,128)(2,1)S(1)}, bf16[1,4,32,512]{3,2,1,0:T(8,128)(2,1)S(1)}, u32[]{:S(2)}, u32[]{:S(2)}) collective-permute-start(bf16[1,4,32,512]{3,2,1,0:T(8,128)(2,1)S(1)} %get-tuple-element.73), channel_id=1, source_target_pairs={{0,16},{4,20},{8,24},{12,28},{16,0},{20,4},{24,8},{28,12},{1,17},{... | collective-permute-start | bytes 393224 | tf_op jit(solution)/shard_map/ppermute | solution.py:335
  36.3 10.3 %collective-permute-start.12 = (bf16[2,4,32,512]{3,2,1,0:T(8,128)(2,1)S(1)}, bf16[2,4,32,512]{3,2,1,0:T(8,128)(2,1)S(1)}, u32[]{:S(2)}, u32[]{:S(2)}) collective-permute-start(bf16[2,4,32,512]{3,2,1,0:T(8,128)(2,1)S(1)} %get-tuple-element.79), channel_id=1, source_target_pairs={{0,8},{4,12},{8,0},{12,4},{16,24},{20,28},{24,16},{28,20},{1,9},{5... | collective-permute-start | bytes 786440 | tf_op jit(solution)/shard_map/ppermute | solution.py:335
  38.0 8.6 %collective-permute-start.9 = (bf16[4,32,512]{2,1,0:T(8,128)(2,1)S(1)}, bf16[4,32,512]{2,1,0:T(8,128)(2,1)S(1)}, u32[]{:S(2)}, u32[]{:S(2)}) collective-permute-start(bf16[4,32,512]{2,1,0:T(8,128)(2,1)S(1)} %get-tuple-element.76.refs_4_), channel_id=1, source_target_pairs={{0,2},{1,3},{2,0},{3,1},{4,6},{5,7},{6,4},{7,5},{8,10},{9,11},{10,... | collective-permute-start | bytes 393224 | tf_op jit(solution)/shard_map/ppermute | solution.py:335
  39.6 7.0 %collective-permute-start.8 = (bf16[4,32,512]{2,1,0:T(8,128)(2,1)S(1)}, bf16[4,32,512]{2,1,0:T(8,128)(2,1)S(1)}, u32[]{:S(2)}, u32[]{:S(2)}) collective-permute-start(bf16[4,32,512]{2,1,0:T(8,128)(2,1)S(1)} %get-tuple-element.76.refs_4_), channel_id=1, source_target_pairs={{0,1},{1,0},{2,3},{3,2},{4,5},{5,4},{6,7},{7,6},{8,9},{9,8},{10,11... | collective-permute-start | bytes 393224 | tf_op jit(solution)/shard_map/ppermute | solution.py:335
  51.0 26.4 %all-to-all-start = ((bf16[8,2,32,512]{3,2,1,0:T(8,128)(2,1)}), bf16[8,2,32,512]{3,2,1,0:T(8,128)(2,1)S(1)}, u32[]{:S(2)}, u32[]{:S(2)}) async-start(bf16[8,2,32,512]{3,2,1,0:T(8,128)(2,1)} %get-tuple-element.89), calls=%async_computation | async-start | bytes 1048576 | tf_op jit(solution)/shard_map/all_to_all | solution.py:378
  55.2 14.8 %collective-permute-start.14 = (bf16[2,4,32,512]{3,2,1,0:T(8,128)(2,1)S(1)}, bf16[2,4,32,512]{3,2,1,0:T(8,128)(2,1)S(1)}, u32[]{:S(2)}, u32[]{:S(2)}) collective-permute-start(bf16[2,4,32,512]{3,2,1,0:T(8,128)(2,1)S(1)} %copy-done.18), channel_id=1, source_target_pairs={{0,4},{4,0},{8,12},{12,8},{16,20},{20,16},{24,28},{28,24},{1,5},{5... | collective-permute-start | bytes 786440 | tf_op jit(solution)/shard_map/ppermute | solution.py:335
  57.2 18.0 %collective-permute-start.13 = (bf16[1,4,32,512]{3,2,1,0:T(8,128)(2,1)S(1)}, bf16[1,4,32,512]{3,2,1,0:T(8,128)(2,1)S(1)}, u32[]{:S(2)}, u32[]{:S(2)}) collective-permute-start(bf16[1,4,32,512]{3,2,1,0:T(8,128)(2,1)S(1)} %get-tuple-element.81), channel_id=1, source_target_pairs={{0,16},{4,20},{8,24},{12,28},{16,0},{20,4},{24,8},{28,12},{1,17},{... | collective-permute-start | bytes 393224 | tf_op jit(solution)/shard_map/ppermute | solution.py:335
  59.6 19.4 %collective-permute-start.18 = (bf16[2,4,32,512]{3,2,1,0:T(8,128)(2,1)S(1)}, bf16[2,4,32,512]{3,2,1,0:T(8,128)(2,1)S(1)}, u32[]{:S(2)}, u32[]{:S(2)}) collective-permute-start(bf16[2,4,32,512]{3,2,1,0:T(8,128)(2,1)S(1)} %copy-done.16), channel_id=1, source_target_pairs={{0,4},{4,0},{8,12},{12,8},{16,20},{20,16},{24,28},{28,24},{1,5},{5... | collective-permute-start | bytes 786440 | tf_op jit(solution)/shard_map/ppermute | solution.py:335
  75.4 7.2 %collective-permute-start.19 = (bf16[2,4,32,512]{3,2,1,0:T(8,128)(2,1)S(1)}, bf16[2,4,32,512]{3,2,1,0:T(8,128)(2,1)S(1)}, u32[]{:S(2)}, u32[]{:S(2)}) collective-permute-start(bf16[2,4,32,512]{3,2,1,0:T(8,128)(2,1)S(1)} %get-tuple-element.87), channel_id=1, source_target_pairs={{0,8},{4,12},{8,0},{12,4},{16,24},{20,28},{24,16},{28,20},{1,9},{5... | collective-permute-start | bytes 786440 | tf_op jit(solution)/shard_map/ppermute | solution.py:335
  86.0 28.2 %all-to-all-start.1 = ((bf16[8,2,32,512]{3,2,1,0:T(8,128)(2,1)}), bf16[8,2,32,512]{3,2,1,0:T(8,128)(2,1)S(1)}, u32[]{:S(2)}, u32[]{:S(2)}) async-start(bf16[8,2,32,512]{3,2,1,0:T(8,128)(2,1)} %get-tuple-element.100), calls=%async_computation.1 | async-start | bytes 1048576 | tf_op jit(solution)/shard_map/all_to_all | solution.py:378
  91.8 11.5 %collective-permute-start.21 = (bf16[2,4,16,512]{3,2,1,0:T(8,128)(2,1)S(1)}, bf16[2,4,16,512]{3,2,1,0:T(8,128)(2,1)S(1)}, u32[]{:S(2)}, u32[]{:S(2)}) collective-permute-start(bf16[2,4,16,512]{3,2,1,0:T(8,128)(2,1)S(1)} %copy-done.27), channel_id=1, source_target_pairs={{0,4},{4,0},{8,12},{12,8},{16,20},{20,16},{24,28},{28,24},{1,5},{5... | collective-permute-start | bytes 393224 | tf_op jit(solution)/shard_map/ppermute | solution.py:335
  93.8 18.3 %collective-permute-start.20 = (bf16[1,4,32,512]{3,2,1,0:T(8,128)(2,1)S(1)}, bf16[1,4,32,512]{3,2,1,0:T(8,128)(2,1)S(1)}, u32[]{:S(2)}, u32[]{:S(2)}) collective-permute-start(bf16[1,4,32,512]{3,2,1,0:T(8,128)(2,1)S(1)} %get-tuple-element.92), channel_id=1, source_target_pairs={{0,16},{4,20},{8,24},{12,28},{16,0},{20,4},{24,8},{28,12},{1,17},{... | collective-permute-start | bytes 393224 | tf_op jit(solution)/shard_map/ppermute | solution.py:335
  96.2 19.5 %collective-permute-start.25 = (bf16[2,4,16,512]{3,2,1,0:T(8,128)(2,1)S(1)}, bf16[2,4,16,512]{3,2,1,0:T(8,128)(2,1)S(1)}, u32[]{:S(2)}, u32[]{:S(2)}) collective-permute-start(bf16[2,4,16,512]{3,2,1,0:T(8,128)(2,1)S(1)} %copy-done.25), channel_id=1, source_target_pairs={{0,4},{4,0},{8,12},{12,8},{16,20},{20,16},{24,28},{28,24},{1,5},{5... | collective-permute-start | bytes 393224 | tf_op jit(solution)/shard_map/ppermute | solution.py:335
  112.4 6.9 %collective-permute-start.23 = (bf16[4,32,512]{2,1,0:T(8,128)(2,1)S(1)}, bf16[4,32,512]{2,1,0:T(8,128)(2,1)S(1)}, u32[]{:S(2)}, u32[]{:S(2)}) collective-permute-start(bf16[4,32,512]{2,1,0:T(8,128)(2,1)S(1)} %get-tuple-element.95.refs_4_), channel_id=1, source_target_pairs={{0,2},{1,3},{2,0},{3,1},{4,6},{5,7},{6,4},{7,5},{8,10},{9,11},{10,... | collective-permute-start | bytes 393224 | tf_op jit(solution)/shard_map/ppermute | solution.py:335
  122.7 25.3 %all-to-all-start.2 = ((bf16[8,2,32,512]{3,2,1,0:T(8,128)(2,1)}), bf16[8,2,32,512]{3,2,1,0:T(8,128)(2,1)S(1)}, u32[]{:S(2)}, u32[]{:S(2)}) async-start(bf16[8,2,32,512]{3,2,1,0:T(8,128)(2,1)} %get-tuple-element.113), calls=%async_computation.2 | async-start | bytes 1048576 | tf_op jit(solution)/shard_map/all_to_all | solution.py:378
  128.4 11.5 %collective-permute-start.28 = (bf16[2,4,16,512]{3,2,1,0:T(8,128)(2,1)S(1)}, bf16[2,4,16,512]{3,2,1,0:T(8,128)(2,1)S(1)}, u32[]{:S(2)}, u32[]{:S(2)}) collective-permute-start(bf16[2,4,16,512]{3,2,1,0:T(8,128)(2,1)S(1)} %copy-done.23), channel_id=1, source_target_pairs={{0,4},{4,0},{8,12},{12,8},{16,20},{20,16},{24,28},{28,24},{1,5},{5... | collective-permute-start | bytes 393224 | tf_op jit(solution)/shard_map/ppermute | solution.py:335
  130.4 15.5 %collective-permute-start.27 = (bf16[1,4,16,512]{3,2,1,0:T(8,128)(2,1)S(1)}, bf16[1,4,16,512]{3,2,1,0:T(8,128)(2,1)S(1)}, u32[]{:S(2)}, u32[]{:S(2)}) collective-permute-start(bf16[1,4,16,512]{3,2,1,0:T(8,128)(2,1)S(1)} %get-tuple-element.105), channel_id=1, source_target_pairs={{0,16},{4,20},{8,24},{12,28},{16,0},{20,4},{24,8},{28,12},{1,17},{... | collective-permute-start | bytes 196616 | tf_op jit(solution)/shard_map/ppermute | solution.py:335
  132.8 16.8 %collective-permute-start.32 = (bf16[2,4,16,512]{3,2,1,0:T(8,128)(2,1)S(1)}, bf16[2,4,16,512]{3,2,1,0:T(8,128)(2,1)S(1)}, u32[]{:S(2)}, u32[]{:S(2)}) collective-permute-start(bf16[2,4,16,512]{3,2,1,0:T(8,128)(2,1)S(1)} %copy-done.21), channel_id=1, source_target_pairs={{0,4},{4,0},{8,12},{12,8},{16,20},{20,16},{24,28},{28,24},{1,5},{5... | collective-permute-start | bytes 393224 | tf_op jit(solution)/shard_map/ppermute | solution.py:335
  154.5 18.7 %all-to-all-start.3 = ((bf16[8,2,16,512]{3,2,1,0:T(8,128)(2,1)}), bf16[8,2,16,512]{3,2,1,0:T(8,128)(2,1)S(1)}, u32[]{:S(2)}, u32[]{:S(2)}) async-start(bf16[8,2,16,512]{3,2,1,0:T(8,128)(2,1)} %get-tuple-element.120), calls=%async_computation.3 | async-start | bytes 524288 | tf_op jit(solution)/shard_map/all_to_all | solution.py:378
  159.3 12.0 %collective-permute-start.34 = (bf16[1,4,16,512]{3,2,1,0:T(8,128)(2,1)S(1)}, bf16[1,4,16,512]{3,2,1,0:T(8,128)(2,1)S(1)}, u32[]{:S(2)}, u32[]{:S(2)}) collective-permute-start(bf16[1,4,16,512]{3,2,1,0:T(8,128)(2,1)S(1)} %get-tuple-element.118), channel_id=1, source_target_pairs={{0,16},{4,20},{8,24},{12,28},{16,0},{20,4},{24,8},{28,12},{1,17},{... | collective-permute-start | bytes 196616 | tf_op jit(solution)/shard_map/ppermute | solution.py:335
  (49 other events, 320.4 us)

commit v4 on v3

v4 whole, which is shorter than its diff:
```python
import jax
import jax.numpy as jnp
from jax import lax
from jax.experimental import pallas as pl
from jax.experimental.pallas import tpu as pltpu
from jax.sharding import PartitionSpec as P

SHARES = (3, 3, 2)
READ_CAP = 2
VMEM_BYTES = 12 * 1024 * 1024
UNIT_TIME, STEP_TIME, LATENCY = 10.5, 1.2, 2.0

SMEM = pl.BlockSpec(memory_space=pltpu.SMEM)
VMEM = pl.BlockSpec(memory_space=pltpu.VMEM)
HBM = pl.BlockSpec(memory_space=pltpu.HBM)
TOKEN = jax.ShapeDtypeStruct((8, 128), jnp.float32)


def call(body, out_shape, in_specs, out_specs, operands, scratch=(), aliases=None, limit=VMEM_BYTES):
    return pl.pallas_call(
        body,
        out_shape=out_shape,
        in_specs=in_specs,
        out_specs=out_specs,
        scratch_shapes=list(scratch),
        input_output_aliases=aliases or {},
        compiler_params=pltpu.CompilerParams(vmem_limit_bytes=limit),
        cost_estimate=pl.CostEstimate(flops=0, bytes_accessed=1, transcendentals=0),
    )(*operands)


def split(value, size):
    if size & (size - 1) == 0:
        return value >> (size.bit_length() - 1), value & (size - 1)
    return lax.div(value, size), lax.rem(value, size)


def reversed_bits(value, bits):
    result = value & 1
    for i in range(1, bits):
        result = (result << 1) | ((value >> i) & 1)
    return result


def offsets_of(size, lowest):
    offsets, bit = [0], size // 2
    while bit >= lowest:
        offsets += [offset | bit for offset in offsets]
        bit //= 2
    return offsets


def lay_tiles(table, base, tiles, lhs, spans, row_base, blocks, block, at=0):
    for b in range(blocks):
        for c in range(blocks):
            entry = table[base + b * blocks + c]
            tile = tiles[jnp.maximum(entry - 1, 0)]
            tile = jnp.where(entry > 0, tile, jnp.zeros_like(tile))
            top = at
            for first, rows in spans:
                lhs[pl.ds(top + b * rows, rows), pl.ds(c * block, block)] = tile[first - row_base : first - row_base + rows]
                top = top + blocks * rows


def first_part(me, slot, col, tile_id, touched, tiles, features, after, first, count, span):
    block = tiles.shape[1]
    blocks = features.shape[0] // block
    width = features.shape[1]
    edges, cap = touched.shape[1], touched.shape[2]
    bits = edges.bit_length() - 1
    products = slot.shape[0]
    start, rows = span
    square = blocks * blocks

    def body(me_ref, slot_hbm, col_hbm, id_hbm, touched_ref, tiles_hbm, x_hbm, after_ref, *refs):
        table, out, x_out, *scratch = refs
        slot_ref, col_ref, id_ref, tiles_ref, lhs, bases, sems = scratch
        loads = [
            pltpu.make_async_copy(slot_hbm, slot_ref, sems.at[0]),
            pltpu.make_async_copy(col_hbm, col_ref, sems.at[1]),
            pltpu.make_async_copy(id_hbm, id_ref, sems.at[2]),
            pltpu.make_async_copy(x_hbm, x_out, sems.at[3]),
            pltpu.make_async_copy(tiles_hbm.at[:, pl.ds(start, rows)], tiles_ref, sems.at[4]),
        ]
        for load in loads:
            load.start()

        def clear(i, carry):
            table[i] = 0
            return carry

        lax.fori_loop(0, edges * square, clear, 0, unroll=16)

        def place_slot(k, carry):
            owner, _ = split(k, cap)
            place = reversed_bits(owner ^ me_ref[0], bits)
            bases[k] = (place * blocks + touched_ref[k]) * blocks
            return carry

        lax.fori_loop(0, edges * cap, place_slot, 0, unroll=8)
        for load in loads[:3]:
            load.wait()

        def enter(k, carry):
            table[bases[slot_ref[k]] + col_ref[k]] = id_ref[k] + 1
            return carry

        lax.fori_loop(0, products, enter, 0, unroll=8)
        for load in loads[3:]:
            load.wait()

        def one_owner(i, carry):
            at = pl.multiple_of(i * blocks * rows, blocks * rows)
            lay_tiles(table, (first + i) * square, tiles_ref, lhs, [span], start, blocks, block, at)
            return carry

        lax.fori_loop(0, count, one_owner, 0)
        total = jnp.dot(lhs[...], x_out[...], preferred_element_type=jnp.float32)
        out[...] = total.astype(jnp.bfloat16).reshape(out.shape)

    return call(
        body,
        [
            jax.ShapeDtypeStruct((edges * square,), jnp.int32),
            jax.ShapeDtypeStruct((count, blocks, rows, width), jnp.bfloat16),
            jax.ShapeDtypeStruct(features.shape, jnp.bfloat16),
        ],
        [SMEM, HBM, HBM, HBM, SMEM, HBM, HBM, SMEM],
        [SMEM, VMEM, VMEM],
        (me, slot, col, tile_id, touched[me[0]].reshape(-1), tiles, features, after),
        [
            pltpu.SMEM((products,), jnp.int32),
            pltpu.SMEM((products,), jnp.int32),
            pltpu.SMEM((products,), jnp.int32),
            pltpu.VMEM((tiles.shape[0], rows, block), jnp.bfloat16),
            pltpu.VMEM((count * blocks * rows, blocks * block), jnp.bfloat16),
            pltpu.SMEM((edges * cap,), jnp.int32),
            pltpu.SemaphoreType.DMA((5,)),
        ],
        limit=62 * 1024 * 1024,
    )


def other_parts(table, tiles, inputs, jobs, weight=None):
    block = tiles.shape[1]
    blocks = inputs.shape[0] // block
    width = inputs.shape[1]
    most = max(sum(rows for _, rows in spans) for _, _, spans in jobs) * blocks
    given = [] if weight is None else [weight]
    shapes = [
        jax.ShapeDtypeStruct((count, blocks, rows, width), jnp.bfloat16) for _, count, spans in jobs for _, rows in spans
    ]

    def body(table_ref, tiles_hbm, x_ref, *refs):
        outs = refs[len(given) :]
        tiles_ref, lhs, sems = outs[-3:]
        load = pltpu.make_async_copy(tiles_hbm, tiles_ref, sems.at[0])
        load.start()
        if given:
            load_weight = pltpu.make_async_copy(refs[0], outs[-5], sems.at[1])
            load_weight.start()
            outs[-4][...] = jnp.zeros_like(outs[-4])
        load.wait()
        for first, count, spans in jobs:
            height = blocks * sum(rows for _, rows in spans)

            def one_owner(i, carry):
                lay_tiles(table_ref, (first + i) * blocks * blocks, tiles_ref, lhs, spans, 0, blocks, block)
                total = jnp.dot(lhs[pl.ds(0, height)], x_ref[...], preferred_element_type=jnp.float32)
                total = total.astype(jnp.bfloat16)
                at = 0
                for out, (_, rows) in zip(outs, spans):
                    out[i] = total[at : at + blocks * rows].reshape(blocks, rows, width)
                    at += blocks * rows
                return carry

            lax.fori_loop(0, count, one_owner, 0)
            outs = outs[len(spans) :]
        if given:
            load_weight.wait()

    extra = [jax.ShapeDtypeStruct(weight.shape, weight.dtype), TOKEN] if given else []
    results = call(
        body,
        shapes + extra,
        [SMEM, HBM, VMEM] + [HBM] * len(given),
        [VMEM] * (len(shapes) + len(extra)),
        (table, tiles, inputs, *given),
        [
            pltpu.VMEM(tiles.shape, jnp.bfloat16),
            pltpu.VMEM((most, blocks * block), jnp.bfloat16),
            pltpu.SemaphoreType.DMA((2,)),
        ],
    )
    grouped, at = [], 0
    for _, _, spans in jobs:
        grouped.append(results[at : at + len(spans)])
        at += len(spans)
    return (grouped, *results[at:]) if given else grouped


def combine(token, total, got):
    count, *shape = total.shape
    left = count // 2

    def body(token_ref, total_ref, got_ref, *outs):
        def add(i, carry):
            value = total_ref[i].astype(jnp.float32) + got_ref[i].astype(jnp.float32)
            if not left:
                outs[0][...] = value.astype(jnp.bfloat16)
            else:

                @pl.when(i < left)
                def _():
                    outs[0][jnp.minimum(i, left - 1)] = value

                @pl.when(i >= left)
                def _():
                    outs[1][jnp.maximum(i - left, 0)] = value.astype(jnp.bfloat16)

            return carry

        lax.fori_loop(0, count, add, 0)
        outs[-1][...] = token_ref[...]

    if left:
        out_shape = [
            jax.ShapeDtypeStruct((left, *shape), jnp.float32),
            jax.ShapeDtypeStruct((count - left, *shape), jnp.bfloat16),
        ]
    else:
        out_shape = [jax.ShapeDtypeStruct(tuple(shape), jnp.bfloat16)]
    out_shape.append(TOKEN)
    return call(body, out_shape, [VMEM] * 3, [VMEM] * len(out_shape), (token, total, got))


def join(token, held, got):
    def body(token_ref, held_ref, got_ref, out, token_out):
        out[pl.ds(0, held.shape[0])] = held_ref[...]
        out[pl.ds(held.shape[0], got.shape[0])] = got_ref[...]
        token_out[...] = token_ref[...]

    both = jax.ShapeDtypeStruct((held.shape[0] + got.shape[0], *held.shape[1:]), held.dtype)
    return call(body, [both, TOKEN], [VMEM] * 3, [VMEM] * 2, (token, held, got))


def mix(token, mine, offsets, held, got, weight):
    _, blocks, rows, depth = held.shape
    width = weight.shape[1]

    def body(token_ref, mine_ref, held_ref, got_ref, w_ref, out_ref, token_out):
        total = jnp.zeros((blocks * rows, width), jnp.float32)
        for n, offset in enumerate(offsets):
            piece = (held_ref if n < held.shape[0] else got_ref)[n % held.shape[0]]
            at = pl.multiple_of((mine_ref[0] ^ offset) * depth, depth)
            total += jnp.dot(
                piece.reshape(blocks * rows, depth), w_ref[pl.ds(at, depth)], preferred_element_type=jnp.float32
            )
        out_ref[0] = jnp.maximum(total, 0.0).astype(jnp.bfloat16).reshape(blocks, rows, width)
        token_out[...] = token_ref[...]

    return call(
        body,
        [jax.ShapeDtypeStruct((1, blocks, rows, width), jnp.bfloat16), TOKEN],
        [VMEM, SMEM, VMEM, VMEM, VMEM],
        [VMEM] * 2,
        (token, mine, held, got, weight),
    )


def pick(token, choice, held, got):
    count = choice.shape[0]

    def body(token_ref, choice_ref, held_ref, got_ref, out, token_out):
        for i in range(count):
            n = i // READ_CAP
            source = held_ref if n < held.shape[0] else got_ref
            out[i] = source[n % held.shape[0], choice_ref[i]]
        token_out[...] = token_ref[...]

    return call(
        body,
        [jax.ShapeDtypeStruct((count, *held.shape[2:]), held.dtype), TOKEN],
        [VMEM, SMEM, VMEM, VMEM],
        [VMEM] * 2,
        (token, choice, held, got),
    )


def lay_out(token, me, readers, entry, offsets, held, got, far, outputs, span, block):
    count = readers.shape[0]
    _, blocks, _, width = held.shape
    start, rows = span
    slots = 2 * len(offsets) * READ_CAP

    def body(token_ref, me_ref, readers_ref, entry_ref, held_ref, got_ref, far_ref, *refs):
        hidden_ref, ghost_ref, token_out, sems = refs[-4:]
        own = pltpu.make_async_copy(held_ref.at[0], hidden_ref.at[:, pl.ds(start, rows)], sems.at[slots])
        own.start()

        def each(act):
            for n, offset in enumerate(offsets):
                for j in range(READ_CAP):
                    i = n * READ_CAP + j
                    listed = entry_ref[(me_ref[0] ^ offset) * READ_CAP + j]
                    source = held_ref if n < held.shape[0] else got_ref

                    @pl.when(listed >= 0)
                    def _():
                        _, b = split(readers_ref[listed], blocks)
                        target = ghost_ref.at[listed, pl.ds(start, rows)]
                        act(pltpu.make_async_copy(source.at[n % held.shape[0], b], target, sems.at[i]))

                    across = entry_ref[(me_ref[0] ^ 1 ^ offset) * READ_CAP + j]

                    @pl.when(across >= 0)
                    def _():
                        target = ghost_ref.at[across, pl.ds(start, rows)]
                        act(pltpu.make_async_copy(far_ref.at[i], target, sems.at[slots // 2 + i]))

        each(lambda copy: copy.start())
        token_out[...] = token_ref[...]
        own.wait()
        each(lambda copy: copy.wait())

    operands = (token, me, readers, entry, held, got, far, *outputs)
    return call(
        body,
        [
            jax.ShapeDtypeStruct((blocks, block, width), jnp.bfloat16),
            jax.ShapeDtypeStruct((count, block, width), jnp.bfloat16),
            TOKEN,
        ],
        [VMEM] + [SMEM] * 3 + [VMEM] * 3 + [HBM] * len(outputs),
        [HBM, HBM, VMEM],
        operands,
        [pltpu.SemaphoreType.DMA((slots + 1,))],
        aliases={len(operands) - 2: 0, len(operands) - 1: 1} if outputs else None,
    )


def local(features, tiles, tile_slot, tile_col, tile_id, touched, weight, readers):
    edges, feats = lax.axis_size("edge"), lax.axis_size("feat")
    half = edges // 2
    me, mine = lax.axis_index("edge"), lax.axis_index("feat")
    block = tiles.shape[1]
    blocks = features.shape[0] // block
    width = features.shape[1]
    unit = block // sum(SHARES)
    spans = [(sum(SHARES[:i]) * unit, share * unit) for i, share in enumerate(SHARES)]

    def flip(value, bit, axis="edge"):
        return lax.ppermute(value, axis, [(d, d ^ bit) for d in range(lax.axis_size(axis))])

    count = readers.shape[0]
    order = jnp.arange(count, dtype=jnp.int32)
    columns = offsets_of(edges, 2)
    neighbour = flip(readers, 1)

    def listed(values, owners):
        owner = values // blocks
        rank = jnp.sum(((owner[:, None] == owner[None, :]) & (order[None, :] < order[:, None])).astype(jnp.int32), axis=1)
        wanted = jnp.repeat(owners, READ_CAP)
        turn = jnp.arange(wanted.shape[0], dtype=jnp.int32) % READ_CAP
        return (owner[None, :] == wanted[:, None]) & (rank[None, :] == turn[:, None])

    hit = listed(neighbour, lax.bitwise_xor(me, jnp.array(columns, jnp.int32)))
    choice = jnp.sum(jnp.where(hit, (neighbour % blocks)[None, :], 0), axis=1)
    hit = listed(readers, jnp.arange(edges, dtype=jnp.int32))
    entry = jnp.sum(jnp.where(hit, order[None, :] + 1, 0), axis=1) - 1
    me, mine = me.reshape(1), mine.reshape(1)

    table, early, inputs = first_part(
        me, tile_slot, tile_col, tile_id, touched, tiles, features, neighbour, half, half, spans[0]
    )
    later, first_kept = other_parts(table, tiles, inputs, [(half, half, spans[1:]), (0, half, spans[:1])])
    away = [early, *later]
    (kept,), weight, token = other_parts(table, tiles, inputs, [(0, half, spans[1:])], weight)
    kept = [*first_kept, *kept]
    outputs = ()

    def chained(function, *operands):
        nonlocal token
        *results, token = function(token, *operands)
        return results

    def spread(held, size, lowest, axis, link, units):
        bit = size // 2
        while True:
            got = flip(held, bit, axis)
            yield link, units
            if bit == lowest:
                return held, got
            (held,) = chained(join, held, got)
            bit, units = bit // 2, units * 2

    def one_part(part):
        nonlocal outputs
        share = spans[part][1] / block
        got = flip(away[part], 1)
        yield "low", share * half
        total, sent = chained(combine, kept[part], got)
        bit = 2
        while bit < edges:
            got = flip(sent, bit)
            yield "high", share * 2
            total, *sent = chained(combine, total, got)
            sent = sent[0] if sent else None
            bit *= 2
        held, got = yield from spread(total[None], feats, 1, "feat", "feat", share * 0.6)
        (mixed,) = chained(mix, mine, offsets_of(feats, 1), held, got, weight)
        held, got = yield from spread(mixed, edges, 2, "edge", "high", share * 1.5)
        (picked,) = chained(pick, choice, held, got)
        far = flip(picked, 1)
        yield "low", share * 2
        outputs = chained(lay_out, me, readers, entry, columns, held, got, far, outputs, spans[part], block)

    now, free, waiting = 0.0, {"low": 0.0, "high": 0.0, "feat": 0.0}, []

    def advance(part, steps):
        nonlocal now
        link, units = next(steps, (None, 0))
        now += STEP_TIME
        if link is not None:
            free[link] = max(free[link], now) + units * UNIT_TIME
            waiting.append((free[link] + LATENCY, part, steps))

    for part in range(len(spans)):
        advance(part, one_part(part))
    while waiting:
        ready, part, steps = min(waiting, key=lambda item: item[:2])
        waiting = [item for item in waiting if item[1] != part]
        now = max(now, ready)
        advance(part, steps)
    hidden, ghosts = outputs
    return hidden.reshape(blocks * block, width), ghosts.reshape(-1, width)


def solution(mesh):
    in_specs = (
        P("edge", "feat"),
        P("edge", None, None),
        P("edge"),
        P("edge"),
        P("edge"),
        P(),
        P(None, "feat"),
        P("edge"),
    )
    out_specs = (P("edge", "feat"), P("edge", "feat"))
    return jax.shard_map(local, mesh=mesh, in_specs=in_specs, out_specs=out_specs, check_vma=False)
```

time: 195 us -> 138 us (0.71)
  starting transfers between devices: 64.5 us -> 34.3 us
  blocking collectives: 13.3 us -> 0 us
  local copies, waits for them, and re-layouts: 14.7 us -> 6.42 us
  Pallas kernels: 25.4 us -> 20.2 us
    all_to_all x4 -> x0, starting transfers between devices: 20.1 us -> none  [one_part(): got = lax.all_to_all(picked, 'edge', split_axis=0, concat_axis=0)]
    all_to_all x1 -> x0, blocking collectives: 13.3 us -> none  [one_part(): got = lax.all_to_all(picked, 'edge', split_axis=0, concat_axis=0)]
    ppermute x38 -> x25, starting transfers between devices: 44.4 us -> 34.3 us  [flip(): lax.ppermute(value, axis, [(d, d ^ bit) for d in range(lax.axis_size(axis...]
    unnamed x62 -> x26, local copies, waits for them, and re-layouts: 13.9 us -> 5.5 us
    pallas_call x20 -> x27, Pallas kernels: 25.4 us -> 20.2 us  [call(): pl.pallas_call(body, out_shape=out_shape, in_specs=in_specs, out_specs=ou...]
    ppermute x38 -> x25, waiting for transfers between devices: 74.6 us -> 74.9 us  [flip(): lax.ppermute(value, axis, [(d, d ^ bit) for d in range(lax.axis_size(axis...]
  transfers between devices with their start and end apart: 42 -> 25, of which waited for: 24 -> 17; matrix products, arithmetic and copies ran while one was open for 1% -> 1% of each run, Pallas kernels for 6% -> 10%
where the time goes in v4:
time: 138 us
  waiting for transfers between devices  74.9 us (54%)
  starting transfers between devices  34.3 us (25%)
  Pallas kernels  20.2 us (15%)
  local copies, waits for them, and re-layouts  6.42 us (5%)
    ppermute x25, waiting for transfers between devices, flip(): lax.ppermute(value, axis, [(d, d ^ bit) for d in range(lax.axis_size(axis...  74.9 us
    ppermute x25, starting transfers between devices, flip(): lax.ppermute(value, axis, [(d, d ^ bit) for d in range(lax.axis_size(axis...  34.3 us
    pallas_call x27, Pallas kernels, call(): pl.pallas_call(body, out_shape=out_shape, in_specs=in_specs, out_specs=ou...  20.2 us
    unnamed x26, local copies, waits for them, and re-layouts  5.5 us
  transfers between devices with their start and end apart: 25, of which 17 were waited for; matrix products, arithmetic and copies ran while one was open for 1% of the time, Pallas kernels for 10%

profile of v4, /device:TPU:0, one launch (start us, length us, event | category | flops | bytes accessed | tf_op | source)
XLA Modules:
  0.0 137.6 jit_solution(18307329877786349631)
XLA Ops:
  0.7 3.0 %collective-permute-start = (s32[16]{0:T(128)}, s32[16]{0:T(128)S(1)}, u32[]{:S(2)}, u32[]{:S(2)}) collective-permute-start(s32[16]{0:T(128)} %readers_ref.5), channel_id=1, source_target_pairs={{0,4},{4,0},{8,12},{12,8},{16,20},{20,16},{24,28},{28,24},{1,5},{5... | collective-permute-start | bytes 200 | tf_op jit(solution)/shard_map/ppermute | solution.py:353
  5.9 3.7 %shard_map.104 = (s32[128]{0:T(128)}, bf16[4,4,48,512]{3,2,1,0:T(8,128)(2,1)}, bf16[512,512]{1,0:T(8,128)(2,1)}) custom-call(s32[1]{0:T(128)} %bitcast.me_ref, s32[96]{0:T(128)} %slot_hbm.1, s32[96]{0:T(128)} %col_hbm.1, s32[96]{0:T(128)} %id_hbm.1, s32[32]{0:T(128)} %reshape_squeeze.3.touched_ref, bf16[48,128,128]{2,1,0:T(8,128)(2,1)} %tiles_hbm.5, ...), custom_call_target="tpu_custom_call" | custom-call | bytes 1 | tf_op jit(solution)/shard_map/pallas_call | solution.py:20
  9.6 2.1 %collective-permute-start.1 = (bf16[4,4,48,512]{3,2,1,0:T(8,128)(2,1)}, bf16[4,4,48,512]{3,2,1,0:T(8,128)(2,1)S(1)}, u32[]{:S(2)}, u32[]{:S(2)}) collective-permute-start(bf16[4,4,48,512]{3,2,1,0:T(8,128)(2,1)} %get-tuple-element.72), channel_id=1, source_target_pairs={{0,4},{4,0},{8,12},{12,8},{16,20},{20,16},{24,28},{28,24},{1,5},{5... | collective-permute-start | bytes 2359304 | tf_op jit(solution)/shard_map/ppermute | solution.py:353
  13.4 3.2 %shard_map.106 = (bf16[4,4,48,512]{3,2,1,0:T(8,128)(2,1)S(1)}, bf16[4,4,32,512]{3,2,1,0:T(8,128)(2,1)S(1)}, bf16[4,4,48,512]{3,2,1,0:T(8,128)(2,1)S(1)}) custom-call(s32[128]{0:T(128)S(1)} %copy-done.8, bf16[48,128,128]{2,1,0:T(8,128)(2,1)S(1)} %copy-done.4, bf16[512,512]{1,0:T(8,128)(2,1)S(1)} %copy-done.5), custom_call_target="tpu_custom_call" | custom-call | bytes 1 | tf_op jit(solution)/shard_map/pallas_call | solution.py:20
  16.8 2.2 %shard_map.105 = (bf16[4,4,48,512]{3,2,1,0:T(8,128)(2,1)S(1)}, bf16[4,4,32,512]{3,2,1,0:T(8,128)(2,1)S(1)}, bf16[2048,512]{1,0:T(8,128)(2,1)S(1)}, f32[8,128]{1,0:T(8,128)S(1)}) custom-call(s32[128]{0:T(128)S(1)} %copy-done.9, bf16[48,128,128]{2,1,0:T(8,128)(2,1)S(1)} %copy-done.4, bf16[512,512]{1,0:T(8,128)(2,1)S(1)} %copy-done.5, ...), custom_call_target="tpu_custom_call" | custom-call | bytes 1 | tf_op jit(solution)/shard_map/pallas_call | solution.py:20
  19.0 11.4 %collective-permute-done.1.got_ref = bf16[4,4,48,512]{3,2,1,0:T(8,128)(2,1)S(1)} collective-permute-done((bf16[4,4,48,512]{3,2,1,0:T(8,128)(2,1)}, bf16[4,4,48,512]{3,2,1,0:T(8,128)(2,1)S(1)}, u32[]{:S(2)}, u32[]{:S(2)}) %collective-permute-start.1) | collective-permute-done | bytes 786464 | tf_op jit(solution)/shard_map/ppermute | solution.py:353
  30.8 2.2 %collective-permute-start.2 = (bf16[2,4,48,512]{3,2,1,0:T(8,128)(2,1)S(1)}, bf16[2,4,48,512]{3,2,1,0:T(8,128)(2,1)S(1)}, u32[]{:S(2)}, u32[]{:S(2)}) collective-permute-start(bf16[2,4,48,512]{3,2,1,0:T(8,128)(2,1)S(1)} %get-tuple-element.75), channel_id=1, source_target_pairs={{0,8},{4,12},{8,0},{12,4},{16,24},{20,28},{24,16},{28,20},{1,9},{5... | collective-permute-start | bytes 1179656 | tf_op jit(solution)/shard_map/ppermute | solution.py:353
  34.5 6.4 %collective-permute-done.2.got_ref = bf16[2,4,48,512]{3,2,1,0:T(8,128)(2,1)S(1)} collective-permute-done((bf16[2,4,48,512]{3,2,1,0:T(8,128)(2,1)S(1)}, bf16[2,4,48,512]{3,2,1,0:T(8,128)(2,1)S(1)}, u32[]{:S(2)}, u32[]{:S(2)}) %collective-permute-start.2) | collective-permute-done | bytes 393248 | tf_op jit(solution)/shard_map/ppermute | solution.py:353
  41.0 3.1 %collective-permute-start.4 = (bf16[1,4,48,512]{3,2,1,0:T(8,128)(2,1)S(1)}, bf16[1,4,48,512]{3,2,1,0:T(8,128)(2,1)S(1)}, u32[]{:S(2)}, u32[]{:S(2)}) collective-permute-start(bf16[1,4,48,512]{3,2,1,0:T(8,128)(2,1)S(1)} %get-tuple-element.81), channel_id=1, source_target_pairs={{0,16},{4,20},{8,24},{12,28},{16,0},{20,4},{24,8},{28,12},{1,17},{... | collective-permute-start | bytes 589832 | tf_op jit(solution)/shard_map/ppermute | solution.py:353
  44.1 3.2 %collective-permute-done.3.got_ref = bf16[4,4,48,512]{3,2,1,0:T(8,128)(2,1)S(1)} collective-permute-done((bf16[4,4,48,512]{3,2,1,0:T(8,128)(2,1)S(1)}, bf16[4,4,48,512]{3,2,1,0:T(8,128)(2,1)S(1)}, u32[]{:S(2)}, u32[]{:S(2)}) %collective-permute-start.3) | collective-permute-done | bytes 786464 | tf_op jit(solution)/shard_map/ppermute | solution.py:353
  47.7 2.2 %collective-permute-start.7 = (bf16[2,4,48,512]{3,2,1,0:T(8,128)(2,1)S(1)}, bf16[2,4,48,512]{3,2,1,0:T(8,128)(2,1)S(1)}, u32[]{:S(2)}, u32[]{:S(2)}) collective-permute-start(bf16[2,4,48,512]{3,2,1,0:T(8,128)(2,1)S(1)} %get-tuple-element.89), channel_id=1, source_target_pairs={{0,8},{4,12},{8,0},{12,4},{16,24},{20,28},{24,16},{28,20},{1,9},{5... | collective-permute-start | bytes 1179656 | tf_op jit(solution)/shard_map/ppermute | solution.py:353
  50.0 1.9 %collective-permute-start.6 = (bf16[1,4,48,512]{3,2,1,0:T(8,128)(2,1)S(1)}, bf16[1,4,48,512]{3,2,1,0:T(8,128)(2,1)S(1)}, u32[]{:S(2)}, u32[]{:S(2)}) collective-permute-start(bf16[1,4,48,512]{3,2,1,0:T(8,128)(2,1)S(1)} %bitcast.9), channel_id=1, source_target_pairs={{0,2},{1,3},{2,0},{3,1},{4,6},{5,7},{6,4},{7,5},{8,10},{9,11},{10,... | collective-permute-start | bytes 589832 | tf_op jit(solution)/shard_map/ppermute | solution.py:353
  51.9 4.5 %collective-permute-done.5.got_ref = bf16[4,4,32,512]{3,2,1,0:T(8,128)(2,1)S(1)} collective-permute-done((bf16[4,4,32,512]{3,2,1,0:T(8,128)(2,1)S(1)}, bf16[4,4,32,512]{3,2,1,0:T(8,128)(2,1)S(1)}, u32[]{:S(2)}, u32[]{:S(2)}) %collective-permute-start.5) | collective-permute-done | bytes 524320 | tf_op jit(solution)/shard_map/ppermute | solution.py:353
  59.5 2.7 %collective-permute-start.10 = (bf16[1,4,48,512]{3,2,1,0:T(8,128)(2,1)S(1)}, bf16[1,4,48,512]{3,2,1,0:T(8,128)(2,1)S(1)}, u32[]{:S(2)}, u32[]{:S(2)}) collective-permute-start(bf16[1,4,48,512]{3,2,1,0:T(8,128)(2,1)S(1)} %get-tuple-element.98), channel_id=1, source_target_pairs={{0,16},{4,20},{8,24},{12,28},{16,0},{20,4},{24,8},{28,12},{1,17},{... | collective-permute-start | bytes 589832 | tf_op jit(solution)/shard_map/ppermute | solution.py:353
  62.2 8.5 %collective-permute-done.8.got_ref = bf16[2,4,32,512]{3,2,1,0:T(8,128)(2,1)S(1)} collective-permute-done((bf16[2,4,32,512]{3,2,1,0:T(8,128)(2,1)}, bf16[2,4,32,512]{3,2,1,0:T(8,128)(2,1)S(1)}, u32[]{:S(2)}, u32[]{:S(2)}) %collective-permute-start.8) | collective-permute-done | bytes 262176 | tf_op jit(solution)/shard_map/ppermute | solution.py:353
  70.8 2.0 %collective-permute-start.11 = (bf16[1,4,32,512]{3,2,1,0:T(8,128)(2,1)S(1)}, bf16[1,4,32,512]{3,2,1,0:T(8,128)(2,1)S(1)}, u32[]{:S(2)}, u32[]{:S(2)}) collective-permute-start(bf16[1,4,32,512]{3,2,1,0:T(8,128)(2,1)S(1)} %get-tuple-element.101), channel_id=1, source_target_pairs={{0,16},{4,20},{8,24},{12,28},{16,0},{20,4},{24,8},{28,12},{1,17},{... | collective-permute-start | bytes 393224 | tf_op jit(solution)/shard_map/ppermute | solution.py:353
  76.7 3.0 %collective-permute-done.11.got_ref = bf16[1,4,32,512]{3,2,1,0:T(8,128)(2,1)S(1)} collective-permute-done((bf16[1,4,32,512]{3,2,1,0:T(8,128)(2,1)S(1)}, bf16[1,4,32,512]{3,2,1,0:T(8,128)(2,1)S(1)}, u32[]{:S(2)}, u32[]{:S(2)}) %collective-permute-start.11) | collective-permute-done | bytes 131104 | tf_op jit(solution)/shard_map/ppermute | solution.py:353
  81.9 2.9 %collective-permute-done.13.got_ref = bf16[1,4,32,512]{3,2,1,0:T(8,128)(2,1)S(1)} collective-permute-done((bf16[1,4,32,512]{3,2,1,0:T(8,128)(2,1)S(1)}, bf16[1,4,32,512]{3,2,1,0:T(8,128)(2,1)S(1)}, u32[]{:S(2)}, u32[]{:S(2)}) %collective-permute-start.13) | collective-permute-done | bytes 131104 | tf_op jit(solution)/shard_map/ppermute | solution.py:353
  84.9 7.2 %collective-permute-done.14.got_ref = bf16[1,4,48,512]{3,2,1,0:T(8,128)(2,1)S(1)} collective-permute-done((bf16[1,4,48,512]{3,2,1,0:T(8,128)(2,1)S(1)}, bf16[1,4,48,512]{3,2,1,0:T(8,128)(2,1)S(1)}, u32[]{:S(2)}, u32[]{:S(2)}) %collective-permute-start.14) | collective-permute-done | bytes 196640 | tf_op jit(solution)/shard_map/ppermute | solution.py:353
  98.3 9.7 %collective-permute-done.17.got_ref = bf16[2,4,48,512]{3,2,1,0:T(8,128)(2,1)S(1)} collective-permute-done((bf16[2,4,48,512]{3,2,1,0:T(8,128)(2,1)S(1)}, bf16[2,4,48,512]{3,2,1,0:T(8,128)(2,1)S(1)}, u32[]{:S(2)}, u32[]{:S(2)}) %collective-permute-start.17) | collective-permute-done | bytes 393248 | tf_op jit(solution)/shard_map/ppermute | solution.py:353
  112.6 5.0 %collective-permute-done.20.far_ref = bf16[8,48,512]{2,1,0:T(8,128)(2,1)S(1)} collective-permute-done((bf16[8,48,512]{2,1,0:T(8,128)(2,1)S(1)}, bf16[8,48,512]{2,1,0:T(8,128)(2,1)S(1)}, u32[]{:S(2)}, u32[]{:S(2)}) %collective-permute-start.20) | collective-permute-done | bytes 393248 | tf_op jit(solution)/shard_map/ppermute | solution.py:353
  119.2 3.0 %collective-permute-done.21.got_ref = bf16[2,4,48,512]{3,2,1,0:T(8,128)(2,1)S(1)} collective-permute-done((bf16[2,4,48,512]{3,2,1,0:T(8,128)(2,1)S(1)}, bf16[2,4,48,512]{3,2,1,0:T(8,128)(2,1)S(1)}, u32[]{:S(2)}, u32[]{:S(2)}) %collective-permute-start.21) | collective-permute-done | bytes 393248 | tf_op jit(solution)/shard_map/ppermute | solution.py:353
  126.9 5.8 %collective-permute-done.23.far_ref = bf16[8,48,512]{2,1,0:T(8,128)(2,1)S(1)} collective-permute-done((bf16[8,48,512]{2,1,0:T(8,128)(2,1)S(1)}, bf16[8,48,512]{2,1,0:T(8,128)(2,1)S(1)}, u32[]{:S(2)}, u32[]{:S(2)}) %collective-permute-start.23) | collective-permute-done | bytes 393248 | tf_op jit(solution)/shard_map/ppermute | solution.py:353
  135.5 2.1 %shard_map.130 = (bf16[4,128,512]{2,1,0:T(8,128)(2,1)}, bf16[16,128,512]{2,1,0:T(8,128)(2,1)}, f32[8,128]{1,0:T(8,128)}) custom-call(f32[8,128]{1,0:T(8,128)S(1)} %get-tuple-element.128.token_ref, s32[1]{0:T(128)} %bitcast.me_ref, s32[16]{0:T(128)S(1)} %copy-done.7, ...), custom_call_target="tpu_custom_call", output_to_operand_aliasing={{0}: (7, {}), {1}: (8, {})} | custom-call | bytes 1 | tf_op jit(solution)/shard_map/pallas_call | solution.py:20
  (96 shorter events, 35.7 us)
Async XLA Ops:
  9.6 20.8 %collective-permute-start.1 = (bf16[4,4,48,512]{3,2,1,0:T(8,128)(2,1)}, bf16[4,4,48,512]{3,2,1,0:T(8,128)(2,1)S(1)}, u32[]{:S(2)}, u32[]{:S(2)}) collective-permute-start(bf16[4,4,48,512]{3,2,1,0:T(8,128)(2,1)} %get-tuple-element.72), channel_id=1, source_target_pairs={{0,4},{4,0},{8,12},{12,8},{16,20},{20,16},{24,28},{28,24},{1,5},{5... | collective-permute-start | bytes 2359304 | tf_op jit(solution)/shard_map/ppermute | solution.py:353
  16.7 30.6 %collective-permute-start.3 = (bf16[4,4,48,512]{3,2,1,0:T(8,128)(2,1)S(1)}, bf16[4,4,48,512]{3,2,1,0:T(8,128)(2,1)S(1)}, u32[]{:S(2)}, u32[]{:S(2)}) collective-permute-start(bf16[4,4,48,512]{3,2,1,0:T(8,128)(2,1)S(1)} %get-tuple-element.78), channel_id=1, source_target_pairs={{0,4},{4,0},{8,12},{12,8},{16,20},{20,16},{24,28},{28,24},{1,5},{5... | collective-permute-start | bytes 2359304 | tf_op jit(solution)/shard_map/ppermute | solution.py:353
  30.8 10.0 %collective-permute-start.2 = (bf16[2,4,48,512]{3,2,1,0:T(8,128)(2,1)S(1)}, bf16[2,4,48,512]{3,2,1,0:T(8,128)(2,1)S(1)}, u32[]{:S(2)}, u32[]{:S(2)}) collective-permute-start(bf16[2,4,48,512]{3,2,1,0:T(8,128)(2,1)S(1)} %get-tuple-element.75), channel_id=1, source_target_pairs={{0,8},{4,12},{8,0},{12,4},{16,24},{20,28},{24,16},{28,20},{1,9},{5... | collective-permute-start | bytes 1179656 | tf_op jit(solution)/shard_map/ppermute | solution.py:353
  33.0 23.4 %collective-permute-start.5 = (bf16[4,4,32,512]{3,2,1,0:T(8,128)(2,1)S(1)}, bf16[4,4,32,512]{3,2,1,0:T(8,128)(2,1)S(1)}, u32[]{:S(2)}, u32[]{:S(2)}) collective-permute-start(bf16[4,4,32,512]{3,2,1,0:T(8,128)(2,1)S(1)} %get-tuple-element.84), channel_id=1, source_target_pairs={{0,4},{4,0},{8,12},{12,8},{16,20},{20,16},{24,28},{28,24},{1,5},{5... | collective-permute-start | bytes 1572872 | tf_op jit(solution)/shard_map/ppermute | solution.py:353
  41.0 9.0 %collective-permute-start.4 = (bf16[1,4,48,512]{3,2,1,0:T(8,128)(2,1)S(1)}, bf16[1,4,48,512]{3,2,1,0:T(8,128)(2,1)S(1)}, u32[]{:S(2)}, u32[]{:S(2)}) collective-permute-start(bf16[1,4,48,512]{3,2,1,0:T(8,128)(2,1)S(1)} %get-tuple-element.81), channel_id=1, source_target_pairs={{0,16},{4,20},{8,24},{12,28},{16,0},{20,4},{24,8},{28,12},{1,17},{... | collective-permute-start | bytes 589832 | tf_op jit(solution)/shard_map/ppermute | solution.py:353
  47.7 11.7 %collective-permute-start.7 = (bf16[2,4,48,512]{3,2,1,0:T(8,128)(2,1)S(1)}, bf16[2,4,48,512]{3,2,1,0:T(8,128)(2,1)S(1)}, u32[]{:S(2)}, u32[]{:S(2)}) collective-permute-start(bf16[2,4,48,512]{3,2,1,0:T(8,128)(2,1)S(1)} %get-tuple-element.89), channel_id=1, source_target_pairs={{0,8},{4,12},{8,0},{12,4},{16,24},{20,28},{24,16},{28,20},{1,9},{5... | collective-permute-start | bytes 1179656 | tf_op jit(solution)/shard_map/ppermute | solution.py:353
  50.0 7.4 %collective-permute-start.6 = (bf16[1,4,48,512]{3,2,1,0:T(8,128)(2,1)S(1)}, bf16[1,4,48,512]{3,2,1,0:T(8,128)(2,1)S(1)}, u32[]{:S(2)}, u32[]{:S(2)}) collective-permute-start(bf16[1,4,48,512]{3,2,1,0:T(8,128)(2,1)S(1)} %bitcast.9), channel_id=1, source_target_pairs={{0,2},{1,3},{2,0},{3,1},{4,6},{5,7},{6,4},{7,5},{8,10},{9,11},{10,... | collective-permute-start | bytes 589832 | tf_op jit(solution)/shard_map/ppermute | solution.py:353
  57.4 15.4 %collective-permute-start.9 = (bf16[2,4,48,512]{3,2,1,0:T(8,128)(2,1)S(1)}, bf16[2,4,48,512]{3,2,1,0:T(8,128)(2,1)S(1)}, u32[]{:S(2)}, u32[]{:S(2)}) collective-permute-start(bf16[2,4,48,512]{3,2,1,0:T(8,128)(2,1)S(1)} %get-tuple-element.94.held_ref), channel_id=1, source_target_pairs={{0,1},{1,0},{2,3},{3,2},{4,5},{5,4},{6,7},{7,6},{8,9},{9,8},{10,11... | collective-permute-start | bytes 1179656 | tf_op jit(solution)/shard_map/ppermute | solution.py:353
  57.5 13.2 %collective-permute-start.8 = (bf16[2,4,32,512]{3,2,1,0:T(8,128)(2,1)}, bf16[2,4,32,512]{3,2,1,0:T(8,128)(2,1)S(1)}, u32[]{:S(2)}, u32[]{:S(2)}) collective-permute-start(bf16[2,4,32,512]{3,2,1,0:T(8,128)(2,1)} %get-tuple-element.92), channel_id=1, source_target_pairs={{0,8},{4,12},{8,0},{12,4},{16,24},{20,28},{24,16},{28,20},{1,9},{5... | collective-permute-start | bytes 786440 | tf_op jit(solution)/shard_map/ppermute | solution.py:353
  59.5 15.5 %collective-permute-start.10 = (bf16[1,4,48,512]{3,2,1,0:T(8,128)(2,1)S(1)}, bf16[1,4,48,512]{3,2,1,0:T(8,128)(2,1)S(1)}, u32[]{:S(2)}, u32[]{:S(2)}) collective-permute-start(bf16[1,4,48,512]{3,2,1,0:T(8,128)(2,1)S(1)} %get-tuple-element.98), channel_id=1, source_target_pairs={{0,16},{4,20},{8,24},{12,28},{16,0},{20,4},{24,8},{28,12},{1,17},{... | collective-permute-start | bytes 589832 | tf_op jit(solution)/shard_map/ppermute | solution.py:353
  70.8 8.9 %collective-permute-start.11 = (bf16[1,4,32,512]{3,2,1,0:T(8,128)(2,1)S(1)}, bf16[1,4,32,512]{3,2,1,0:T(8,128)(2,1)S(1)}, u32[]{:S(2)}, u32[]{:S(2)}) collective-permute-start(bf16[1,4,32,512]{3,2,1,0:T(8,128)(2,1)S(1)} %get-tuple-element.101), channel_id=1, source_target_pairs={{0,16},{4,20},{8,24},{12,28},{16,0},{20,4},{24,8},{28,12},{1,17},{... | collective-permute-start | bytes 393224 | tf_op jit(solution)/shard_map/ppermute | solution.py:353
  75.1 6.4 %collective-permute-start.12 = (bf16[1,4,48,512]{3,2,1,0:T(8,128)(2,1)S(1)}, bf16[1,4,48,512]{3,2,1,0:T(8,128)(2,1)S(1)}, u32[]{:S(2)}, u32[]{:S(2)}) collective-permute-start(bf16[1,4,48,512]{3,2,1,0:T(8,128)(2,1)S(1)} %bitcast.7), channel_id=1, source_target_pairs={{0,2},{1,3},{2,0},{3,1},{4,6},{5,7},{6,4},{7,5},{8,10},{9,11},{10,... | collective-permute-start | bytes 589832 | tf_op jit(solution)/shard_map/ppermute | solution.py:353
  79.7 5.0 %collective-permute-start.13 = (bf16[1,4,32,512]{3,2,1,0:T(8,128)(2,1)S(1)}, bf16[1,4,32,512]{3,2,1,0:T(8,128)(2,1)S(1)}, u32[]{:S(2)}, u32[]{:S(2)}) collective-permute-start(bf16[1,4,32,512]{3,2,1,0:T(8,128)(2,1)S(1)} %bitcast.11), channel_id=1, source_target_pairs={{0,2},{1,3},{2,0},{3,1},{4,6},{5,7},{6,4},{7,5},{8,10},{9,11},{10,... | collective-permute-start | bytes 393224 | tf_op jit(solution)/shard_map/ppermute | solution.py:353
  81.4 10.7 %collective-permute-start.14 = (bf16[1,4,48,512]{3,2,1,0:T(8,128)(2,1)S(1)}, bf16[1,4,48,512]{3,2,1,0:T(8,128)(2,1)S(1)}, u32[]{:S(2)}, u32[]{:S(2)}) collective-permute-start(bf16[1,4,48,512]{3,2,1,0:T(8,128)(2,1)S(1)} %get-tuple-element.107.held_ref), channel_id=1, source_target_pairs={{0,16},{4,20},{8,24},{12,28},{16,0},{20,4},{24,8},{28,12},{1,17},{... | collective-permute-start | bytes 589832 | tf_op jit(solution)/shard_map/ppermute | solution.py:353
  81.5 10.8 %collective-permute-start.15 = (bf16[2,4,48,512]{3,2,1,0:T(8,128)(2,1)S(1)}, bf16[2,4,48,512]{3,2,1,0:T(8,128)(2,1)S(1)}, u32[]{:S(2)}, u32[]{:S(2)}) collective-permute-start(bf16[2,4,48,512]{3,2,1,0:T(8,128)(2,1)S(1)} %get-tuple-element.109.held_ref), channel_id=1, source_target_pairs={{0,1},{1,0},{2,3},{3,2},{4,5},{5,4},{6,7},{7,6},{8,9},{9,8},{10,11... | collective-permute-start | bytes 1179656 | tf_op jit(solution)/shard_map/ppermute | solution.py:353
  84.8 11.8 %collective-permute-start.16 = (bf16[2,4,32,512]{3,2,1,0:T(8,128)(2,1)S(1)}, bf16[2,4,32,512]{3,2,1,0:T(8,128)(2,1)S(1)}, u32[]{:S(2)}, u32[]{:S(2)}) collective-permute-start(bf16[2,4,32,512]{3,2,1,0:T(8,128)(2,1)S(1)} %get-tuple-element.111.held_ref), channel_id=1, source_target_pairs={{0,1},{1,0},{2,3},{3,2},{4,5},{5,4},{6,7},{7,6},{8,9},{9,8},{10,11... | collective-permute-start | bytes 786440 | tf_op jit(solution)/shard_map/ppermute | solution.py:353
  92.1 15.8 %collective-permute-start.17 = (bf16[2,4,48,512]{3,2,1,0:T(8,128)(2,1)S(1)}, bf16[2,4,48,512]{3,2,1,0:T(8,128)(2,1)S(1)}, u32[]{:S(2)}, u32[]{:S(2)}) collective-permute-start(bf16[2,4,48,512]{3,2,1,0:T(8,128)(2,1)S(1)} %get-tuple-element.113.held_ref), channel_id=1, source_target_pairs={{0,8},{4,12},{8,0},{12,4},{16,24},{20,28},{24,16},{28,20},{1,9},{5... | collective-permute-start | bytes 1179656 | tf_op jit(solution)/shard_map/ppermute | solution.py:353
  94.4 15.7 %collective-permute-start.18 = (bf16[1,4,48,512]{3,2,1,0:T(8,128)(2,1)S(1)}, bf16[1,4,48,512]{3,2,1,0:T(8,128)(2,1)S(1)}, u32[]{:S(2)}, u32[]{:S(2)}) collective-permute-start(bf16[1,4,48,512]{3,2,1,0:T(8,128)(2,1)S(1)} %get-tuple-element.115.held_ref), channel_id=1, source_target_pairs={{0,16},{4,20},{8,24},{12,28},{16,0},{20,4},{24,8},{28,12},{1,17},{... | collective-permute-start | bytes 589832 | tf_op jit(solution)/shard_map/ppermute | solution.py:353
  97.0 14.0 %collective-permute-start.19 = (bf16[1,4,32,512]{3,2,1,0:T(8,128)(2,1)S(1)}, bf16[1,4,32,512]{3,2,1,0:T(8,128)(2,1)S(1)}, u32[]{:S(2)}, u32[]{:S(2)}) collective-permute-start(bf16[1,4,32,512]{3,2,1,0:T(8,128)(2,1)S(1)} %get-tuple-element.117.held_ref), channel_id=1, source_target_pairs={{0,16},{4,20},{8,24},{12,28},{16,0},{20,4},{24,8},{28,12},{1,17},{... | collective-permute-start | bytes 393224 | tf_op jit(solution)/shard_map/ppermute | solution.py:353
  108.5 9.1 %collective-permute-start.20 = (bf16[8,48,512]{2,1,0:T(8,128)(2,1)S(1)}, bf16[8,48,512]{2,1,0:T(8,128)(2,1)S(1)}, u32[]{:S(2)}, u32[]{:S(2)}) collective-permute-start(bf16[8,48,512]{2,1,0:T(8,128)(2,1)S(1)} %get-tuple-element.119), channel_id=1, source_target_pairs={{0,4},{4,0},{8,12},{12,8},{16,20},{20,16},{24,28},{28,24},{1,5},{5... | collective-permute-start | bytes 1179656 | tf_op jit(solution)/shard_map/ppermute | solution.py:353
  110.1 12.1 %collective-permute-start.21 = (bf16[2,4,48,512]{3,2,1,0:T(8,128)(2,1)S(1)}, bf16[2,4,48,512]{3,2,1,0:T(8,128)(2,1)S(1)}, u32[]{:S(2)}, u32[]{:S(2)}) collective-permute-start(bf16[2,4,48,512]{3,2,1,0:T(8,128)(2,1)S(1)} %get-tuple-element.121.held_ref), channel_id=1, source_target_pairs={{0,8},{4,12},{8,0},{12,4},{16,24},{20,28},{24,16},{28,20},{1,9},{5... | collective-permute-start | bytes 1179656 | tf_op jit(solution)/shard_map/ppermute | solution.py:353
  111.0 14.0 %collective-permute-start.22 = (bf16[2,4,32,512]{3,2,1,0:T(8,128)(2,1)S(1)}, bf16[2,4,32,512]{3,2,1,0:T(8,128)(2,1)S(1)}, u32[]{:S(2)}, u32[]{:S(2)}) collective-permute-start(bf16[2,4,32,512]{3,2,1,0:T(8,128)(2,1)S(1)} %get-tuple-element.123.held_ref), channel_id=1, source_target_pairs={{0,8},{4,12},{8,0},{12,4},{16,24},{20,28},{24,16},{28,20},{1,9},{5... | collective-permute-start | bytes 786440 | tf_op jit(solution)/shard_map/ppermute | solution.py:353
  122.8 9.9 %collective-permute-start.23 = (bf16[8,48,512]{2,1,0:T(8,128)(2,1)S(1)}, bf16[8,48,512]{2,1,0:T(8,128)(2,1)S(1)}, u32[]{:S(2)}, u32[]{:S(2)}) collective-permute-start(bf16[8,48,512]{2,1,0:T(8,128)(2,1)S(1)} %get-tuple-element.125), channel_id=1, source_target_pairs={{0,4},{4,0},{8,12},{12,8},{16,20},{20,16},{24,28},{28,24},{1,5},{5... | collective-permute-start | bytes 1179656 | tf_op jit(solution)/shard_map/ppermute | solution.py:353
  125.6 9.9 %collective-permute-start.24 = (bf16[8,32,512]{2,1,0:T(8,128)(2,1)S(1)}, bf16[8,32,512]{2,1,0:T(8,128)(2,1)S(1)}, u32[]{:S(2)}, u32[]{:S(2)}) collective-permute-start(bf16[8,32,512]{2,1,0:T(8,128)(2,1)S(1)} %get-tuple-element.129), channel_id=1, source_target_pairs={{0,4},{4,0},{8,12},{12,8},{16,20},{20,16},{24,28},{28,24},{1,5},{5... | collective-permute-start | bytes 786440 | tf_op jit(solution)/shard_map/ppermute | solution.py:353
  (14 other events, 102.0 us)

commit v5 on v4

--- a/solution.py
+++ b/solution.py
@@ -5,10 +5,10 @@
 from jax.experimental.pallas import tpu as pltpu
 from jax.sharding import PartitionSpec as P
 
-SHARES = (3, 3, 2)
+SHARES = (2, 2, 2, 2)
 READ_CAP = 2
 VMEM_BYTES = 12 * 1024 * 1024
-UNIT_TIME, STEP_TIME, LATENCY = 10.5, 1.2, 2.0
+UNIT_TIME, START_TIME, STEP_TIME, LATENCY = 11.3, 0.9, 0.4, 0.6
 
 SMEM = pl.BlockSpec(memory_space=pltpu.SMEM)
 VMEM = pl.BlockSpec(memory_space=pltpu.VMEM)
@@ -40,6 +40,53 @@
     for i in range(1, bits):
         result = (result << 1) | ((value >> i) & 1)
     return result
+
+
+def planned_order(ways):
+    now, order, flows, current, place = 0.0, [], [], {}, [0] * len(ways)
+
+    def active():
+        waiting = [f for f in flows if "x" in f["links"]][1:]
+        running = [f for f in flows if not any(f is w for w in waiting)]
+        load = {}
+        for f in running:
+            for link, weight in f["links"].items():
+                load[link] = load.get(link, 0.0) + weight
+        return [(f, min(1.0 / load[link] for link in f["links"])) for f in running]
+
+    def advance(until):
+        nonlocal now
+        while now < until:
+            running = active()
+            step = min([until - now] + [f["left"] / rate for f, rate in running])
+            now += max(step, 1e-3)
+            for f, rate in running:
+                f["left"] -= step * rate
+                if f["left"] <= 1e-6:
+                    f["end"] = now + LATENCY
+            flows[:] = [f for f in flows if f["left"] > 1e-6]
+
+    def begin(n):
+        links, units = ways[n][place[n]]
+        advance(now + START_TIME)
+        current[n] = {"links": links, "left": units * UNIT_TIME, "end": None}
+        flows.append(current[n])
+
+    for n in range(len(ways)):
+        begin(n)
+    while current:
+        ended = [(f["end"], n) for n, f in current.items() if f["end"] is not None and f["end"] <= now]
+        if not ended:
+            advance(now + 0.05)
+            continue
+        _, n = min(ended)
+        order.append(n)
+        del current[n]
+        place[n] += 1
+        advance(now + STEP_TIME)
+        if place[n] < len(ways[n]):
+            begin(n)
+    return order
 
 
 def offsets_of(size, lowest):
@@ -199,11 +246,11 @@
     return (grouped, *results[at:]) if given else grouped
 
 
-def combine(token, total, got):
+def combine(token, total, got, at_hand):
     count, *shape = total.shape
     left = count // 2
 
-    def body(token_ref, total_ref, got_ref, *outs):
+    def body(token_ref, total_ref, got_ref, at_hand_ref, *outs):
         def add(i, carry):
             value = total_ref[i].astype(jnp.float32) + got_ref[i].astype(jnp.float32)
             if not left:
@@ -231,7 +278,7 @@
     else:
         out_shape = [jax.ShapeDtypeStruct(tuple(shape), jnp.bfloat16)]
     out_shape.append(TOKEN)
-    return call(body, out_shape, [VMEM] * 3, [VMEM] * len(out_shape), (token, total, got))
+    return call(body, out_shape, [VMEM] * 4, [VMEM] * len(out_shape), (token, total, got, at_hand))
 
 
 def join(token, held, got):
@@ -384,54 +431,54 @@
         *results, token = function(token, *operands)
         return results
 
-    def spread(held, size, lowest, axis, link, units):
+    def spread(held, size, lowest, axis):
         bit = size // 2
         while True:
             got = flip(held, bit, axis)
-            yield link, units
+            yield
             if bit == lowest:
                 return held, got
             (held,) = chained(join, held, got)
-            bit, units = bit // 2, units * 2
+            bit //= 2
 
     def one_part(part):
         nonlocal outputs
-        share = spans[part][1] / block
         got = flip(away[part], 1)
-        yield "low", share * half
-        total, sent = chained(combine, kept[part], got)
+        yield
+        total, sent = chained(combine, kept[part], got, weight)
         bit = 2
         while bit < edges:
             got = flip(sent, bit)
-            yield "high", share * 2
-            total, *sent = chained(combine, total, got)
+            yield
+            total, *sent = chained(combine, total, got, weight)
             sent = sent[0] if sent else None
             bit *= 2
-        held, got = yield from spread(total[None], feats, 1, "feat", "feat", share * 0.6)
+        held, got = yield from spread(total[None], feats, 1, "feat")
         (mixed,) = chained(mix, mine, offsets_of(feats, 1), held, got, weight)
-        held, got = yield from spread(mixed, edges, 2, "edge", "high", share * 1.5)
+        held, got = yield from spread(mixed, edges, 2, "edge")
         (picked,) = chained(pick, choice, held, got)
         far = flip(picked, 1)
-        yield "low", share * 2
+        yield
         outputs = chained(lay_out, me, readers, entry, columns, held, got, far, outputs, spans[part], block)
 
-    now, free, waiting = 0.0, {"low": 0.0, "high": 0.0, "feat": 0.0}, []
-
-    def advance(part, steps):
-        nonlocal now
-        link, units = next(steps, (None, 0))
-        now += STEP_TIME
-        if link is not None:
-            free[link] = max(free[link], now) + units * UNIT_TIME
-            waiting.append((free[link] + LATENCY, part, steps))
-
-    for part in range(len(spans)):
-        advance(part, one_part(part))
-    while waiting:
-        ready, part, steps = min(waiting, key=lambda item: item[:2])
-        waiting = [item for item in waiting if item[1] != part]
-        now = max(now, ready)
-        advance(part, steps)
+    def links_of(bit):
+        return {"end": 1.0} if bit == 2 else {"end": 1.0, "middle": 2.0}
+
+    column_bits = [1 << i for i in range(1, edges.bit_length() - 1)]
+    feat_bits = [1 << i for i in reversed(range(feats.bit_length() - 1))]
+    ways = []
+    for _, rows in spans:
+        share = rows / block
+        way = [({"x": 1.0}, share * half * 1.15)]
+        way += [(links_of(bit), share * half / bit) for bit in column_bits]
+        way += [({"chip" if bit == 1 else "feat": 1.0}, share * (1.0 if bit > 1 else 0.3)) for bit in feat_bits]
+        way += [(links_of(bit), share * half / bit) for bit in reversed(column_bits)]
+        ways.append(way + [({"x": 1.0}, share * READ_CAP / blocks * half)])
+    steps = [one_part(part) for part in range(len(spans))]
+    for step in steps:
+        next(step)
+    for part in planned_order(ways):
+        next(steps[part], None)
     hidden, ghosts = outputs
     return hidden.reshape(blocks * block, width), ghosts.reshape(-1, width)
 

time: 138 us -> 135 us (0.978)
  waiting for transfers between devices: 74.9 us -> 50 us
  starting transfers between devices: 34.3 us -> 50.8 us
  local copies, waits for them, and re-layouts: 6.42 us -> 10.4 us
  Pallas kernels: 20.2 us -> 21.9 us
    ppermute x25 -> x33, waiting for transfers between devices: 74.9 us -> 50 us  [flip(): lax.ppermute(value, axis, [(d, d ^ bit) for d in range(lax.axis_size(axis...]
    ppermute x25 -> x33, starting transfers between devices: 34.3 us -> 50.8 us  [flip(): lax.ppermute(value, axis, [(d, d ^ bit) for d in range(lax.axis_size(axis...]
    unnamed x26 -> x36, local copies, waits for them, and re-layouts: 5.5 us -> 9.42 us
    pallas_call x27 -> x35, Pallas kernels: 20.2 us -> 21.9 us  [call(): pl.pallas_call(body, out_shape=out_shape, in_specs=in_specs, out_specs=ou...]
  transfers between devices with their start and end apart: 25 -> 33, of which waited for: 17 -> 15; matrix products, arithmetic and copies ran while one was open for 1% -> 1% of each run, Pallas kernels for 10% -> 12%
where the time goes in v5:
time: 135 us
  starting transfers between devices  50.8 us (38%)
  waiting for transfers between devices  50 us (37%)
  Pallas kernels  21.9 us (16%)
  local copies, waits for them, and re-layouts  10.4 us (8%)
    ppermute x33, starting transfers between devices, flip(): lax.ppermute(value, axis, [(d, d ^ bit) for d in range(lax.axis_size(axis...  50.8 us
    ppermute x33, waiting for transfers between devices, flip(): lax.ppermute(value, axis, [(d, d ^ bit) for d in range(lax.axis_size(axis...  50 us
    pallas_call x35, Pallas kernels, call(): pl.pallas_call(body, out_shape=out_shape, in_specs=in_specs, out_specs=ou...  21.9 us
    unnamed x36, local copies, waits for them, and re-layouts  9.42 us
  transfers between devices with their start and end apart: 33, of which 15 were waited for; matrix products, arithmetic and copies ran while one was open for 1% of the time, Pallas kernels for 12%

profile of v5, /device:TPU:0, one launch (start us, length us, event | category | flops | bytes accessed | tf_op | source)
XLA Modules:
  0.0 134.9 jit_solution(15820047100073243383)
XLA Ops:
  0.7 3.0 %collective-permute-start = (s32[16]{0:T(128)}, s32[16]{0:T(128)S(1)}, u32[]{:S(2)}, u32[]{:S(2)}) collective-permute-start(s32[16]{0:T(128)} %readers_ref.7), channel_id=1, source_target_pairs={{0,4},{4,0},{8,12},{12,8},{16,20},{20,16},{24,28},{28,24},{1,5},{5... | collective-permute-start | bytes 200 | tf_op jit(solution)/shard_map/ppermute | solution.py:400
  5.9 3.4 %shard_map.104 = (s32[128]{0:T(128)}, bf16[4,4,32,512]{3,2,1,0:T(8,128)(2,1)}, bf16[512,512]{1,0:T(8,128)(2,1)}) custom-call(s32[1]{0:T(128)} %bitcast.me_ref, s32[96]{0:T(128)} %slot_hbm.1, s32[96]{0:T(128)} %col_hbm.1, s32[96]{0:T(128)} %id_hbm.1, s32[32]{0:T(128)} %reshape_squeeze.3.touched_ref, bf16[48,128,128]{2,1,0:T(8,128)(2,1)} %tiles_hbm.5, ...), custom_call_target="tpu_custom_call" | custom-call | bytes 1 | tf_op jit(solution)/shard_map/pallas_call | solution.py:20
  13.0 3.8 %shard_map.106 = (bf16[4,4,32,512]{3,2,1,0:T(8,128)(2,1)S(1)}, bf16[4,4,32,512]{3,2,1,0:T(8,128)(2,1)}, bf16[4,4,32,512]{3,2,1,0:T(8,128)(2,1)S(1)}, bf16[4,4,32,512]{3,2,1,0:T(8,128)(2,1)S(1)}) custom-call(s32[128]{0:T(128)S(1)} %copy-done.13, bf16[48,128,128]{2,1,0:T(8,128)(2,1)S(1)} %copy-done.9, bf16[512,512]{1,0:T(8,128)(2,1)S(1)} %copy-done.10), custom_call_target="tpu_custom_call" | custom-call | bytes 1 | tf_op jit(solution)/shard_map/pallas_call | solution.py:20
  17.7 2.4 %shard_map.105 = (bf16[4,4,32,512]{3,2,1,0:T(8,128)(2,1)S(1)}, bf16[4,4,32,512]{3,2,1,0:T(8,128)(2,1)S(1)}, bf16[4,4,32,512]{3,2,1,0:T(8,128)(2,1)S(1)}, bf16[2048,512]{1,0:T(8,128)(2,1)S(1)}, f32[8,128]{1,0:T(8,128)S(1)}) custom-call(s32[128]{0:T(128)S(1)} %copy-done.13, bf16[48,128,128]{2,1,0:T(8,128)(2,1)S(1)} %copy-done.9, ...), custom_call_target="tpu_custom_call" | custom-call | bytes 1 | tf_op jit(solution)/shard_map/pallas_call | solution.py:20
  20.0 4.4 %collective-permute-done.1.got_ref = bf16[4,4,32,512]{3,2,1,0:T(8,128)(2,1)S(1)} collective-permute-done((bf16[4,4,32,512]{3,2,1,0:T(8,128)(2,1)}, bf16[4,4,32,512]{3,2,1,0:T(8,128)(2,1)S(1)}, u32[]{:S(2)}, u32[]{:S(2)}) %collective-permute-start.1) | collective-permute-done | bytes 524320 | tf_op jit(solution)/shard_map/ppermute | solution.py:400
  24.7 2.2 %collective-permute-start.2 = (bf16[2,4,32,512]{3,2,1,0:T(8,128)(2,1)S(1)}, bf16[2,4,32,512]{3,2,1,0:T(8,128)(2,1)S(1)}, u32[]{:S(2)}, u32[]{:S(2)}) collective-permute-start(bf16[2,4,32,512]{3,2,1,0:T(8,128)(2,1)S(1)} %get-tuple-element.97), channel_id=1, source_target_pairs={{0,8},{4,12},{8,0},{12,4},{16,24},{20,28},{24,16},{28,20},{1,9},{5... | collective-permute-start | bytes 786440 | tf_op jit(solution)/shard_map/ppermute | solution.py:400
  26.8 5.8 %collective-permute-done.2.got_ref = bf16[2,4,32,512]{3,2,1,0:T(8,128)(2,1)S(1)} collective-permute-done((bf16[2,4,32,512]{3,2,1,0:T(8,128)(2,1)S(1)}, bf16[2,4,32,512]{3,2,1,0:T(8,128)(2,1)S(1)}, u32[]{:S(2)}, u32[]{:S(2)}) %collective-permute-start.2) | collective-permute-done | bytes 262176 | tf_op jit(solution)/shard_map/ppermute | solution.py:400
  32.7 3.1 %collective-permute-start.4 = (bf16[1,4,32,512]{3,2,1,0:T(8,128)(2,1)S(1)}, bf16[1,4,32,512]{3,2,1,0:T(8,128)(2,1)S(1)}, u32[]{:S(2)}, u32[]{:S(2)}) collective-permute-start(bf16[1,4,32,512]{3,2,1,0:T(8,128)(2,1)S(1)} %get-tuple-element.103), channel_id=1, source_target_pairs={{0,16},{4,20},{8,24},{12,28},{16,0},{20,4},{24,8},{28,12},{1,17},{... | collective-permute-start | bytes 393224 | tf_op jit(solution)/shard_map/ppermute | solution.py:400
  41.0 3.2 %collective-permute-done.5.got_ref = bf16[1,4,32,512]{3,2,1,0:T(8,128)(2,1)S(1)} collective-permute-done((bf16[1,4,32,512]{3,2,1,0:T(8,128)(2,1)S(1)}, bf16[1,4,32,512]{3,2,1,0:T(8,128)(2,1)S(1)}, u32[]{:S(2)}, u32[]{:S(2)}) %collective-permute-start.5) | collective-permute-done | bytes 131104 | tf_op jit(solution)/shard_map/ppermute | solution.py:400
  46.1 2.6 %collective-permute-start.9 = (bf16[1,4,32,512]{3,2,1,0:T(8,128)(2,1)S(1)}, bf16[1,4,32,512]{3,2,1,0:T(8,128)(2,1)S(1)}, u32[]{:S(2)}, u32[]{:S(2)}) collective-permute-start(bf16[1,4,32,512]{3,2,1,0:T(8,128)(2,1)S(1)} %get-tuple-element.116), channel_id=1, source_target_pairs={{0,16},{4,20},{8,24},{12,28},{16,0},{20,4},{24,8},{28,12},{1,17},{... | collective-permute-start | bytes 393224 | tf_op jit(solution)/shard_map/ppermute | solution.py:400
  51.6 4.5 %collective-permute-done.9.got_ref = bf16[1,4,32,512]{3,2,1,0:T(8,128)(2,1)S(1)} collective-permute-done((bf16[1,4,32,512]{3,2,1,0:T(8,128)(2,1)S(1)}, bf16[1,4,32,512]{3,2,1,0:T(8,128)(2,1)S(1)}, u32[]{:S(2)}, u32[]{:S(2)}) %collective-permute-start.9) | collective-permute-done | bytes 131104 | tf_op jit(solution)/shard_map/ppermute | solution.py:400
  58.0 2.9 %collective-permute-start.12 = (bf16[2,4,32,512]{3,2,1,0:T(8,128)(2,1)S(1)}, bf16[2,4,32,512]{3,2,1,0:T(8,128)(2,1)S(1)}, u32[]{:S(2)}, u32[]{:S(2)}) collective-permute-start(bf16[2,4,32,512]{3,2,1,0:T(8,128)(2,1)S(1)} %get-tuple-element.123), channel_id=1, source_target_pairs={{0,8},{4,12},{8,0},{12,4},{16,24},{20,28},{24,16},{28,20},{1,9},{5... | collective-permute-start | bytes 786440 | tf_op jit(solution)/shard_map/ppermute | solution.py:400
  61.5 3.4 %collective-permute-start.15 = (bf16[2,4,32,512]{3,2,1,0:T(8,128)(2,1)S(1)}, bf16[2,4,32,512]{3,2,1,0:T(8,128)(2,1)S(1)}, u32[]{:S(2)}, u32[]{:S(2)}) collective-permute-start(bf16[2,4,32,512]{3,2,1,0:T(8,128)(2,1)S(1)} %get-tuple-element.130.held_ref), channel_id=1, source_target_pairs={{0,8},{4,12},{8,0},{12,4},{16,24},{20,28},{24,16},{28,20},{1,9},{5... | collective-permute-start | bytes 786440 | tf_op jit(solution)/shard_map/ppermute | solution.py:400
  65.0 2.9 %collective-permute-done.12.got_ref = bf16[2,4,32,512]{3,2,1,0:T(8,128)(2,1)S(1)} collective-permute-done((bf16[2,4,32,512]{3,2,1,0:T(8,128)(2,1)S(1)}, bf16[2,4,32,512]{3,2,1,0:T(8,128)(2,1)S(1)}, u32[]{:S(2)}, u32[]{:S(2)}) %collective-permute-start.12) | collective-permute-done | bytes 262176 | tf_op jit(solution)/shard_map/ppermute | solution.py:400
  69.6 3.4 %collective-permute-start.16 = (bf16[1,4,32,512]{3,2,1,0:T(8,128)(2,1)S(1)}, bf16[1,4,32,512]{3,2,1,0:T(8,128)(2,1)S(1)}, u32[]{:S(2)}, u32[]{:S(2)}) collective-permute-start(bf16[1,4,32,512]{3,2,1,0:T(8,128)(2,1)S(1)} %get-tuple-element.133), channel_id=1, source_target_pairs={{0,16},{4,20},{8,24},{12,28},{16,0},{20,4},{24,8},{28,12},{1,17},{... | collective-permute-start | bytes 393224 | tf_op jit(solution)/shard_map/ppermute | solution.py:400
  81.0 2.9 %collective-permute-done.17.got_ref = bf16[1,4,32,512]{3,2,1,0:T(8,128)(2,1)S(1)} collective-permute-done((bf16[1,4,32,512]{3,2,1,0:T(8,128)(2,1)S(1)}, bf16[1,4,32,512]{3,2,1,0:T(8,128)(2,1)S(1)}, u32[]{:S(2)}, u32[]{:S(2)}) %collective-permute-start.17) | collective-permute-done | bytes 131104 | tf_op jit(solution)/shard_map/ppermute | solution.py:400
  87.0 2.5 %collective-permute-start.22 = (bf16[1,4,32,512]{3,2,1,0:T(8,128)(2,1)S(1)}, bf16[1,4,32,512]{3,2,1,0:T(8,128)(2,1)S(1)}, u32[]{:S(2)}, u32[]{:S(2)}) collective-permute-start(bf16[1,4,32,512]{3,2,1,0:T(8,128)(2,1)S(1)} %get-tuple-element.147), channel_id=1, source_target_pairs={{0,16},{4,20},{8,24},{12,28},{16,0},{20,4},{24,8},{28,12},{1,17},{... | collective-permute-start | bytes 393224 | tf_op jit(solution)/shard_map/ppermute | solution.py:400
  94.4 2.3 %collective-permute-done.22.got_ref = bf16[1,4,32,512]{3,2,1,0:T(8,128)(2,1)S(1)} collective-permute-done((bf16[1,4,32,512]{3,2,1,0:T(8,128)(2,1)S(1)}, bf16[1,4,32,512]{3,2,1,0:T(8,128)(2,1)S(1)}, u32[]{:S(2)}, u32[]{:S(2)}) %collective-permute-start.22) | collective-permute-done | bytes 131104 | tf_op jit(solution)/shard_map/ppermute | solution.py:400
  97.4 4.8 %collective-permute-done.23.got_ref = bf16[2,4,32,512]{3,2,1,0:T(8,128)(2,1)S(1)} collective-permute-done((bf16[2,4,32,512]{3,2,1,0:T(8,128)(2,1)S(1)}, bf16[2,4,32,512]{3,2,1,0:T(8,128)(2,1)S(1)}, u32[]{:S(2)}, u32[]{:S(2)}) %collective-permute-start.23) | collective-permute-done | bytes 262176 | tf_op jit(solution)/shard_map/ppermute | solution.py:400
  106.9 2.3 %collective-permute-start.29 = (bf16[1,4,32,512]{3,2,1,0:T(8,128)(2,1)S(1)}, bf16[1,4,32,512]{3,2,1,0:T(8,128)(2,1)S(1)}, u32[]{:S(2)}, u32[]{:S(2)}) collective-permute-start(bf16[1,4,32,512]{3,2,1,0:T(8,128)(2,1)S(1)} %get-tuple-element.163.held_ref), channel_id=1, source_target_pairs={{0,16},{4,20},{8,24},{12,28},{16,0},{20,4},{24,8},{28,12},{1,17},{... | collective-permute-start | bytes 393224 | tf_op jit(solution)/shard_map/ppermute | solution.py:400
  109.2 2.5 %collective-permute-done.27.far_ref = bf16[8,32,512]{2,1,0:T(8,128)(2,1)S(1)} collective-permute-done((bf16[8,32,512]{2,1,0:T(8,128)(2,1)S(1)}, bf16[8,32,512]{2,1,0:T(8,128)(2,1)S(1)}, u32[]{:S(2)}, u32[]{:S(2)}) %collective-permute-start.27) | collective-permute-done | bytes 262176 | tf_op jit(solution)/shard_map/ppermute | solution.py:400
  113.2 2.7 %collective-permute-done.28.got_ref = bf16[2,4,32,512]{3,2,1,0:T(8,128)(2,1)S(1)} collective-permute-done((bf16[2,4,32,512]{3,2,1,0:T(8,128)(2,1)S(1)}, bf16[2,4,32,512]{3,2,1,0:T(8,128)(2,1)S(1)}, u32[]{:S(2)}, u32[]{:S(2)}) %collective-permute-start.28) | collective-permute-done | bytes 262176 | tf_op jit(solution)/shard_map/ppermute | solution.py:400
  118.2 5.8 %collective-permute-done.30.far_ref = bf16[8,32,512]{2,1,0:T(8,128)(2,1)S(1)} collective-permute-done((bf16[8,32,512]{2,1,0:T(8,128)(2,1)S(1)}, bf16[8,32,512]{2,1,0:T(8,128)(2,1)S(1)}, u32[]{:S(2)}, u32[]{:S(2)}) %collective-permute-start.30) | collective-permute-done | bytes 262176 | tf_op jit(solution)/shard_map/ppermute | solution.py:400
  126.9 5.9 %collective-permute-done.32.far_ref = bf16[8,32,512]{2,1,0:T(8,128)(2,1)S(1)} collective-permute-done((bf16[8,32,512]{2,1,0:T(8,128)(2,1)S(1)}, bf16[8,32,512]{2,1,0:T(8,128)(2,1)S(1)}, u32[]{:S(2)}, u32[]{:S(2)}) %collective-permute-start.32) | collective-permute-done | bytes 262176 | tf_op jit(solution)/shard_map/ppermute | solution.py:400
  (130 shorter events, 51.2 us)
Async XLA Ops:
  9.3 15.1 %collective-permute-start.1 = (bf16[4,4,32,512]{3,2,1,0:T(8,128)(2,1)}, bf16[4,4,32,512]{3,2,1,0:T(8,128)(2,1)S(1)}, u32[]{:S(2)}, u32[]{:S(2)}) collective-permute-start(bf16[4,4,32,512]{3,2,1,0:T(8,128)(2,1)} %get-tuple-element.93), channel_id=1, source_target_pairs={{0,4},{4,0},{8,12},{12,8},{16,20},{20,16},{24,28},{28,24},{1,5},{5... | collective-permute-start | bytes 1572872 | tf_op jit(solution)/shard_map/ppermute | solution.py:400
  17.6 19.6 %collective-permute-start.3 = (bf16[4,4,32,512]{3,2,1,0:T(8,128)(2,1)S(1)}, bf16[4,4,32,512]{3,2,1,0:T(8,128)(2,1)S(1)}, u32[]{:S(2)}, u32[]{:S(2)}) collective-permute-start(bf16[4,4,32,512]{3,2,1,0:T(8,128)(2,1)S(1)} %get-tuple-element.100), channel_id=1, source_target_pairs={{0,4},{4,0},{8,12},{12,8},{16,20},{20,16},{24,28},{28,24},{1,5},{5... | collective-permute-start | bytes 1572872 | tf_op jit(solution)/shard_map/ppermute | solution.py:400
  24.7 7.9 %collective-permute-start.2 = (bf16[2,4,32,512]{3,2,1,0:T(8,128)(2,1)S(1)}, bf16[2,4,32,512]{3,2,1,0:T(8,128)(2,1)S(1)}, u32[]{:S(2)}, u32[]{:S(2)}) collective-permute-start(bf16[2,4,32,512]{3,2,1,0:T(8,128)(2,1)S(1)} %get-tuple-element.97), channel_id=1, source_target_pairs={{0,8},{4,12},{8,0},{12,4},{16,24},{20,28},{24,16},{28,20},{1,9},{5... | collective-permute-start | bytes 786440 | tf_op jit(solution)/shard_map/ppermute | solution.py:400
  35.8 15.6 %collective-permute-start.8 = (bf16[4,4,32,512]{3,2,1,0:T(8,128)(2,1)}, bf16[4,4,32,512]{3,2,1,0:T(8,128)(2,1)S(1)}, u32[]{:S(2)}, u32[]{:S(2)}) collective-permute-start(bf16[4,4,32,512]{3,2,1,0:T(8,128)(2,1)} %get-tuple-element.113), channel_id=1, source_target_pairs={{0,4},{4,0},{8,12},{12,8},{16,20},{20,16},{24,28},{28,24},{1,5},{5... | collective-permute-start | bytes 1572872 | tf_op jit(solution)/shard_map/ppermute | solution.py:400
  37.5 6.8 %collective-permute-start.6 = (bf16[2,4,32,512]{3,2,1,0:T(8,128)(2,1)S(1)}, bf16[2,4,32,512]{3,2,1,0:T(8,128)(2,1)S(1)}, u32[]{:S(2)}, u32[]{:S(2)}) collective-permute-start(bf16[2,4,32,512]{3,2,1,0:T(8,128)(2,1)S(1)} %get-tuple-element.108), channel_id=1, source_target_pairs={{0,8},{4,12},{8,0},{12,4},{16,24},{20,28},{24,16},{28,20},{1,9},{5... | collective-permute-start | bytes 786440 | tf_op jit(solution)/shard_map/ppermute | solution.py:400
  46.1 10.1 %collective-permute-start.9 = (bf16[1,4,32,512]{3,2,1,0:T(8,128)(2,1)S(1)}, bf16[1,4,32,512]{3,2,1,0:T(8,128)(2,1)S(1)}, u32[]{:S(2)}, u32[]{:S(2)}) collective-permute-start(bf16[1,4,32,512]{3,2,1,0:T(8,128)(2,1)S(1)} %get-tuple-element.116), channel_id=1, source_target_pairs={{0,16},{4,20},{8,24},{12,28},{16,0},{20,4},{24,8},{28,12},{1,17},{... | collective-permute-start | bytes 393224 | tf_op jit(solution)/shard_map/ppermute | solution.py:400
  48.7 24.5 %collective-permute-start.13 = (bf16[4,4,32,512]{3,2,1,0:T(8,128)(2,1)}, bf16[4,4,32,512]{3,2,1,0:T(8,128)(2,1)S(1)}, u32[]{:S(2)}, u32[]{:S(2)}) collective-permute-start(bf16[4,4,32,512]{3,2,1,0:T(8,128)(2,1)} %copy-done.14), channel_id=1, source_target_pairs={{0,4},{4,0},{8,12},{12,8},{16,20},{20,16},{24,28},{28,24},{1,5},{5... | collective-permute-start | bytes 1572872 | tf_op jit(solution)/shard_map/ppermute | solution.py:400
  50.7 10.6 %collective-permute-start.10 = (bf16[1,4,32,512]{3,2,1,0:T(8,128)(2,1)S(1)}, bf16[1,4,32,512]{3,2,1,0:T(8,128)(2,1)S(1)}, u32[]{:S(2)}, u32[]{:S(2)}) collective-permute-start(bf16[1,4,32,512]{3,2,1,0:T(8,128)(2,1)S(1)} %get-tuple-element.118.held_ref), channel_id=1, source_target_pairs={{0,16},{4,20},{8,24},{12,28},{16,0},{20,4},{24,8},{28,12},{1,17},{... | collective-permute-start | bytes 393224 | tf_op jit(solution)/shard_map/ppermute | solution.py:400
  58.0 9.9 %collective-permute-start.12 = (bf16[2,4,32,512]{3,2,1,0:T(8,128)(2,1)S(1)}, bf16[2,4,32,512]{3,2,1,0:T(8,128)(2,1)S(1)}, u32[]{:S(2)}, u32[]{:S(2)}) collective-permute-start(bf16[2,4,32,512]{3,2,1,0:T(8,128)(2,1)S(1)} %get-tuple-element.123), channel_id=1, source_target_pairs={{0,8},{4,12},{8,0},{12,4},{16,24},{20,28},{24,16},{28,20},{1,9},{5... | collective-permute-start | bytes 786440 | tf_op jit(solution)/shard_map/ppermute | solution.py:400
  61.4 15.6 %collective-permute-start.14 = (bf16[2,4,32,512]{3,2,1,0:T(8,128)(2,1)S(1)}, bf16[2,4,32,512]{3,2,1,0:T(8,128)(2,1)S(1)}, u32[]{:S(2)}, u32[]{:S(2)}) collective-permute-start(bf16[2,4,32,512]{3,2,1,0:T(8,128)(2,1)S(1)} %get-tuple-element.128.held_ref), channel_id=1, source_target_pairs={{0,1},{1,0},{2,3},{3,2},{4,5},{5,4},{6,7},{7,6},{8,9},{9,8},{10,11... | collective-permute-start | bytes 786440 | tf_op jit(solution)/shard_map/ppermute | solution.py:400
  61.5 16.3 %collective-permute-start.15 = (bf16[2,4,32,512]{3,2,1,0:T(8,128)(2,1)S(1)}, bf16[2,4,32,512]{3,2,1,0:T(8,128)(2,1)S(1)}, u32[]{:S(2)}, u32[]{:S(2)}) collective-permute-start(bf16[2,4,32,512]{3,2,1,0:T(8,128)(2,1)S(1)} %get-tuple-element.130.held_ref), channel_id=1, source_target_pairs={{0,8},{4,12},{8,0},{12,4},{16,24},{20,28},{24,16},{28,20},{1,9},{5... | collective-permute-start | bytes 786440 | tf_op jit(solution)/shard_map/ppermute | solution.py:400
  69.6 8.8 %collective-permute-start.16 = (bf16[1,4,32,512]{3,2,1,0:T(8,128)(2,1)S(1)}, bf16[1,4,32,512]{3,2,1,0:T(8,128)(2,1)S(1)}, u32[]{:S(2)}, u32[]{:S(2)}) collective-permute-start(bf16[1,4,32,512]{3,2,1,0:T(8,128)(2,1)S(1)} %get-tuple-element.133), channel_id=1, source_target_pairs={{0,16},{4,20},{8,24},{12,28},{16,0},{20,4},{24,8},{28,12},{1,17},{... | collective-permute-start | bytes 393224 | tf_op jit(solution)/shard_map/ppermute | solution.py:400
  75.1 9.9 %collective-permute-start.18 = (bf16[2,4,32,512]{3,2,1,0:T(8,128)(2,1)S(1)}, bf16[2,4,32,512]{3,2,1,0:T(8,128)(2,1)S(1)}, u32[]{:S(2)}, u32[]{:S(2)}) collective-permute-start(bf16[2,4,32,512]{3,2,1,0:T(8,128)(2,1)S(1)} %get-tuple-element.138), channel_id=1, source_target_pairs={{0,8},{4,12},{8,0},{12,4},{16,24},{20,28},{24,16},{28,20},{1,9},{5... | collective-permute-start | bytes 786440 | tf_op jit(solution)/shard_map/ppermute | solution.py:400
  78.4 8.2 %collective-permute-start.19 = (bf16[1,4,32,512]{3,2,1,0:T(8,128)(2,1)S(1)}, bf16[1,4,32,512]{3,2,1,0:T(8,128)(2,1)S(1)}, u32[]{:S(2)}, u32[]{:S(2)}) collective-permute-start(bf16[1,4,32,512]{3,2,1,0:T(8,128)(2,1)S(1)} %bitcast.8), channel_id=1, source_target_pairs={{0,2},{1,3},{2,0},{3,1},{4,6},{5,7},{6,4},{7,5},{8,10},{9,11},{10,... | collective-permute-start | bytes 393224 | tf_op jit(solution)/shard_map/ppermute | solution.py:400
  80.5 10.6 %collective-permute-start.20 = (bf16[8,32,512]{2,1,0:T(8,128)(2,1)S(1)}, bf16[8,32,512]{2,1,0:T(8,128)(2,1)S(1)}, u32[]{:S(2)}, u32[]{:S(2)}) collective-permute-start(bf16[8,32,512]{2,1,0:T(8,128)(2,1)S(1)} %get-tuple-element.142), channel_id=1, source_target_pairs={{0,4},{4,0},{8,12},{12,8},{16,20},{20,16},{24,28},{28,24},{1,5},{5... | collective-permute-start | bytes 786440 | tf_op jit(solution)/shard_map/ppermute | solution.py:400
  87.0 9.8 %collective-permute-start.22 = (bf16[1,4,32,512]{3,2,1,0:T(8,128)(2,1)S(1)}, bf16[1,4,32,512]{3,2,1,0:T(8,128)(2,1)S(1)}, u32[]{:S(2)}, u32[]{:S(2)}) collective-permute-start(bf16[1,4,32,512]{3,2,1,0:T(8,128)(2,1)S(1)} %get-tuple-element.147), channel_id=1, source_target_pairs={{0,16},{4,20},{8,24},{12,28},{16,0},{20,4},{24,8},{28,12},{1,17},{... | collective-permute-start | bytes 393224 | tf_op jit(solution)/shard_map/ppermute | solution.py:400
  89.4 12.8 %collective-permute-start.23 = (bf16[2,4,32,512]{3,2,1,0:T(8,128)(2,1)S(1)}, bf16[2,4,32,512]{3,2,1,0:T(8,128)(2,1)S(1)}, u32[]{:S(2)}, u32[]{:S(2)}) collective-permute-start(bf16[2,4,32,512]{3,2,1,0:T(8,128)(2,1)S(1)} %get-tuple-element.149.held_ref), channel_id=1, source_target_pairs={{0,8},{4,12},{8,0},{12,4},{16,24},{20,28},{24,16},{28,20},{1,9},{5... | collective-permute-start | bytes 786440 | tf_op jit(solution)/shard_map/ppermute | solution.py:400
  93.1 9.7 %collective-permute-start.24 = (bf16[1,4,32,512]{3,2,1,0:T(8,128)(2,1)S(1)}, bf16[1,4,32,512]{3,2,1,0:T(8,128)(2,1)S(1)}, u32[]{:S(2)}, u32[]{:S(2)}) collective-permute-start(bf16[1,4,32,512]{3,2,1,0:T(8,128)(2,1)S(1)} %get-tuple-element.151.held_ref), channel_id=1, source_target_pairs={{0,16},{4,20},{8,24},{12,28},{16,0},{20,4},{24,8},{28,12},{1,17},{... | collective-permute-start | bytes 393224 | tf_op jit(solution)/shard_map/ppermute | solution.py:400
  103.0 8.7 %collective-permute-start.27 = (bf16[8,32,512]{2,1,0:T(8,128)(2,1)S(1)}, bf16[8,32,512]{2,1,0:T(8,128)(2,1)S(1)}, u32[]{:S(2)}, u32[]{:S(2)}) collective-permute-start(bf16[8,32,512]{2,1,0:T(8,128)(2,1)S(1)} %get-tuple-element.157), channel_id=1, source_target_pairs={{0,4},{4,0},{8,12},{12,8},{16,20},{20,16},{24,28},{28,24},{1,5},{5... | collective-permute-start | bytes 786440 | tf_op jit(solution)/shard_map/ppermute | solution.py:400
  104.7 11.2 %collective-permute-start.28 = (bf16[2,4,32,512]{3,2,1,0:T(8,128)(2,1)S(1)}, bf16[2,4,32,512]{3,2,1,0:T(8,128)(2,1)S(1)}, u32[]{:S(2)}, u32[]{:S(2)}) collective-permute-start(bf16[2,4,32,512]{3,2,1,0:T(8,128)(2,1)S(1)} %get-tuple-element.161.held_ref), channel_id=1, source_target_pairs={{0,8},{4,12},{8,0},{12,4},{16,24},{20,28},{24,16},{28,20},{1,9},{5... | collective-permute-start | bytes 786440 | tf_op jit(solution)/shard_map/ppermute | solution.py:400
  106.9 10.2 %collective-permute-start.29 = (bf16[1,4,32,512]{3,2,1,0:T(8,128)(2,1)S(1)}, bf16[1,4,32,512]{3,2,1,0:T(8,128)(2,1)S(1)}, u32[]{:S(2)}, u32[]{:S(2)}) collective-permute-start(bf16[1,4,32,512]{3,2,1,0:T(8,128)(2,1)S(1)} %get-tuple-element.163.held_ref), channel_id=1, source_target_pairs={{0,16},{4,20},{8,24},{12,28},{16,0},{20,4},{24,8},{28,12},{1,17},{... | collective-permute-start | bytes 393224 | tf_op jit(solution)/shard_map/ppermute | solution.py:400
  116.4 7.6 %collective-permute-start.30 = (bf16[8,32,512]{2,1,0:T(8,128)(2,1)S(1)}, bf16[8,32,512]{2,1,0:T(8,128)(2,1)S(1)}, u32[]{:S(2)}, u32[]{:S(2)}) collective-permute-start(bf16[8,32,512]{2,1,0:T(8,128)(2,1)S(1)} %get-tuple-element.165), channel_id=1, source_target_pairs={{0,4},{4,0},{8,12},{12,8},{16,20},{20,16},{24,28},{28,24},{1,5},{5... | collective-permute-start | bytes 786440 | tf_op jit(solution)/shard_map/ppermute | solution.py:400
  117.1 8.5 %collective-permute-start.31 = (bf16[2,4,32,512]{3,2,1,0:T(8,128)(2,1)S(1)}, bf16[2,4,32,512]{3,2,1,0:T(8,128)(2,1)S(1)}, u32[]{:S(2)}, u32[]{:S(2)}) collective-permute-start(bf16[2,4,32,512]{3,2,1,0:T(8,128)(2,1)S(1)} %get-tuple-element.169.held_ref), channel_id=1, source_target_pairs={{0,8},{4,12},{8,0},{12,4},{16,24},{20,28},{24,16},{28,20},{1,9},{5... | collective-permute-start | bytes 786440 | tf_op jit(solution)/shard_map/ppermute | solution.py:400
  126.2 6.7 %collective-permute-start.32 = (bf16[8,32,512]{2,1,0:T(8,128)(2,1)S(1)}, bf16[8,32,512]{2,1,0:T(8,128)(2,1)S(1)}, u32[]{:S(2)}, u32[]{:S(2)}) collective-permute-start(bf16[8,32,512]{2,1,0:T(8,128)(2,1)S(1)} %get-tuple-element.171), channel_id=1, source_target_pairs={{0,4},{4,0},{8,12},{12,8},{16,20},{20,16},{24,28},{28,24},{1,5},{5... | collective-permute-start | bytes 786440 | tf_op jit(solution)/shard_map/ppermute | solution.py:400
  (27 other events, 144.9 us)

commit v6 on v5

--- a/solution.py
+++ b/solution.py
@@ -5,7 +5,11 @@
 from jax.experimental.pallas import tpu as pltpu
 from jax.sharding import PartitionSpec as P
 
-SHARES = (2, 2, 2, 2)
+SHARES = (2, 2, 1, 2, 1)
+ORDER = (
+    0, 0, 0, 1, 3, 1, 0, 3, 2, 0, 1, 4, 3, 2, 0, 2, 1, 4, 3, 1, 2, 3, 4, 1, 4, 3, 4, 2, 0, 1, 0, 4,
+    3, 2, 1, 4, 2, 3, 4, 2,
+)
 READ_CAP = 2
 VMEM_BYTES = 12 * 1024 * 1024
 UNIT_TIME, START_TIME, STEP_TIME, LATENCY = 11.3, 0.9, 0.4, 0.6
@@ -109,19 +113,22 @@
                 top = top + blocks * rows
 
 
-def first_part(me, slot, col, tile_id, touched, tiles, features, after, first, count, span):
+def first_part(me, slot, col, tile_id, touched, tiles, features, readers, neighbour, first, count, span):
     block = tiles.shape[1]
     blocks = features.shape[0] // block
     width = features.shape[1]
     edges, cap = touched.shape[1], touched.shape[2]
     bits = edges.bit_length() - 1
     products = slot.shape[0]
+    half = edges // 2
     start, rows = span
     square = blocks * blocks
 
-    def body(me_ref, slot_hbm, col_hbm, id_hbm, touched_ref, tiles_hbm, x_hbm, after_ref, *refs):
-        table, out, x_out, *scratch = refs
-        slot_ref, col_ref, id_ref, tiles_ref, lhs, bases, sems = scratch
+    listed = readers.shape[0]
+
+    def body(me_ref, slot_hbm, col_hbm, id_hbm, touched_ref, tiles_hbm, x_hbm, readers_ref, neighbour_ref, *refs):
+        table, choice, entry, out, x_out, *scratch = refs
+        slot_ref, col_ref, id_ref, tiles_ref, lhs, bases, seen, sems = scratch
         loads = [
             pltpu.make_async_copy(slot_hbm, slot_ref, sems.at[0]),
             pltpu.make_async_copy(col_hbm, col_ref, sems.at[1]),
@@ -148,6 +155,28 @@
         for load in loads[:3]:
             load.wait()
 
+        for i in range(half * READ_CAP + 1):
+            choice[i] = 0
+        for i in range(edges * READ_CAP):
+            entry[i] = -1
+        for i in range(2 * edges):
+            seen[i] = 0
+
+        def enter_lists(r, carry):
+            owner, _ = split(readers_ref[r], blocks)
+            turn = seen[owner]
+            seen[owner] = turn + 1
+            entry[owner * READ_CAP + jnp.minimum(turn, READ_CAP - 1)] = r
+            owner, b = split(neighbour_ref[r], blocks)
+            turn = seen[edges + owner]
+            seen[edges + owner] = turn + 1
+            peer = owner ^ me_ref[0]
+            row = reversed_bits(peer >> 1, bits - 1) * READ_CAP + jnp.minimum(turn, READ_CAP - 1)
+            choice[jnp.where(peer & 1 == 0, row, half * READ_CAP)] = b
+            return carry
+
+        lax.fori_loop(0, listed, enter_lists, 0)
+
         def enter(k, carry):
             table[bases[slot_ref[k]] + col_ref[k]] = id_ref[k] + 1
             return carry
@@ -169,12 +198,14 @@
         body,
         [
             jax.ShapeDtypeStruct((edges * square,), jnp.int32),
+            jax.ShapeDtypeStruct((half * READ_CAP + 1,), jnp.int32),
+            jax.ShapeDtypeStruct((edges * READ_CAP,), jnp.int32),
             jax.ShapeDtypeStruct((count, blocks, rows, width), jnp.bfloat16),
             jax.ShapeDtypeStruct(features.shape, jnp.bfloat16),
         ],
-        [SMEM, HBM, HBM, HBM, SMEM, HBM, HBM, SMEM],
-        [SMEM, VMEM, VMEM],
-        (me, slot, col, tile_id, touched[me[0]].reshape(-1), tiles, features, after),
+        [SMEM, HBM, HBM, HBM, SMEM, HBM, HBM, SMEM, SMEM],
+        [SMEM, SMEM, SMEM, VMEM, VMEM],
+        (me, slot, col, tile_id, touched[me[0]].reshape(-1), tiles, features, readers, neighbour),
         [
             pltpu.SMEM((products,), jnp.int32),
             pltpu.SMEM((products,), jnp.int32),
@@ -182,31 +213,28 @@
             pltpu.VMEM((tiles.shape[0], rows, block), jnp.bfloat16),
             pltpu.VMEM((count * blocks * rows, blocks * block), jnp.bfloat16),
             pltpu.SMEM((edges * cap,), jnp.int32),
+            pltpu.SMEM((2 * edges,), jnp.int32),
             pltpu.SemaphoreType.DMA((5,)),
         ],
         limit=62 * 1024 * 1024,
     )
 
 
-def other_parts(table, tiles, inputs, jobs, weight=None):
+def other_parts(table, tiles, inputs, jobs):
     block = tiles.shape[1]
     blocks = inputs.shape[0] // block
     width = inputs.shape[1]
     most = max(sum(rows for _, rows in spans) for _, _, spans in jobs) * blocks
-    given = [] if weight is None else [weight]
     shapes = [
         jax.ShapeDtypeStruct((count, blocks, rows, width), jnp.bfloat16) for _, count, spans in jobs for _, rows in spans
     ]
 
     def body(table_ref, tiles_hbm, x_ref, *refs):
-        outs = refs[len(given) :]
-        tiles_ref, lhs, sems = outs[-3:]
+        outs = refs
+        token, tiles_ref, lhs, sems = outs[-4:]
+        token[...] = jnp.zeros_like(token)
         load = pltpu.make_async_copy(tiles_hbm, tiles_ref, sems.at[0])
         load.start()
-        if given:
-            load_weight = pltpu.make_async_copy(refs[0], outs[-5], sems.at[1])
-            load_weight.start()
-            outs[-4][...] = jnp.zeros_like(outs[-4])
         load.wait()
         for first, count, spans in jobs:
             height = blocks * sum(rows for _, rows in spans)
@@ -223,27 +251,24 @@
 
             lax.fori_loop(0, count, one_owner, 0)
             outs = outs[len(spans) :]
-        if given:
-            load_weight.wait()
-
-    extra = [jax.ShapeDtypeStruct(weight.shape, weight.dtype), TOKEN] if given else []
+
     results = call(
         body,
-        shapes + extra,
-        [SMEM, HBM, VMEM] + [HBM] * len(given),
-        [VMEM] * (len(shapes) + len(extra)),
-        (table, tiles, inputs, *given),
+        shapes + [TOKEN],
+        [SMEM, HBM, VMEM],
+        [VMEM] * (len(shapes) + 1),
+        (table, tiles, inputs),
         [
             pltpu.VMEM(tiles.shape, jnp.bfloat16),
             pltpu.VMEM((most, blocks * block), jnp.bfloat16),
-            pltpu.SemaphoreType.DMA((2,)),
+            pltpu.SemaphoreType.DMA((1,)),
         ],
     )
     grouped, at = [], 0
     for _, _, spans in jobs:
         grouped.append(results[at : at + len(spans)])
         at += len(spans)
-    return (grouped, *results[at:]) if given else grouped
+    return (*grouped, results[-1])
 
 
 def combine(token, total, got, at_hand):
@@ -316,7 +341,7 @@
 
 
 def pick(token, choice, held, got):
-    count = choice.shape[0]
+    count = 2 * held.shape[0] * READ_CAP
 
     def body(token_ref, choice_ref, held_ref, got_ref, out, token_out):
         for i in range(count):
@@ -399,30 +424,15 @@
     def flip(value, bit, axis="edge"):
         return lax.ppermute(value, axis, [(d, d ^ bit) for d in range(lax.axis_size(axis))])
 
-    count = readers.shape[0]
-    order = jnp.arange(count, dtype=jnp.int32)
     columns = offsets_of(edges, 2)
+    me, mine = me.reshape(1), mine.reshape(1)
     neighbour = flip(readers, 1)
-
-    def listed(values, owners):
-        owner = values // blocks
-        rank = jnp.sum(((owner[:, None] == owner[None, :]) & (order[None, :] < order[:, None])).astype(jnp.int32), axis=1)
-        wanted = jnp.repeat(owners, READ_CAP)
-        turn = jnp.arange(wanted.shape[0], dtype=jnp.int32) % READ_CAP
-        return (owner[None, :] == wanted[:, None]) & (rank[None, :] == turn[:, None])
-
-    hit = listed(neighbour, lax.bitwise_xor(me, jnp.array(columns, jnp.int32)))
-    choice = jnp.sum(jnp.where(hit, (neighbour % blocks)[None, :], 0), axis=1)
-    hit = listed(readers, jnp.arange(edges, dtype=jnp.int32))
-    entry = jnp.sum(jnp.where(hit, order[None, :] + 1, 0), axis=1) - 1
-    me, mine = me.reshape(1), mine.reshape(1)
-
-    table, early, inputs = first_part(
-        me, tile_slot, tile_col, tile_id, touched, tiles, features, neighbour, half, half, spans[0]
-    )
-    later, first_kept = other_parts(table, tiles, inputs, [(half, half, spans[1:]), (0, half, spans[:1])])
+    table, choice, entry, early, inputs = first_part(
+        me, tile_slot, tile_col, tile_id, touched, tiles, features, readers, neighbour, half, half, spans[0]
+    )
+    later, first_kept, _ = other_parts(table, tiles, inputs, [(half, half, spans[1:]), (0, half, spans[:1])])
     away = [early, *later]
-    (kept,), weight, token = other_parts(table, tiles, inputs, [(0, half, spans[1:])], weight)
+    kept, token = other_parts(table, tiles, inputs, [(0, half, spans[1:])])
     kept = [*first_kept, *kept]
     outputs = ()
 
@@ -477,7 +487,8 @@
     steps = [one_part(part) for part in range(len(spans))]
     for step in steps:
         next(step)
-    for part in planned_order(ways):
+    known = all(ORDER.count(part) == len(way) for part, way in enumerate(ways))
+    for part in ORDER if known else planned_order(ways):
         next(steps[part], None)
     hidden, ghosts = outputs
     return hidden.reshape(blocks * block, width), ghosts.reshape(-1, width)

time: 135 us -> 125 us (0.926)
  waiting for transfers between devices: 50 us -> 37.8 us
  starting transfers between devices: 50.8 us -> 57.7 us
  local copies, waits for them, and re-layouts: 10.4 us -> 4.58 us
  Pallas kernels: 21.9 us -> 24.1 us
    ppermute x33 -> x41, waiting for transfers between devices: 50 us -> 37.8 us  [flip(): lax.ppermute(value, axis, [(d, d ^ bit) for d in range(lax.axis_size(axis...]
    ppermute x33 -> x41, starting transfers between devices: 50.8 us -> 57.7 us  [flip(): lax.ppermute(value, axis, [(d, d ^ bit) for d in range(lax.axis_size(axis...]
    unnamed x36 -> x24, local copies, waits for them, and re-layouts: 9.42 us -> 3.87 us
    pallas_call x35 -> x43, Pallas kernels: 21.9 us -> 24.1 us  [call(): pl.pallas_call(body, out_shape=out_shape, in_specs=in_specs, out_specs=ou...]
  transfers between devices with their start and end apart: 33 -> 41, of which waited for: 15 -> 18; matrix products, arithmetic and copies ran while one was open for 1% -> 1% of each run, Pallas kernels for 12% -> 15%
where the time goes in v6:
time: 125 us
  starting transfers between devices  57.7 us (46%)
  waiting for transfers between devices  37.8 us (30%)
  Pallas kernels  24.1 us (19%)
  local copies, waits for them, and re-layouts  4.58 us (4%)
    ppermute x41, starting transfers between devices, flip(): lax.ppermute(value, axis, [(d, d ^ bit) for d in range(lax.axis_size(axis...  57.7 us
    ppermute x41, waiting for transfers between devices, flip(): lax.ppermute(value, axis, [(d, d ^ bit) for d in range(lax.axis_size(axis...  37.8 us
    pallas_call x43, Pallas kernels, call(): pl.pallas_call(body, out_shape=out_shape, in_specs=in_specs, out_specs=ou...  24.1 us
    unnamed x24, local copies, waits for them, and re-layouts  3.87 us
  transfers between devices with their start and end apart: 41, of which 18 were waited for; matrix products, arithmetic and copies ran while one was open for 1% of the time, Pallas kernels for 15%

profile of v6, /device:TPU:0, one launch (start us, length us, event | category | flops | bytes accessed | tf_op | source)
XLA Modules:
  0.0 125.2 jit_solution(14778511027020409107)
XLA Ops:
  0.7 3.0 %collective-permute-start = (s32[16]{0:T(128)}, s32[16]{0:T(128)S(1)}, u32[]{:S(2)}, u32[]{:S(2)}) collective-permute-start(s32[16]{0:T(128)} %readers_ref.11), channel_id=1, source_target_pairs={{0,4},{4,0},{8,12},{12,8},{16,20},{20,16},{24,28},{28,24},{1,5},{5... | collective-permute-start | bytes 200 | tf_op jit(solution)/shard_map/ppermute | solution.py:425
  5.9 3.5 %shard_map.95 = (s32[128]{0:T(128)}, s32[9]{0:T(128)}, s32[16]{0:T(128)}, bf16[4,4,32,512]{3,2,1,0:T(8,128)(2,1)}, bf16[512,512]{1,0:T(8,128)(2,1)}) custom-call(s32[1]{0:T(128)} %bitcast.me_ref, s32[96]{0:T(128)} %slot_hbm.1, s32[96]{0:T(128)} %col_hbm.1, s32[96]{0:T(128)} %id_hbm.1, s32[32]{0:T(128)} %reshape_squeeze.3.touched_ref, ...), custom_call_target="tpu_custom_call" | custom-call | bytes 1 | tf_op jit(solution)/shard_map/pallas_call | solution.py:24
  9.4 2.1 %collective-permute-start.1 = (bf16[4,4,32,512]{3,2,1,0:T(8,128)(2,1)}, bf16[4,4,32,512]{3,2,1,0:T(8,128)(2,1)S(1)}, u32[]{:S(2)}, u32[]{:S(2)}) collective-permute-start(bf16[4,4,32,512]{3,2,1,0:T(8,128)(2,1)} %get-tuple-element.115), channel_id=1, source_target_pairs={{0,4},{4,0},{8,12},{12,8},{16,20},{20,16},{24,28},{28,24},{1,5},{5... | collective-permute-start | bytes 1572872 | tf_op jit(solution)/shard_map/ppermute | solution.py:425
  13.2 3.6 %shard_map.97 = (bf16[4,4,32,512]{3,2,1,0:T(8,128)(2,1)S(1)}, bf16[4,4,16,512]{3,2,1,0:T(8,128)(2,1)S(1)}, bf16[4,4,32,512]{3,2,1,0:T(8,128)(2,1)S(1)}, bf16[4,4...) custom-call(s32[128]{0:T(128)S(1)} %copy-done.9, ...), custom_call_target="tpu_custom_call" | custom-call | bytes 1 | tf_op jit(solution)/shard_map/pallas_call | solution.py:24
  16.9 2.2 %shard_map.96 = (bf16[4,4,32,512]{3,2,1,0:T(8,128)(2,1)S(1)}, bf16[4,4,16,512]{3,2,1,0:T(8,128)(2,1)S(1)}, bf16[4,4,32,512]{3,2,1,0:T(8,128)(2,1)S(1)}, bf16[4,4,16,512]{3,2,1,0:T(8,128)(2,1)S(1)}, f32[8,128]{1,0:T(8,128)S(1)}) custom-call(s32[128]{0:T(128)S(1)} %copy-done.10, bf16[48,128,128]{2,1,0:T(8,128)(2,1)S(1)} %copy-done.4, ...), custom_call_target="tpu_custom_call" | custom-call | bytes 1 | tf_op jit(solution)/shard_map/pallas_call | solution.py:24
  19.1 5.4 %collective-permute-done.1.got_ref = bf16[4,4,32,512]{3,2,1,0:T(8,128)(2,1)S(1)} collective-permute-done((bf16[4,4,32,512]{3,2,1,0:T(8,128)(2,1)}, bf16[4,4,32,512]{3,2,1,0:T(8,128)(2,1)S(1)}, u32[]{:S(2)}, u32[]{:S(2)}) %collective-permute-start.1) | collective-permute-done | bytes 524320 | tf_op jit(solution)/shard_map/ppermute | solution.py:425
  24.8 2.2 %collective-permute-start.2 = (bf16[2,4,32,512]{3,2,1,0:T(8,128)(2,1)S(1)}, bf16[2,4,32,512]{3,2,1,0:T(8,128)(2,1)S(1)}, u32[]{:S(2)}, u32[]{:S(2)}) collective-permute-start(bf16[2,4,32,512]{3,2,1,0:T(8,128)(2,1)S(1)} %get-tuple-element.118), channel_id=1, source_target_pairs={{0,8},{4,12},{8,0},{12,4},{16,24},{20,28},{24,16},{28,20},{1,9},{5... | collective-permute-start | bytes 786440 | tf_op jit(solution)/shard_map/ppermute | solution.py:425
  28.5 4.3 %collective-permute-done.2.got_ref = bf16[2,4,32,512]{3,2,1,0:T(8,128)(2,1)S(1)} collective-permute-done((bf16[2,4,32,512]{3,2,1,0:T(8,128)(2,1)S(1)}, bf16[2,4,32,512]{3,2,1,0:T(8,128)(2,1)S(1)}, u32[]{:S(2)}, u32[]{:S(2)}) %collective-permute-start.2) | collective-permute-done | bytes 262176 | tf_op jit(solution)/shard_map/ppermute | solution.py:425
  32.8 3.1 %collective-permute-start.3 = (bf16[1,4,32,512]{3,2,1,0:T(8,128)(2,1)S(1)}, bf16[1,4,32,512]{3,2,1,0:T(8,128)(2,1)S(1)}, u32[]{:S(2)}, u32[]{:S(2)}) collective-permute-start(bf16[1,4,32,512]{3,2,1,0:T(8,128)(2,1)S(1)} %get-tuple-element.121), channel_id=1, source_target_pairs={{0,16},{4,20},{8,24},{12,28},{16,0},{20,4},{24,8},{28,12},{1,17},{... | collective-permute-start | bytes 393224 | tf_op jit(solution)/shard_map/ppermute | solution.py:425
  35.9 3.1 %collective-permute-done.3.got_ref = bf16[1,4,32,512]{3,2,1,0:T(8,128)(2,1)S(1)} collective-permute-done((bf16[1,4,32,512]{3,2,1,0:T(8,128)(2,1)S(1)}, bf16[1,4,32,512]{3,2,1,0:T(8,128)(2,1)S(1)}, u32[]{:S(2)}, u32[]{:S(2)}) %collective-permute-start.3) | collective-permute-done | bytes 131104 | tf_op jit(solution)/shard_map/ppermute | solution.py:425
  39.3 3.3 %collective-permute-start.6 = (bf16[2,4,32,512]{3,2,1,0:T(8,128)(2,1)S(1)}, bf16[2,4,32,512]{3,2,1,0:T(8,128)(2,1)S(1)}, u32[]{:S(2)}, u32[]{:S(2)}) collective-permute-start(bf16[2,4,32,512]{3,2,1,0:T(8,128)(2,1)S(1)} %get-tuple-element.130), channel_id=1, source_target_pairs={{0,8},{4,12},{8,0},{12,4},{16,24},{20,28},{24,16},{28,20},{1,9},{5... | collective-permute-start | bytes 786440 | tf_op jit(solution)/shard_map/ppermute | solution.py:425
  45.2 1.9 %collective-permute-start.8 = (bf16[2,4,32,512]{3,2,1,0:T(8,128)(2,1)S(1)}, bf16[2,4,32,512]{3,2,1,0:T(8,128)(2,1)S(1)}, u32[]{:S(2)}, u32[]{:S(2)}) collective-permute-start(bf16[2,4,32,512]{3,2,1,0:T(8,128)(2,1)S(1)} %get-tuple-element.135), channel_id=1, source_target_pairs={{0,8},{4,12},{8,0},{12,4},{16,24},{20,28},{24,16},{28,20},{1,9},{5... | collective-permute-start | bytes 786440 | tf_op jit(solution)/shard_map/ppermute | solution.py:425
  49.7 2.5 %collective-permute-start.11 = (bf16[1,4,32,512]{3,2,1,0:T(8,128)(2,1)S(1)}, bf16[1,4,32,512]{3,2,1,0:T(8,128)(2,1)S(1)}, u32[]{:S(2)}, u32[]{:S(2)}) collective-permute-start(bf16[1,4,32,512]{3,2,1,0:T(8,128)(2,1)S(1)} %get-tuple-element.143), channel_id=1, source_target_pairs={{0,16},{4,20},{8,24},{12,28},{16,0},{20,4},{24,8},{28,12},{1,17},{... | collective-permute-start | bytes 393224 | tf_op jit(solution)/shard_map/ppermute | solution.py:425
  52.6 2.6 %collective-permute-start.13 = (bf16[1,4,32,512]{3,2,1,0:T(8,128)(2,1)S(1)}, bf16[1,4,32,512]{3,2,1,0:T(8,128)(2,1)S(1)}, u32[]{:S(2)}, u32[]{:S(2)}) collective-permute-start(bf16[1,4,32,512]{3,2,1,0:T(8,128)(2,1)S(1)} %get-tuple-element.149), channel_id=1, source_target_pairs={{0,16},{4,20},{8,24},{12,28},{16,0},{20,4},{24,8},{28,12},{1,17},{... | collective-permute-start | bytes 393224 | tf_op jit(solution)/shard_map/ppermute | solution.py:425
  55.4 2.1 %collective-permute-start.14 = (bf16[2,4,16,512]{3,2,1,0:T(8,128)(2,1)S(1)}, bf16[2,4,16,512]{3,2,1,0:T(8,128)(2,1)S(1)}, u32[]{:S(2)}, u32[]{:S(2)}) collective-permute-start(bf16[2,4,16,512]{3,2,1,0:T(8,128)(2,1)S(1)} %get-tuple-element.152), channel_id=1, source_target_pairs={{0,8},{4,12},{8,0},{12,4},{16,24},{20,28},{24,16},{28,20},{1,9},{5... | collective-permute-start | bytes 393224 | tf_op jit(solution)/shard_map/ppermute | solution.py:425
  60.1 2.5 %collective-permute-done.11.got_ref = bf16[1,4,32,512]{3,2,1,0:T(8,128)(2,1)S(1)} collective-permute-done((bf16[1,4,32,512]{3,2,1,0:T(8,128)(2,1)S(1)}, bf16[1,4,32,512]{3,2,1,0:T(8,128)(2,1)S(1)}, u32[]{:S(2)}, u32[]{:S(2)}) %collective-permute-start.11) | collective-permute-done | bytes 131104 | tf_op jit(solution)/shard_map/ppermute | solution.py:425
  65.1 3.1 %collective-permute-done.13.got_ref = bf16[1,4,32,512]{3,2,1,0:T(8,128)(2,1)S(1)} collective-permute-done((bf16[1,4,32,512]{3,2,1,0:T(8,128)(2,1)S(1)}, bf16[1,4,32,512]{3,2,1,0:T(8,128)(2,1)S(1)}, u32[]{:S(2)}, u32[]{:S(2)}) %collective-permute-start.13) | collective-permute-done | bytes 131104 | tf_op jit(solution)/shard_map/ppermute | solution.py:425
  71.0 3.0 %collective-permute-done.16.got_ref = bf16[1,4,16,512]{3,2,1,0:T(8,128)(2,1)S(1)} collective-permute-done((bf16[1,4,16,512]{3,2,1,0:T(8,128)(2,1)S(1)}, bf16[1,4,16,512]{3,2,1,0:T(8,128)(2,1)S(1)}, u32[]{:S(2)}, u32[]{:S(2)}) %collective-permute-start.16) | collective-permute-done | bytes 65568 | tf_op jit(solution)/shard_map/ppermute | solution.py:425
  79.9 2.0 %collective-permute-start.29 = (bf16[2,4,32,512]{3,2,1,0:T(8,128)(2,1)S(1)}, bf16[2,4,32,512]{3,2,1,0:T(8,128)(2,1)S(1)}, u32[]{:S(2)}, u32[]{:S(2)}) collective-permute-start(bf16[2,4,32,512]{3,2,1,0:T(8,128)(2,1)S(1)} %get-tuple-element.186.held_ref), channel_id=1, source_target_pairs={{0,8},{4,12},{8,0},{12,4},{16,24},{20,28},{24,16},{28,20},{1,9},{5... | collective-permute-start | bytes 786440 | tf_op jit(solution)/shard_map/ppermute | solution.py:425
  84.7 4.1 %collective-permute-done.24.got_ref = bf16[1,4,32,512]{3,2,1,0:T(8,128)(2,1)S(1)} collective-permute-done((bf16[1,4,32,512]{3,2,1,0:T(8,128)(2,1)S(1)}, bf16[1,4,32,512]{3,2,1,0:T(8,128)(2,1)S(1)}, u32[]{:S(2)}, u32[]{:S(2)}) %collective-permute-start.24) | collective-permute-done | bytes 131104 | tf_op jit(solution)/shard_map/ppermute | solution.py:425
  94.9 3.9 %collective-permute-start.31 = (bf16[8,32,512]{2,1,0:T(8,128)(2,1)S(1)}, bf16[8,32,512]{2,1,0:T(8,128)(2,1)S(1)}, u32[]{:S(2)}, u32[]{:S(2)}) collective-permute-start(bf16[8,32,512]{2,1,0:T(8,128)(2,1)S(1)} %get-tuple-element.191), channel_id=1, source_target_pairs={{0,4},{4,0},{8,12},{12,8},{16,20},{20,16},{24,28},{28,24},{1,5},{5... | collective-permute-start | bytes 786440 | tf_op jit(solution)/shard_map/ppermute | solution.py:425
  106.7 2.7 %collective-permute-done.32.got_ref = bf16[1,4,16,512]{3,2,1,0:T(8,128)(2,1)S(1)} collective-permute-done((bf16[1,4,16,512]{3,2,1,0:T(8,128)(2,1)S(1)}, bf16[1,4,16,512]{3,2,1,0:T(8,128)(2,1)S(1)}, u32[]{:S(2)}, u32[]{:S(2)}) %collective-permute-start.32) | collective-permute-done | bytes 65568 | tf_op jit(solution)/shard_map/ppermute | solution.py:425
  110.9 2.1 %collective-permute-start.37 = (bf16[2,4,16,512]{3,2,1,0:T(8,128)(2,1)S(1)}, bf16[2,4,16,512]{3,2,1,0:T(8,128)(2,1)S(1)}, u32[]{:S(2)}, u32[]{:S(2)}) collective-permute-start(bf16[2,4,16,512]{3,2,1,0:T(8,128)(2,1)S(1)} %get-tuple-element.205.held_ref), channel_id=1, source_target_pairs={{0,8},{4,12},{8,0},{12,4},{16,24},{20,28},{24,16},{28,20},{1,9},{5... | collective-permute-start | bytes 393224 | tf_op jit(solution)/shard_map/ppermute | solution.py:425
  123.2 2.0 %shard_map.137 = (bf16[4,128,512]{2,1,0:T(8,128)(2,1)}, bf16[16,128,512]{2,1,0:T(8,128)(2,1)}, f32[8,128]{1,0:T(8,128)}) custom-call(f32[8,128]{1,0:T(8,128)S(1)} %get-tuple-element.214.token_ref, s32[1]{0:T(128)} %bitcast.me_ref, s32[16]{0:T(128)S(1)} %copy-done.6, s32[16]{0:T(128)S(1)} %copy-done.8, ...), custom_call_target="tpu_custom_call", output_to_operand_aliasing={{0}: (7, {}), {1}: (8, {})} | custom-call | bytes 1 | tf_op jit(solution)/shard_map/pallas_call | solution.py:24
  (128 shorter events, 54.1 us)
Async XLA Ops:
  9.4 15.1 %collective-permute-start.1 = (bf16[4,4,32,512]{3,2,1,0:T(8,128)(2,1)}, bf16[4,4,32,512]{3,2,1,0:T(8,128)(2,1)S(1)}, u32[]{:S(2)}, u32[]{:S(2)}) collective-permute-start(bf16[4,4,32,512]{3,2,1,0:T(8,128)(2,1)} %get-tuple-element.115), channel_id=1, source_target_pairs={{0,4},{4,0},{8,12},{12,8},{16,20},{20,16},{24,28},{28,24},{1,5},{5... | collective-permute-start | bytes 1572872 | tf_op jit(solution)/shard_map/ppermute | solution.py:425
  16.8 22.2 %collective-permute-start.4 = (bf16[4,4,32,512]{3,2,1,0:T(8,128)(2,1)S(1)}, bf16[4,4,32,512]{3,2,1,0:T(8,128)(2,1)S(1)}, u32[]{:S(2)}, u32[]{:S(2)}) collective-permute-start(bf16[4,4,32,512]{3,2,1,0:T(8,128)(2,1)S(1)} %get-tuple-element.124), channel_id=1, source_target_pairs={{0,4},{4,0},{8,12},{12,8},{16,20},{20,16},{24,28},{28,24},{1,5},{5... | collective-permute-start | bytes 1572872 | tf_op jit(solution)/shard_map/ppermute | solution.py:425
  24.8 7.9 %collective-permute-start.2 = (bf16[2,4,32,512]{3,2,1,0:T(8,128)(2,1)S(1)}, bf16[2,4,32,512]{3,2,1,0:T(8,128)(2,1)S(1)}, u32[]{:S(2)}, u32[]{:S(2)}) collective-permute-start(bf16[2,4,32,512]{3,2,1,0:T(8,128)(2,1)S(1)} %get-tuple-element.118), channel_id=1, source_target_pairs={{0,8},{4,12},{8,0},{12,4},{16,24},{20,28},{24,16},{28,20},{1,9},{5... | collective-permute-start | bytes 786440 | tf_op jit(solution)/shard_map/ppermute | solution.py:425
  27.0 18.0 %collective-permute-start.5 = (bf16[4,4,32,512]{3,2,1,0:T(8,128)(2,1)S(1)}, bf16[4,4,32,512]{3,2,1,0:T(8,128)(2,1)S(1)}, u32[]{:S(2)}, u32[]{:S(2)}) collective-permute-start(bf16[4,4,32,512]{3,2,1,0:T(8,128)(2,1)S(1)} %get-tuple-element.127), channel_id=1, source_target_pairs={{0,4},{4,0},{8,12},{12,8},{16,20},{20,16},{24,28},{28,24},{1,5},{5... | collective-permute-start | bytes 1572872 | tf_op jit(solution)/shard_map/ppermute | solution.py:425
  39.3 9.3 %collective-permute-start.6 = (bf16[2,4,32,512]{3,2,1,0:T(8,128)(2,1)S(1)}, bf16[2,4,32,512]{3,2,1,0:T(8,128)(2,1)S(1)}, u32[]{:S(2)}, u32[]{:S(2)}) collective-permute-start(bf16[2,4,32,512]{3,2,1,0:T(8,128)(2,1)S(1)} %get-tuple-element.130), channel_id=1, source_target_pairs={{0,8},{4,12},{8,0},{12,4},{16,24},{20,28},{24,16},{28,20},{1,9},{5... | collective-permute-start | bytes 786440 | tf_op jit(solution)/shard_map/ppermute | solution.py:425
  45.2 7.3 %collective-permute-start.8 = (bf16[2,4,32,512]{3,2,1,0:T(8,128)(2,1)S(1)}, bf16[2,4,32,512]{3,2,1,0:T(8,128)(2,1)S(1)}, u32[]{:S(2)}, u32[]{:S(2)}) collective-permute-start(bf16[2,4,32,512]{3,2,1,0:T(8,128)(2,1)S(1)} %get-tuple-element.135), channel_id=1, source_target_pairs={{0,8},{4,12},{8,0},{12,4},{16,24},{20,28},{24,16},{28,20},{1,9},{5... | collective-permute-start | bytes 786440 | tf_op jit(solution)/shard_map/ppermute | solution.py:425
  47.1 8.2 %collective-permute-start.9 = (bf16[4,4,16,512]{3,2,1,0:T(8,128)(2,1)S(1)}, bf16[4,4,16,512]{3,2,1,0:T(8,128)(2,1)S(1)}, u32[]{:S(2)}, u32[]{:S(2)}) collective-permute-start(bf16[4,4,16,512]{3,2,1,0:T(8,128)(2,1)S(1)} %get-tuple-element.138), channel_id=1, source_target_pairs={{0,4},{4,0},{8,12},{12,8},{16,20},{20,16},{24,28},{28,24},{1,5},{5... | collective-permute-start | bytes 786440 | tf_op jit(solution)/shard_map/ppermute | solution.py:425
  48.7 8.8 %collective-permute-start.10 = (bf16[2,4,32,512]{3,2,1,0:T(8,128)(2,1)S(1)}, bf16[2,4,32,512]{3,2,1,0:T(8,128)(2,1)S(1)}, u32[]{:S(2)}, u32[]{:S(2)}) collective-permute-start(bf16[2,4,32,512]{3,2,1,0:T(8,128)(2,1)S(1)} %get-tuple-element.140.held_ref), channel_id=1, source_target_pairs={{0,1},{1,0},{2,3},{3,2},{4,5},{5,4},{6,7},{7,6},{8,9},{9,8},{10,11... | collective-permute-start | bytes 786440 | tf_op jit(solution)/shard_map/ppermute | solution.py:425
  48.8 15.4 %collective-permute-start.12 = (bf16[4,4,16,512]{3,2,1,0:T(8,128)(2,1)S(1)}, bf16[4,4,16,512]{3,2,1,0:T(8,128)(2,1)S(1)}, u32[]{:S(2)}, u32[]{:S(2)}) collective-permute-start(bf16[4,4,16,512]{3,2,1,0:T(8,128)(2,1)S(1)} %get-tuple-element.146), channel_id=1, source_target_pairs={{0,4},{4,0},{8,12},{12,8},{16,20},{20,16},{24,28},{28,24},{1,5},{5... | collective-permute-start | bytes 786440 | tf_op jit(solution)/shard_map/ppermute | solution.py:425
  49.7 12.9 %collective-permute-start.11 = (bf16[1,4,32,512]{3,2,1,0:T(8,128)(2,1)S(1)}, bf16[1,4,32,512]{3,2,1,0:T(8,128)(2,1)S(1)}, u32[]{:S(2)}, u32[]{:S(2)}) collective-permute-start(bf16[1,4,32,512]{3,2,1,0:T(8,128)(2,1)S(1)} %get-tuple-element.143), channel_id=1, source_target_pairs={{0,16},{4,20},{8,24},{12,28},{16,0},{20,4},{24,8},{28,12},{1,17},{... | collective-permute-start | bytes 393224 | tf_op jit(solution)/shard_map/ppermute | solution.py:425
  52.6 15.6 %collective-permute-start.13 = (bf16[1,4,32,512]{3,2,1,0:T(8,128)(2,1)S(1)}, bf16[1,4,32,512]{3,2,1,0:T(8,128)(2,1)S(1)}, u32[]{:S(2)}, u32[]{:S(2)}) collective-permute-start(bf16[1,4,32,512]{3,2,1,0:T(8,128)(2,1)S(1)} %get-tuple-element.149), channel_id=1, source_target_pairs={{0,16},{4,20},{8,24},{12,28},{16,0},{20,4},{24,8},{28,12},{1,17},{... | collective-permute-start | bytes 393224 | tf_op jit(solution)/shard_map/ppermute | solution.py:425
  55.4 12.8 %collective-permute-start.14 = (bf16[2,4,16,512]{3,2,1,0:T(8,128)(2,1)S(1)}, bf16[2,4,16,512]{3,2,1,0:T(8,128)(2,1)S(1)}, u32[]{:S(2)}, u32[]{:S(2)}) collective-permute-start(bf16[2,4,16,512]{3,2,1,0:T(8,128)(2,1)S(1)} %get-tuple-element.152), channel_id=1, source_target_pairs={{0,8},{4,12},{8,0},{12,4},{16,24},{20,28},{24,16},{28,20},{1,9},{5... | collective-permute-start | bytes 393224 | tf_op jit(solution)/shard_map/ppermute | solution.py:425
  59.5 11.5 %collective-permute-start.15 = (bf16[1,4,32,512]{3,2,1,0:T(8,128)(2,1)S(1)}, bf16[1,4,32,512]{3,2,1,0:T(8,128)(2,1)S(1)}, u32[]{:S(2)}, u32[]{:S(2)}) collective-permute-start(bf16[1,4,32,512]{3,2,1,0:T(8,128)(2,1)S(1)} %get-tuple-element.154.held_ref), channel_id=1, source_target_pairs={{0,16},{4,20},{8,24},{12,28},{16,0},{20,4},{24,8},{28,12},{1,17},{... | collective-permute-start | bytes 393224 | tf_op jit(solution)/shard_map/ppermute | solution.py:425
  62.6 11.5 %collective-permute-start.17 = (bf16[1,4,32,512]{3,2,1,0:T(8,128)(2,1)S(1)}, bf16[1,4,32,512]{3,2,1,0:T(8,128)(2,1)S(1)}, u32[]{:S(2)}, u32[]{:S(2)}) collective-permute-start(bf16[1,4,32,512]{3,2,1,0:T(8,128)(2,1)S(1)} %bitcast.9), channel_id=1, source_target_pairs={{0,2},{1,3},{2,0},{3,1},{4,6},{5,7},{6,4},{7,5},{8,10},{9,11},{10,... | collective-permute-start | bytes 393224 | tf_op jit(solution)/shard_map/ppermute | solution.py:425
  64.3 9.9 %collective-permute-start.18 = (bf16[2,4,16,512]{3,2,1,0:T(8,128)(2,1)S(1)}, bf16[2,4,16,512]{3,2,1,0:T(8,128)(2,1)S(1)}, u32[]{:S(2)}, u32[]{:S(2)}) collective-permute-start(bf16[2,4,16,512]{3,2,1,0:T(8,128)(2,1)S(1)} %get-tuple-element.162), channel_id=1, source_target_pairs={{0,8},{4,12},{8,0},{12,4},{16,24},{20,28},{24,16},{28,20},{1,9},{5... | collective-permute-start | bytes 393224 | tf_op jit(solution)/shard_map/ppermute | solution.py:425
  74.3 7.5 %collective-permute-start.22 = (bf16[2,4,32,512]{3,2,1,0:T(8,128)(2,1)S(1)}, bf16[2,4,32,512]{3,2,1,0:T(8,128)(2,1)S(1)}, u32[]{:S(2)}, u32[]{:S(2)}) collective-permute-start(bf16[2,4,32,512]{3,2,1,0:T(8,128)(2,1)S(1)} %get-tuple-element.170.held_ref), channel_id=1, source_target_pairs={{0,1},{1,0},{2,3},{3,2},{4,5},{5,4},{6,7},{7,6},{8,9},{9,8},{10,11... | collective-permute-start | bytes 786440 | tf_op jit(solution)/shard_map/ppermute | solution.py:425
  78.5 10.2 %collective-permute-start.24 = (bf16[1,4,32,512]{3,2,1,0:T(8,128)(2,1)S(1)}, bf16[1,4,32,512]{3,2,1,0:T(8,128)(2,1)S(1)}, u32[]{:S(2)}, u32[]{:S(2)}) collective-permute-start(bf16[1,4,32,512]{3,2,1,0:T(8,128)(2,1)S(1)} %get-tuple-element.175.held_ref), channel_id=1, source_target_pairs={{0,16},{4,20},{8,24},{12,28},{16,0},{20,4},{24,8},{28,12},{1,17},{... | collective-permute-start | bytes 393224 | tf_op jit(solution)/shard_map/ppermute | solution.py:425
  79.9 14.5 %collective-permute-start.29 = (bf16[2,4,32,512]{3,2,1,0:T(8,128)(2,1)S(1)}, bf16[2,4,32,512]{3,2,1,0:T(8,128)(2,1)S(1)}, u32[]{:S(2)}, u32[]{:S(2)}) collective-permute-start(bf16[2,4,32,512]{3,2,1,0:T(8,128)(2,1)S(1)} %get-tuple-element.186.held_ref), channel_id=1, source_target_pairs={{0,8},{4,12},{8,0},{12,4},{16,24},{20,28},{24,16},{28,20},{1,9},{5... | collective-permute-start | bytes 786440 | tf_op jit(solution)/shard_map/ppermute | solution.py:425
  82.9 9.1 %collective-permute-start.26 = (bf16[1,4,32,512]{3,2,1,0:T(8,128)(2,1)S(1)}, bf16[1,4,32,512]{3,2,1,0:T(8,128)(2,1)S(1)}, u32[]{:S(2)}, u32[]{:S(2)}) collective-permute-start(bf16[1,4,32,512]{3,2,1,0:T(8,128)(2,1)S(1)} %get-tuple-element.179.held_ref), channel_id=1, source_target_pairs={{0,16},{4,20},{8,24},{12,28},{16,0},{20,4},{24,8},{28,12},{1,17},{... | collective-permute-start | bytes 393224 | tf_op jit(solution)/shard_map/ppermute | solution.py:425
  89.4 10.6 %collective-permute-start.30 = (bf16[2,4,32,512]{3,2,1,0:T(8,128)(2,1)S(1)}, bf16[2,4,32,512]{3,2,1,0:T(8,128)(2,1)S(1)}, u32[]{:S(2)}, u32[]{:S(2)}) collective-permute-start(bf16[2,4,32,512]{3,2,1,0:T(8,128)(2,1)S(1)} %get-tuple-element.188.held_ref), channel_id=1, source_target_pairs={{0,8},{4,12},{8,0},{12,4},{16,24},{20,28},{24,16},{28,20},{1,9},{5... | collective-permute-start | bytes 786440 | tf_op jit(solution)/shard_map/ppermute | solution.py:425
  94.9 10.3 %collective-permute-start.31 = (bf16[8,32,512]{2,1,0:T(8,128)(2,1)S(1)}, bf16[8,32,512]{2,1,0:T(8,128)(2,1)S(1)}, u32[]{:S(2)}, u32[]{:S(2)}) collective-permute-start(bf16[8,32,512]{2,1,0:T(8,128)(2,1)S(1)} %get-tuple-element.191), channel_id=1, source_target_pairs={{0,4},{4,0},{8,12},{12,8},{16,20},{20,16},{24,28},{28,24},{1,5},{5... | collective-permute-start | bytes 786440 | tf_op jit(solution)/shard_map/ppermute | solution.py:425
  98.8 10.6 %collective-permute-start.33 = (bf16[2,4,32,512]{3,2,1,0:T(8,128)(2,1)S(1)}, bf16[2,4,32,512]{3,2,1,0:T(8,128)(2,1)S(1)}, u32[]{:S(2)}, u32[]{:S(2)}) collective-permute-start(bf16[2,4,32,512]{3,2,1,0:T(8,128)(2,1)S(1)} %get-tuple-element.195.held_ref), channel_id=1, source_target_pairs={{0,8},{4,12},{8,0},{12,4},{16,24},{20,28},{24,16},{28,20},{1,9},{5... | collective-permute-start | bytes 786440 | tf_op jit(solution)/shard_map/ppermute | solution.py:425
  100.5 12.4 %collective-permute-start.35 = (bf16[8,32,512]{2,1,0:T(8,128)(2,1)S(1)}, bf16[8,32,512]{2,1,0:T(8,128)(2,1)S(1)}, u32[]{:S(2)}, u32[]{:S(2)}) collective-permute-start(bf16[8,32,512]{2,1,0:T(8,128)(2,1)S(1)} %get-tuple-element.199), channel_id=1, source_target_pairs={{0,4},{4,0},{8,12},{12,8},{16,20},{20,16},{24,28},{28,24},{1,5},{5... | collective-permute-start | bytes 786440 | tf_op jit(solution)/shard_map/ppermute | solution.py:425
  110.0 9.1 %collective-permute-start.38 = (bf16[8,32,512]{2,1,0:T(8,128)(2,1)S(1)}, bf16[8,32,512]{2,1,0:T(8,128)(2,1)S(1)}, u32[]{:S(2)}, u32[]{:S(2)}) collective-permute-start(bf16[8,32,512]{2,1,0:T(8,128)(2,1)S(1)} %get-tuple-element.207), channel_id=1, source_target_pairs={{0,4},{4,0},{8,12},{12,8},{16,20},{20,16},{24,28},{28,24},{1,5},{5... | collective-permute-start | bytes 786440 | tf_op jit(solution)/shard_map/ppermute | solution.py:425
  (29 other events, 163.5 us)

commit v7 on v6

--- a/solution.py
+++ b/solution.py
@@ -5,10 +5,10 @@
 from jax.experimental.pallas import tpu as pltpu
 from jax.sharding import PartitionSpec as P
 
-SHARES = (2, 2, 1, 2, 1)
+SHARES = (2, 2, 2, 1, 1)
 ORDER = (
-    0, 0, 0, 1, 3, 1, 0, 3, 2, 0, 1, 4, 3, 2, 0, 2, 1, 4, 3, 1, 2, 3, 4, 1, 4, 3, 4, 2, 0, 1, 0, 4,
-    3, 2, 1, 4, 2, 3, 4, 2,
+    1, 0, 1, 2, 0, 2, 1, 3, 0, 2, 0, 3, 4, 1, 0, 1, 3, 4, 4, 0, 3, 2, 2, 1, 4, 0, 4, 4, 2, 1, 0, 3,
+    2, 3, 1, 4, 3, 4, 2, 3,
 )
 READ_CAP = 2
 VMEM_BYTES = 12 * 1024 * 1024
@@ -39,11 +39,11 @@
     return lax.div(value, size), lax.rem(value, size)
 
 
-def reversed_bits(value, bits):
-    result = value & 1
-    for i in range(1, bits):
-        result = (result << 1) | ((value >> i) & 1)
-    return result
+def place_of(peer, bits):
+    place = 0
+    for bit in bits:
+        place = (place << 1) | ((peer >> (bit.bit_length() - 1)) & 1)
+    return place
 
 
 def planned_order(ways):
@@ -113,28 +113,30 @@
                 top = top + blocks * rows
 
 
-def first_part(me, slot, col, tile_id, touched, tiles, features, readers, neighbour, first, count, span):
+def first_part(me, slot, col, tile_id, touched, tiles, features, readers, neighbour, orders, first, count, spans):
     block = tiles.shape[1]
     blocks = features.shape[0] // block
     width = features.shape[1]
     edges, cap = touched.shape[1], touched.shape[2]
-    bits = edges.bit_length() - 1
+    column_bits = [1 << i for i in range(1, edges.bit_length() - 1)]
     products = slot.shape[0]
     half = edges // 2
-    start, rows = span
+    loaded = sum(rows for _, rows in spans)
+    tallest = max(rows for _, rows in spans)
     square = blocks * blocks
 
     listed = readers.shape[0]
 
     def body(me_ref, slot_hbm, col_hbm, id_hbm, touched_ref, tiles_hbm, x_hbm, readers_ref, neighbour_ref, *refs):
-        table, choice, entry, out, x_out, *scratch = refs
+        table, choice, entry, *outs = refs[: 3 + len(spans)]
+        x_out, *scratch = refs[3 + len(spans) :]
         slot_ref, col_ref, id_ref, tiles_ref, lhs, bases, seen, sems = scratch
         loads = [
             pltpu.make_async_copy(slot_hbm, slot_ref, sems.at[0]),
             pltpu.make_async_copy(col_hbm, col_ref, sems.at[1]),
             pltpu.make_async_copy(id_hbm, id_ref, sems.at[2]),
             pltpu.make_async_copy(x_hbm, x_out, sems.at[3]),
-            pltpu.make_async_copy(tiles_hbm.at[:, pl.ds(start, rows)], tiles_ref, sems.at[4]),
+            pltpu.make_async_copy(tiles_hbm.at[:, pl.ds(0, loaded)], tiles_ref, sems.at[4]),
         ]
         for load in loads:
             load.start()
@@ -143,12 +145,13 @@
             table[i] = 0
             return carry
 
-        lax.fori_loop(0, edges * square, clear, 0, unroll=16)
+        lax.fori_loop(0, len(orders) * edges * square, clear, 0, unroll=16)
 
         def place_slot(k, carry):
             owner, _ = split(k, cap)
-            place = reversed_bits(owner ^ me_ref[0], bits)
-            bases[k] = (place * blocks + touched_ref[k]) * blocks
+            for n, order in enumerate(orders):
+                place = place_of(owner ^ me_ref[0], order)
+                bases[n * edges * cap + k] = ((n * edges + place) * blocks + touched_ref[k]) * blocks
             return carry
 
         lax.fori_loop(0, edges * cap, place_slot, 0, unroll=8)
@@ -171,48 +174,53 @@
             turn = seen[edges + owner]
             seen[edges + owner] = turn + 1
             peer = owner ^ me_ref[0]
-            row = reversed_bits(peer >> 1, bits - 1) * READ_CAP + jnp.minimum(turn, READ_CAP - 1)
+            row = place_of(peer, column_bits) * READ_CAP + jnp.minimum(turn, READ_CAP - 1)
             choice[jnp.where(peer & 1 == 0, row, half * READ_CAP)] = b
             return carry
 
         lax.fori_loop(0, listed, enter_lists, 0)
 
         def enter(k, carry):
-            table[bases[slot_ref[k]] + col_ref[k]] = id_ref[k] + 1
+            for n in range(len(orders)):
+                table[bases[n * edges * cap + slot_ref[k]] + col_ref[k]] = id_ref[k] + 1
             return carry
 
         lax.fori_loop(0, products, enter, 0, unroll=8)
         for load in loads[3:]:
             load.wait()
 
-        def one_owner(i, carry):
-            at = pl.multiple_of(i * blocks * rows, blocks * rows)
-            lay_tiles(table, (first + i) * square, tiles_ref, lhs, [span], start, blocks, block, at)
-            return carry
-
-        lax.fori_loop(0, count, one_owner, 0)
-        total = jnp.dot(lhs[...], x_out[...], preferred_element_type=jnp.float32)
-        out[...] = total.astype(jnp.bfloat16).reshape(out.shape)
+        for n, (span, out) in enumerate(zip(spans, outs)):
+            height = blocks * span[1]
+
+            def one_owner(i, carry):
+                at = pl.multiple_of(i * height, height)
+                base = (n * edges + first + i) * square
+                lay_tiles(table, base, tiles_ref, lhs, [span], 0, blocks, block, at)
+                return carry
+
+            lax.fori_loop(0, count, one_owner, 0)
+            total = jnp.dot(lhs[pl.ds(0, count * height)], x_out[...], preferred_element_type=jnp.float32)
+            out[...] = total.astype(jnp.bfloat16).reshape(out.shape)
 
     return call(
         body,
         [
-            jax.ShapeDtypeStruct((edges * square,), jnp.int32),
+            jax.ShapeDtypeStruct((len(orders) * edges * square,), jnp.int32),
             jax.ShapeDtypeStruct((half * READ_CAP + 1,), jnp.int32),
             jax.ShapeDtypeStruct((edges * READ_CAP,), jnp.int32),
-            jax.ShapeDtypeStruct((count, blocks, rows, width), jnp.bfloat16),
+            *[jax.ShapeDtypeStruct((count, blocks, rows, width), jnp.bfloat16) for _, rows in spans],
             jax.ShapeDtypeStruct(features.shape, jnp.bfloat16),
         ],
         [SMEM, HBM, HBM, HBM, SMEM, HBM, HBM, SMEM, SMEM],
-        [SMEM, SMEM, SMEM, VMEM, VMEM],
+        [SMEM] * 3 + [VMEM] * (len(spans) + 1),
         (me, slot, col, tile_id, touched[me[0]].reshape(-1), tiles, features, readers, neighbour),
         [
             pltpu.SMEM((products,), jnp.int32),
             pltpu.SMEM((products,), jnp.int32),
             pltpu.SMEM((products,), jnp.int32),
-            pltpu.VMEM((tiles.shape[0], rows, block), jnp.bfloat16),
-            pltpu.VMEM((count * blocks * rows, blocks * block), jnp.bfloat16),
-            pltpu.SMEM((edges * cap,), jnp.int32),
+            pltpu.VMEM((tiles.shape[0], loaded, block), jnp.bfloat16),
+            pltpu.VMEM((count * blocks * tallest, blocks * block), jnp.bfloat16),
+            pltpu.SMEM((len(orders) * edges * cap,), jnp.int32),
             pltpu.SMEM((2 * edges,), jnp.int32),
             pltpu.SemaphoreType.DMA((5,)),
         ],
@@ -359,43 +367,50 @@
     )
 
 
-def lay_out(token, me, readers, entry, offsets, held, got, far, outputs, span, block):
+def touch(token, value):
+    def body(token_ref, value_ref, token_out):
+        token_out[...] = token_ref[...]
+
+    return call(body, [TOKEN], [VMEM] * 2, [VMEM], (token, value))
+
+
+def lay_out(token, me, readers, entry, offsets, items, outputs, block):
     count = readers.shape[0]
-    _, blocks, _, width = held.shape
-    start, rows = span
-    slots = 2 * len(offsets) * READ_CAP
-
-    def body(token_ref, me_ref, readers_ref, entry_ref, held_ref, got_ref, far_ref, *refs):
+    half_held, blocks, _, width = items[0][0].shape
+    slots = len(offsets) * READ_CAP
+    arrays = [array for item in items for array in item[:3]]
+
+    def body(token_ref, me_ref, readers_ref, entry_ref, *refs):
         hidden_ref, ghost_ref, token_out, sems = refs[-4:]
-        own = pltpu.make_async_copy(held_ref.at[0], hidden_ref.at[:, pl.ds(start, rows)], sems.at[slots])
-        own.start()
 
         def each(act):
-            for n, offset in enumerate(offsets):
-                for j in range(READ_CAP):
-                    i = n * READ_CAP + j
-                    listed = entry_ref[(me_ref[0] ^ offset) * READ_CAP + j]
-                    source = held_ref if n < held.shape[0] else got_ref
-
-                    @pl.when(listed >= 0)
+            for number, item in enumerate(items):
+                held_ref, got_ref, far_ref = refs[3 * number : 3 * number + 3]
+                rows = pl.ds(*item[3])
+                act(pltpu.make_async_copy(held_ref.at[0], hidden_ref.at[:, rows], sems.at[number, 2 * slots]))
+                for i in range(slots):
+                    n, j = i // READ_CAP, i % READ_CAP
+                    near = entry_ref[(me_ref[0] ^ offsets[n]) * READ_CAP + j]
+                    source = held_ref if n < half_held else got_ref
+
+                    @pl.when(near >= 0)
                     def _():
-                        _, b = split(readers_ref[listed], blocks)
-                        target = ghost_ref.at[listed, pl.ds(start, rows)]
-                        act(pltpu.make_async_copy(source.at[n % held.shape[0], b], target, sems.at[i]))
-
-                    across = entry_ref[(me_ref[0] ^ 1 ^ offset) * READ_CAP + j]
+                        _, b = split(readers_ref[near], blocks)
+                        target = ghost_ref.at[near, rows]
+                        act(pltpu.make_async_copy(source.at[n % half_held, b], target, sems.at[number, i]))
+
+                    across = entry_ref[(me_ref[0] ^ 1 ^ offsets[n]) * READ_CAP + j]
 
                     @pl.when(across >= 0)
                     def _():
-                        target = ghost_ref.at[across, pl.ds(start, rows)]
-                        act(pltpu.make_async_copy(far_ref.at[i], target, sems.at[slots // 2 + i]))
+                        target = ghost_ref.at[across, rows]
+                        act(pltpu.make_async_copy(far_ref.at[i], target, sems.at[number, slots + i]))
 
         each(lambda copy: copy.start())
         token_out[...] = token_ref[...]
-        own.wait()
         each(lambda copy: copy.wait())
 
-    operands = (token, me, readers, entry, held, got, far, *outputs)
+    operands = (token, me, readers, entry, *arrays, *outputs)
     return call(
         body,
         [
@@ -403,10 +418,10 @@
             jax.ShapeDtypeStruct((count, block, width), jnp.bfloat16),
             TOKEN,
         ],
-        [VMEM] + [SMEM] * 3 + [VMEM] * 3 + [HBM] * len(outputs),
+        [VMEM] + [SMEM] * 3 + [VMEM] * len(arrays) + [HBM] * len(outputs),
         [HBM, HBM, VMEM],
         operands,
-        [pltpu.SemaphoreType.DMA((slots + 1,))],
+        [pltpu.SemaphoreType.DMA((len(items), 2 * slots + 1))],
         aliases={len(operands) - 2: 0, len(operands) - 1: 1} if outputs else None,
     )
 
@@ -427,14 +442,17 @@
     columns = offsets_of(edges, 2)
     me, mine = me.reshape(1), mine.reshape(1)
     neighbour = flip(readers, 1)
-    table, choice, entry, early, inputs = first_part(
-        me, tile_slot, tile_col, tile_id, touched, tiles, features, readers, neighbour, half, half, spans[0]
-    )
-    later, first_kept, _ = other_parts(table, tiles, inputs, [(half, half, spans[1:]), (0, half, spans[:1])])
-    away = [early, *later]
-    kept, token = other_parts(table, tiles, inputs, [(0, half, spans[1:])])
+    column_bits = [1 << i for i in range(1, edges.bit_length() - 1)]
+    orders = [[*column_bits, 1], [1, *column_bits]]
+    table, choice, entry, *early, inputs = first_part(
+        me, tile_slot, tile_col, tile_id, touched, tiles, features, readers, neighbour, orders, half, half, spans[:2]
+    )
+    later, first_kept, _ = other_parts(
+        table, tiles, inputs, [(edges + half, half, spans[2:]), (0, half, spans[:1])]
+    )
+    away = [*early, *later]
+    kept, token = other_parts(table, tiles, inputs, [(edges, half, spans[1:])])
     kept = [*first_kept, *kept]
-    outputs = ()
 
     def chained(function, *operands):
         nonlocal token
@@ -452,44 +470,51 @@
             bit //= 2
 
     def one_part(part):
-        nonlocal outputs
-        got = flip(away[part], 1)
+        first, *rest = orders[min(part, 1)]
+        got = flip(away[part], first)
         yield
         total, sent = chained(combine, kept[part], got, weight)
-        bit = 2
-        while bit < edges:
+        for bit in rest:
             got = flip(sent, bit)
             yield
             total, *sent = chained(combine, total, got, weight)
             sent = sent[0] if sent else None
-            bit *= 2
         held, got = yield from spread(total[None], feats, 1, "feat")
         (mixed,) = chained(mix, mine, offsets_of(feats, 1), held, got, weight)
         held, got = yield from spread(mixed, edges, 2, "edge")
         (picked,) = chained(pick, choice, held, got)
         far = flip(picked, 1)
         yield
-        outputs = chained(lay_out, me, readers, entry, columns, held, got, far, outputs, spans[part], block)
+        return held, got, far, spans[part]
 
     def links_of(bit):
-        return {"end": 1.0} if bit == 2 else {"end": 1.0, "middle": 2.0}
-
-    column_bits = [1 << i for i in range(1, edges.bit_length() - 1)]
+        return {"x": 1.0} if bit == 1 else {"end": 1.0} if bit == 2 else {"end": 1.0, "middle": 2.0}
+
     feat_bits = [1 << i for i in reversed(range(feats.bit_length() - 1))]
     ways = []
-    for _, rows in spans:
+    for part, (_, rows) in enumerate(spans):
         share = rows / block
-        way = [({"x": 1.0}, share * half * 1.15)]
-        way += [(links_of(bit), share * half / bit) for bit in column_bits]
+        way = [(links_of(bit), share * half / (1 << n)) for n, bit in enumerate(orders[min(part, 1)])]
         way += [({"chip" if bit == 1 else "feat": 1.0}, share * (1.0 if bit > 1 else 0.3)) for bit in feat_bits]
         way += [(links_of(bit), share * half / bit) for bit in reversed(column_bits)]
         ways.append(way + [({"x": 1.0}, share * READ_CAP / blocks * half)])
     steps = [one_part(part) for part in range(len(spans))]
     for step in steps:
         next(step)
-    known = all(ORDER.count(part) == len(way) for part, way in enumerate(ways))
-    for part in ORDER if known else planned_order(ways):
-        next(steps[part], None)
+    known = sorted(ORDER) == [part for part, way in enumerate(ways) for _ in way]
+    *order, last = ORDER if known else planned_order(ways)
+    ended = []
+    for part in order:
+        try:
+            next(steps[part])
+        except StopIteration as end:
+            ended.append(end.value)
+            chained(touch, end.value[2])
+    outputs = chained(lay_out, me, readers, entry, columns, ended, (), block)
+    try:
+        next(steps[last])
+    except StopIteration as end:
+        outputs = chained(lay_out, me, readers, entry, columns, [end.value], outputs, block)
     hidden, ghosts = outputs
     return hidden.reshape(blocks * block, width), ghosts.reshape(-1, width)
 

time: 125 us -> 122 us (0.976)
  Pallas kernels: 24.1 us -> 21.5 us
  starting transfers between devices: 57.7 us -> 56.3 us
    pallas_call x43 -> x44, Pallas kernels: 24.1 us -> 21.5 us  [call(): pl.pallas_call(body, out_shape=out_shape, in_specs=in_specs, out_specs=ou...]
    ppermute x41, starting transfers between devices: 57.7 us -> 56.3 us  [flip(): lax.ppermute(value, axis, [(d, d ^ bit) for d in range(lax.axis_size(axis...]
    unnamed x24 -> x22, local copies, waits for them, and re-layouts: 3.87 us -> 3.87 us
  transfers between devices with their start and end apart: 41 -> 41, of which waited for: 18 -> 16; matrix products, arithmetic and copies ran while one was open for 1% -> 1% of each run, Pallas kernels for 15% -> 12%
where the time goes in v7:
time: 122 us
  starting transfers between devices  56.3 us (46%)
  waiting for transfers between devices  38.5 us (32%)
  Pallas kernels  21.5 us (18%)
  local copies, waits for them, and re-layouts  4.56 us (4%)
    ppermute x41, starting transfers between devices, flip(): lax.ppermute(value, axis, [(d, d ^ bit) for d in range(lax.axis_size(axis...  56.3 us
    ppermute x41, waiting for transfers between devices, flip(): lax.ppermute(value, axis, [(d, d ^ bit) for d in range(lax.axis_size(axis...  38.5 us
    pallas_call x44, Pallas kernels, call(): pl.pallas_call(body, out_shape=out_shape, in_specs=in_specs, out_specs=ou...  21.5 us
    unnamed x22, local copies, waits for them, and re-layouts  3.87 us
  transfers between devices with their start and end apart: 41, of which 16 were waited for; matrix products, arithmetic and copies ran while one was open for 1% of the time, Pallas kernels for 12%

profile of v7, /device:TPU:0, one launch (start us, length us, event | category | flops | bytes accessed | tf_op | source)
XLA Modules:
  0.0 121.9 jit_solution(12617885316639275077)
XLA Ops:
  0.7 3.0 %collective-permute-start = (s32[16]{0:T(128)}, s32[16]{0:T(128)S(1)}, u32[]{:S(2)}, u32[]{:S(2)}) collective-permute-start(s32[16]{0:T(128)} %readers_ref.5), channel_id=1, source_target_pairs={{0,4},{4,0},{8,12},{12,8},{16,20},{20,16},{24,28},{28,24},{1,5},{5... | collective-permute-start | bytes 200 | tf_op jit(solution)/shard_map/ppermute | solution.py:440
  5.9 4.7 %shard_map.95 = (s32[256]{0:T(256)}, s32[9]{0:T(128)}, s32[16]{0:T(128)}, bf16[4,4,32,512]{3,2,1,0:T(8,128)(2,1)}, bf16[4,4,32,512]{3,2,1,0:T(8,128)(2,1)}, /*index=5*/bf16[512,512]{1,0:T(8,128)(2,1)}) custom-call(s32[1]{0:T(128)} %bitcast.me_ref, s32[96]{0:T(128)} %slot_hbm.1, s32[96]{0:T(128)} %col_hbm.1, s32[96]{0:T(128)} %id_hbm.1, ...), custom_call_target="tpu_custom_call" | custom-call | bytes 1 | tf_op jit(solution)/shard_map/pallas_call | solution.py:24
  10.5 2.1 %collective-permute-start.1 = (bf16[4,4,32,512]{3,2,1,0:T(8,128)(2,1)}, bf16[4,4,32,512]{3,2,1,0:T(8,128)(2,1)S(1)}, u32[]{:S(2)}, u32[]{:S(2)}) collective-permute-start(bf16[4,4,32,512]{3,2,1,0:T(8,128)(2,1)} %get-tuple-element.106), channel_id=1, source_target_pairs={{0,4},{4,0},{8,12},{12,8},{16,20},{20,16},{24,28},{28,24},{1,5},{5... | collective-permute-start | bytes 1572872 | tf_op jit(solution)/shard_map/ppermute | solution.py:440
  15.9 3.3 %shard_map.98 = (bf16[4,4,32,512]{3,2,1,0:T(8,128)(2,1)S(1)}, bf16[4,4,16,512]{3,2,1,0:T(8,128)(2,1)S(1)}, bf16[4,4,16,512]{3,2,1,0:T(8,128)(2,1)S(1)}, bf16[4,4,32,512]{3,2,1,0:T(8,128)(2,1)S(1)}, f32[8,128]{1,0:T(8,128)}) custom-call(s32[256]{0:T(256)S(1)} %copy-done.8, bf16[48,128,128]{2,1,0:T(8,128)(2,1)S(1)} %copy-done.4, bf16[512,512]{1,0:T(8,128)(2,1)S(1)} %copy-done.5), custom_call_target="tpu_custom_call" | custom-call | bytes 1 | tf_op jit(solution)/shard_map/pallas_call | solution.py:24
  19.8 2.2 %shard_map.96 = (bf16[4,4,32,512]{3,2,1,0:T(8,128)(2,1)S(1)}, bf16[4,4,32,512]{3,2,1,0:T(8,128)(2,1)S(1)}, bf16[4,4,16,512]{3,2,1,0:T(8,128)(2,1)S(1)}, bf16[4,4,16,512]{3,2,1,0:T(8,128)(2,1)S(1)}, f32[8,128]{1,0:T(8,128)S(1)}) custom-call(s32[256]{0:T(256)S(1)} %copy-done.8, bf16[48,128,128]{2,1,0:T(8,128)(2,1)S(1)} %copy-done.4, bf16[512,512]{1,0:T(8,128)(2,1)S(1)} %copy-done.5), custom_call_target="tpu_custom_call" | custom-call | bytes 1 | tf_op jit(solution)/shard_map/pallas_call | solution.py:24
  22.0 3.6 %collective-permute-done.1.got_ref = bf16[4,4,32,512]{3,2,1,0:T(8,128)(2,1)S(1)} collective-permute-done((bf16[4,4,32,512]{3,2,1,0:T(8,128)(2,1)}, bf16[4,4,32,512]{3,2,1,0:T(8,128)(2,1)S(1)}, u32[]{:S(2)}, u32[]{:S(2)}) %collective-permute-start.1) | collective-permute-done | bytes 524320 | tf_op jit(solution)/shard_map/ppermute | solution.py:440
  25.9 2.2 %collective-permute-start.3 = (bf16[2,4,32,512]{3,2,1,0:T(8,128)(2,1)S(1)}, bf16[2,4,32,512]{3,2,1,0:T(8,128)(2,1)S(1)}, u32[]{:S(2)}, u32[]{:S(2)}) collective-permute-start(bf16[2,4,32,512]{3,2,1,0:T(8,128)(2,1)S(1)} %get-tuple-element.112), channel_id=1, source_target_pairs={{0,8},{4,12},{8,0},{12,4},{16,24},{20,28},{24,16},{28,20},{1,9},{5... | collective-permute-start | bytes 786440 | tf_op jit(solution)/shard_map/ppermute | solution.py:440
  28.4 2.7 %collective-permute-start.5 = (bf16[2,4,32,512]{3,2,1,0:T(8,128)(2,1)S(1)}, bf16[2,4,32,512]{3,2,1,0:T(8,128)(2,1)S(1)}, u32[]{:S(2)}, u32[]{:S(2)}) collective-permute-start(bf16[2,4,32,512]{3,2,1,0:T(8,128)(2,1)S(1)} %get-tuple-element.118), channel_id=1, source_target_pairs={{0,16},{4,20},{8,24},{12,28},{16,0},{20,4},{24,8},{28,12},{1,17},{... | collective-permute-start | bytes 786440 | tf_op jit(solution)/shard_map/ppermute | solution.py:440
  31.0 5.1 %collective-permute-done.3.got_ref = bf16[2,4,32,512]{3,2,1,0:T(8,128)(2,1)S(1)} collective-permute-done((bf16[2,4,32,512]{3,2,1,0:T(8,128)(2,1)S(1)}, bf16[2,4,32,512]{3,2,1,0:T(8,128)(2,1)S(1)}, u32[]{:S(2)}, u32[]{:S(2)}) %collective-permute-start.3) | collective-permute-done | bytes 262176 | tf_op jit(solution)/shard_map/ppermute | solution.py:440
  38.5 3.1 %collective-permute-start.7 = (bf16[1,4,32,512]{3,2,1,0:T(8,128)(2,1)S(1)}, bf16[1,4,32,512]{3,2,1,0:T(8,128)(2,1)S(1)}, u32[]{:S(2)}, u32[]{:S(2)}) collective-permute-start(bf16[1,4,32,512]{3,2,1,0:T(8,128)(2,1)S(1)} %get-tuple-element.124), channel_id=1, source_target_pairs={{0,16},{4,20},{8,24},{12,28},{16,0},{20,4},{24,8},{28,12},{1,17},{... | collective-permute-start | bytes 393224 | tf_op jit(solution)/shard_map/ppermute | solution.py:440
  43.9 3.6 %collective-permute-start.10 = (bf16[1,4,32,512]{3,2,1,0:T(8,128)(2,1)S(1)}, bf16[1,4,32,512]{3,2,1,0:T(8,128)(2,1)S(1)}, u32[]{:S(2)}, u32[]{:S(2)}) collective-permute-start(bf16[1,4,32,512]{3,2,1,0:T(8,128)(2,1)S(1)} %get-tuple-element.133), channel_id=1, source_target_pairs={{0,16},{4,20},{8,24},{12,28},{16,0},{20,4},{24,8},{28,12},{1,17},{... | collective-permute-start | bytes 393224 | tf_op jit(solution)/shard_map/ppermute | solution.py:440
  52.8 2.4 %collective-permute-done.11.got_ref = bf16[1,4,32,512]{3,2,1,0:T(8,128)(2,1)S(1)} collective-permute-done((bf16[1,4,32,512]{3,2,1,0:T(8,128)(2,1)S(1)}, bf16[1,4,32,512]{3,2,1,0:T(8,128)(2,1)S(1)}, u32[]{:S(2)}, u32[]{:S(2)}) %collective-permute-start.11) | collective-permute-done | bytes 131104 | tf_op jit(solution)/shard_map/ppermute | solution.py:440
  57.5 2.1 %collective-permute-start.17 = (bf16[1,4,16,512]{3,2,1,0:T(8,128)(2,1)S(1)}, bf16[1,4,16,512]{3,2,1,0:T(8,128)(2,1)S(1)}, u32[]{:S(2)}, u32[]{:S(2)}) collective-permute-start(bf16[1,4,16,512]{3,2,1,0:T(8,128)(2,1)S(1)} %get-tuple-element.150), channel_id=1, source_target_pairs={{0,16},{4,20},{8,24},{12,28},{16,0},{20,4},{24,8},{28,12},{1,17},{... | collective-permute-start | bytes 196616 | tf_op jit(solution)/shard_map/ppermute | solution.py:440
  67.4 6.1 %collective-permute-done.19.got_ref = bf16[1,4,16,512]{3,2,1,0:T(8,128)(2,1)S(1)} collective-permute-done((bf16[1,4,16,512]{3,2,1,0:T(8,128)(2,1)S(1)}, bf16[1,4,16,512]{3,2,1,0:T(8,128)(2,1)S(1)}, u32[]{:S(2)}, u32[]{:S(2)}) %collective-permute-start.19) | collective-permute-done | bytes 65568 | tf_op jit(solution)/shard_map/ppermute | solution.py:440
  73.8 2.3 %collective-permute-start.26 = (bf16[2,4,32,512]{3,2,1,0:T(8,128)(2,1)S(1)}, bf16[2,4,32,512]{3,2,1,0:T(8,128)(2,1)S(1)}, u32[]{:S(2)}, u32[]{:S(2)}) collective-permute-start(bf16[2,4,32,512]{3,2,1,0:T(8,128)(2,1)S(1)} %get-tuple-element.171.held_ref.refs_0_), channel_id=1, source_target_pairs={{0,8},{4,12},{8,0},{12,4},{16,24},{20,28},{24,16},{28,20},{1,9},{5... | collective-permute-start | bytes 786440 | tf_op jit(solution)/shard_map/ppermute | solution.py:440
  77.6 4.9 %collective-permute-done.24.got_ref = bf16[1,4,32,512]{3,2,1,0:T(8,128)(2,1)S(1)} collective-permute-done((bf16[1,4,32,512]{3,2,1,0:T(8,128)(2,1)S(1)}, bf16[1,4,32,512]{3,2,1,0:T(8,128)(2,1)S(1)}, u32[]{:S(2)}, u32[]{:S(2)}) %collective-permute-start.24) | collective-permute-done | bytes 131104 | tf_op jit(solution)/shard_map/ppermute | solution.py:440
  82.7 2.6 %collective-permute-start.30 = (bf16[2,4,32,512]{3,2,1,0:T(8,128)(2,1)S(1)}, bf16[2,4,32,512]{3,2,1,0:T(8,128)(2,1)S(1)}, u32[]{:S(2)}, u32[]{:S(2)}) collective-permute-start(bf16[2,4,32,512]{3,2,1,0:T(8,128)(2,1)S(1)} %get-tuple-element.179.held_ref.refs_3_), channel_id=1, source_target_pairs={{0,8},{4,12},{8,0},{12,4},{16,24},{20,28},{24,16},{28,20},{1,9},{5... | collective-permute-start | bytes 786440 | tf_op jit(solution)/shard_map/ppermute | solution.py:440
  88.6 4.8 %collective-permute-done.28.got_ref = bf16[1,4,16,512]{3,2,1,0:T(8,128)(2,1)S(1)} collective-permute-done((bf16[1,4,16,512]{3,2,1,0:T(8,128)(2,1)S(1)}, bf16[1,4,16,512]{3,2,1,0:T(8,128)(2,1)S(1)}, u32[]{:S(2)}, u32[]{:S(2)}) %collective-permute-start.28) | collective-permute-done | bytes 65568 | tf_op jit(solution)/shard_map/ppermute | solution.py:440
  93.4 3.2 %collective-permute-start.33 = (bf16[2,4,32,512]{3,2,1,0:T(8,128)(2,1)S(1)}, bf16[2,4,32,512]{3,2,1,0:T(8,128)(2,1)S(1)}, u32[]{:S(2)}, u32[]{:S(2)}) collective-permute-start(bf16[2,4,32,512]{3,2,1,0:T(8,128)(2,1)S(1)} %get-tuple-element.184.held_ref.refs_9_), channel_id=1, source_target_pairs={{0,8},{4,12},{8,0},{12,4},{16,24},{20,28},{24,16},{28,20},{1,9},{5... | collective-permute-start | bytes 786440 | tf_op jit(solution)/shard_map/ppermute | solution.py:440
  99.9 1.9 %collective-permute-start.36 = (bf16[2,4,16,512]{3,2,1,0:T(8,128)(2,1)S(1)}, bf16[2,4,16,512]{3,2,1,0:T(8,128)(2,1)S(1)}, u32[]{:S(2)}, u32[]{:S(2)}) collective-permute-start(bf16[2,4,16,512]{3,2,1,0:T(8,128)(2,1)S(1)} %get-tuple-element.189.held_ref.refs_6_), channel_id=1, source_target_pairs={{0,8},{4,12},{8,0},{12,4},{16,24},{20,28},{24,16},{28,20},{1,9},{5... | collective-permute-start | bytes 393224 | tf_op jit(solution)/shard_map/ppermute | solution.py:440
  105.2 2.4 %collective-permute-start.37 = (bf16[2,4,16,512]{3,2,1,0:T(8,128)(2,1)S(1)}, bf16[2,4,16,512]{3,2,1,0:T(8,128)(2,1)S(1)}, u32[]{:S(2)}, u32[]{:S(2)}) collective-permute-start(bf16[2,4,16,512]{3,2,1,0:T(8,128)(2,1)S(1)} %get-tuple-element.191.held_ref.refs_0_), channel_id=1, source_target_pairs={{0,8},{4,12},{8,0},{12,4},{16,24},{20,28},{24,16},{28,20},{1,9},{5... | collective-permute-start | bytes 393224 | tf_op jit(solution)/shard_map/ppermute | solution.py:440
  112.9 4.5 %collective-permute-done.38.value_ref.refs_8_ = bf16[8,16,512]{2,1,0:T(8,128)(2,1)S(1)} collective-permute-done((bf16[8,16,512]{2,1,0:T(8,128)(2,1)S(1)}, bf16[8,16,512]{2,1,0:T(8,128)(2,1)S(1)}, u32[]{:S(2)}, u32[]{:S(2)}) %collective-permute-start.38) | collective-permute-done | bytes 131104 | tf_op jit(solution)/shard_map/ppermute | solution.py:440
  117.4 2.5 %shard_map.137 = (bf16[4,128,512]{2,1,0:T(8,128)(2,1)}, bf16[16,128,512]{2,1,0:T(8,128)(2,1)}, f32[8,128]{1,0:T(8,128)S(1)}) custom-call(f32[8,128]{1,0:T(8,128)S(1)} %shard_map.136.token_ref, s32[1]{0:T(128)} %bitcast.me_ref, s32[16]{0:T(128)S(1)} %copy-done.7, s32[16]{0:T(128)S(1)} %copy-done.9, ...), custom_call_target="tpu_custom_call" | custom-call | bytes 1 | tf_op jit(solution)/shard_map/pallas_call | solution.py:24
  119.9 2.0 %shard_map.138 = (bf16[4,128,512]{2,1,0:T(8,128)(2,1)}, bf16[16,128,512]{2,1,0:T(8,128)(2,1)}, f32[8,128]{1,0:T(8,128)}) custom-call(f32[8,128]{1,0:T(8,128)S(1)} %get-tuple-element.196.token_ref, s32[1]{0:T(128)} %bitcast.me_ref, s32[16]{0:T(128)S(1)} %copy-done.7, s32[16]{0:T(128)S(1)} %copy-done.9, ...), custom_call_target="tpu_custom_call", output_to_operand_aliasing={{0}: (7, {}), {1}: (8, {})} | custom-call | bytes 1 | tf_op jit(solution)/shard_map/pallas_call | solution.py:24
  (127 shorter events, 43.6 us)
Async XLA Ops:
  10.5 15.1 %collective-permute-start.1 = (bf16[4,4,32,512]{3,2,1,0:T(8,128)(2,1)}, bf16[4,4,32,512]{3,2,1,0:T(8,128)(2,1)S(1)}, u32[]{:S(2)}, u32[]{:S(2)}) collective-permute-start(bf16[4,4,32,512]{3,2,1,0:T(8,128)(2,1)} %get-tuple-element.106), channel_id=1, source_target_pairs={{0,4},{4,0},{8,12},{12,8},{16,20},{20,16},{24,28},{28,24},{1,5},{5... | collective-permute-start | bytes 1572872 | tf_op jit(solution)/shard_map/ppermute | solution.py:440
  12.6 15.5 %collective-permute-start.2 = (bf16[4,4,32,512]{3,2,1,0:T(8,128)(2,1)}, bf16[4,4,32,512]{3,2,1,0:T(8,128)(2,1)S(1)}, u32[]{:S(2)}, u32[]{:S(2)}) collective-permute-start(bf16[4,4,32,512]{3,2,1,0:T(8,128)(2,1)} %get-tuple-element.109), channel_id=1, source_target_pairs={{0,8},{4,12},{8,0},{12,4},{16,24},{20,28},{24,16},{28,20},{1,9},{5... | collective-permute-start | bytes 1572872 | tf_op jit(solution)/shard_map/ppermute | solution.py:440
  19.2 17.0 %collective-permute-start.4 = (bf16[4,4,32,512]{3,2,1,0:T(8,128)(2,1)S(1)}, bf16[4,4,32,512]{3,2,1,0:T(8,128)(2,1)S(1)}, u32[]{:S(2)}, u32[]{:S(2)}) collective-permute-start(bf16[4,4,32,512]{3,2,1,0:T(8,128)(2,1)S(1)} %get-tuple-element.115), channel_id=1, source_target_pairs={{0,4},{4,0},{8,12},{12,8},{16,20},{20,16},{24,28},{28,24},{1,5},{5... | collective-permute-start | bytes 1572872 | tf_op jit(solution)/shard_map/ppermute | solution.py:440
  25.9 10.2 %collective-permute-start.3 = (bf16[2,4,32,512]{3,2,1,0:T(8,128)(2,1)S(1)}, bf16[2,4,32,512]{3,2,1,0:T(8,128)(2,1)S(1)}, u32[]{:S(2)}, u32[]{:S(2)}) collective-permute-start(bf16[2,4,32,512]{3,2,1,0:T(8,128)(2,1)S(1)} %get-tuple-element.112), channel_id=1, source_target_pairs={{0,8},{4,12},{8,0},{12,4},{16,24},{20,28},{24,16},{28,20},{1,9},{5... | collective-permute-start | bytes 786440 | tf_op jit(solution)/shard_map/ppermute | solution.py:440
  28.4 13.3 %collective-permute-start.5 = (bf16[2,4,32,512]{3,2,1,0:T(8,128)(2,1)S(1)}, bf16[2,4,32,512]{3,2,1,0:T(8,128)(2,1)S(1)}, u32[]{:S(2)}, u32[]{:S(2)}) collective-permute-start(bf16[2,4,32,512]{3,2,1,0:T(8,128)(2,1)S(1)} %get-tuple-element.118), channel_id=1, source_target_pairs={{0,16},{4,20},{8,24},{12,28},{16,0},{20,4},{24,8},{28,12},{1,17},{... | collective-permute-start | bytes 786440 | tf_op jit(solution)/shard_map/ppermute | solution.py:440
  37.0 10.5 %collective-permute-start.8 = (bf16[4,4,16,512]{3,2,1,0:T(8,128)(2,1)S(1)}, bf16[4,4,16,512]{3,2,1,0:T(8,128)(2,1)S(1)}, u32[]{:S(2)}, u32[]{:S(2)}) collective-permute-start(bf16[4,4,16,512]{3,2,1,0:T(8,128)(2,1)S(1)} %get-tuple-element.127), channel_id=1, source_target_pairs={{0,4},{4,0},{8,12},{12,8},{16,20},{20,16},{24,28},{28,24},{1,5},{5... | collective-permute-start | bytes 786440 | tf_op jit(solution)/shard_map/ppermute | solution.py:440
  38.5 9.0 %collective-permute-start.7 = (bf16[1,4,32,512]{3,2,1,0:T(8,128)(2,1)S(1)}, bf16[1,4,32,512]{3,2,1,0:T(8,128)(2,1)S(1)}, u32[]{:S(2)}, u32[]{:S(2)}) collective-permute-start(bf16[1,4,32,512]{3,2,1,0:T(8,128)(2,1)S(1)} %get-tuple-element.124), channel_id=1, source_target_pairs={{0,16},{4,20},{8,24},{12,28},{16,0},{20,4},{24,8},{28,12},{1,17},{... | collective-permute-start | bytes 393224 | tf_op jit(solution)/shard_map/ppermute | solution.py:440
  42.5 12.9 %collective-permute-start.13 = (bf16[4,4,16,512]{3,2,1,0:T(8,128)(2,1)S(1)}, bf16[4,4,16,512]{3,2,1,0:T(8,128)(2,1)S(1)}, u32[]{:S(2)}, u32[]{:S(2)}) collective-permute-start(bf16[4,4,16,512]{3,2,1,0:T(8,128)(2,1)S(1)} %get-tuple-element.141), channel_id=1, source_target_pairs={{0,4},{4,0},{8,12},{12,8},{16,20},{20,16},{24,28},{28,24},{1,5},{5... | collective-permute-start | bytes 786440 | tf_op jit(solution)/shard_map/ppermute | solution.py:440
  43.9 8.8 %collective-permute-start.10 = (bf16[1,4,32,512]{3,2,1,0:T(8,128)(2,1)S(1)}, bf16[1,4,32,512]{3,2,1,0:T(8,128)(2,1)S(1)}, u32[]{:S(2)}, u32[]{:S(2)}) collective-permute-start(bf16[1,4,32,512]{3,2,1,0:T(8,128)(2,1)S(1)} %get-tuple-element.133), channel_id=1, source_target_pairs={{0,16},{4,20},{8,24},{12,28},{16,0},{20,4},{24,8},{28,12},{1,17},{... | collective-permute-start | bytes 393224 | tf_op jit(solution)/shard_map/ppermute | solution.py:440
  61.7 11.8 %collective-permute-start.20 = (bf16[1,4,32,512]{3,2,1,0:T(8,128)(2,1)S(1)}, bf16[1,4,32,512]{3,2,1,0:T(8,128)(2,1)S(1)}, u32[]{:S(2)}, u32[]{:S(2)}) collective-permute-start(bf16[1,4,32,512]{3,2,1,0:T(8,128)(2,1)S(1)} %get-tuple-element.158.held_ref), channel_id=1, source_target_pairs={{0,16},{4,20},{8,24},{12,28},{16,0},{20,4},{24,8},{28,12},{1,17},{... | collective-permute-start | bytes 393224 | tf_op jit(solution)/shard_map/ppermute | solution.py:440
  62.6 11.0 %collective-permute-start.22 = (bf16[1,4,32,512]{3,2,1,0:T(8,128)(2,1)S(1)}, bf16[1,4,32,512]{3,2,1,0:T(8,128)(2,1)S(1)}, u32[]{:S(2)}, u32[]{:S(2)}) collective-permute-start(bf16[1,4,32,512]{3,2,1,0:T(8,128)(2,1)S(1)} %bitcast.9), channel_id=1, source_target_pairs={{0,2},{1,3},{2,0},{3,1},{4,6},{5,7},{6,4},{7,5},{8,10},{9,11},{10,... | collective-permute-start | bytes 393224 | tf_op jit(solution)/shard_map/ppermute | solution.py:440
  64.4 9.0 %collective-permute-start.19 = (bf16[1,4,16,512]{3,2,1,0:T(8,128)(2,1)S(1)}, bf16[1,4,16,512]{3,2,1,0:T(8,128)(2,1)S(1)}, u32[]{:S(2)}, u32[]{:S(2)}) collective-permute-start(bf16[1,4,16,512]{3,2,1,0:T(8,128)(2,1)S(1)} %get-tuple-element.156), channel_id=1, source_target_pairs={{0,16},{4,20},{8,24},{12,28},{16,0},{20,4},{24,8},{28,12},{1,17},{... | collective-permute-start | bytes 196616 | tf_op jit(solution)/shard_map/ppermute | solution.py:440
  66.0 7.6 %collective-permute-start.21 = (bf16[1,4,16,512]{3,2,1,0:T(8,128)(2,1)S(1)}, bf16[1,4,16,512]{3,2,1,0:T(8,128)(2,1)S(1)}, u32[]{:S(2)}, u32[]{:S(2)}) collective-permute-start(bf16[1,4,16,512]{3,2,1,0:T(8,128)(2,1)S(1)} %bitcast.17), channel_id=1, source_target_pairs={{0,2},{1,3},{2,0},{3,1},{4,6},{5,7},{6,4},{7,5},{8,10},{9,11},{10,... | collective-permute-start | bytes 196616 | tf_op jit(solution)/shard_map/ppermute | solution.py:440
  73.7 8.8 %collective-permute-start.24 = (bf16[1,4,32,512]{3,2,1,0:T(8,128)(2,1)S(1)}, bf16[1,4,32,512]{3,2,1,0:T(8,128)(2,1)S(1)}, u32[]{:S(2)}, u32[]{:S(2)}) collective-permute-start(bf16[1,4,32,512]{3,2,1,0:T(8,128)(2,1)S(1)} %get-tuple-element.166.held_ref), channel_id=1, source_target_pairs={{0,16},{4,20},{8,24},{12,28},{16,0},{20,4},{24,8},{28,12},{1,17},{... | collective-permute-start | bytes 393224 | tf_op jit(solution)/shard_map/ppermute | solution.py:440
  73.8 11.8 %collective-permute-start.26 = (bf16[2,4,32,512]{3,2,1,0:T(8,128)(2,1)S(1)}, bf16[2,4,32,512]{3,2,1,0:T(8,128)(2,1)S(1)}, u32[]{:S(2)}, u32[]{:S(2)}) collective-permute-start(bf16[2,4,32,512]{3,2,1,0:T(8,128)(2,1)S(1)} %get-tuple-element.171.held_ref.refs_0_), channel_id=1, source_target_pairs={{0,8},{4,12},{8,0},{12,4},{16,24},{20,28},{24,16},{28,20},{1,9},{5... | collective-permute-start | bytes 786440 | tf_op jit(solution)/shard_map/ppermute | solution.py:440
  82.6 10.8 %collective-permute-start.29 = (bf16[1,4,32,512]{3,2,1,0:T(8,128)(2,1)S(1)}, bf16[1,4,32,512]{3,2,1,0:T(8,128)(2,1)S(1)}, u32[]{:S(2)}, u32[]{:S(2)}) collective-permute-start(bf16[1,4,32,512]{3,2,1,0:T(8,128)(2,1)S(1)} %get-tuple-element.177.held_ref), channel_id=1, source_target_pairs={{0,16},{4,20},{8,24},{12,28},{16,0},{20,4},{24,8},{28,12},{1,17},{... | collective-permute-start | bytes 393224 | tf_op jit(solution)/shard_map/ppermute | solution.py:440
  82.7 13.9 %collective-permute-start.30 = (bf16[2,4,32,512]{3,2,1,0:T(8,128)(2,1)S(1)}, bf16[2,4,32,512]{3,2,1,0:T(8,128)(2,1)S(1)}, u32[]{:S(2)}, u32[]{:S(2)}) collective-permute-start(bf16[2,4,32,512]{3,2,1,0:T(8,128)(2,1)S(1)} %get-tuple-element.179.held_ref.refs_3_), channel_id=1, source_target_pairs={{0,8},{4,12},{8,0},{12,4},{16,24},{20,28},{24,16},{28,20},{1,9},{5... | collective-permute-start | bytes 786440 | tf_op jit(solution)/shard_map/ppermute | solution.py:440
  86.9 11.8 %collective-permute-start.31 = (bf16[8,32,512]{2,1,0:T(8,128)(2,1)S(1)}, bf16[8,32,512]{2,1,0:T(8,128)(2,1)S(1)}, u32[]{:S(2)}, u32[]{:S(2)}) collective-permute-start(bf16[8,32,512]{2,1,0:T(8,128)(2,1)S(1)} %get-tuple-element.181), channel_id=1, source_target_pairs={{0,4},{4,0},{8,12},{12,8},{16,20},{20,16},{24,28},{28,24},{1,5},{5... | collective-permute-start | bytes 786440 | tf_op jit(solution)/shard_map/ppermute | solution.py:440
  93.4 10.1 %collective-permute-start.33 = (bf16[2,4,32,512]{3,2,1,0:T(8,128)(2,1)S(1)}, bf16[2,4,32,512]{3,2,1,0:T(8,128)(2,1)S(1)}, u32[]{:S(2)}, u32[]{:S(2)}) collective-permute-start(bf16[2,4,32,512]{3,2,1,0:T(8,128)(2,1)S(1)} %get-tuple-element.184.held_ref.refs_9_), channel_id=1, source_target_pairs={{0,8},{4,12},{8,0},{12,4},{16,24},{20,28},{24,16},{28,20},{1,9},{5... | collective-permute-start | bytes 786440 | tf_op jit(solution)/shard_map/ppermute | solution.py:440
  97.2 12.1 %collective-permute-start.35 = (bf16[8,32,512]{2,1,0:T(8,128)(2,1)S(1)}, bf16[8,32,512]{2,1,0:T(8,128)(2,1)S(1)}, u32[]{:S(2)}, u32[]{:S(2)}) collective-permute-start(bf16[8,32,512]{2,1,0:T(8,128)(2,1)S(1)} %get-tuple-element.188), channel_id=1, source_target_pairs={{0,4},{4,0},{8,12},{12,8},{16,20},{20,16},{24,28},{28,24},{1,5},{5... | collective-permute-start | bytes 786440 | tf_op jit(solution)/shard_map/ppermute | solution.py:440
  99.9 9.4 %collective-permute-start.36 = (bf16[2,4,16,512]{3,2,1,0:T(8,128)(2,1)S(1)}, bf16[2,4,16,512]{3,2,1,0:T(8,128)(2,1)S(1)}, u32[]{:S(2)}, u32[]{:S(2)}) collective-permute-start(bf16[2,4,16,512]{3,2,1,0:T(8,128)(2,1)S(1)} %get-tuple-element.189.held_ref.refs_6_), channel_id=1, source_target_pairs={{0,8},{4,12},{8,0},{12,4},{16,24},{20,28},{24,16},{28,20},{1,9},{5... | collective-permute-start | bytes 393224 | tf_op jit(solution)/shard_map/ppermute | solution.py:440
  107.6 9.8 %collective-permute-start.39 = (bf16[8,32,512]{2,1,0:T(8,128)(2,1)S(1)}, bf16[8,32,512]{2,1,0:T(8,128)(2,1)S(1)}, u32[]{:S(2)}, u32[]{:S(2)}) collective-permute-start(bf16[8,32,512]{2,1,0:T(8,128)(2,1)S(1)} %get-tuple-element.194), channel_id=1, source_target_pairs={{0,4},{4,0},{8,12},{12,8},{16,20},{20,16},{24,28},{28,24},{1,5},{5... | collective-permute-start | bytes 786440 | tf_op jit(solution)/shard_map/ppermute | solution.py:440
  109.8 7.6 %collective-permute-start.38 = (bf16[8,16,512]{2,1,0:T(8,128)(2,1)S(1)}, bf16[8,16,512]{2,1,0:T(8,128)(2,1)S(1)}, u32[]{:S(2)}, u32[]{:S(2)}) collective-permute-start(bf16[8,16,512]{2,1,0:T(8,128)(2,1)S(1)} %get-tuple-element.193), channel_id=1, source_target_pairs={{0,4},{4,0},{8,12},{12,8},{16,20},{20,16},{24,28},{28,24},{1,5},{5... | collective-permute-start | bytes 393224 | tf_op jit(solution)/shard_map/ppermute | solution.py:440
  111.1 8.9 %collective-permute-start.40 = (bf16[8,16,512]{2,1,0:T(8,128)(2,1)S(1)}, bf16[8,16,512]{2,1,0:T(8,128)(2,1)S(1)}, u32[]{:S(2)}, u32[]{:S(2)}) collective-permute-start(bf16[8,16,512]{2,1,0:T(8,128)(2,1)S(1)} %get-tuple-element.197), channel_id=1, source_target_pairs={{0,4},{4,0},{8,12},{12,8},{16,20},{20,16},{24,28},{28,24},{1,5},{5... | collective-permute-start | bytes 393224 | tf_op jit(solution)/shard_map/ppermute | solution.py:440
  (28 other events, 187.1 us)

commit v8 on v7

--- a/solution.py
+++ b/solution.py
@@ -5,10 +5,10 @@
 from jax.experimental.pallas import tpu as pltpu
 from jax.sharding import PartitionSpec as P
 
-SHARES = (2, 2, 2, 1, 1)
+SHARES = (2, 2, 1, 2, 1)
 ORDER = (
-    1, 0, 1, 2, 0, 2, 1, 3, 0, 2, 0, 3, 4, 1, 0, 1, 3, 4, 4, 0, 3, 2, 2, 1, 4, 0, 4, 4, 2, 1, 0, 3,
-    2, 3, 1, 4, 3, 4, 2, 3,
+    1, 0, 3, 1, 4, 0, 1, 2, 3, 0, 2, 3, 1, 2, 4, 0, 0, 4, 2, 1, 4, 0, 3, 3, 1, 4, 2, 0, 3, 1, 4, 0,
+    3, 4, 2, 4, 1, 2, 3, 2,
 )
 READ_CAP = 2
 VMEM_BYTES = 12 * 1024 * 1024
@@ -113,7 +113,7 @@
                 top = top + blocks * rows
 
 
-def first_part(me, slot, col, tile_id, touched, tiles, features, readers, neighbour, orders, first, count, spans):
+def first_part(me, slot, col, tile_id, touched, tiles, features, readers, orders, first, count, spans):
     block = tiles.shape[1]
     blocks = features.shape[0] // block
     width = features.shape[1]
@@ -126,15 +126,20 @@
     square = blocks * blocks
 
     listed = readers.shape[0]
-
-    def body(me_ref, slot_hbm, col_hbm, id_hbm, touched_ref, tiles_hbm, x_hbm, readers_ref, neighbour_ref, *refs):
-        table, choice, entry, *outs = refs[: 3 + len(spans)]
-        x_out, *scratch = refs[3 + len(spans) :]
-        slot_ref, col_ref, id_ref, tiles_ref, lhs, bases, seen, sems = scratch
+    extra = -(-half * READ_CAP // 16) * 16
+    shapes = [(count, blocks, rows, width) for _, rows in spans]
+    shapes[1] = (count * blocks * spans[1][1] + extra, width)
+
+    def body(me_ref, slot_hbm, col_hbm, id_hbm, touched_hbm, readers_hbm, tiles_hbm, x_hbm, *refs):
+        table, entry, *outs = refs[: 2 + len(spans)]
+        x_out, *scratch = refs[2 + len(spans) :]
+        slot_ref, col_ref, id_ref, touched_ref, readers_ref, choice, tiles_ref, lhs, bases, seen, sems = scratch
         loads = [
             pltpu.make_async_copy(slot_hbm, slot_ref, sems.at[0]),
             pltpu.make_async_copy(col_hbm, col_ref, sems.at[1]),
             pltpu.make_async_copy(id_hbm, id_ref, sems.at[2]),
+            pltpu.make_async_copy(touched_hbm.at[me_ref[0]], touched_ref, sems.at[5]),
+            pltpu.make_async_copy(readers_hbm, readers_ref, sems.at[6]),
             pltpu.make_async_copy(x_hbm, x_out, sems.at[3]),
             pltpu.make_async_copy(tiles_hbm.at[:, pl.ds(0, loaded)], tiles_ref, sems.at[4]),
         ]
@@ -148,34 +153,32 @@
         lax.fori_loop(0, len(orders) * edges * square, clear, 0, unroll=16)
 
         def place_slot(k, carry):
-            owner, _ = split(k, cap)
+            owner, slot_at = split(k, cap)
             for n, order in enumerate(orders):
                 place = place_of(owner ^ me_ref[0], order)
-                bases[n * edges * cap + k] = ((n * edges + place) * blocks + touched_ref[k]) * blocks
+                bases[n * edges * cap + k] = ((n * edges + place) * blocks + touched_ref[slot_at, owner]) * blocks
             return carry
 
+        for load in loads[:5]:
+            load.wait()
         lax.fori_loop(0, edges * cap, place_slot, 0, unroll=8)
-        for load in loads[:3]:
-            load.wait()
-
-        for i in range(half * READ_CAP + 1):
+
+        for i in range(extra + 1):
             choice[i] = 0
         for i in range(edges * READ_CAP):
             entry[i] = -1
-        for i in range(2 * edges):
+        for i in range(edges):
             seen[i] = 0
 
         def enter_lists(r, carry):
-            owner, _ = split(readers_ref[r], blocks)
+            owner, b = split(readers_ref[r], blocks)
             turn = seen[owner]
             seen[owner] = turn + 1
-            entry[owner * READ_CAP + jnp.minimum(turn, READ_CAP - 1)] = r
-            owner, b = split(neighbour_ref[r], blocks)
-            turn = seen[edges + owner]
-            seen[edges + owner] = turn + 1
-            peer = owner ^ me_ref[0]
-            row = place_of(peer, column_bits) * READ_CAP + jnp.minimum(turn, READ_CAP - 1)
-            choice[jnp.where(peer & 1 == 0, row, half * READ_CAP)] = b
+            turn = jnp.minimum(turn, READ_CAP - 1)
+            entry[owner * READ_CAP + turn] = r
+            peer = owner ^ me_ref[0] ^ 1
+            row = place_of(peer, column_bits) * READ_CAP + turn
+            choice[jnp.where(peer & 1 == 0, row, extra)] = b
             return carry
 
         lax.fori_loop(0, listed, enter_lists, 0)
@@ -186,7 +189,7 @@
             return carry
 
         lax.fori_loop(0, products, enter, 0, unroll=8)
-        for load in loads[3:]:
+        for load in loads[5:]:
             load.wait()
 
         for n, (span, out) in enumerate(zip(spans, outs)):
@@ -200,29 +203,37 @@
 
             lax.fori_loop(0, count, one_owner, 0)
             total = jnp.dot(lhs[pl.ds(0, count * height)], x_out[...], preferred_element_type=jnp.float32)
-            out[...] = total.astype(jnp.bfloat16).reshape(out.shape)
+            if n == 1:
+                out[pl.ds(0, count * height)] = total.astype(jnp.bfloat16)
+                for i in range(extra):
+                    line = jnp.full((1, width), choice[i].astype(jnp.float32), jnp.float32)
+                    out[pl.ds(count * height + i, 1)] = line.astype(jnp.bfloat16)
+            else:
+                out[...] = total.astype(jnp.bfloat16).reshape(out.shape)
 
     return call(
         body,
         [
             jax.ShapeDtypeStruct((len(orders) * edges * square,), jnp.int32),
-            jax.ShapeDtypeStruct((half * READ_CAP + 1,), jnp.int32),
             jax.ShapeDtypeStruct((edges * READ_CAP,), jnp.int32),
-            *[jax.ShapeDtypeStruct((count, blocks, rows, width), jnp.bfloat16) for _, rows in spans],
+            *[jax.ShapeDtypeStruct(shape, jnp.bfloat16) for shape in shapes],
             jax.ShapeDtypeStruct(features.shape, jnp.bfloat16),
         ],
-        [SMEM, HBM, HBM, HBM, SMEM, HBM, HBM, SMEM, SMEM],
-        [SMEM] * 3 + [VMEM] * (len(spans) + 1),
-        (me, slot, col, tile_id, touched[me[0]].reshape(-1), tiles, features, readers, neighbour),
+        [SMEM] + [HBM] * 7,
+        [SMEM] * 2 + [VMEM] * (len(spans) + 1),
+        (me, slot, col, tile_id, touched.transpose(0, 2, 1), readers, tiles, features),
         [
             pltpu.SMEM((products,), jnp.int32),
             pltpu.SMEM((products,), jnp.int32),
             pltpu.SMEM((products,), jnp.int32),
+            pltpu.SMEM((cap, edges), jnp.int32),
+            pltpu.SMEM((listed,), jnp.int32),
+            pltpu.SMEM((extra + 1,), jnp.int32),
             pltpu.VMEM((tiles.shape[0], loaded, block), jnp.bfloat16),
             pltpu.VMEM((count * blocks * tallest, blocks * block), jnp.bfloat16),
             pltpu.SMEM((len(orders) * edges * cap,), jnp.int32),
-            pltpu.SMEM((2 * edges,), jnp.int32),
-            pltpu.SemaphoreType.DMA((5,)),
+            pltpu.SMEM((edges,), jnp.int32),
+            pltpu.SemaphoreType.DMA((7,)),
         ],
         limit=62 * 1024 * 1024,
     )
@@ -285,7 +296,12 @@
 
     def body(token_ref, total_ref, got_ref, at_hand_ref, *outs):
         def add(i, carry):
-            value = total_ref[i].astype(jnp.float32) + got_ref[i].astype(jnp.float32)
+            if got.ndim == total.ndim:
+                value = got_ref[i]
+            else:
+                height = shape[0] * shape[1]
+                value = got_ref[pl.ds(pl.multiple_of(i * height, height), height)].reshape(shape)
+            value = total_ref[i].astype(jnp.float32) + value.astype(jnp.float32)
             if not left:
                 outs[0][...] = value.astype(jnp.bfloat16)
             else:
@@ -364,6 +380,21 @@
         [VMEM, SMEM, VMEM, VMEM],
         [VMEM] * 2,
         (token, choice, held, got),
+    )
+
+
+def read_choice(token, got, count):
+    extra = -(-count // 16) * 16
+    first = got.shape[0] - extra
+
+    def body(token_ref, got_ref, choice, token_out):
+        lines = got_ref[pl.ds(first, extra)].astype(jnp.float32)
+        for i in range(count):
+            choice[i] = jnp.max(lines[i : i + 1]).astype(jnp.int32)
+        token_out[...] = token_ref[...]
+
+    return call(
+        body, [jax.ShapeDtypeStruct((count,), jnp.int32), TOKEN], [VMEM] * 2, [SMEM, VMEM], (token, got)
     )
 
 
@@ -441,11 +472,10 @@
 
     columns = offsets_of(edges, 2)
     me, mine = me.reshape(1), mine.reshape(1)
-    neighbour = flip(readers, 1)
     column_bits = [1 << i for i in range(1, edges.bit_length() - 1)]
     orders = [[*column_bits, 1], [1, *column_bits]]
-    table, choice, entry, *early, inputs = first_part(
-        me, tile_slot, tile_col, tile_id, touched, tiles, features, readers, neighbour, orders, half, half, spans[:2]
+    table, entry, *early, inputs = first_part(
+        me, tile_slot, tile_col, tile_id, touched, tiles, features, readers, orders, half, half, spans[:2]
     )
     later, first_kept, _ = other_parts(
         table, tiles, inputs, [(edges + half, half, spans[2:]), (0, half, spans[:1])]
@@ -469,11 +499,16 @@
             (held,) = chained(join, held, got)
             bit //= 2
 
+    choice = None
+
     def one_part(part):
+        nonlocal choice
         first, *rest = orders[min(part, 1)]
         got = flip(away[part], first)
         yield
         total, sent = chained(combine, kept[part], got, weight)
+        if part == 1:
+            (choice,) = chained(read_choice, got, half * READ_CAP)
         for bit in rest:
             got = flip(sent, bit)
             yield

time: 122 us -> 125 us (1.025)
  waiting for transfers between devices: 38.5 us -> 42.9 us
  local copies, waits for them, and re-layouts: 4.56 us -> 3.13 us
    ppermute x41 -> x40, waiting for transfers between devices: 38.5 us -> 42.9 us  [flip(): lax.ppermute(value, axis, [(d, d ^ bit) for d in range(lax.axis_size(axis...]
    pallas_call x44 -> x45, Pallas kernels: 21.5 us -> 22.7 us  [call(): pl.pallas_call(body, out_shape=out_shape, in_specs=in_specs, out_specs=ou...]
    ppermute x41 -> x40, starting transfers between devices: 56.3 us -> 55.3 us  [flip(): lax.ppermute(value, axis, [(d, d ^ bit) for d in range(lax.axis_size(axis...]
    unnamed x22 -> x12, local copies, waits for them, and re-layouts: 3.87 us -> 3.13 us
  transfers between devices with their start and end apart: 41 -> 40, of which waited for: 16 -> 19; matrix products, arithmetic and copies ran while one was open for 1% -> 0% of each run, Pallas kernels for 12% -> 13%
where the time goes in v8:
time: 125 us
  starting transfers between devices  55.3 us (44%)
  waiting for transfers between devices  42.9 us (34%)
  Pallas kernels  22.7 us (18%)
  local copies, waits for them, and re-layouts  3.13 us (3%)
    ppermute x40, starting transfers between devices, flip(): lax.ppermute(value, axis, [(d, d ^ bit) for d in range(lax.axis_size(axis...  55.3 us
    ppermute x40, waiting for transfers between devices, flip(): lax.ppermute(value, axis, [(d, d ^ bit) for d in range(lax.axis_size(axis...  42.9 us
    pallas_call x45, Pallas kernels, call(): pl.pallas_call(body, out_shape=out_shape, in_specs=in_specs, out_specs=ou...  22.7 us
    unnamed x12, local copies, waits for them, and re-layouts  3.13 us
  transfers between devices with their start and end apart: 40, of which 19 were waited for; matrix products, arithmetic and copies ran while one was open for 0% of the time, Pallas kernels for 13%

profile of v8, /device:TPU:0, one launch (start us, length us, event | category | flops | bytes accessed | tf_op | source)
XLA Modules:
  0.0 125.1 jit_solution(9034059881437409036)
XLA Ops:
  0.6 4.4 %shard_map.95 = (s32[256]{0:T(256)}, s32[16]{0:T(128)}, bf16[4,4,32,512]{3,2,1,0:T(8,128)(2,1)}, bf16[528,512]{1,0:T(8,128)(2,1)}, bf16[512,512]{1,0:T(8,128)(2,1)}) custom-call(s32[1]{0:T(128)} %bitcast.me_ref, s32[96]{0:T(128)} %slot_hbm.1, s32[96]{0:T(128)} %col_hbm.1, s32[96]{0:T(128)} %id_hbm.1, s32[8,4,8]{2,1,0:T(4,128)} %bitcast.22, s32[16]{0:T(128)} %readers_ref.3, ...), custom_call_target="tpu_custom_call" | custom-call | bytes 1 | tf_op jit(solution)/shard_map/pallas_call | solution.py:24
  5.1 3.0 %collective-permute-start = (bf16[528,512]{1,0:T(8,128)(2,1)}, bf16[528,512]{1,0:T(8,128)(2,1)S(1)}, u32[]{:S(2)}, u32[]{:S(2)}) collective-permute-start(bf16[528,512]{1,0:T(8,128)(2,1)} %get-tuple-element.107), channel_id=1, source_target_pairs={{0,4},{4,0},{8,12},{12,8},{16,20},{20,16},{24,28},{28,24},{1,5},{5... | collective-permute-start | bytes 1622024 | tf_op jit(solution)/shard_map/ppermute | solution.py:471
  12.8 3.4 %shard_map.99 = (bf16[4,4,16,512]{3,2,1,0:T(8,128)(2,1)S(1)}, bf16[4,4,32,512]{3,2,1,0:T(8,128)(2,1)S(1)}, bf16[4,4,16,512]{3,2,1,0:T(8,128)(2,1)S(1)}, bf16[4,4,32,512]{3,2,1,0:T(8,128)(2,1)S(1)}, f32[8,128]{1,0:T(8,128)}) custom-call(s32[256]{0:T(256)S(1)} %copy-done.4, bf16[48,128,128]{2,1,0:T(8,128)(2,1)S(1)} %copy-done.1, bf16[512,512]{1,0:T(8,128)(2,1)S(1)} %copy-done.2), custom_call_target="tpu_custom_call" | custom-call | bytes 1 | tf_op jit(solution)/shard_map/pallas_call | solution.py:24
  16.7 2.2 %shard_map.96 = (bf16[4,4,32,512]{3,2,1,0:T(8,128)(2,1)S(1)}, bf16[4,4,16,512]{3,2,1,0:T(8,128)(2,1)S(1)}, bf16[4,4,32,512]{3,2,1,0:T(8,128)(2,1)S(1)}, bf16[4,4,16,512]{3,2,1,0:T(8,128)(2,1)S(1)}, f32[8,128]{1,0:T(8,128)S(1)}) custom-call(s32[256]{0:T(256)S(1)} %copy-done.4, bf16[48,128,128]{2,1,0:T(8,128)(2,1)S(1)} %copy-done.1, bf16[512,512]{1,0:T(8,128)(2,1)S(1)} %copy-done.2), custom_call_target="tpu_custom_call" | custom-call | bytes 1 | tf_op jit(solution)/shard_map/pallas_call | solution.py:24
  19.0 2.4 %collective-permute-done.got_ref = bf16[528,512]{1,0:T(8,128)(2,1)S(1)} collective-permute-done((bf16[528,512]{1,0:T(8,128)(2,1)}, bf16[528,512]{1,0:T(8,128)(2,1)S(1)}, u32[]{:S(2)}, u32[]{:S(2)}) %collective-permute-start) | collective-permute-done | bytes 540704 | tf_op jit(solution)/shard_map/ppermute | solution.py:471
  26.4 2.7 %collective-permute-start.5 = (bf16[2,4,32,512]{3,2,1,0:T(8,128)(2,1)S(1)}, bf16[2,4,32,512]{3,2,1,0:T(8,128)(2,1)S(1)}, u32[]{:S(2)}, u32[]{:S(2)}) collective-permute-start(bf16[2,4,32,512]{3,2,1,0:T(8,128)(2,1)S(1)} %get-tuple-element.123), channel_id=1, source_target_pairs={{0,16},{4,20},{8,24},{12,28},{16,0},{20,4},{24,8},{28,12},{1,17},{... | collective-permute-start | bytes 786440 | tf_op jit(solution)/shard_map/ppermute | solution.py:471
  29.6 3.1 %collective-permute-done.2.got_ref = bf16[4,4,32,512]{3,2,1,0:T(8,128)(2,1)S(1)} collective-permute-done((bf16[4,4,32,512]{3,2,1,0:T(8,128)(2,1)S(1)}, bf16[4,4,32,512]{3,2,1,0:T(8,128)(2,1)S(1)}, u32[]{:S(2)}, u32[]{:S(2)}) %collective-permute-start.2) | collective-permute-done | bytes 524320 | tf_op jit(solution)/shard_map/ppermute | solution.py:471
  32.9 2.2 %collective-permute-start.8 = (bf16[2,4,32,512]{3,2,1,0:T(8,128)(2,1)S(1)}, bf16[2,4,32,512]{3,2,1,0:T(8,128)(2,1)S(1)}, u32[]{:S(2)}, u32[]{:S(2)}) collective-permute-start(bf16[2,4,32,512]{3,2,1,0:T(8,128)(2,1)S(1)} %get-tuple-element.132), channel_id=1, source_target_pairs={{0,8},{4,12},{8,0},{12,4},{16,24},{20,28},{24,16},{28,20},{1,9},{5... | collective-permute-start | bytes 786440 | tf_op jit(solution)/shard_map/ppermute | solution.py:471
  35.2 2.7 %collective-permute-start.6 = (bf16[1,4,32,512]{3,2,1,0:T(8,128)(2,1)S(1)}, bf16[1,4,32,512]{3,2,1,0:T(8,128)(2,1)S(1)}, u32[]{:S(2)}, u32[]{:S(2)}) collective-permute-start(bf16[1,4,32,512]{3,2,1,0:T(8,128)(2,1)S(1)} %get-tuple-element.126), channel_id=1, source_target_pairs={{0,16},{4,20},{8,24},{12,28},{16,0},{20,4},{24,8},{28,12},{1,17},{... | collective-permute-start | bytes 393224 | tf_op jit(solution)/shard_map/ppermute | solution.py:471
  38.4 2.9 %collective-permute-done.5.got_ref = bf16[2,4,32,512]{3,2,1,0:T(8,128)(2,1)S(1)} collective-permute-done((bf16[2,4,32,512]{3,2,1,0:T(8,128)(2,1)S(1)}, bf16[2,4,32,512]{3,2,1,0:T(8,128)(2,1)S(1)}, u32[]{:S(2)}, u32[]{:S(2)}) %collective-permute-start.5) | collective-permute-done | bytes 262176 | tf_op jit(solution)/shard_map/ppermute | solution.py:471
  46.3 2.7 %collective-permute-start.11 = (bf16[1,4,32,512]{3,2,1,0:T(8,128)(2,1)S(1)}, bf16[1,4,32,512]{3,2,1,0:T(8,128)(2,1)S(1)}, u32[]{:S(2)}, u32[]{:S(2)}) collective-permute-start(bf16[1,4,32,512]{3,2,1,0:T(8,128)(2,1)S(1)} %get-tuple-element.141), channel_id=1, source_target_pairs={{0,16},{4,20},{8,24},{12,28},{16,0},{20,4},{24,8},{28,12},{1,17},{... | collective-permute-start | bytes 393224 | tf_op jit(solution)/shard_map/ppermute | solution.py:471
  55.1 3.3 %collective-permute-done.13.got_ref = bf16[1,4,16,512]{3,2,1,0:T(8,128)(2,1)S(1)} collective-permute-done((bf16[1,4,16,512]{3,2,1,0:T(8,128)(2,1)S(1)}, bf16[1,4,16,512]{3,2,1,0:T(8,128)(2,1)S(1)}, u32[]{:S(2)}, u32[]{:S(2)}) %collective-permute-start.13) | collective-permute-done | bytes 65568 | tf_op jit(solution)/shard_map/ppermute | solution.py:471
  65.2 4.0 %collective-permute-done.17.got_ref = bf16[1,4,16,512]{3,2,1,0:T(8,128)(2,1)S(1)} collective-permute-done((bf16[1,4,16,512]{3,2,1,0:T(8,128)(2,1)}, bf16[1,4,16,512]{3,2,1,0:T(8,128)(2,1)S(1)}, u32[]{:S(2)}, u32[]{:S(2)}) %collective-permute-start.17) | collective-permute-done | bytes 65568 | tf_op jit(solution)/shard_map/ppermute | solution.py:471
  70.0 3.6 %collective-permute-done.20.got_ref = bf16[1,4,16,512]{3,2,1,0:T(8,128)(2,1)S(1)} collective-permute-done((bf16[1,4,16,512]{3,2,1,0:T(8,128)(2,1)S(1)}, bf16[1,4,16,512]{3,2,1,0:T(8,128)(2,1)S(1)}, u32[]{:S(2)}, u32[]{:S(2)}) %collective-permute-start.20) | collective-permute-done | bytes 65568 | tf_op jit(solution)/shard_map/ppermute | solution.py:471
  73.9 2.4 %collective-permute-start.27 = (bf16[2,4,32,512]{3,2,1,0:T(8,128)(2,1)S(1)}, bf16[2,4,32,512]{3,2,1,0:T(8,128)(2,1)S(1)}, u32[]{:S(2)}, u32[]{:S(2)}) collective-permute-start(bf16[2,4,32,512]{3,2,1,0:T(8,128)(2,1)S(1)} %get-tuple-element.177.held_ref.refs_0_), channel_id=1, source_target_pairs={{0,8},{4,12},{8,0},{12,4},{16,24},{20,28},{24,16},{28,20},{1,9},{5... | collective-permute-start | bytes 786440 | tf_op jit(solution)/shard_map/ppermute | solution.py:471
  77.2 5.5 %collective-permute-done.24.got_ref = bf16[1,4,32,512]{3,2,1,0:T(8,128)(2,1)S(1)} collective-permute-done((bf16[1,4,32,512]{3,2,1,0:T(8,128)(2,1)S(1)}, bf16[1,4,32,512]{3,2,1,0:T(8,128)(2,1)S(1)}, u32[]{:S(2)}, u32[]{:S(2)}) %collective-permute-start.24) | collective-permute-done | bytes 131104 | tf_op jit(solution)/shard_map/ppermute | solution.py:471
  82.9 2.5 %collective-permute-start.28 = (bf16[1,4,32,512]{3,2,1,0:T(8,128)(2,1)S(1)}, bf16[1,4,32,512]{3,2,1,0:T(8,128)(2,1)S(1)}, u32[]{:S(2)}, u32[]{:S(2)}) collective-permute-start(bf16[1,4,32,512]{3,2,1,0:T(8,128)(2,1)S(1)} %get-tuple-element.179.held_ref), channel_id=1, source_target_pairs={{0,16},{4,20},{8,24},{12,28},{16,0},{20,4},{24,8},{28,12},{1,17},{... | collective-permute-start | bytes 393224 | tf_op jit(solution)/shard_map/ppermute | solution.py:471
  86.9 3.8 %collective-permute-start.31 = (bf16[8,32,512]{2,1,0:T(8,128)(2,1)S(1)}, bf16[8,32,512]{2,1,0:T(8,128)(2,1)S(1)}, u32[]{:S(2)}, u32[]{:S(2)}) collective-permute-start(bf16[8,32,512]{2,1,0:T(8,128)(2,1)S(1)} %get-tuple-element.185), channel_id=1, source_target_pairs={{0,4},{4,0},{8,12},{12,8},{16,20},{20,16},{24,28},{28,24},{1,5},{5... | collective-permute-start | bytes 786440 | tf_op jit(solution)/shard_map/ppermute | solution.py:471
  91.7 3.0 %collective-permute-start.32 = (bf16[2,4,32,512]{3,2,1,0:T(8,128)(2,1)S(1)}, bf16[2,4,32,512]{3,2,1,0:T(8,128)(2,1)S(1)}, u32[]{:S(2)}, u32[]{:S(2)}) collective-permute-start(bf16[2,4,32,512]{3,2,1,0:T(8,128)(2,1)S(1)} %get-tuple-element.186.held_ref.refs_9_), channel_id=1, source_target_pairs={{0,8},{4,12},{8,0},{12,4},{16,24},{20,28},{24,16},{28,20},{1,9},{5... | collective-permute-start | bytes 786440 | tf_op jit(solution)/shard_map/ppermute | solution.py:471
  95.8 5.5 %collective-permute-done.30.got_ref = bf16[1,4,16,512]{3,2,1,0:T(8,128)(2,1)S(1)} collective-permute-done((bf16[1,4,16,512]{3,2,1,0:T(8,128)(2,1)S(1)}, bf16[1,4,16,512]{3,2,1,0:T(8,128)(2,1)S(1)}, u32[]{:S(2)}, u32[]{:S(2)}) %collective-permute-start.30) | collective-permute-done | bytes 65568 | tf_op jit(solution)/shard_map/ppermute | solution.py:471
  101.3 3.0 %collective-permute-start.33 = (bf16[2,4,16,512]{3,2,1,0:T(8,128)(2,1)S(1)}, bf16[2,4,16,512]{3,2,1,0:T(8,128)(2,1)S(1)}, u32[]{:S(2)}, u32[]{:S(2)}) collective-permute-start(bf16[2,4,16,512]{3,2,1,0:T(8,128)(2,1)S(1)} %get-tuple-element.188.held_ref.refs_3_), channel_id=1, source_target_pairs={{0,8},{4,12},{8,0},{12,4},{16,24},{20,28},{24,16},{28,20},{1,9},{5... | collective-permute-start | bytes 393224 | tf_op jit(solution)/shard_map/ppermute | solution.py:471
  113.4 2.4 %collective-permute-done.35.value_ref.refs_5_ = bf16[8,16,512]{2,1,0:T(8,128)(2,1)S(1)} collective-permute-done((bf16[8,16,512]{2,1,0:T(8,128)(2,1)S(1)}, bf16[8,16,512]{2,1,0:T(8,128)(2,1)S(1)}, u32[]{:S(2)}, u32[]{:S(2)}) %collective-permute-start.35) | collective-permute-done | bytes 131104 | tf_op jit(solution)/shard_map/ppermute | solution.py:471
  118.0 2.5 %collective-permute-done.38.value_ref.refs_11_ = bf16[8,32,512]{2,1,0:T(8,128)(2,1)S(1)} collective-permute-done((bf16[8,32,512]{2,1,0:T(8,128)(2,1)S(1)}, bf16[8,32,512]{2,1,0:T(8,128)(2,1)S(1)}, u32[]{:S(2)}, u32[]{:S(2)}) %collective-permute-start.38) | collective-permute-done | bytes 262176 | tf_op jit(solution)/shard_map/ppermute | solution.py:471
  120.5 2.5 %shard_map.138 = (bf16[4,128,512]{2,1,0:T(8,128)(2,1)}, bf16[16,128,512]{2,1,0:T(8,128)(2,1)}, f32[8,128]{1,0:T(8,128)S(1)}) custom-call(f32[8,128]{1,0:T(8,128)S(1)} %shard_map.137.token_ref, s32[1]{0:T(128)} %bitcast.me_ref, s32[16]{0:T(128)S(1)} %copy-done.3, s32[16]{0:T(128)S(1)} %copy-done.5, ...), custom_call_target="tpu_custom_call" | custom-call | bytes 1 | tf_op jit(solution)/shard_map/pallas_call | solution.py:24
  (113 shorter events, 48.3 us)
Async XLA Ops:
  5.1 16.3 %collective-permute-start = (bf16[528,512]{1,0:T(8,128)(2,1)}, bf16[528,512]{1,0:T(8,128)(2,1)S(1)}, u32[]{:S(2)}, u32[]{:S(2)}) collective-permute-start(bf16[528,512]{1,0:T(8,128)(2,1)} %get-tuple-element.107), channel_id=1, source_target_pairs={{0,4},{4,0},{8,12},{12,8},{16,20},{20,16},{24,28},{28,24},{1,5},{5... | collective-permute-start | bytes 1622024 | tf_op jit(solution)/shard_map/ppermute | solution.py:471
  8.1 18.0 %collective-permute-start.1 = (bf16[4,4,32,512]{3,2,1,0:T(8,128)(2,1)}, bf16[4,4,32,512]{3,2,1,0:T(8,128)(2,1)S(1)}, u32[]{:S(2)}, u32[]{:S(2)}) collective-permute-start(bf16[4,4,32,512]{3,2,1,0:T(8,128)(2,1)} %get-tuple-element.111), channel_id=1, source_target_pairs={{0,8},{4,12},{8,0},{12,4},{16,24},{20,28},{24,16},{28,20},{1,9},{5... | collective-permute-start | bytes 1572872 | tf_op jit(solution)/shard_map/ppermute | solution.py:471
  16.1 16.5 %collective-permute-start.2 = (bf16[4,4,32,512]{3,2,1,0:T(8,128)(2,1)S(1)}, bf16[4,4,32,512]{3,2,1,0:T(8,128)(2,1)S(1)}, u32[]{:S(2)}, u32[]{:S(2)}) collective-permute-start(bf16[4,4,32,512]{3,2,1,0:T(8,128)(2,1)S(1)} %get-tuple-element.114), channel_id=1, source_target_pairs={{0,4},{4,0},{8,12},{12,8},{16,20},{20,16},{24,28},{28,24},{1,5},{5... | collective-permute-start | bytes 1572872 | tf_op jit(solution)/shard_map/ppermute | solution.py:471
  21.7 13.4 %collective-permute-start.3 = (bf16[2,4,32,512]{3,2,1,0:T(8,128)(2,1)S(1)}, bf16[2,4,32,512]{3,2,1,0:T(8,128)(2,1)S(1)}, u32[]{:S(2)}, u32[]{:S(2)}) collective-permute-start(bf16[2,4,32,512]{3,2,1,0:T(8,128)(2,1)S(1)} %get-tuple-element.117), channel_id=1, source_target_pairs={{0,8},{4,12},{8,0},{12,4},{16,24},{20,28},{24,16},{28,20},{1,9},{5... | collective-permute-start | bytes 786440 | tf_op jit(solution)/shard_map/ppermute | solution.py:471
  23.9 14.4 %collective-permute-start.4 = (bf16[4,4,16,512]{3,2,1,0:T(8,128)(2,1)S(1)}, bf16[4,4,16,512]{3,2,1,0:T(8,128)(2,1)S(1)}, u32[]{:S(2)}, u32[]{:S(2)}) collective-permute-start(bf16[4,4,16,512]{3,2,1,0:T(8,128)(2,1)S(1)} %get-tuple-element.120), channel_id=1, source_target_pairs={{0,4},{4,0},{8,12},{12,8},{16,20},{20,16},{24,28},{28,24},{1,5},{5... | collective-permute-start | bytes 786440 | tf_op jit(solution)/shard_map/ppermute | solution.py:471
  26.4 14.9 %collective-permute-start.5 = (bf16[2,4,32,512]{3,2,1,0:T(8,128)(2,1)S(1)}, bf16[2,4,32,512]{3,2,1,0:T(8,128)(2,1)S(1)}, u32[]{:S(2)}, u32[]{:S(2)}) collective-permute-start(bf16[2,4,32,512]{3,2,1,0:T(8,128)(2,1)S(1)} %get-tuple-element.123), channel_id=1, source_target_pairs={{0,16},{4,20},{8,24},{12,28},{16,0},{20,4},{24,8},{28,12},{1,17},{... | collective-permute-start | bytes 786440 | tf_op jit(solution)/shard_map/ppermute | solution.py:471
  29.0 14.8 %collective-permute-start.7 = (bf16[4,4,16,512]{3,2,1,0:T(8,128)(2,1)S(1)}, bf16[4,4,16,512]{3,2,1,0:T(8,128)(2,1)S(1)}, u32[]{:S(2)}, u32[]{:S(2)}) collective-permute-start(bf16[4,4,16,512]{3,2,1,0:T(8,128)(2,1)S(1)} %get-tuple-element.129), channel_id=1, source_target_pairs={{0,4},{4,0},{8,12},{12,8},{16,20},{20,16},{24,28},{28,24},{1,5},{5... | collective-permute-start | bytes 786440 | tf_op jit(solution)/shard_map/ppermute | solution.py:471
  32.9 13.3 %collective-permute-start.8 = (bf16[2,4,32,512]{3,2,1,0:T(8,128)(2,1)S(1)}, bf16[2,4,32,512]{3,2,1,0:T(8,128)(2,1)S(1)}, u32[]{:S(2)}, u32[]{:S(2)}) collective-permute-start(bf16[2,4,32,512]{3,2,1,0:T(8,128)(2,1)S(1)} %get-tuple-element.132), channel_id=1, source_target_pairs={{0,8},{4,12},{8,0},{12,4},{16,24},{20,28},{24,16},{28,20},{1,9},{5... | collective-permute-start | bytes 786440 | tf_op jit(solution)/shard_map/ppermute | solution.py:471
  41.4 10.4 %collective-permute-start.9 = (bf16[1,4,32,512]{3,2,1,0:T(8,128)(2,1)S(1)}, bf16[1,4,32,512]{3,2,1,0:T(8,128)(2,1)S(1)}, u32[]{:S(2)}, u32[]{:S(2)}) collective-permute-start(bf16[1,4,32,512]{3,2,1,0:T(8,128)(2,1)S(1)} %get-tuple-element.135), channel_id=1, source_target_pairs={{0,4},{4,0},{8,12},{12,8},{16,20},{20,16},{24,28},{28,24},{1,5},{5... | collective-permute-start | bytes 393224 | tf_op jit(solution)/shard_map/ppermute | solution.py:471
  44.0 8.4 %collective-permute-start.10 = (bf16[2,4,16,512]{3,2,1,0:T(8,128)(2,1)S(1)}, bf16[2,4,16,512]{3,2,1,0:T(8,128)(2,1)S(1)}, u32[]{:S(2)}, u32[]{:S(2)}) collective-permute-start(bf16[2,4,16,512]{3,2,1,0:T(8,128)(2,1)S(1)} %get-tuple-element.138), channel_id=1, source_target_pairs={{0,8},{4,12},{8,0},{12,4},{16,24},{20,28},{24,16},{28,20},{1,9},{5... | collective-permute-start | bytes 393224 | tf_op jit(solution)/shard_map/ppermute | solution.py:471
  59.2 10.3 %collective-permute-start.19 = (bf16[2,4,32,512]{3,2,1,0:T(8,128)(2,1)S(1)}, bf16[2,4,32,512]{3,2,1,0:T(8,128)(2,1)S(1)}, u32[]{:S(2)}, u32[]{:S(2)}) collective-permute-start(bf16[2,4,32,512]{3,2,1,0:T(8,128)(2,1)S(1)} %get-tuple-element.160.held_ref), channel_id=1, source_target_pairs={{0,1},{1,0},{2,3},{3,2},{4,5},{5,4},{6,7},{7,6},{8,9},{9,8},{10,11... | collective-permute-start | bytes 786440 | tf_op jit(solution)/shard_map/ppermute | solution.py:471
  59.7 9.5 %collective-permute-start.17 = (bf16[1,4,16,512]{3,2,1,0:T(8,128)(2,1)}, bf16[1,4,16,512]{3,2,1,0:T(8,128)(2,1)S(1)}, u32[]{:S(2)}, u32[]{:S(2)}) collective-permute-start(bf16[1,4,16,512]{3,2,1,0:T(8,128)(2,1)} %get-tuple-element.156), channel_id=1, source_target_pairs={{0,16},{4,20},{8,24},{12,28},{16,0},{20,4},{24,8},{28,12},{1,17},{... | collective-permute-start | bytes 196616 | tf_op jit(solution)/shard_map/ppermute | solution.py:471
  61.2 12.4 %collective-permute-start.21 = (bf16[1,4,32,512]{3,2,1,0:T(8,128)(2,1)S(1)}, bf16[1,4,32,512]{3,2,1,0:T(8,128)(2,1)S(1)}, u32[]{:S(2)}, u32[]{:S(2)}) collective-permute-start(bf16[1,4,32,512]{3,2,1,0:T(8,128)(2,1)S(1)} %get-tuple-element.164.held_ref), channel_id=1, source_target_pairs={{0,16},{4,20},{8,24},{12,28},{16,0},{20,4},{24,8},{28,12},{1,17},{... | collective-permute-start | bytes 393224 | tf_op jit(solution)/shard_map/ppermute | solution.py:471
  63.2 10.5 %collective-permute-start.22 = (bf16[1,4,32,512]{3,2,1,0:T(8,128)(2,1)S(1)}, bf16[1,4,32,512]{3,2,1,0:T(8,128)(2,1)S(1)}, u32[]{:S(2)}, u32[]{:S(2)}) collective-permute-start(bf16[1,4,32,512]{3,2,1,0:T(8,128)(2,1)S(1)} %bitcast.10), channel_id=1, source_target_pairs={{0,2},{1,3},{2,0},{3,1},{4,6},{5,7},{6,4},{7,5},{8,10},{9,11},{10,... | collective-permute-start | bytes 393224 | tf_op jit(solution)/shard_map/ppermute | solution.py:471
  73.8 9.0 %collective-permute-start.24 = (bf16[1,4,32,512]{3,2,1,0:T(8,128)(2,1)S(1)}, bf16[1,4,32,512]{3,2,1,0:T(8,128)(2,1)S(1)}, u32[]{:S(2)}, u32[]{:S(2)}) collective-permute-start(bf16[1,4,32,512]{3,2,1,0:T(8,128)(2,1)S(1)} %get-tuple-element.170.held_ref), channel_id=1, source_target_pairs={{0,16},{4,20},{8,24},{12,28},{16,0},{20,4},{24,8},{28,12},{1,17},{... | collective-permute-start | bytes 393224 | tf_op jit(solution)/shard_map/ppermute | solution.py:471
  73.9 12.5 %collective-permute-start.27 = (bf16[2,4,32,512]{3,2,1,0:T(8,128)(2,1)S(1)}, bf16[2,4,32,512]{3,2,1,0:T(8,128)(2,1)S(1)}, u32[]{:S(2)}, u32[]{:S(2)}) collective-permute-start(bf16[2,4,32,512]{3,2,1,0:T(8,128)(2,1)S(1)} %get-tuple-element.177.held_ref.refs_0_), channel_id=1, source_target_pairs={{0,8},{4,12},{8,0},{12,4},{16,24},{20,28},{24,16},{28,20},{1,9},{5... | collective-permute-start | bytes 786440 | tf_op jit(solution)/shard_map/ppermute | solution.py:471
  76.3 9.0 %collective-permute-start.25 = (bf16[2,4,16,512]{3,2,1,0:T(8,128)(2,1)S(1)}, bf16[2,4,16,512]{3,2,1,0:T(8,128)(2,1)S(1)}, u32[]{:S(2)}, u32[]{:S(2)}) collective-permute-start(bf16[2,4,16,512]{3,2,1,0:T(8,128)(2,1)S(1)} %get-tuple-element.172.held_ref), channel_id=1, source_target_pairs={{0,1},{1,0},{2,3},{3,2},{4,5},{5,4},{6,7},{7,6},{8,9},{9,8},{10,11... | collective-permute-start | bytes 393224 | tf_op jit(solution)/shard_map/ppermute | solution.py:471
  76.3 9.5 %collective-permute-start.26 = (bf16[2,4,16,512]{3,2,1,0:T(8,128)(2,1)S(1)}, bf16[2,4,16,512]{3,2,1,0:T(8,128)(2,1)S(1)}, u32[]{:S(2)}, u32[]{:S(2)}) collective-permute-start(bf16[2,4,16,512]{3,2,1,0:T(8,128)(2,1)S(1)} %get-tuple-element.174.held_ref), channel_id=1, source_target_pairs={{0,1},{1,0},{2,3},{3,2},{4,5},{5,4},{6,7},{7,6},{8,9},{9,8},{10,11... | collective-permute-start | bytes 393224 | tf_op jit(solution)/shard_map/ppermute | solution.py:471
  82.8 12.4 %collective-permute-start.29 = (bf16[2,4,32,512]{3,2,1,0:T(8,128)(2,1)S(1)}, bf16[2,4,32,512]{3,2,1,0:T(8,128)(2,1)S(1)}, u32[]{:S(2)}, u32[]{:S(2)}) collective-permute-start(bf16[2,4,32,512]{3,2,1,0:T(8,128)(2,1)S(1)} %get-tuple-element.181.held_ref.refs_6_), channel_id=1, source_target_pairs={{0,8},{4,12},{8,0},{12,4},{16,24},{20,28},{24,16},{28,20},{1,9},{5... | collective-permute-start | bytes 786440 | tf_op jit(solution)/shard_map/ppermute | solution.py:471
  82.9 8.8 %collective-permute-start.28 = (bf16[1,4,32,512]{3,2,1,0:T(8,128)(2,1)S(1)}, bf16[1,4,32,512]{3,2,1,0:T(8,128)(2,1)S(1)}, u32[]{:S(2)}, u32[]{:S(2)}) collective-permute-start(bf16[1,4,32,512]{3,2,1,0:T(8,128)(2,1)S(1)} %get-tuple-element.179.held_ref), channel_id=1, source_target_pairs={{0,16},{4,20},{8,24},{12,28},{16,0},{20,4},{24,8},{28,12},{1,17},{... | collective-permute-start | bytes 393224 | tf_op jit(solution)/shard_map/ppermute | solution.py:471
  86.9 21.2 %collective-permute-start.31 = (bf16[8,32,512]{2,1,0:T(8,128)(2,1)S(1)}, bf16[8,32,512]{2,1,0:T(8,128)(2,1)S(1)}, u32[]{:S(2)}, u32[]{:S(2)}) collective-permute-start(bf16[8,32,512]{2,1,0:T(8,128)(2,1)S(1)} %get-tuple-element.185), channel_id=1, source_target_pairs={{0,4},{4,0},{8,12},{12,8},{16,20},{20,16},{24,28},{28,24},{1,5},{5... | collective-permute-start | bytes 786440 | tf_op jit(solution)/shard_map/ppermute | solution.py:471
  91.7 16.4 %collective-permute-start.32 = (bf16[2,4,32,512]{3,2,1,0:T(8,128)(2,1)S(1)}, bf16[2,4,32,512]{3,2,1,0:T(8,128)(2,1)S(1)}, u32[]{:S(2)}, u32[]{:S(2)}) collective-permute-start(bf16[2,4,32,512]{3,2,1,0:T(8,128)(2,1)S(1)} %get-tuple-element.186.held_ref.refs_9_), channel_id=1, source_target_pairs={{0,8},{4,12},{8,0},{12,4},{16,24},{20,28},{24,16},{28,20},{1,9},{5... | collective-permute-start | bytes 786440 | tf_op jit(solution)/shard_map/ppermute | solution.py:471
  104.3 11.4 %collective-permute-start.36 = (bf16[8,32,512]{2,1,0:T(8,128)(2,1)S(1)}, bf16[8,32,512]{2,1,0:T(8,128)(2,1)S(1)}, u32[]{:S(2)}, u32[]{:S(2)}) collective-permute-start(bf16[8,32,512]{2,1,0:T(8,128)(2,1)S(1)} %get-tuple-element.193), channel_id=1, source_target_pairs={{0,4},{4,0},{8,12},{12,8},{16,20},{20,16},{24,28},{28,24},{1,5},{5... | collective-permute-start | bytes 786440 | tf_op jit(solution)/shard_map/ppermute | solution.py:471
  110.3 10.2 %collective-permute-start.38 = (bf16[8,32,512]{2,1,0:T(8,128)(2,1)S(1)}, bf16[8,32,512]{2,1,0:T(8,128)(2,1)S(1)}, u32[]{:S(2)}, u32[]{:S(2)}) collective-permute-start(bf16[8,32,512]{2,1,0:T(8,128)(2,1)S(1)} %get-tuple-element.196), channel_id=1, source_target_pairs={{0,4},{4,0},{8,12},{12,8},{16,20},{20,16},{24,28},{28,24},{1,5},{5... | collective-permute-start | bytes 786440 | tf_op jit(solution)/shard_map/ppermute | solution.py:471
  (22 other events, 173.6 us)

commit v9 on v8

--- a/solution.py
+++ b/solution.py
@@ -7,8 +7,8 @@
 
 SHARES = (2, 2, 1, 2, 1)
 ORDER = (
-    1, 0, 3, 1, 4, 0, 1, 2, 3, 0, 2, 3, 1, 2, 4, 0, 0, 4, 2, 1, 4, 0, 3, 3, 1, 4, 2, 0, 3, 1, 4, 0,
-    3, 4, 2, 4, 1, 2, 3, 2,
+    1, 0, 3, 2, 1, 0, 4, 3, 1, 2, 0, 3, 1, 4, 0, 0, 2, 1, 2, 0, 3, 4, 4, 3, 1, 0, 3, 4, 1, 4, 2, 0,
+    3, 2, 4, 1, 2, 3, 4, 2,
 )
 READ_CAP = 2
 VMEM_BYTES = 12 * 1024 * 1024

time: 125 us -> 120 us (0.960)
  waiting for transfers between devices: 42.9 us -> 36.1 us
    ppermute x40, waiting for transfers between devices: 42.9 us -> 36.1 us  [flip(): lax.ppermute(value, axis, [(d, d ^ bit) for d in range(lax.axis_size(axis...]
    unnamed x12 -> x16, local copies, waits for them, and re-layouts: 3.13 us -> 3.14 us
  transfers between devices with their start and end apart: 40 -> 40, of which waited for: 19 -> 19; matrix products, arithmetic and copies ran while one was open for 0% -> 0% of each run, Pallas kernels for 13% -> 14%
where the time goes in v9:
time: 120 us
  starting transfers between devices  55.9 us (47%)
  waiting for transfers between devices  36.1 us (30%)
  Pallas kernels  23.6 us (20%)
  local copies, waits for them, and re-layouts  3.14 us (3%)
    ppermute x40, starting transfers between devices, flip(): lax.ppermute(value, axis, [(d, d ^ bit) for d in range(lax.axis_size(axis...  55.9 us
    ppermute x40, waiting for transfers between devices, flip(): lax.ppermute(value, axis, [(d, d ^ bit) for d in range(lax.axis_size(axis...  36.1 us
    pallas_call x45, Pallas kernels, call(): pl.pallas_call(body, out_shape=out_shape, in_specs=in_specs, out_specs=ou...  23.6 us
    unnamed x16, local copies, waits for them, and re-layouts  3.14 us
  transfers between devices with their start and end apart: 40, of which 19 were waited for; matrix products, arithmetic and copies ran while one was open for 0% of the time, Pallas kernels for 14%

profile of v9, /device:TPU:0, one launch (start us, length us, event | category | flops | bytes accessed | tf_op | source)
XLA Modules:
  0.0 119.8 jit_solution(8592640508157541018)
XLA Ops:
  0.6 4.4 %shard_map.95 = (s32[256]{0:T(256)}, s32[16]{0:T(128)}, bf16[4,4,32,512]{3,2,1,0:T(8,128)(2,1)}, bf16[528,512]{1,0:T(8,128)(2,1)}, bf16[512,512]{1,0:T(8,128)(2,1)}) custom-call(s32[1]{0:T(128)} %bitcast.me_ref, s32[96]{0:T(128)} %slot_hbm.1, s32[96]{0:T(128)} %col_hbm.1, s32[96]{0:T(128)} %id_hbm.1, s32[8,4,8]{2,1,0:T(4,128)} %bitcast.22, s32[16]{0:T(128)} %readers_ref.3, ...), custom_call_target="tpu_custom_call" | custom-call | bytes 1 | tf_op jit(solution)/shard_map/pallas_call | solution.py:24
  5.1 3.0 %collective-permute-start = (bf16[528,512]{1,0:T(8,128)(2,1)}, bf16[528,512]{1,0:T(8,128)(2,1)S(1)}, u32[]{:S(2)}, u32[]{:S(2)}) collective-permute-start(bf16[528,512]{1,0:T(8,128)(2,1)} %get-tuple-element.107), channel_id=1, source_target_pairs={{0,4},{4,0},{8,12},{12,8},{16,20},{20,16},{24,28},{28,24},{1,5},{5... | collective-permute-start | bytes 1622024 | tf_op jit(solution)/shard_map/ppermute | solution.py:471
  12.8 3.4 %shard_map.99 = (bf16[4,4,16,512]{3,2,1,0:T(8,128)(2,1)S(1)}, bf16[4,4,32,512]{3,2,1,0:T(8,128)(2,1)S(1)}, bf16[4,4,16,512]{3,2,1,0:T(8,128)(2,1)S(1)}, bf16[4,4,32,512]{3,2,1,0:T(8,128)(2,1)S(1)}, f32[8,128]{1,0:T(8,128)}) custom-call(s32[256]{0:T(256)S(1)} %copy-done.4, bf16[48,128,128]{2,1,0:T(8,128)(2,1)S(1)} %copy-done.1, bf16[512,512]{1,0:T(8,128)(2,1)S(1)} %copy-done.2), custom_call_target="tpu_custom_call" | custom-call | bytes 1 | tf_op jit(solution)/shard_map/pallas_call | solution.py:24
  18.2 2.2 %shard_map.96 = (bf16[4,4,32,512]{3,2,1,0:T(8,128)(2,1)S(1)}, bf16[4,4,16,512]{3,2,1,0:T(8,128)(2,1)S(1)}, bf16[4,4,32,512]{3,2,1,0:T(8,128)(2,1)S(1)}, bf16[4,4,16,512]{3,2,1,0:T(8,128)(2,1)S(1)}, f32[8,128]{1,0:T(8,128)S(1)}) custom-call(s32[256]{0:T(256)S(1)} %copy-done.4, bf16[48,128,128]{2,1,0:T(8,128)(2,1)S(1)} %copy-done.1, bf16[512,512]{1,0:T(8,128)(2,1)S(1)} %copy-done.2), custom_call_target="tpu_custom_call" | custom-call | bytes 1 | tf_op jit(solution)/shard_map/pallas_call | solution.py:24
  21.7 2.2 %collective-permute-start.4 = (bf16[2,4,32,512]{3,2,1,0:T(8,128)(2,1)S(1)}, bf16[2,4,32,512]{3,2,1,0:T(8,128)(2,1)S(1)}, u32[]{:S(2)}, u32[]{:S(2)}) collective-permute-start(bf16[2,4,32,512]{3,2,1,0:T(8,128)(2,1)S(1)} %get-tuple-element.120), channel_id=1, source_target_pairs={{0,8},{4,12},{8,0},{12,4},{16,24},{20,28},{24,16},{28,20},{1,9},{5... | collective-permute-start | bytes 786440 | tf_op jit(solution)/shard_map/ppermute | solution.py:471
  24.9 2.7 %collective-permute-start.5 = (bf16[2,4,32,512]{3,2,1,0:T(8,128)(2,1)S(1)}, bf16[2,4,32,512]{3,2,1,0:T(8,128)(2,1)S(1)}, u32[]{:S(2)}, u32[]{:S(2)}) collective-permute-start(bf16[2,4,32,512]{3,2,1,0:T(8,128)(2,1)S(1)} %get-tuple-element.123), channel_id=1, source_target_pairs={{0,16},{4,20},{8,24},{12,28},{16,0},{20,4},{24,8},{28,12},{1,17},{... | collective-permute-start | bytes 786440 | tf_op jit(solution)/shard_map/ppermute | solution.py:471
  29.0 3.6 %collective-permute-done.2.got_ref = bf16[4,4,32,512]{3,2,1,0:T(8,128)(2,1)S(1)} collective-permute-done((bf16[4,4,32,512]{3,2,1,0:T(8,128)(2,1)S(1)}, bf16[4,4,32,512]{3,2,1,0:T(8,128)(2,1)S(1)}, u32[]{:S(2)}, u32[]{:S(2)}) %collective-permute-start.2) | collective-permute-done | bytes 524320 | tf_op jit(solution)/shard_map/ppermute | solution.py:471
  32.9 2.2 %collective-permute-start.7 = (bf16[2,4,32,512]{3,2,1,0:T(8,128)(2,1)S(1)}, bf16[2,4,32,512]{3,2,1,0:T(8,128)(2,1)S(1)}, u32[]{:S(2)}, u32[]{:S(2)}) collective-permute-start(bf16[2,4,32,512]{3,2,1,0:T(8,128)(2,1)S(1)} %get-tuple-element.129), channel_id=1, source_target_pairs={{0,8},{4,12},{8,0},{12,4},{16,24},{20,28},{24,16},{28,20},{1,9},{5... | collective-permute-start | bytes 786440 | tf_op jit(solution)/shard_map/ppermute | solution.py:471
  35.1 3.1 %collective-permute-done.3.got_ref = bf16[4,4,16,512]{3,2,1,0:T(8,128)(2,1)S(1)} collective-permute-done((bf16[4,4,16,512]{3,2,1,0:T(8,128)(2,1)S(1)}, bf16[4,4,16,512]{3,2,1,0:T(8,128)(2,1)S(1)}, u32[]{:S(2)}, u32[]{:S(2)}) %collective-permute-start.3) | collective-permute-done | bytes 262176 | tf_op jit(solution)/shard_map/ppermute | solution.py:471
  38.5 3.2 %collective-permute-start.8 = (bf16[1,4,32,512]{3,2,1,0:T(8,128)(2,1)S(1)}, bf16[1,4,32,512]{3,2,1,0:T(8,128)(2,1)S(1)}, u32[]{:S(2)}, u32[]{:S(2)}) collective-permute-start(bf16[1,4,32,512]{3,2,1,0:T(8,128)(2,1)S(1)} %get-tuple-element.132), channel_id=1, source_target_pairs={{0,16},{4,20},{8,24},{12,28},{16,0},{20,4},{24,8},{28,12},{1,17},{... | collective-permute-start | bytes 393224 | tf_op jit(solution)/shard_map/ppermute | solution.py:471
  46.2 2.8 %collective-permute-start.11 = (bf16[1,4,32,512]{3,2,1,0:T(8,128)(2,1)S(1)}, bf16[1,4,32,512]{3,2,1,0:T(8,128)(2,1)S(1)}, u32[]{:S(2)}, u32[]{:S(2)}) collective-permute-start(bf16[1,4,32,512]{3,2,1,0:T(8,128)(2,1)S(1)} %get-tuple-element.141), channel_id=1, source_target_pairs={{0,16},{4,20},{8,24},{12,28},{16,0},{20,4},{24,8},{28,12},{1,17},{... | collective-permute-start | bytes 393224 | tf_op jit(solution)/shard_map/ppermute | solution.py:471
  54.2 2.2 %collective-permute-done.14.got_ref = bf16[1,4,32,512]{3,2,1,0:T(8,128)(2,1)S(1)} collective-permute-done((bf16[1,4,32,512]{3,2,1,0:T(8,128)(2,1)S(1)}, bf16[1,4,32,512]{3,2,1,0:T(8,128)(2,1)S(1)}, u32[]{:S(2)}, u32[]{:S(2)}) %collective-permute-start.14) | collective-permute-done | bytes 131104 | tf_op jit(solution)/shard_map/ppermute | solution.py:471
  61.0 5.5 %collective-permute-done.16.got_ref = bf16[1,4,16,512]{3,2,1,0:T(8,128)(2,1)} collective-permute-done((bf16[1,4,16,512]{3,2,1,0:T(8,128)(2,1)}, bf16[1,4,16,512]{3,2,1,0:T(8,128)(2,1)}, u32[]{:S(2)}, u32[]{:S(2)}) %collective-permute-start.16) | collective-permute-done | bytes 65568 | tf_op jit(solution)/shard_map/ppermute | solution.py:471
  69.1 2.7 %collective-permute-done.18.got_ref = bf16[1,4,16,512]{3,2,1,0:T(8,128)(2,1)S(1)} collective-permute-done((bf16[1,4,16,512]{3,2,1,0:T(8,128)(2,1)S(1)}, bf16[1,4,16,512]{3,2,1,0:T(8,128)(2,1)S(1)}, u32[]{:S(2)}, u32[]{:S(2)}) %collective-permute-start.18) | collective-permute-done | bytes 65568 | tf_op jit(solution)/shard_map/ppermute | solution.py:471
  72.0 2.3 %collective-permute-start.25 = (bf16[2,4,32,512]{3,2,1,0:T(8,128)(2,1)S(1)}, bf16[2,4,32,512]{3,2,1,0:T(8,128)(2,1)S(1)}, u32[]{:S(2)}, u32[]{:S(2)}) collective-permute-start(bf16[2,4,32,512]{3,2,1,0:T(8,128)(2,1)S(1)} %get-tuple-element.173.held_ref.refs_0_), channel_id=1, source_target_pairs={{0,8},{4,12},{8,0},{12,4},{16,24},{20,28},{24,16},{28,20},{1,9},{5... | collective-permute-start | bytes 786440 | tf_op jit(solution)/shard_map/ppermute | solution.py:471
  74.9 3.1 %collective-permute-done.21.got_ref = bf16[1,4,16,512]{3,2,1,0:T(8,128)(2,1)S(1)} collective-permute-done((bf16[1,4,16,512]{3,2,1,0:T(8,128)(2,1)S(1)}, bf16[1,4,16,512]{3,2,1,0:T(8,128)(2,1)S(1)}, u32[]{:S(2)}, u32[]{:S(2)}) %collective-permute-start.21) | collective-permute-done | bytes 65568 | tf_op jit(solution)/shard_map/ppermute | solution.py:471
  79.3 3.0 %collective-permute-done.22.got_ref = bf16[1,4,16,512]{3,2,1,0:T(8,128)(2,1)S(1)} collective-permute-done((bf16[1,4,16,512]{3,2,1,0:T(8,128)(2,1)S(1)}, bf16[1,4,16,512]{3,2,1,0:T(8,128)(2,1)S(1)}, u32[]{:S(2)}, u32[]{:S(2)}) %collective-permute-start.22) | collective-permute-done | bytes 65568 | tf_op jit(solution)/shard_map/ppermute | solution.py:471
  83.6 3.2 %collective-permute-start.28 = (bf16[2,4,32,512]{3,2,1,0:T(8,128)(2,1)S(1)}, bf16[2,4,32,512]{3,2,1,0:T(8,128)(2,1)S(1)}, u32[]{:S(2)}, u32[]{:S(2)}) collective-permute-start(bf16[2,4,32,512]{3,2,1,0:T(8,128)(2,1)S(1)} %get-tuple-element.179.held_ref.refs_3_), channel_id=1, source_target_pairs={{0,8},{4,12},{8,0},{12,4},{16,24},{20,28},{24,16},{28,20},{1,9},{5... | collective-permute-start | bytes 786440 | tf_op jit(solution)/shard_map/ppermute | solution.py:471
  88.9 2.3 %collective-permute-done.26.got_ref = bf16[1,4,32,512]{3,2,1,0:T(8,128)(2,1)S(1)} collective-permute-done((bf16[1,4,32,512]{3,2,1,0:T(8,128)(2,1)S(1)}, bf16[1,4,32,512]{3,2,1,0:T(8,128)(2,1)S(1)}, u32[]{:S(2)}, u32[]{:S(2)}) %collective-permute-start.26) | collective-permute-done | bytes 131104 | tf_op jit(solution)/shard_map/ppermute | solution.py:471
  91.9 2.3 %collective-permute-start.29 = (bf16[1,4,16,512]{3,2,1,0:T(8,128)(2,1)S(1)}, bf16[1,4,16,512]{3,2,1,0:T(8,128)(2,1)S(1)}, u32[]{:S(2)}, u32[]{:S(2)}) collective-permute-start(bf16[1,4,16,512]{3,2,1,0:T(8,128)(2,1)S(1)} %get-tuple-element.181.held_ref), channel_id=1, source_target_pairs={{0,16},{4,20},{8,24},{12,28},{16,0},{20,4},{24,8},{28,12},{1,17},{... | collective-permute-start | bytes 196616 | tf_op jit(solution)/shard_map/ppermute | solution.py:471
  99.2 3.4 %collective-permute-start.33 = (bf16[1,4,16,512]{3,2,1,0:T(8,128)(2,1)S(1)}, bf16[1,4,16,512]{3,2,1,0:T(8,128)(2,1)S(1)}, u32[]{:S(2)}, u32[]{:S(2)}) collective-permute-start(bf16[1,4,16,512]{3,2,1,0:T(8,128)(2,1)S(1)} %get-tuple-element.188.held_ref), channel_id=1, source_target_pairs={{0,16},{4,20},{8,24},{12,28},{16,0},{20,4},{24,8},{28,12},{1,17},{... | collective-permute-start | bytes 196616 | tf_op jit(solution)/shard_map/ppermute | solution.py:471
  105.7 2.3 %collective-permute-start.36 = (bf16[2,4,16,512]{3,2,1,0:T(8,128)(2,1)S(1)}, bf16[2,4,16,512]{3,2,1,0:T(8,128)(2,1)S(1)}, u32[]{:S(2)}, u32[]{:S(2)}) collective-permute-start(bf16[2,4,16,512]{3,2,1,0:T(8,128)(2,1)S(1)} %get-tuple-element.193.held_ref.refs_0_), channel_id=1, source_target_pairs={{0,8},{4,12},{8,0},{12,4},{16,24},{20,28},{24,16},{28,20},{1,9},{5... | collective-permute-start | bytes 393224 | tf_op jit(solution)/shard_map/ppermute | solution.py:471
  113.2 2.1 %collective-permute-done.38.value_ref.refs_11_ = bf16[8,16,512]{2,1,0:T(8,128)(2,1)S(1)} collective-permute-done((bf16[8,16,512]{2,1,0:T(8,128)(2,1)S(1)}, bf16[8,16,512]{2,1,0:T(8,128)(2,1)S(1)}, u32[]{:S(2)}, u32[]{:S(2)}) %collective-permute-start.38) | collective-permute-done | bytes 131104 | tf_op jit(solution)/shard_map/ppermute | solution.py:471
  115.3 2.5 %shard_map.138 = (bf16[4,128,512]{2,1,0:T(8,128)(2,1)}, bf16[16,128,512]{2,1,0:T(8,128)(2,1)}, f32[8,128]{1,0:T(8,128)S(1)}) custom-call(f32[8,128]{1,0:T(8,128)S(1)} %shard_map.137.token_ref, s32[1]{0:T(128)} %bitcast.me_ref, s32[16]{0:T(128)S(1)} %copy-done.3, s32[16]{0:T(128)S(1)} %copy-done.5, ...), custom_call_target="tpu_custom_call" | custom-call | bytes 1 | tf_op jit(solution)/shard_map/pallas_call | solution.py:24
  (117 shorter events, 48.9 us)
Async XLA Ops:
  5.1 16.3 %collective-permute-start = (bf16[528,512]{1,0:T(8,128)(2,1)}, bf16[528,512]{1,0:T(8,128)(2,1)S(1)}, u32[]{:S(2)}, u32[]{:S(2)}) collective-permute-start(bf16[528,512]{1,0:T(8,128)(2,1)} %get-tuple-element.107), channel_id=1, source_target_pairs={{0,4},{4,0},{8,12},{12,8},{16,20},{20,16},{24,28},{28,24},{1,5},{5... | collective-permute-start | bytes 1622024 | tf_op jit(solution)/shard_map/ppermute | solution.py:471
  8.1 16.5 %collective-permute-start.1 = (bf16[4,4,32,512]{3,2,1,0:T(8,128)(2,1)}, bf16[4,4,32,512]{3,2,1,0:T(8,128)(2,1)S(1)}, u32[]{:S(2)}, u32[]{:S(2)}) collective-permute-start(bf16[4,4,32,512]{3,2,1,0:T(8,128)(2,1)} %get-tuple-element.111), channel_id=1, source_target_pairs={{0,8},{4,12},{8,0},{12,4},{16,24},{20,28},{24,16},{28,20},{1,9},{5... | collective-permute-start | bytes 1572872 | tf_op jit(solution)/shard_map/ppermute | solution.py:471
  16.2 16.5 %collective-permute-start.2 = (bf16[4,4,32,512]{3,2,1,0:T(8,128)(2,1)S(1)}, bf16[4,4,32,512]{3,2,1,0:T(8,128)(2,1)S(1)}, u32[]{:S(2)}, u32[]{:S(2)}) collective-permute-start(bf16[4,4,32,512]{3,2,1,0:T(8,128)(2,1)S(1)} %get-tuple-element.114), channel_id=1, source_target_pairs={{0,4},{4,0},{8,12},{12,8},{16,20},{20,16},{24,28},{28,24},{1,5},{5... | collective-permute-start | bytes 1572872 | tf_op jit(solution)/shard_map/ppermute | solution.py:471
  16.8 21.5 %collective-permute-start.3 = (bf16[4,4,16,512]{3,2,1,0:T(8,128)(2,1)S(1)}, bf16[4,4,16,512]{3,2,1,0:T(8,128)(2,1)S(1)}, u32[]{:S(2)}, u32[]{:S(2)}) collective-permute-start(bf16[4,4,16,512]{3,2,1,0:T(8,128)(2,1)S(1)} %get-tuple-element.117), channel_id=1, source_target_pairs={{0,4},{4,0},{8,12},{12,8},{16,20},{20,16},{24,28},{28,24},{1,5},{5... | collective-permute-start | bytes 786440 | tf_op jit(solution)/shard_map/ppermute | solution.py:471
  21.7 16.7 %collective-permute-start.4 = (bf16[2,4,32,512]{3,2,1,0:T(8,128)(2,1)S(1)}, bf16[2,4,32,512]{3,2,1,0:T(8,128)(2,1)S(1)}, u32[]{:S(2)}, u32[]{:S(2)}) collective-permute-start(bf16[2,4,32,512]{3,2,1,0:T(8,128)(2,1)S(1)} %get-tuple-element.120), channel_id=1, source_target_pairs={{0,8},{4,12},{8,0},{12,4},{16,24},{20,28},{24,16},{28,20},{1,9},{5... | collective-permute-start | bytes 786440 | tf_op jit(solution)/shard_map/ppermute | solution.py:471
  24.9 18.4 %collective-permute-start.5 = (bf16[2,4,32,512]{3,2,1,0:T(8,128)(2,1)S(1)}, bf16[2,4,32,512]{3,2,1,0:T(8,128)(2,1)S(1)}, u32[]{:S(2)}, u32[]{:S(2)}) collective-permute-start(bf16[2,4,32,512]{3,2,1,0:T(8,128)(2,1)S(1)} %get-tuple-element.123), channel_id=1, source_target_pairs={{0,16},{4,20},{8,24},{12,28},{16,0},{20,4},{24,8},{28,12},{1,17},{... | collective-permute-start | bytes 786440 | tf_op jit(solution)/shard_map/ppermute | solution.py:471
  27.5 17.4 %collective-permute-start.6 = (bf16[4,4,16,512]{3,2,1,0:T(8,128)(2,1)S(1)}, bf16[4,4,16,512]{3,2,1,0:T(8,128)(2,1)S(1)}, u32[]{:S(2)}, u32[]{:S(2)}) collective-permute-start(bf16[4,4,16,512]{3,2,1,0:T(8,128)(2,1)S(1)} %get-tuple-element.126), channel_id=1, source_target_pairs={{0,4},{4,0},{8,12},{12,8},{16,20},{20,16},{24,28},{28,24},{1,5},{5... | collective-permute-start | bytes 786440 | tf_op jit(solution)/shard_map/ppermute | solution.py:471
  32.9 13.2 %collective-permute-start.7 = (bf16[2,4,32,512]{3,2,1,0:T(8,128)(2,1)S(1)}, bf16[2,4,32,512]{3,2,1,0:T(8,128)(2,1)S(1)}, u32[]{:S(2)}, u32[]{:S(2)}) collective-permute-start(bf16[2,4,32,512]{3,2,1,0:T(8,128)(2,1)S(1)} %get-tuple-element.129), channel_id=1, source_target_pairs={{0,8},{4,12},{8,0},{12,4},{16,24},{20,28},{24,16},{28,20},{1,9},{5... | collective-permute-start | bytes 786440 | tf_op jit(solution)/shard_map/ppermute | solution.py:471
  38.5 10.5 %collective-permute-start.8 = (bf16[1,4,32,512]{3,2,1,0:T(8,128)(2,1)S(1)}, bf16[1,4,32,512]{3,2,1,0:T(8,128)(2,1)S(1)}, u32[]{:S(2)}, u32[]{:S(2)}) collective-permute-start(bf16[1,4,32,512]{3,2,1,0:T(8,128)(2,1)S(1)} %get-tuple-element.132), channel_id=1, source_target_pairs={{0,16},{4,20},{8,24},{12,28},{16,0},{20,4},{24,8},{28,12},{1,17},{... | collective-permute-start | bytes 393224 | tf_op jit(solution)/shard_map/ppermute | solution.py:471
  41.7 8.9 %collective-permute-start.9 = (bf16[2,4,16,512]{3,2,1,0:T(8,128)(2,1)S(1)}, bf16[2,4,16,512]{3,2,1,0:T(8,128)(2,1)S(1)}, u32[]{:S(2)}, u32[]{:S(2)}) collective-permute-start(bf16[2,4,16,512]{3,2,1,0:T(8,128)(2,1)S(1)} %get-tuple-element.135), channel_id=1, source_target_pairs={{0,8},{4,12},{8,0},{12,4},{16,24},{20,28},{24,16},{28,20},{1,9},{5... | collective-permute-start | bytes 393224 | tf_op jit(solution)/shard_map/ppermute | solution.py:471
  45.1 9.0 %collective-permute-start.13 = (bf16[2,4,16,512]{3,2,1,0:T(8,128)(2,1)S(1)}, bf16[2,4,16,512]{3,2,1,0:T(8,128)(2,1)S(1)}, u32[]{:S(2)}, u32[]{:S(2)}) collective-permute-start(bf16[2,4,16,512]{3,2,1,0:T(8,128)(2,1)S(1)} %get-tuple-element.146), channel_id=1, source_target_pairs={{0,8},{4,12},{8,0},{12,4},{16,24},{20,28},{24,16},{28,20},{1,9},{5... | collective-permute-start | bytes 393224 | tf_op jit(solution)/shard_map/ppermute | solution.py:471
  56.5 12.2 %collective-permute-start.17 = (bf16[2,4,32,512]{3,2,1,0:T(8,128)(2,1)S(1)}, bf16[2,4,32,512]{3,2,1,0:T(8,128)(2,1)S(1)}, u32[]{:S(2)}, u32[]{:S(2)}) collective-permute-start(bf16[2,4,32,512]{3,2,1,0:T(8,128)(2,1)S(1)} %get-tuple-element.155.held_ref), channel_id=1, source_target_pairs={{0,1},{1,0},{2,3},{3,2},{4,5},{5,4},{6,7},{7,6},{8,9},{9,8},{10,11... | collective-permute-start | bytes 786440 | tf_op jit(solution)/shard_map/ppermute | solution.py:471
  56.9 9.6 %collective-permute-start.16 = (bf16[1,4,16,512]{3,2,1,0:T(8,128)(2,1)}, bf16[1,4,16,512]{3,2,1,0:T(8,128)(2,1)}, u32[]{:S(2)}, u32[]{:S(2)}) collective-permute-start(bf16[1,4,16,512]{3,2,1,0:T(8,128)(2,1)} %get-tuple-element.153), channel_id=1, source_target_pairs={{0,16},{4,20},{8,24},{12,28},{16,0},{20,4},{24,8},{28,12},{1,17},{... | collective-permute-start | bytes 196616 | tf_op jit(solution)/shard_map/ppermute | solution.py:471
  58.4 13.3 %collective-permute-start.19 = (bf16[1,4,32,512]{3,2,1,0:T(8,128)(2,1)S(1)}, bf16[1,4,32,512]{3,2,1,0:T(8,128)(2,1)S(1)}, u32[]{:S(2)}, u32[]{:S(2)}) collective-permute-start(bf16[1,4,32,512]{3,2,1,0:T(8,128)(2,1)S(1)} %get-tuple-element.159.held_ref), channel_id=1, source_target_pairs={{0,16},{4,20},{8,24},{12,28},{16,0},{20,4},{24,8},{28,12},{1,17},{... | collective-permute-start | bytes 393224 | tf_op jit(solution)/shard_map/ppermute | solution.py:471
  60.4 11.4 %collective-permute-start.20 = (bf16[1,4,32,512]{3,2,1,0:T(8,128)(2,1)S(1)}, bf16[1,4,32,512]{3,2,1,0:T(8,128)(2,1)S(1)}, u32[]{:S(2)}, u32[]{:S(2)}) collective-permute-start(bf16[1,4,32,512]{3,2,1,0:T(8,128)(2,1)S(1)} %bitcast.10), channel_id=1, source_target_pairs={{0,2},{1,3},{2,0},{3,1},{4,6},{5,7},{6,4},{7,5},{8,10},{9,11},{10,... | collective-permute-start | bytes 393224 | tf_op jit(solution)/shard_map/ppermute | solution.py:471
  71.8 10.5 %collective-permute-start.23 = (bf16[2,4,32,512]{3,2,1,0:T(8,128)(2,1)S(1)}, bf16[2,4,32,512]{3,2,1,0:T(8,128)(2,1)S(1)}, u32[]{:S(2)}, u32[]{:S(2)}) collective-permute-start(bf16[2,4,32,512]{3,2,1,0:T(8,128)(2,1)S(1)} %get-tuple-element.168.held_ref), channel_id=1, source_target_pairs={{0,1},{1,0},{2,3},{3,2},{4,5},{5,4},{6,7},{7,6},{8,9},{9,8},{10,11... | collective-permute-start | bytes 786440 | tf_op jit(solution)/shard_map/ppermute | solution.py:471
  72.0 14.8 %collective-permute-start.25 = (bf16[2,4,32,512]{3,2,1,0:T(8,128)(2,1)S(1)}, bf16[2,4,32,512]{3,2,1,0:T(8,128)(2,1)S(1)}, u32[]{:S(2)}, u32[]{:S(2)}) collective-permute-start(bf16[2,4,32,512]{3,2,1,0:T(8,128)(2,1)S(1)} %get-tuple-element.173.held_ref.refs_0_), channel_id=1, source_target_pairs={{0,8},{4,12},{8,0},{12,4},{16,24},{20,28},{24,16},{28,20},{1,9},{5... | collective-permute-start | bytes 786440 | tf_op jit(solution)/shard_map/ppermute | solution.py:471
  74.3 9.3 %collective-permute-start.24 = (bf16[1,4,32,512]{3,2,1,0:T(8,128)(2,1)S(1)}, bf16[1,4,32,512]{3,2,1,0:T(8,128)(2,1)S(1)}, u32[]{:S(2)}, u32[]{:S(2)}) collective-permute-start(bf16[1,4,32,512]{3,2,1,0:T(8,128)(2,1)S(1)} %get-tuple-element.170.held_ref), channel_id=1, source_target_pairs={{0,16},{4,20},{8,24},{12,28},{16,0},{20,4},{24,8},{28,12},{1,17},{... | collective-permute-start | bytes 393224 | tf_op jit(solution)/shard_map/ppermute | solution.py:471
  82.8 8.4 %collective-permute-start.26 = (bf16[1,4,32,512]{3,2,1,0:T(8,128)(2,1)S(1)}, bf16[1,4,32,512]{3,2,1,0:T(8,128)(2,1)S(1)}, u32[]{:S(2)}, u32[]{:S(2)}) collective-permute-start(bf16[1,4,32,512]{3,2,1,0:T(8,128)(2,1)S(1)} %get-tuple-element.175.held_ref), channel_id=1, source_target_pairs={{0,16},{4,20},{8,24},{12,28},{16,0},{20,4},{24,8},{28,12},{1,17},{... | collective-permute-start | bytes 393224 | tf_op jit(solution)/shard_map/ppermute | solution.py:471
  83.6 11.9 %collective-permute-start.28 = (bf16[2,4,32,512]{3,2,1,0:T(8,128)(2,1)S(1)}, bf16[2,4,32,512]{3,2,1,0:T(8,128)(2,1)S(1)}, u32[]{:S(2)}, u32[]{:S(2)}) collective-permute-start(bf16[2,4,32,512]{3,2,1,0:T(8,128)(2,1)S(1)} %get-tuple-element.179.held_ref.refs_3_), channel_id=1, source_target_pairs={{0,8},{4,12},{8,0},{12,4},{16,24},{20,28},{24,16},{28,20},{1,9},{5... | collective-permute-start | bytes 786440 | tf_op jit(solution)/shard_map/ppermute | solution.py:471
  87.4 15.3 %collective-permute-start.31 = (bf16[8,32,512]{2,1,0:T(8,128)(2,1)S(1)}, bf16[8,32,512]{2,1,0:T(8,128)(2,1)S(1)}, u32[]{:S(2)}, u32[]{:S(2)}) collective-permute-start(bf16[8,32,512]{2,1,0:T(8,128)(2,1)S(1)} %get-tuple-element.185), channel_id=1, source_target_pairs={{0,4},{4,0},{8,12},{12,8},{16,20},{20,16},{24,28},{28,24},{1,5},{5... | collective-permute-start | bytes 786440 | tf_op jit(solution)/shard_map/ppermute | solution.py:471
  91.3 11.4 %collective-permute-start.32 = (bf16[2,4,32,512]{3,2,1,0:T(8,128)(2,1)S(1)}, bf16[2,4,32,512]{3,2,1,0:T(8,128)(2,1)S(1)}, u32[]{:S(2)}, u32[]{:S(2)}) collective-permute-start(bf16[2,4,32,512]{3,2,1,0:T(8,128)(2,1)S(1)} %get-tuple-element.186.held_ref.refs_6_), channel_id=1, source_target_pairs={{0,8},{4,12},{8,0},{12,4},{16,24},{20,28},{24,16},{28,20},{1,9},{5... | collective-permute-start | bytes 786440 | tf_op jit(solution)/shard_map/ppermute | solution.py:471
  96.0 14.8 %collective-permute-start.35 = (bf16[8,32,512]{2,1,0:T(8,128)(2,1)S(1)}, bf16[8,32,512]{2,1,0:T(8,128)(2,1)S(1)}, u32[]{:S(2)}, u32[]{:S(2)}) collective-permute-start(bf16[8,32,512]{2,1,0:T(8,128)(2,1)S(1)} %get-tuple-element.192), channel_id=1, source_target_pairs={{0,4},{4,0},{8,12},{12,8},{16,20},{20,16},{24,28},{28,24},{1,5},{5... | collective-permute-start | bytes 786440 | tf_op jit(solution)/shard_map/ppermute | solution.py:471
  103.3 9.9 %collective-permute-start.37 = (bf16[8,32,512]{2,1,0:T(8,128)(2,1)S(1)}, bf16[8,32,512]{2,1,0:T(8,128)(2,1)S(1)}, u32[]{:S(2)}, u32[]{:S(2)}) collective-permute-start(bf16[8,32,512]{2,1,0:T(8,128)(2,1)S(1)} %get-tuple-element.195), channel_id=1, source_target_pairs={{0,4},{4,0},{8,12},{12,8},{16,20},{20,16},{24,28},{28,24},{1,5},{5... | collective-permute-start | bytes 786440 | tf_op jit(solution)/shard_map/ppermute | solution.py:471
  (24 other events, 142.2 us)

commit v10 on v9

--- a/solution.py
+++ b/solution.py
@@ -5,10 +5,10 @@
 from jax.experimental.pallas import tpu as pltpu
 from jax.sharding import PartitionSpec as P
 
-SHARES = (2, 2, 1, 2, 1)
+SHARES = (2, 2, 2, 1, 1)
 ORDER = (
-    1, 0, 3, 2, 1, 0, 4, 3, 1, 2, 0, 3, 1, 4, 0, 0, 2, 1, 2, 0, 3, 4, 4, 3, 1, 0, 3, 4, 1, 4, 2, 0,
-    3, 2, 4, 1, 2, 3, 4, 2,
+    0, 1, 2, 0, 1, 2, 1, 3, 4, 0, 2, 1, 1, 4, 1, 2, 3, 4, 0, 2, 0, 3, 3, 2, 4, 1, 0, 4, 2, 4, 3, 1,
+    0, 3, 4, 2, 3, 0, 4, 3,
 )
 READ_CAP = 2
 VMEM_BYTES = 12 * 1024 * 1024

time: 120 us -> 119 us (level)
  starting transfers between devices: 55.9 us -> 50.2 us
  waiting for transfers between devices: 36.1 us -> 41.2 us
    ppermute x40, starting transfers between devices: 55.9 us -> 50.2 us  [flip(): lax.ppermute(value, axis, [(d, d ^ bit) for d in range(lax.axis_size(axis...]
    ppermute x40, waiting for transfers between devices: 36.1 us -> 41.2 us  [flip(): lax.ppermute(value, axis, [(d, d ^ bit) for d in range(lax.axis_size(axis...]
  transfers between devices with their start and end apart: 40 -> 40, of which waited for: 19 -> 21; matrix products, arithmetic and copies ran while one was open for 0% -> 0% of each run, Pallas kernels for 14% -> 14%
where the time goes in v10:
time: 119 us; the launch traced here: 118 us
  starting transfers between devices  50.2 us (42%)
  waiting for transfers between devices  41.2 us (35%)
  Pallas kernels  22.7 us (19%)
  local copies, waits for them, and re-layouts  3.14 us (3%)
    ppermute x40, starting transfers between devices, flip(): lax.ppermute(value, axis, [(d, d ^ bit) for d in range(lax.axis_size(axis...  50.2 us
    ppermute x40, waiting for transfers between devices, flip(): lax.ppermute(value, axis, [(d, d ^ bit) for d in range(lax.axis_size(axis...  41.2 us
    pallas_call x45, Pallas kernels, call(): pl.pallas_call(body, out_shape=out_shape, in_specs=in_specs, out_specs=ou...  22.7 us
    unnamed x16, local copies, waits for them, and re-layouts  3.14 us
  transfers between devices with their start and end apart: 40, of which 21 were waited for; matrix products, arithmetic and copies ran while one was open for 0% of the time, Pallas kernels for 14%

profile of v10, /device:TPU:0, one launch (start us, length us, event | category | flops | bytes accessed | tf_op | source)
XLA Modules:
  0.0 118.4 jit_solution(342024126933781780)
XLA Ops:
  0.6 4.4 %shard_map.95 = (s32[256]{0:T(256)}, s32[16]{0:T(128)}, bf16[4,4,32,512]{3,2,1,0:T(8,128)(2,1)}, bf16[528,512]{1,0:T(8,128)(2,1)}, bf16[512,512]{1,0:T(8,128)(2,1)}) custom-call(s32[1]{0:T(128)} %bitcast.me_ref, s32[96]{0:T(128)} %slot_hbm.1, s32[96]{0:T(128)} %col_hbm.1, s32[96]{0:T(128)} %id_hbm.1, s32[8,4,8]{2,1,0:T(4,128)} %bitcast.22, s32[16]{0:T(128)} %readers_ref.3, ...), custom_call_target="tpu_custom_call" | custom-call | bytes 1 | tf_op jit(solution)/shard_map/pallas_call | solution.py:24
  5.1 3.0 %collective-permute-start.1 = (bf16[528,512]{1,0:T(8,128)(2,1)}, bf16[528,512]{1,0:T(8,128)(2,1)S(1)}, u32[]{:S(2)}, u32[]{:S(2)}) collective-permute-start(bf16[528,512]{1,0:T(8,128)(2,1)} %get-tuple-element.110), channel_id=1, source_target_pairs={{0,4},{4,0},{8,12},{12,8},{16,20},{20,16},{24,28},{28,24},{1,5},{5... | collective-permute-start | bytes 1622024 | tf_op jit(solution)/shard_map/ppermute | solution.py:471
  12.8 3.4 %shard_map.97 = (bf16[4,4,32,512]{3,2,1,0:T(8,128)(2,1)S(1)}, bf16[4,4,16,512]{3,2,1,0:T(8,128)(2,1)S(1)}, bf16[4,4,16,512]{3,2,1,0:T(8,128)(2,1)S(1)}, bf16[4,4,32,512]{3,2,1,0:T(8,128)(2,1)S(1)}, f32[8,128]{1,0:T(8,128)}) custom-call(s32[256]{0:T(256)S(1)} %copy-done.4, bf16[48,128,128]{2,1,0:T(8,128)(2,1)S(1)} %copy-done.1, bf16[512,512]{1,0:T(8,128)(2,1)S(1)} %copy-done.2), custom_call_target="tpu_custom_call" | custom-call | bytes 1 | tf_op jit(solution)/shard_map/pallas_call | solution.py:24
  16.7 2.3 %shard_map.96 = (bf16[4,4,32,512]{3,2,1,0:T(8,128)(2,1)S(1)}, bf16[4,4,32,512]{3,2,1,0:T(8,128)(2,1)S(1)}, bf16[4,4,16,512]{3,2,1,0:T(8,128)(2,1)S(1)}, bf16[4,4,16,512]{3,2,1,0:T(8,128)(2,1)S(1)}, f32[8,128]{1,0:T(8,128)S(1)}) custom-call(s32[256]{0:T(256)S(1)} %copy-done.4, bf16[48,128,128]{2,1,0:T(8,128)(2,1)S(1)} %copy-done.1, bf16[512,512]{1,0:T(8,128)(2,1)S(1)} %copy-done.2), custom_call_target="tpu_custom_call" | custom-call | bytes 1 | tf_op jit(solution)/shard_map/pallas_call | solution.py:24
  19.0 2.7 %collective-permute-done.got_ref = bf16[4,4,32,512]{3,2,1,0:T(8,128)(2,1)S(1)} collective-permute-done((bf16[4,4,32,512]{3,2,1,0:T(8,128)(2,1)}, bf16[4,4,32,512]{3,2,1,0:T(8,128)(2,1)S(1)}, u32[]{:S(2)}, u32[]{:S(2)}) %collective-permute-start) | collective-permute-done | bytes 524320 | tf_op jit(solution)/shard_map/ppermute | solution.py:471
  21.9 2.7 %collective-permute-start.3 = (bf16[2,4,32,512]{3,2,1,0:T(8,128)(2,1)S(1)}, bf16[2,4,32,512]{3,2,1,0:T(8,128)(2,1)S(1)}, u32[]{:S(2)}, u32[]{:S(2)}) collective-permute-start(bf16[2,4,32,512]{3,2,1,0:T(8,128)(2,1)S(1)} %get-tuple-element.117), channel_id=1, source_target_pairs={{0,16},{4,20},{8,24},{12,28},{16,0},{20,4},{24,8},{28,12},{1,17},{... | collective-permute-start | bytes 786440 | tf_op jit(solution)/shard_map/ppermute | solution.py:471
  27.2 4.6 %collective-permute-done.2.got_ref = bf16[4,4,32,512]{3,2,1,0:T(8,128)(2,1)S(1)} collective-permute-done((bf16[4,4,32,512]{3,2,1,0:T(8,128)(2,1)S(1)}, bf16[4,4,32,512]{3,2,1,0:T(8,128)(2,1)S(1)}, u32[]{:S(2)}, u32[]{:S(2)}) %collective-permute-start.2) | collective-permute-done | bytes 524320 | tf_op jit(solution)/shard_map/ppermute | solution.py:471
  36.6 2.3 %collective-permute-start.6 = (bf16[1,4,32,512]{3,2,1,0:T(8,128)(2,1)S(1)}, bf16[1,4,32,512]{3,2,1,0:T(8,128)(2,1)S(1)}, u32[]{:S(2)}, u32[]{:S(2)}) collective-permute-start(bf16[1,4,32,512]{3,2,1,0:T(8,128)(2,1)S(1)} %get-tuple-element.126), channel_id=1, source_target_pairs={{0,16},{4,20},{8,24},{12,28},{16,0},{20,4},{24,8},{28,12},{1,17},{... | collective-permute-start | bytes 393224 | tf_op jit(solution)/shard_map/ppermute | solution.py:471
  40.4 4.0 %collective-permute-done.5.got_ref = bf16[2,4,32,512]{3,2,1,0:T(8,128)(2,1)S(1)} collective-permute-done((bf16[2,4,32,512]{3,2,1,0:T(8,128)(2,1)S(1)}, bf16[2,4,32,512]{3,2,1,0:T(8,128)(2,1)S(1)}, u32[]{:S(2)}, u32[]{:S(2)}) %collective-permute-start.5) | collective-permute-done | bytes 262176 | tf_op jit(solution)/shard_map/ppermute | solution.py:471
  49.3 2.6 %collective-permute-done.10.got_ref = bf16[1,4,32,512]{3,2,1,0:T(8,128)(2,1)S(1)} collective-permute-done((bf16[1,4,32,512]{3,2,1,0:T(8,128)(2,1)S(1)}, bf16[1,4,32,512]{3,2,1,0:T(8,128)(2,1)S(1)}, u32[]{:S(2)}, u32[]{:S(2)}) %collective-permute-start.10) | collective-permute-done | bytes 131104 | tf_op jit(solution)/shard_map/ppermute | solution.py:471
  60.0 4.2 %collective-permute-done.14.got_ref = bf16[1,4,32,512]{3,2,1,0:T(8,128)(2,1)S(1)} collective-permute-done((bf16[1,4,32,512]{3,2,1,0:T(8,128)(2,1)S(1)}, bf16[1,4,32,512]{3,2,1,0:T(8,128)(2,1)S(1)}, u32[]{:S(2)}, u32[]{:S(2)}) %collective-permute-start.14) | collective-permute-done | bytes 131104 | tf_op jit(solution)/shard_map/ppermute | solution.py:471
  66.8 2.7 %collective-permute-start.25 = (bf16[2,4,32,512]{3,2,1,0:T(8,128)(2,1)S(1)}, bf16[2,4,32,512]{3,2,1,0:T(8,128)(2,1)S(1)}, u32[]{:S(2)}, u32[]{:S(2)}) collective-permute-start(bf16[2,4,32,512]{3,2,1,0:T(8,128)(2,1)S(1)} %get-tuple-element.173.held_ref.refs_0_), channel_id=1, source_target_pairs={{0,8},{4,12},{8,0},{12,4},{16,24},{20,28},{24,16},{28,20},{1,9},{5... | collective-permute-start | bytes 786440 | tf_op jit(solution)/shard_map/ppermute | solution.py:471
  70.9 2.4 %collective-permute-done.21.got_ref = bf16[1,4,16,512]{3,2,1,0:T(8,128)(2,1)S(1)} collective-permute-done((bf16[1,4,16,512]{3,2,1,0:T(8,128)(2,1)S(1)}, bf16[1,4,16,512]{3,2,1,0:T(8,128)(2,1)S(1)}, u32[]{:S(2)}, u32[]{:S(2)}) %collective-permute-start.21) | collective-permute-done | bytes 65568 | tf_op jit(solution)/shard_map/ppermute | solution.py:471
  75.1 2.5 %collective-permute-done.22.got_ref = bf16[1,4,16,512]{3,2,1,0:T(8,128)(2,1)S(1)} collective-permute-done((bf16[1,4,16,512]{3,2,1,0:T(8,128)(2,1)S(1)}, bf16[1,4,16,512]{3,2,1,0:T(8,128)(2,1)S(1)}, u32[]{:S(2)}, u32[]{:S(2)}) %collective-permute-start.22) | collective-permute-done | bytes 65568 | tf_op jit(solution)/shard_map/ppermute | solution.py:471
  79.1 2.4 %collective-permute-start.28 = (bf16[2,4,32,512]{3,2,1,0:T(8,128)(2,1)S(1)}, bf16[2,4,32,512]{3,2,1,0:T(8,128)(2,1)S(1)}, u32[]{:S(2)}, u32[]{:S(2)}) collective-permute-start(bf16[2,4,32,512]{3,2,1,0:T(8,128)(2,1)S(1)} %get-tuple-element.179.held_ref.refs_3_), channel_id=1, source_target_pairs={{0,8},{4,12},{8,0},{12,4},{16,24},{20,28},{24,16},{28,20},{1,9},{5... | collective-permute-start | bytes 786440 | tf_op jit(solution)/shard_map/ppermute | solution.py:471
  83.3 2.5 %collective-permute-done.24.got_ref = bf16[1,4,16,512]{3,2,1,0:T(8,128)(2,1)S(1)} collective-permute-done((bf16[1,4,16,512]{3,2,1,0:T(8,128)(2,1)S(1)}, bf16[1,4,16,512]{3,2,1,0:T(8,128)(2,1)S(1)}, u32[]{:S(2)}, u32[]{:S(2)}) %collective-permute-start.24) | collective-permute-done | bytes 65568 | tf_op jit(solution)/shard_map/ppermute | solution.py:471
  86.5 2.7 %collective-permute-start.31 = (bf16[8,32,512]{2,1,0:T(8,128)(2,1)S(1)}, bf16[8,32,512]{2,1,0:T(8,128)(2,1)S(1)}, u32[]{:S(2)}, u32[]{:S(2)}) collective-permute-start(bf16[8,32,512]{2,1,0:T(8,128)(2,1)S(1)} %get-tuple-element.185), channel_id=1, source_target_pairs={{0,4},{4,0},{8,12},{12,8},{16,20},{20,16},{24,28},{28,24},{1,5},{5... | collective-permute-start | bytes 786440 | tf_op jit(solution)/shard_map/ppermute | solution.py:471
  90.1 3.1 %collective-permute-start.29 = (bf16[1,4,16,512]{3,2,1,0:T(8,128)(2,1)S(1)}, bf16[1,4,16,512]{3,2,1,0:T(8,128)(2,1)S(1)}, u32[]{:S(2)}, u32[]{:S(2)}) collective-permute-start(bf16[1,4,16,512]{3,2,1,0:T(8,128)(2,1)S(1)} %get-tuple-element.181.held_ref), channel_id=1, source_target_pairs={{0,16},{4,20},{8,24},{12,28},{16,0},{20,4},{24,8},{28,12},{1,17},{... | collective-permute-start | bytes 196616 | tf_op jit(solution)/shard_map/ppermute | solution.py:471
  94.1 2.8 %collective-permute-done.29.got_ref = bf16[1,4,16,512]{3,2,1,0:T(8,128)(2,1)S(1)} collective-permute-done((bf16[1,4,16,512]{3,2,1,0:T(8,128)(2,1)S(1)}, bf16[1,4,16,512]{3,2,1,0:T(8,128)(2,1)S(1)}, u32[]{:S(2)}, u32[]{:S(2)}) %collective-permute-start.29) | collective-permute-done | bytes 65568 | tf_op jit(solution)/shard_map/ppermute | solution.py:471
  97.4 3.4 %collective-permute-start.33 = (bf16[1,4,16,512]{3,2,1,0:T(8,128)(2,1)S(1)}, bf16[1,4,16,512]{3,2,1,0:T(8,128)(2,1)S(1)}, u32[]{:S(2)}, u32[]{:S(2)}) collective-permute-start(bf16[1,4,16,512]{3,2,1,0:T(8,128)(2,1)S(1)} %get-tuple-element.188.held_ref), channel_id=1, source_target_pairs={{0,16},{4,20},{8,24},{12,28},{16,0},{20,4},{24,8},{28,12},{1,17},{... | collective-permute-start | bytes 196616 | tf_op jit(solution)/shard_map/ppermute | solution.py:471
  103.4 3.9 %collective-permute-start.36 = (bf16[2,4,16,512]{3,2,1,0:T(8,128)(2,1)S(1)}, bf16[2,4,16,512]{3,2,1,0:T(8,128)(2,1)S(1)}, u32[]{:S(2)}, u32[]{:S(2)}) collective-permute-start(bf16[2,4,16,512]{3,2,1,0:T(8,128)(2,1)S(1)} %get-tuple-element.193.held_ref.refs_0_), channel_id=1, source_target_pairs={{0,8},{4,12},{8,0},{12,4},{16,24},{20,28},{24,16},{28,20},{1,9},{5... | collective-permute-start | bytes 393224 | tf_op jit(solution)/shard_map/ppermute | solution.py:471
  108.2 2.0 %collective-permute-done.36.got_ref.refs_1_ = bf16[2,4,16,512]{3,2,1,0:T(8,128)(2,1)S(1)} collective-permute-done((bf16[2,4,16,512]{3,2,1,0:T(8,128)(2,1)S(1)}, bf16[2,4,16,512]{3,2,1,0:T(8,128)(2,1)S(1)}, u32[]{:S(2)}, u32[]{:S(2)}) %collective-permute-start.36) | collective-permute-done | bytes 131104 | tf_op jit(solution)/shard_map/ppermute | solution.py:471
  111.2 2.6 %collective-permute-done.38.value_ref.refs_11_ = bf16[8,16,512]{2,1,0:T(8,128)(2,1)S(1)} collective-permute-done((bf16[8,16,512]{2,1,0:T(8,128)(2,1)S(1)}, bf16[8,16,512]{2,1,0:T(8,128)(2,1)S(1)}, u32[]{:S(2)}, u32[]{:S(2)}) %collective-permute-start.38) | collective-permute-done | bytes 131104 | tf_op jit(solution)/shard_map/ppermute | solution.py:471
  113.8 2.5 %shard_map.138 = (bf16[4,128,512]{2,1,0:T(8,128)(2,1)}, bf16[16,128,512]{2,1,0:T(8,128)(2,1)}, f32[8,128]{1,0:T(8,128)S(1)}) custom-call(f32[8,128]{1,0:T(8,128)S(1)} %shard_map.137.token_ref, s32[1]{0:T(128)} %bitcast.me_ref, s32[16]{0:T(128)S(1)} %copy-done.3, s32[16]{0:T(128)S(1)} %copy-done.5, ...), custom_call_target="tpu_custom_call" | custom-call | bytes 1 | tf_op jit(solution)/shard_map/pallas_call | solution.py:24
  (117 shorter events, 45.5 us)
Async XLA Ops:
  5.1 19.5 %collective-permute-start.1 = (bf16[528,512]{1,0:T(8,128)(2,1)}, bf16[528,512]{1,0:T(8,128)(2,1)S(1)}, u32[]{:S(2)}, u32[]{:S(2)}) collective-permute-start(bf16[528,512]{1,0:T(8,128)(2,1)} %get-tuple-element.110), channel_id=1, source_target_pairs={{0,4},{4,0},{8,12},{12,8},{16,20},{20,16},{24,28},{28,24},{1,5},{5... | collective-permute-start | bytes 1622024 | tf_op jit(solution)/shard_map/ppermute | solution.py:471
  8.1 13.6 %collective-permute-start = (bf16[4,4,32,512]{3,2,1,0:T(8,128)(2,1)}, bf16[4,4,32,512]{3,2,1,0:T(8,128)(2,1)S(1)}, u32[]{:S(2)}, u32[]{:S(2)}) collective-permute-start(bf16[4,4,32,512]{3,2,1,0:T(8,128)(2,1)} %get-tuple-element.107), channel_id=1, source_target_pairs={{0,8},{4,12},{8,0},{12,4},{16,24},{20,28},{24,16},{28,20},{1,9},{5... | collective-permute-start | bytes 1572872 | tf_op jit(solution)/shard_map/ppermute | solution.py:471
  16.2 15.6 %collective-permute-start.2 = (bf16[4,4,32,512]{3,2,1,0:T(8,128)(2,1)S(1)}, bf16[4,4,32,512]{3,2,1,0:T(8,128)(2,1)S(1)}, u32[]{:S(2)}, u32[]{:S(2)}) collective-permute-start(bf16[4,4,32,512]{3,2,1,0:T(8,128)(2,1)S(1)} %get-tuple-element.114), channel_id=1, source_target_pairs={{0,4},{4,0},{8,12},{12,8},{16,20},{20,16},{24,28},{28,24},{1,5},{5... | collective-permute-start | bytes 1572872 | tf_op jit(solution)/shard_map/ppermute | solution.py:471
  21.9 14.0 %collective-permute-start.3 = (bf16[2,4,32,512]{3,2,1,0:T(8,128)(2,1)S(1)}, bf16[2,4,32,512]{3,2,1,0:T(8,128)(2,1)S(1)}, u32[]{:S(2)}, u32[]{:S(2)}) collective-permute-start(bf16[2,4,32,512]{3,2,1,0:T(8,128)(2,1)S(1)} %get-tuple-element.117), channel_id=1, source_target_pairs={{0,16},{4,20},{8,24},{12,28},{16,0},{20,4},{24,8},{28,12},{1,17},{... | collective-permute-start | bytes 786440 | tf_op jit(solution)/shard_map/ppermute | solution.py:471
  24.9 11.6 %collective-permute-start.4 = (bf16[2,4,32,512]{3,2,1,0:T(8,128)(2,1)S(1)}, bf16[2,4,32,512]{3,2,1,0:T(8,128)(2,1)S(1)}, u32[]{:S(2)}, u32[]{:S(2)}) collective-permute-start(bf16[2,4,32,512]{3,2,1,0:T(8,128)(2,1)S(1)} %get-tuple-element.120), channel_id=1, source_target_pairs={{0,8},{4,12},{8,0},{12,4},{16,24},{20,28},{24,16},{28,20},{1,9},{5... | collective-permute-start | bytes 786440 | tf_op jit(solution)/shard_map/ppermute | solution.py:471
  32.1 12.3 %collective-permute-start.5 = (bf16[2,4,32,512]{3,2,1,0:T(8,128)(2,1)S(1)}, bf16[2,4,32,512]{3,2,1,0:T(8,128)(2,1)S(1)}, u32[]{:S(2)}, u32[]{:S(2)}) collective-permute-start(bf16[2,4,32,512]{3,2,1,0:T(8,128)(2,1)S(1)} %get-tuple-element.123), channel_id=1, source_target_pairs={{0,8},{4,12},{8,0},{12,4},{16,24},{20,28},{24,16},{28,20},{1,9},{5... | collective-permute-start | bytes 786440 | tf_op jit(solution)/shard_map/ppermute | solution.py:471
  34.0 12.7 %collective-permute-start.7 = (bf16[4,4,16,512]{3,2,1,0:T(8,128)(2,1)S(1)}, bf16[4,4,16,512]{3,2,1,0:T(8,128)(2,1)S(1)}, u32[]{:S(2)}, u32[]{:S(2)}) collective-permute-start(bf16[4,4,16,512]{3,2,1,0:T(8,128)(2,1)S(1)} %get-tuple-element.129), channel_id=1, source_target_pairs={{0,4},{4,0},{8,12},{12,8},{16,20},{20,16},{24,28},{28,24},{1,5},{5... | collective-permute-start | bytes 786440 | tf_op jit(solution)/shard_map/ppermute | solution.py:471
  35.4 12.4 %collective-permute-start.8 = (bf16[4,4,16,512]{3,2,1,0:T(8,128)(2,1)S(1)}, bf16[4,4,16,512]{3,2,1,0:T(8,128)(2,1)S(1)}, u32[]{:S(2)}, u32[]{:S(2)}) collective-permute-start(bf16[4,4,16,512]{3,2,1,0:T(8,128)(2,1)S(1)} %get-tuple-element.132), channel_id=1, source_target_pairs={{0,4},{4,0},{8,12},{12,8},{16,20},{20,16},{24,28},{28,24},{1,5},{5... | collective-permute-start | bytes 786440 | tf_op jit(solution)/shard_map/ppermute | solution.py:471
  36.6 8.4 %collective-permute-start.6 = (bf16[1,4,32,512]{3,2,1,0:T(8,128)(2,1)S(1)}, bf16[1,4,32,512]{3,2,1,0:T(8,128)(2,1)S(1)}, u32[]{:S(2)}, u32[]{:S(2)}) collective-permute-start(bf16[1,4,32,512]{3,2,1,0:T(8,128)(2,1)S(1)} %get-tuple-element.126), channel_id=1, source_target_pairs={{0,16},{4,20},{8,24},{12,28},{16,0},{20,4},{24,8},{28,12},{1,17},{... | collective-permute-start | bytes 393224 | tf_op jit(solution)/shard_map/ppermute | solution.py:471
  38.9 10.4 %collective-permute-start.9 = (bf16[1,4,32,512]{3,2,1,0:T(8,128)(2,1)S(1)}, bf16[1,4,32,512]{3,2,1,0:T(8,128)(2,1)S(1)}, u32[]{:S(2)}, u32[]{:S(2)}) collective-permute-start(bf16[1,4,32,512]{3,2,1,0:T(8,128)(2,1)S(1)} %get-tuple-element.135), channel_id=1, source_target_pairs={{0,4},{4,0},{8,12},{12,8},{16,20},{20,16},{24,28},{28,24},{1,5},{5... | collective-permute-start | bytes 393224 | tf_op jit(solution)/shard_map/ppermute | solution.py:471
  52.1 7.5 %collective-permute-start.13 = (bf16[2,4,16,512]{3,2,1,0:T(8,128)(2,1)}, bf16[2,4,16,512]{3,2,1,0:T(8,128)(2,1)S(1)}, u32[]{:S(2)}, u32[]{:S(2)}) collective-permute-start(bf16[2,4,16,512]{3,2,1,0:T(8,128)(2,1)} %get-tuple-element.145), channel_id=1, source_target_pairs={{0,8},{4,12},{8,0},{12,4},{16,24},{20,28},{24,16},{28,20},{1,9},{5... | collective-permute-start | bytes 393224 | tf_op jit(solution)/shard_map/ppermute | solution.py:471
  54.1 10.2 %collective-permute-start.14 = (bf16[1,4,32,512]{3,2,1,0:T(8,128)(2,1)S(1)}, bf16[1,4,32,512]{3,2,1,0:T(8,128)(2,1)S(1)}, u32[]{:S(2)}, u32[]{:S(2)}) collective-permute-start(bf16[1,4,32,512]{3,2,1,0:T(8,128)(2,1)S(1)} %get-tuple-element.147.held_ref), channel_id=1, source_target_pairs={{0,16},{4,20},{8,24},{12,28},{16,0},{20,4},{24,8},{28,12},{1,17},{... | collective-permute-start | bytes 393224 | tf_op jit(solution)/shard_map/ppermute | solution.py:471
  55.8 8.4 %collective-permute-start.15 = (bf16[1,4,32,512]{3,2,1,0:T(8,128)(2,1)S(1)}, bf16[1,4,32,512]{3,2,1,0:T(8,128)(2,1)S(1)}, u32[]{:S(2)}, u32[]{:S(2)}) collective-permute-start(bf16[1,4,32,512]{3,2,1,0:T(8,128)(2,1)S(1)} %bitcast.12), channel_id=1, source_target_pairs={{0,2},{1,3},{2,0},{3,1},{4,6},{5,7},{6,4},{7,5},{8,10},{9,11},{10,... | collective-permute-start | bytes 393224 | tf_op jit(solution)/shard_map/ppermute | solution.py:471
  57.3 7.8 %collective-permute-start.16 = (bf16[2,4,16,512]{3,2,1,0:T(8,128)(2,1)S(1)}, bf16[2,4,16,512]{3,2,1,0:T(8,128)(2,1)S(1)}, u32[]{:S(2)}, u32[]{:S(2)}) collective-permute-start(bf16[2,4,16,512]{3,2,1,0:T(8,128)(2,1)S(1)} %copy-done.7), channel_id=1, source_target_pairs={{0,8},{4,12},{8,0},{12,4},{16,24},{20,28},{24,16},{28,20},{1,9},{5... | collective-permute-start | bytes 393224 | tf_op jit(solution)/shard_map/ppermute | solution.py:471
  58.8 7.5 %collective-permute-start.18 = (bf16[1,4,32,512]{3,2,1,0:T(8,128)(2,1)S(1)}, bf16[1,4,32,512]{3,2,1,0:T(8,128)(2,1)S(1)}, u32[]{:S(2)}, u32[]{:S(2)}) collective-permute-start(bf16[1,4,32,512]{3,2,1,0:T(8,128)(2,1)S(1)} %bitcast.10), channel_id=1, source_target_pairs={{0,2},{1,3},{2,0},{3,1},{4,6},{5,7},{6,4},{7,5},{8,10},{9,11},{10,... | collective-permute-start | bytes 393224 | tf_op jit(solution)/shard_map/ppermute | solution.py:471
  66.8 19.1 %collective-permute-start.25 = (bf16[2,4,32,512]{3,2,1,0:T(8,128)(2,1)S(1)}, bf16[2,4,32,512]{3,2,1,0:T(8,128)(2,1)S(1)}, u32[]{:S(2)}, u32[]{:S(2)}) collective-permute-start(bf16[2,4,32,512]{3,2,1,0:T(8,128)(2,1)S(1)} %get-tuple-element.173.held_ref.refs_0_), channel_id=1, source_target_pairs={{0,8},{4,12},{8,0},{12,4},{16,24},{20,28},{24,16},{28,20},{1,9},{5... | collective-permute-start | bytes 786440 | tf_op jit(solution)/shard_map/ppermute | solution.py:471
  70.0 9.1 %collective-permute-start.23 = (bf16[1,4,32,512]{3,2,1,0:T(8,128)(2,1)S(1)}, bf16[1,4,32,512]{3,2,1,0:T(8,128)(2,1)S(1)}, u32[]{:S(2)}, u32[]{:S(2)}) collective-permute-start(bf16[1,4,32,512]{3,2,1,0:T(8,128)(2,1)S(1)} %get-tuple-element.168.held_ref), channel_id=1, source_target_pairs={{0,16},{4,20},{8,24},{12,28},{16,0},{20,4},{24,8},{28,12},{1,17},{... | collective-permute-start | bytes 393224 | tf_op jit(solution)/shard_map/ppermute | solution.py:471
  74.9 14.3 %collective-permute-start.26 = (bf16[1,4,32,512]{3,2,1,0:T(8,128)(2,1)S(1)}, bf16[1,4,32,512]{3,2,1,0:T(8,128)(2,1)S(1)}, u32[]{:S(2)}, u32[]{:S(2)}) collective-permute-start(bf16[1,4,32,512]{3,2,1,0:T(8,128)(2,1)S(1)} %get-tuple-element.175.held_ref), channel_id=1, source_target_pairs={{0,16},{4,20},{8,24},{12,28},{16,0},{20,4},{24,8},{28,12},{1,17},{... | collective-permute-start | bytes 393224 | tf_op jit(solution)/shard_map/ppermute | solution.py:471
  79.1 14.1 %collective-permute-start.28 = (bf16[2,4,32,512]{3,2,1,0:T(8,128)(2,1)S(1)}, bf16[2,4,32,512]{3,2,1,0:T(8,128)(2,1)S(1)}, u32[]{:S(2)}, u32[]{:S(2)}) collective-permute-start(bf16[2,4,32,512]{3,2,1,0:T(8,128)(2,1)S(1)} %get-tuple-element.179.held_ref.refs_3_), channel_id=1, source_target_pairs={{0,8},{4,12},{8,0},{12,4},{16,24},{20,28},{24,16},{28,20},{1,9},{5... | collective-permute-start | bytes 786440 | tf_op jit(solution)/shard_map/ppermute | solution.py:471
  86.5 14.9 %collective-permute-start.31 = (bf16[8,32,512]{2,1,0:T(8,128)(2,1)S(1)}, bf16[8,32,512]{2,1,0:T(8,128)(2,1)S(1)}, u32[]{:S(2)}, u32[]{:S(2)}) collective-permute-start(bf16[8,32,512]{2,1,0:T(8,128)(2,1)S(1)} %get-tuple-element.185), channel_id=1, source_target_pairs={{0,4},{4,0},{8,12},{12,8},{16,20},{20,16},{24,28},{28,24},{1,5},{5... | collective-permute-start | bytes 786440 | tf_op jit(solution)/shard_map/ppermute | solution.py:471
  89.2 12.2 %collective-permute-start.32 = (bf16[2,4,32,512]{3,2,1,0:T(8,128)(2,1)S(1)}, bf16[2,4,32,512]{3,2,1,0:T(8,128)(2,1)S(1)}, u32[]{:S(2)}, u32[]{:S(2)}) collective-permute-start(bf16[2,4,32,512]{3,2,1,0:T(8,128)(2,1)S(1)} %get-tuple-element.186.held_ref.refs_6_), channel_id=1, source_target_pairs={{0,8},{4,12},{8,0},{12,4},{16,24},{20,28},{24,16},{28,20},{1,9},{5... | collective-permute-start | bytes 786440 | tf_op jit(solution)/shard_map/ppermute | solution.py:471
  89.4 7.6 %collective-permute-start.30 = (bf16[2,4,16,512]{3,2,1,0:T(8,128)(2,1)S(1)}, bf16[2,4,16,512]{3,2,1,0:T(8,128)(2,1)S(1)}, u32[]{:S(2)}, u32[]{:S(2)}) collective-permute-start(bf16[2,4,16,512]{3,2,1,0:T(8,128)(2,1)S(1)} %get-tuple-element.183.held_ref), channel_id=1, source_target_pairs={{0,1},{1,0},{2,3},{3,2},{4,5},{5,4},{6,7},{7,6},{8,9},{9,8},{10,11... | collective-permute-start | bytes 393224 | tf_op jit(solution)/shard_map/ppermute | solution.py:471
  93.8 14.5 %collective-permute-start.35 = (bf16[8,32,512]{2,1,0:T(8,128)(2,1)S(1)}, bf16[8,32,512]{2,1,0:T(8,128)(2,1)S(1)}, u32[]{:S(2)}, u32[]{:S(2)}) collective-permute-start(bf16[8,32,512]{2,1,0:T(8,128)(2,1)S(1)} %get-tuple-element.192), channel_id=1, source_target_pairs={{0,4},{4,0},{8,12},{12,8},{16,20},{20,16},{24,28},{28,24},{1,5},{5... | collective-permute-start | bytes 786440 | tf_op jit(solution)/shard_map/ppermute | solution.py:471
  102.0 9.2 %collective-permute-start.37 = (bf16[8,32,512]{2,1,0:T(8,128)(2,1)S(1)}, bf16[8,32,512]{2,1,0:T(8,128)(2,1)S(1)}, u32[]{:S(2)}, u32[]{:S(2)}) collective-permute-start(bf16[8,32,512]{2,1,0:T(8,128)(2,1)S(1)} %get-tuple-element.195), channel_id=1, source_target_pairs={{0,4},{4,0},{8,12},{12,8},{16,20},{20,16},{24,28},{28,24},{1,5},{5... | collective-permute-start | bytes 786440 | tf_op jit(solution)/shard_map/ppermute | solution.py:471
  (24 other events, 142.1 us)

commit v11 on v10

--- a/solution.py
+++ b/solution.py
@@ -5,10 +5,9 @@
 from jax.experimental.pallas import tpu as pltpu
 from jax.sharding import PartitionSpec as P
 
-SHARES = (2, 2, 2, 1, 1)
+SHARES = (2, 3, 2, 1)
 ORDER = (
-    0, 1, 2, 0, 1, 2, 1, 3, 4, 0, 2, 1, 1, 4, 1, 2, 3, 4, 0, 2, 0, 3, 3, 2, 4, 1, 0, 4, 2, 4, 3, 1,
-    0, 3, 4, 2, 3, 0, 4, 3,
+    0, 1, 0, 2, 0, 1, 3, 2, 1, 0, 0, 2, 1, 1, 0, 3, 2, 1, 0, 2, 3, 3, 2, 0, 3, 1, 3, 2, 3, 1, 2, 3,
 )
 READ_CAP = 2
 VMEM_BYTES = 12 * 1024 * 1024
@@ -405,37 +404,44 @@
     return call(body, [TOKEN], [VMEM] * 2, [VMEM], (token, value))
 
 
-def lay_out(token, me, readers, entry, offsets, items, outputs, block):
+def lay_out(token, me, readers, entry, offsets, nears, fars, outputs, block):
     count = readers.shape[0]
-    half_held, blocks, _, width = items[0][0].shape
+    width = fars[0][0].shape[2]
+    blocks = outputs[0].shape[0] if outputs else nears[0][0].shape[1]
     slots = len(offsets) * READ_CAP
-    arrays = [array for item in items for array in item[:3]]
+    arrays = [array for held, got, _ in nears for array in (held, got)] + [far for far, _ in fars]
 
     def body(token_ref, me_ref, readers_ref, entry_ref, *refs):
-        hidden_ref, ghost_ref, token_out, sems = refs[-4:]
+        hidden_ref, ghost_ref, token_out, near_sems, far_sems = refs[-5:]
+        near_refs, far_refs = refs[: 2 * len(nears)], refs[2 * len(nears) : len(arrays)]
 
         def each(act):
-            for number, item in enumerate(items):
-                held_ref, got_ref, far_ref = refs[3 * number : 3 * number + 3]
-                rows = pl.ds(*item[3])
-                act(pltpu.make_async_copy(held_ref.at[0], hidden_ref.at[:, rows], sems.at[number, 2 * slots]))
+            for number, (held, _, span) in enumerate(nears):
+                held_ref, got_ref = near_refs[2 * number : 2 * number + 2]
+                part = pl.ds(*span)
+                act(pltpu.make_async_copy(held_ref.at[0], hidden_ref.at[:, part], near_sems.at[number, slots]))
                 for i in range(slots):
                     n, j = i // READ_CAP, i % READ_CAP
-                    near = entry_ref[(me_ref[0] ^ offsets[n]) * READ_CAP + j]
-                    source = held_ref if n < half_held else got_ref
-
-                    @pl.when(near >= 0)
+                    listed = entry_ref[(me_ref[0] ^ offsets[n]) * READ_CAP + j]
+                    source = held_ref if n < held.shape[0] else got_ref
+                    row = n % held.shape[0]
+
+                    @pl.when(listed >= 0)
                     def _():
-                        _, b = split(readers_ref[near], blocks)
-                        target = ghost_ref.at[near, rows]
-                        act(pltpu.make_async_copy(source.at[n % half_held, b], target, sems.at[number, i]))
-
-                    across = entry_ref[(me_ref[0] ^ 1 ^ offsets[n]) * READ_CAP + j]
-
-                    @pl.when(across >= 0)
+                        _, b = split(readers_ref[listed], blocks)
+                        target = ghost_ref.at[listed, part]
+                        act(pltpu.make_async_copy(source.at[row, b], target, near_sems.at[number, i]))
+
+            for number, (_, span) in enumerate(fars):
+                part = pl.ds(*span)
+                for i in range(slots):
+                    n, j = i // READ_CAP, i % READ_CAP
+                    listed = entry_ref[(me_ref[0] ^ 1 ^ offsets[n]) * READ_CAP + j]
+
+                    @pl.when(listed >= 0)
                     def _():
-                        target = ghost_ref.at[across, rows]
-                        act(pltpu.make_async_copy(far_ref.at[i], target, sems.at[number, slots + i]))
+                        target = ghost_ref.at[listed, part]
+                        act(pltpu.make_async_copy(far_refs[number].at[i], target, far_sems.at[number, i]))
 
         each(lambda copy: copy.start())
         token_out[...] = token_ref[...]
@@ -452,7 +458,10 @@
         [VMEM] + [SMEM] * 3 + [VMEM] * len(arrays) + [HBM] * len(outputs),
         [HBM, HBM, VMEM],
         operands,
-        [pltpu.SemaphoreType.DMA((len(items), 2 * slots + 1))],
+        [
+            pltpu.SemaphoreType.DMA((max(len(nears), 1), slots + 1)),
+            pltpu.SemaphoreType.DMA((len(fars), slots)),
+        ],
         aliases={len(operands) - 2: 0, len(operands) - 1: 1} if outputs else None,
     )
 
@@ -499,7 +508,8 @@
             (held,) = chained(join, held, got)
             bit //= 2
 
-    choice = None
+    choice, nears, fars = None, [], []
+    ended = object()
 
     def one_part(part):
         nonlocal choice
@@ -518,9 +528,10 @@
         (mixed,) = chained(mix, mine, offsets_of(feats, 1), held, got, weight)
         held, got = yield from spread(mixed, edges, 2, "edge")
         (picked,) = chained(pick, choice, held, got)
+        nears.append((held, got, spans[part]))
         far = flip(picked, 1)
         yield
-        return held, got, far, spans[part]
+        fars.append((far, spans[part]))
 
     def links_of(bit):
         return {"x": 1.0} if bit == 1 else {"end": 1.0} if bit == 2 else {"end": 1.0, "middle": 2.0}
@@ -538,18 +549,12 @@
         next(step)
     known = sorted(ORDER) == [part for part, way in enumerate(ways) for _ in way]
     *order, last = ORDER if known else planned_order(ways)
-    ended = []
     for part in order:
-        try:
-            next(steps[part])
-        except StopIteration as end:
-            ended.append(end.value)
-            chained(touch, end.value[2])
-    outputs = chained(lay_out, me, readers, entry, columns, ended, (), block)
-    try:
-        next(steps[last])
-    except StopIteration as end:
-        outputs = chained(lay_out, me, readers, entry, columns, [end.value], outputs, block)
+        if next(steps[part], ended) is ended:
+            chained(touch, fars[-1][0])
+    outputs = chained(lay_out, me, readers, entry, columns, nears, fars, (), block)
+    next(steps[last], None)
+    outputs = chained(lay_out, me, readers, entry, columns, [], fars[-1:], outputs, block)
     hidden, ghosts = outputs
     return hidden.reshape(blocks * block, width), ghosts.reshape(-1, width)
 

time: 119 us -> 126 us (1.059)
  waiting for transfers between devices: 41.2 us -> 62.1 us
  starting transfers between devices: 50.2 us -> 36.9 us
    ppermute x40 -> x32, waiting for transfers between devices: 41.2 us -> 62.1 us  [flip(): lax.ppermute(value, axis, [(d, d ^ bit) for d in range(lax.axis_size(axis...]
    ppermute x40 -> x32, starting transfers between devices: 50.2 us -> 36.9 us  [flip(): lax.ppermute(value, axis, [(d, d ^ bit) for d in range(lax.axis_size(axis...]
    pallas_call x45 -> x37, Pallas kernels: 22.7 us -> 22.8 us  [call(): pl.pallas_call(body, out_shape=out_shape, in_specs=in_specs, out_specs=ou...]
  transfers between devices with their start and end apart: 40 -> 32, of which waited for: 21 -> 18; matrix products, arithmetic and copies ran while one was open for 0% -> 0% of each run, Pallas kernels for 14% -> 13%
where the time goes in v11:
time: 126 us
  waiting for transfers between devices  62.1 us (49%)
  starting transfers between devices  36.9 us (29%)
  Pallas kernels  22.8 us (18%)
  local copies, waits for them, and re-layouts  3.15 us (2%)
    ppermute x32, waiting for transfers between devices, flip(): lax.ppermute(value, axis, [(d, d ^ bit) for d in range(lax.axis_size(axis...  62.1 us
    ppermute x32, starting transfers between devices, flip(): lax.ppermute(value, axis, [(d, d ^ bit) for d in range(lax.axis_size(axis...  36.9 us
    pallas_call x37, Pallas kernels, call(): pl.pallas_call(body, out_shape=out_shape, in_specs=in_specs, out_specs=ou...  22.8 us
    unnamed x16, local copies, waits for them, and re-layouts  3.15 us
  transfers between devices with their start and end apart: 32, of which 18 were waited for; matrix products, arithmetic and copies ran while one was open for 0% of the time, Pallas kernels for 13%

profile of v11, /device:TPU:0, one launch (start us, length us, event | category | flops | bytes accessed | tf_op | source)
XLA Modules:
  0.0 126.0 jit_solution(9453078155762650020)
XLA Ops:
  0.6 4.7 %shard_map.95 = (s32[256]{0:T(256)}, s32[16]{0:T(128)}, bf16[4,4,32,512]{3,2,1,0:T(8,128)(2,1)}, bf16[784,512]{1,0:T(8,128)(2,1)}, bf16[512,512]{1,0:T(8,128)(2,1)}) custom-call(s32[1]{0:T(128)} %bitcast.me_ref, s32[96]{0:T(128)} %slot_hbm.1, s32[96]{0:T(128)} %col_hbm.1, s32[96]{0:T(128)} %id_hbm.1, s32[8,4,8]{2,1,0:T(4,128)} %bitcast.19, s32[16]{0:T(128)} %readers_ref.3, ...), custom_call_target="tpu_custom_call" | custom-call | bytes 1 | tf_op jit(solution)/shard_map/pallas_call | solution.py:23
  5.4 3.0 %collective-permute-start.1 = (bf16[784,512]{1,0:T(8,128)(2,1)}, bf16[784,512]{1,0:T(8,128)(2,1)S(1)}, u32[]{:S(2)}, u32[]{:S(2)}) collective-permute-start(bf16[784,512]{1,0:T(8,128)(2,1)} %get-tuple-element.92), channel_id=1, source_target_pairs={{0,4},{4,0},{8,12},{12,8},{16,20},{20,16},{24,28},{28,24},{1,5},{5... | collective-permute-start | bytes 2408456 | tf_op jit(solution)/shard_map/ppermute | solution.py:480
  13.1 3.2 %shard_map.97 = (bf16[4,4,32,512]{3,2,1,0:T(8,128)(2,1)S(1)}, bf16[4,4,16,512]{3,2,1,0:T(8,128)(2,1)S(1)}, bf16[4,4,32,512]{3,2,1,0:T(8,128)(2,1)S(1)}, f32[8,128]{1,0:T(8,128)}) custom-call(s32[256]{0:T(256)S(1)} %copy-done.4, bf16[48,128,128]{2,1,0:T(8,128)(2,1)S(1)} %copy-done.1, bf16[512,512]{1,0:T(8,128)(2,1)S(1)} %copy-done.2), custom_call_target="tpu_custom_call" | custom-call | bytes 1 | tf_op jit(solution)/shard_map/pallas_call | solution.py:23
  16.9 2.2 %shard_map.96 = (bf16[4,4,48,512]{3,2,1,0:T(8,128)(2,1)S(1)}, bf16[4,4,32,512]{3,2,1,0:T(8,128)(2,1)S(1)}, bf16[4,4,16,512]{3,2,1,0:T(8,128)(2,1)S(1)}, f32[8,128]{1,0:T(8,128)S(1)}) custom-call(s32[256]{0:T(256)S(1)} %copy-done.4, bf16[48,128,128]{2,1,0:T(8,128)(2,1)S(1)} %copy-done.1, bf16[512,512]{1,0:T(8,128)(2,1)S(1)} %copy-done.2), custom_call_target="tpu_custom_call" | custom-call | bytes 1 | tf_op jit(solution)/shard_map/pallas_call | solution.py:23
  19.1 2.8 %collective-permute-done.got_ref = bf16[4,4,32,512]{3,2,1,0:T(8,128)(2,1)S(1)} collective-permute-done((bf16[4,4,32,512]{3,2,1,0:T(8,128)(2,1)}, bf16[4,4,32,512]{3,2,1,0:T(8,128)(2,1)S(1)}, u32[]{:S(2)}, u32[]{:S(2)}) %collective-permute-start) | collective-permute-done | bytes 524320 | tf_op jit(solution)/shard_map/ppermute | solution.py:480
  22.2 2.7 %collective-permute-start.2 = (bf16[2,4,32,512]{3,2,1,0:T(8,128)(2,1)S(1)}, bf16[2,4,32,512]{3,2,1,0:T(8,128)(2,1)S(1)}, u32[]{:S(2)}, u32[]{:S(2)}) collective-permute-start(bf16[2,4,32,512]{3,2,1,0:T(8,128)(2,1)S(1)} %get-tuple-element.96), channel_id=1, source_target_pairs={{0,16},{4,20},{8,24},{12,28},{16,0},{20,4},{24,8},{28,12},{1,17},{... | collective-permute-start | bytes 786440 | tf_op jit(solution)/shard_map/ppermute | solution.py:480
  24.9 2.4 %collective-permute-done.1.got_ref = bf16[784,512]{1,0:T(8,128)(2,1)S(1)} collective-permute-done((bf16[784,512]{1,0:T(8,128)(2,1)}, bf16[784,512]{1,0:T(8,128)(2,1)S(1)}, u32[]{:S(2)}, u32[]{:S(2)}) %collective-permute-start.1) | collective-permute-done | bytes 802848 | tf_op jit(solution)/shard_map/ppermute | solution.py:480
  27.7 2.2 %collective-permute-start.5 = (bf16[2,4,48,512]{3,2,1,0:T(8,128)(2,1)S(1)}, bf16[2,4,48,512]{3,2,1,0:T(8,128)(2,1)S(1)}, u32[]{:S(2)}, u32[]{:S(2)}) collective-permute-start(bf16[2,4,48,512]{3,2,1,0:T(8,128)(2,1)S(1)} %get-tuple-element.105), channel_id=1, source_target_pairs={{0,8},{4,12},{8,0},{12,4},{16,24},{20,28},{24,16},{28,20},{1,9},{5... | collective-permute-start | bytes 1179656 | tf_op jit(solution)/shard_map/ppermute | solution.py:480
  30.7 5.1 %collective-permute-done.2.got_ref = bf16[2,4,32,512]{3,2,1,0:T(8,128)(2,1)S(1)} collective-permute-done((bf16[2,4,32,512]{3,2,1,0:T(8,128)(2,1)S(1)}, bf16[2,4,32,512]{3,2,1,0:T(8,128)(2,1)S(1)}, u32[]{:S(2)}, u32[]{:S(2)}) %collective-permute-start.2) | collective-permute-done | bytes 262176 | tf_op jit(solution)/shard_map/ppermute | solution.py:480
  40.2 2.2 %collective-permute-done.4.got_ref = bf16[1,4,32,512]{3,2,1,0:T(8,128)(2,1)S(1)} collective-permute-done((bf16[1,4,32,512]{3,2,1,0:T(8,128)(2,1)S(1)}, bf16[1,4,32,512]{3,2,1,0:T(8,128)(2,1)S(1)}, u32[]{:S(2)}, u32[]{:S(2)}) %collective-permute-start.4) | collective-permute-done | bytes 131104 | tf_op jit(solution)/shard_map/ppermute | solution.py:480
  43.7 2.4 %collective-permute-start.8 = (bf16[1,4,48,512]{3,2,1,0:T(8,128)(2,1)S(1)}, bf16[1,4,48,512]{3,2,1,0:T(8,128)(2,1)S(1)}, u32[]{:S(2)}, u32[]{:S(2)}) collective-permute-start(bf16[1,4,48,512]{3,2,1,0:T(8,128)(2,1)S(1)} %get-tuple-element.114), channel_id=1, source_target_pairs={{0,16},{4,20},{8,24},{12,28},{16,0},{20,4},{24,8},{28,12},{1,17},{... | collective-permute-start | bytes 589832 | tf_op jit(solution)/shard_map/ppermute | solution.py:480
  47.7 2.5 %collective-permute-done.7.got_ref = bf16[2,4,32,512]{3,2,1,0:T(8,128)(2,1)S(1)} collective-permute-done((bf16[2,4,32,512]{3,2,1,0:T(8,128)(2,1)S(1)}, bf16[2,4,32,512]{3,2,1,0:T(8,128)(2,1)S(1)}, u32[]{:S(2)}, u32[]{:S(2)}) %collective-permute-start.7) | collective-permute-done | bytes 262176 | tf_op jit(solution)/shard_map/ppermute | solution.py:480
  51.0 2.5 %collective-permute-done.8.got_ref = bf16[1,4,48,512]{3,2,1,0:T(8,128)(2,1)S(1)} collective-permute-done((bf16[1,4,48,512]{3,2,1,0:T(8,128)(2,1)S(1)}, bf16[1,4,48,512]{3,2,1,0:T(8,128)(2,1)S(1)}, u32[]{:S(2)}, u32[]{:S(2)}) %collective-permute-start.8) | collective-permute-done | bytes 196640 | tf_op jit(solution)/shard_map/ppermute | solution.py:480
  55.6 9.1 %collective-permute-done.11.got_ref = bf16[1,4,32,512]{3,2,1,0:T(8,128)(2,1)} collective-permute-done((bf16[1,4,32,512]{3,2,1,0:T(8,128)(2,1)}, bf16[1,4,32,512]{3,2,1,0:T(8,128)(2,1)}, u32[]{:S(2)}, u32[]{:S(2)}) %collective-permute-start.11) | collective-permute-done | bytes 131104 | tf_op jit(solution)/shard_map/ppermute | solution.py:480
  70.0 4.7 %collective-permute-done.14.got_ref = bf16[1,4,32,512]{3,2,1,0:T(8,128)(2,1)S(1)} collective-permute-done((bf16[1,4,32,512]{3,2,1,0:T(8,128)(2,1)S(1)}, bf16[1,4,32,512]{3,2,1,0:T(8,128)(2,1)S(1)}, u32[]{:S(2)}, u32[]{:S(2)}) %collective-permute-start.14) | collective-permute-done | bytes 131104 | tf_op jit(solution)/shard_map/ppermute | solution.py:480
  75.0 7.6 %collective-permute-done.17.got_ref = bf16[1,4,48,512]{3,2,1,0:T(8,128)(2,1)S(1)} collective-permute-done((bf16[1,4,48,512]{3,2,1,0:T(8,128)(2,1)S(1)}, bf16[1,4,48,512]{3,2,1,0:T(8,128)(2,1)S(1)}, u32[]{:S(2)}, u32[]{:S(2)}) %collective-permute-start.17) | collective-permute-done | bytes 196640 | tf_op jit(solution)/shard_map/ppermute | solution.py:480
  82.6 3.2 %collective-permute-start.20 = (bf16[1,4,16,512]{3,2,1,0:T(8,128)(2,1)S(1)}, bf16[1,4,16,512]{3,2,1,0:T(8,128)(2,1)S(1)}, u32[]{:S(2)}, u32[]{:S(2)}) collective-permute-start(bf16[1,4,16,512]{3,2,1,0:T(8,128)(2,1)S(1)} %get-tuple-element.142), channel_id=1, source_target_pairs={{0,16},{4,20},{8,24},{12,28},{16,0},{20,4},{24,8},{28,12},{1,17},{... | collective-permute-start | bytes 196616 | tf_op jit(solution)/shard_map/ppermute | solution.py:480
  85.8 3.5 %collective-permute-done.18.got_ref.refs_1_ = bf16[2,4,32,512]{3,2,1,0:T(8,128)(2,1)S(1)} collective-permute-done((bf16[2,4,32,512]{3,2,1,0:T(8,128)(2,1)S(1)}, bf16[2,4,32,512]{3,2,1,0:T(8,128)(2,1)S(1)}, u32[]{:S(2)}, u32[]{:S(2)}) %collective-permute-start.18) | collective-permute-done | bytes 262176 | tf_op jit(solution)/shard_map/ppermute | solution.py:480
  94.2 3.7 %collective-permute-done.21.got_ref = bf16[1,4,16,512]{3,2,1,0:T(8,128)(2,1)S(1)} collective-permute-done((bf16[1,4,16,512]{3,2,1,0:T(8,128)(2,1)S(1)}, bf16[1,4,16,512]{3,2,1,0:T(8,128)(2,1)S(1)}, u32[]{:S(2)}, u32[]{:S(2)}) %collective-permute-start.21) | collective-permute-done | bytes 65568 | tf_op jit(solution)/shard_map/ppermute | solution.py:480
  98.0 2.2 %collective-permute-done.22.got_ref = bf16[1,4,32,512]{3,2,1,0:T(8,128)(2,1)S(1)} collective-permute-done((bf16[1,4,32,512]{3,2,1,0:T(8,128)(2,1)S(1)}, bf16[1,4,32,512]{3,2,1,0:T(8,128)(2,1)S(1)}, u32[]{:S(2)}, u32[]{:S(2)}) %collective-permute-start.22) | collective-permute-done | bytes 131104 | tf_op jit(solution)/shard_map/ppermute | solution.py:480
  105.8 5.7 %collective-permute-done.26.got_ref = bf16[1,4,16,512]{3,2,1,0:T(8,128)(2,1)S(1)} collective-permute-done((bf16[1,4,16,512]{3,2,1,0:T(8,128)(2,1)S(1)}, bf16[1,4,16,512]{3,2,1,0:T(8,128)(2,1)S(1)}, u32[]{:S(2)}, u32[]{:S(2)}) %collective-permute-start.26) | collective-permute-done | bytes 65568 | tf_op jit(solution)/shard_map/ppermute | solution.py:480
  114.2 2.3 %collective-permute-done.28.got_ref.refs_7_ = bf16[2,4,16,512]{3,2,1,0:T(8,128)(2,1)S(1)} collective-permute-done((bf16[2,4,16,512]{3,2,1,0:T(8,128)(2,1)S(1)}, bf16[2,4,16,512]{3,2,1,0:T(8,128)(2,1)S(1)}, u32[]{:S(2)}, u32[]{:S(2)}) %collective-permute-start.28) | collective-permute-done | bytes 131104 | tf_op jit(solution)/shard_map/ppermute | solution.py:480
  117.6 3.9 %collective-permute-done.30.value_ref.refs_10_ = bf16[8,32,512]{2,1,0:T(8,128)(2,1)S(1)} collective-permute-done((bf16[8,32,512]{2,1,0:T(8,128)(2,1)S(1)}, bf16[8,32,512]{2,1,0:T(8,128)(2,1)S(1)}, u32[]{:S(2)}, u32[]{:S(2)}) %collective-permute-start.30) | collective-permute-done | bytes 262176 | tf_op jit(solution)/shard_map/ppermute | solution.py:480
  121.5 2.5 %shard_map.130 = (bf16[4,128,512]{2,1,0:T(8,128)(2,1)}, bf16[16,128,512]{2,1,0:T(8,128)(2,1)}, f32[8,128]{1,0:T(8,128)S(1)}) custom-call(f32[8,128]{1,0:T(8,128)S(1)} %shard_map.129.token_ref, s32[1]{0:T(128)} %bitcast.me_ref, s32[16]{0:T(128)S(1)} %copy-done.3, s32[16]{0:T(128)S(1)} %copy-done.5, ...), custom_call_target="tpu_custom_call" | custom-call | bytes 1 | tf_op jit(solution)/shard_map/pallas_call | solution.py:23
  (93 shorter events, 38.7 us)
Async XLA Ops:
  5.4 21.9 %collective-permute-start.1 = (bf16[784,512]{1,0:T(8,128)(2,1)}, bf16[784,512]{1,0:T(8,128)(2,1)S(1)}, u32[]{:S(2)}, u32[]{:S(2)}) collective-permute-start(bf16[784,512]{1,0:T(8,128)(2,1)} %get-tuple-element.92), channel_id=1, source_target_pairs={{0,4},{4,0},{8,12},{12,8},{16,20},{20,16},{24,28},{28,24},{1,5},{5... | collective-permute-start | bytes 2408456 | tf_op jit(solution)/shard_map/ppermute | solution.py:480
  8.4 13.6 %collective-permute-start = (bf16[4,4,32,512]{3,2,1,0:T(8,128)(2,1)}, bf16[4,4,32,512]{3,2,1,0:T(8,128)(2,1)S(1)}, u32[]{:S(2)}, u32[]{:S(2)}) collective-permute-start(bf16[4,4,32,512]{3,2,1,0:T(8,128)(2,1)} %get-tuple-element.89), channel_id=1, source_target_pairs={{0,8},{4,12},{8,0},{12,4},{16,24},{20,28},{24,16},{28,20},{1,9},{5... | collective-permute-start | bytes 1572872 | tf_op jit(solution)/shard_map/ppermute | solution.py:480
  16.3 21.8 %collective-permute-start.3 = (bf16[4,4,32,512]{3,2,1,0:T(8,128)(2,1)S(1)}, bf16[4,4,32,512]{3,2,1,0:T(8,128)(2,1)S(1)}, u32[]{:S(2)}, u32[]{:S(2)}) collective-permute-start(bf16[4,4,32,512]{3,2,1,0:T(8,128)(2,1)S(1)} %get-tuple-element.99), channel_id=1, source_target_pairs={{0,4},{4,0},{8,12},{12,8},{16,20},{20,16},{24,28},{28,24},{1,5},{5... | collective-permute-start | bytes 1572872 | tf_op jit(solution)/shard_map/ppermute | solution.py:480
  22.2 13.5 %collective-permute-start.2 = (bf16[2,4,32,512]{3,2,1,0:T(8,128)(2,1)S(1)}, bf16[2,4,32,512]{3,2,1,0:T(8,128)(2,1)S(1)}, u32[]{:S(2)}, u32[]{:S(2)}) collective-permute-start(bf16[2,4,32,512]{3,2,1,0:T(8,128)(2,1)S(1)} %get-tuple-element.96), channel_id=1, source_target_pairs={{0,16},{4,20},{8,24},{12,28},{16,0},{20,4},{24,8},{28,12},{1,17},{... | collective-permute-start | bytes 786440 | tf_op jit(solution)/shard_map/ppermute | solution.py:480
  27.7 15.8 %collective-permute-start.5 = (bf16[2,4,48,512]{3,2,1,0:T(8,128)(2,1)S(1)}, bf16[2,4,48,512]{3,2,1,0:T(8,128)(2,1)S(1)}, u32[]{:S(2)}, u32[]{:S(2)}) collective-permute-start(bf16[2,4,48,512]{3,2,1,0:T(8,128)(2,1)S(1)} %get-tuple-element.105), channel_id=1, source_target_pairs={{0,8},{4,12},{8,0},{12,4},{16,24},{20,28},{24,16},{28,20},{1,9},{5... | collective-permute-start | bytes 1179656 | tf_op jit(solution)/shard_map/ppermute | solution.py:480
  36.6 10.9 %collective-permute-start.6 = (bf16[4,4,16,512]{3,2,1,0:T(8,128)(2,1)S(1)}, bf16[4,4,16,512]{3,2,1,0:T(8,128)(2,1)S(1)}, u32[]{:S(2)}, u32[]{:S(2)}) collective-permute-start(bf16[4,4,16,512]{3,2,1,0:T(8,128)(2,1)S(1)} %get-tuple-element.108), channel_id=1, source_target_pairs={{0,4},{4,0},{8,12},{12,8},{16,20},{20,16},{24,28},{28,24},{1,5},{5... | collective-permute-start | bytes 786440 | tf_op jit(solution)/shard_map/ppermute | solution.py:480
  38.4 11.8 %collective-permute-start.7 = (bf16[2,4,32,512]{3,2,1,0:T(8,128)(2,1)S(1)}, bf16[2,4,32,512]{3,2,1,0:T(8,128)(2,1)S(1)}, u32[]{:S(2)}, u32[]{:S(2)}) collective-permute-start(bf16[2,4,32,512]{3,2,1,0:T(8,128)(2,1)S(1)} %get-tuple-element.111), channel_id=1, source_target_pairs={{0,8},{4,12},{8,0},{12,4},{16,24},{20,28},{24,16},{28,20},{1,9},{5... | collective-permute-start | bytes 786440 | tf_op jit(solution)/shard_map/ppermute | solution.py:480
  43.7 9.7 %collective-permute-start.8 = (bf16[1,4,48,512]{3,2,1,0:T(8,128)(2,1)S(1)}, bf16[1,4,48,512]{3,2,1,0:T(8,128)(2,1)S(1)}, u32[]{:S(2)}, u32[]{:S(2)}) collective-permute-start(bf16[1,4,48,512]{3,2,1,0:T(8,128)(2,1)S(1)} %get-tuple-element.114), channel_id=1, source_target_pairs={{0,16},{4,20},{8,24},{12,28},{16,0},{20,4},{24,8},{28,12},{1,17},{... | collective-permute-start | bytes 589832 | tf_op jit(solution)/shard_map/ppermute | solution.py:480
  46.0 7.4 %collective-permute-start.9 = (bf16[1,4,32,512]{3,2,1,0:T(8,128)(2,1)S(1)}, bf16[1,4,32,512]{3,2,1,0:T(8,128)(2,1)S(1)}, u32[]{:S(2)}, u32[]{:S(2)}) collective-permute-start(bf16[1,4,32,512]{3,2,1,0:T(8,128)(2,1)S(1)} %bitcast.13), channel_id=1, source_target_pairs={{0,2},{1,3},{2,0},{3,1},{4,6},{5,7},{6,4},{7,5},{8,10},{9,11},{10,... | collective-permute-start | bytes 393224 | tf_op jit(solution)/shard_map/ppermute | solution.py:480
  53.6 12.1 %collective-permute-start.12 = (bf16[1,4,48,512]{3,2,1,0:T(8,128)(2,1)S(1)}, bf16[1,4,48,512]{3,2,1,0:T(8,128)(2,1)S(1)}, u32[]{:S(2)}, u32[]{:S(2)}) collective-permute-start(bf16[1,4,48,512]{3,2,1,0:T(8,128)(2,1)S(1)} %bitcast.9), channel_id=1, source_target_pairs={{0,2},{1,3},{2,0},{3,1},{4,6},{5,7},{6,4},{7,5},{8,10},{9,11},{10,... | collective-permute-start | bytes 589832 | tf_op jit(solution)/shard_map/ppermute | solution.py:480
  55.2 9.6 %collective-permute-start.11 = (bf16[1,4,32,512]{3,2,1,0:T(8,128)(2,1)}, bf16[1,4,32,512]{3,2,1,0:T(8,128)(2,1)}, u32[]{:S(2)}, u32[]{:S(2)}) collective-permute-start(bf16[1,4,32,512]{3,2,1,0:T(8,128)(2,1)} %get-tuple-element.121), channel_id=1, source_target_pairs={{0,16},{4,20},{8,24},{12,28},{16,0},{20,4},{24,8},{28,12},{1,17},{... | collective-permute-start | bytes 393224 | tf_op jit(solution)/shard_map/ppermute | solution.py:480
  65.8 8.9 %collective-permute-start.14 = (bf16[1,4,32,512]{3,2,1,0:T(8,128)(2,1)S(1)}, bf16[1,4,32,512]{3,2,1,0:T(8,128)(2,1)S(1)}, u32[]{:S(2)}, u32[]{:S(2)}) collective-permute-start(bf16[1,4,32,512]{3,2,1,0:T(8,128)(2,1)S(1)} %get-tuple-element.127.held_ref), channel_id=1, source_target_pairs={{0,16},{4,20},{8,24},{12,28},{16,0},{20,4},{24,8},{28,12},{1,17},{... | collective-permute-start | bytes 393224 | tf_op jit(solution)/shard_map/ppermute | solution.py:480
  65.9 8.9 %collective-permute-start.15 = (bf16[2,4,16,512]{3,2,1,0:T(8,128)(2,1)S(1)}, bf16[2,4,16,512]{3,2,1,0:T(8,128)(2,1)S(1)}, u32[]{:S(2)}, u32[]{:S(2)}) collective-permute-start(bf16[2,4,16,512]{3,2,1,0:T(8,128)(2,1)S(1)} %copy-done.7), channel_id=1, source_target_pairs={{0,8},{4,12},{8,0},{12,4},{16,24},{20,28},{24,16},{28,20},{1,9},{5... | collective-permute-start | bytes 393224 | tf_op jit(solution)/shard_map/ppermute | solution.py:480
  67.6 7.2 %collective-permute-start.16 = (bf16[1,4,32,512]{3,2,1,0:T(8,128)(2,1)S(1)}, bf16[1,4,32,512]{3,2,1,0:T(8,128)(2,1)S(1)}, u32[]{:S(2)}, u32[]{:S(2)}) collective-permute-start(bf16[1,4,32,512]{3,2,1,0:T(8,128)(2,1)S(1)} %bitcast.11), channel_id=1, source_target_pairs={{0,2},{1,3},{2,0},{3,1},{4,6},{5,7},{6,4},{7,5},{8,10},{9,11},{10,... | collective-permute-start | bytes 393224 | tf_op jit(solution)/shard_map/ppermute | solution.py:480
  68.8 13.8 %collective-permute-start.17 = (bf16[1,4,48,512]{3,2,1,0:T(8,128)(2,1)S(1)}, bf16[1,4,48,512]{3,2,1,0:T(8,128)(2,1)S(1)}, u32[]{:S(2)}, u32[]{:S(2)}) collective-permute-start(bf16[1,4,48,512]{3,2,1,0:T(8,128)(2,1)S(1)} %get-tuple-element.134.held_ref), channel_id=1, source_target_pairs={{0,16},{4,20},{8,24},{12,28},{16,0},{20,4},{24,8},{28,12},{1,17},{... | collective-permute-start | bytes 589832 | tf_op jit(solution)/shard_map/ppermute | solution.py:480
  74.7 14.7 %collective-permute-start.18 = (bf16[2,4,32,512]{3,2,1,0:T(8,128)(2,1)S(1)}, bf16[2,4,32,512]{3,2,1,0:T(8,128)(2,1)S(1)}, u32[]{:S(2)}, u32[]{:S(2)}) collective-permute-start(bf16[2,4,32,512]{3,2,1,0:T(8,128)(2,1)S(1)} %get-tuple-element.137.held_ref.refs_0_), channel_id=1, source_target_pairs={{0,8},{4,12},{8,0},{12,4},{16,24},{20,28},{24,16},{28,20},{1,9},{5... | collective-permute-start | bytes 786440 | tf_op jit(solution)/shard_map/ppermute | solution.py:480
  74.9 17.0 %collective-permute-start.19 = (bf16[2,4,32,512]{3,2,1,0:T(8,128)(2,1)S(1)}, bf16[2,4,32,512]{3,2,1,0:T(8,128)(2,1)S(1)}, u32[]{:S(2)}, u32[]{:S(2)}) collective-permute-start(bf16[2,4,32,512]{3,2,1,0:T(8,128)(2,1)S(1)} %get-tuple-element.139.held_ref), channel_id=1, source_target_pairs={{0,1},{1,0},{2,3},{3,2},{4,5},{5,4},{6,7},{7,6},{8,9},{9,8},{10,11... | collective-permute-start | bytes 786440 | tf_op jit(solution)/shard_map/ppermute | solution.py:480
  82.6 19.7 %collective-permute-start.25 = (bf16[2,4,48,512]{3,2,1,0:T(8,128)(2,1)S(1)}, bf16[2,4,48,512]{3,2,1,0:T(8,128)(2,1)S(1)}, u32[]{:S(2)}, u32[]{:S(2)}) collective-permute-start(bf16[2,4,48,512]{3,2,1,0:T(8,128)(2,1)S(1)} %get-tuple-element.151.held_ref.refs_2_), channel_id=1, source_target_pairs={{0,8},{4,12},{8,0},{12,4},{16,24},{20,28},{24,16},{28,20},{1,9},{5... | collective-permute-start | bytes 1179656 | tf_op jit(solution)/shard_map/ppermute | solution.py:480
  82.6 10.9 %collective-permute-start.20 = (bf16[1,4,16,512]{3,2,1,0:T(8,128)(2,1)S(1)}, bf16[1,4,16,512]{3,2,1,0:T(8,128)(2,1)S(1)}, u32[]{:S(2)}, u32[]{:S(2)}) collective-permute-start(bf16[1,4,16,512]{3,2,1,0:T(8,128)(2,1)S(1)} %get-tuple-element.142), channel_id=1, source_target_pairs={{0,16},{4,20},{8,24},{12,28},{16,0},{20,4},{24,8},{28,12},{1,17},{... | collective-permute-start | bytes 196616 | tf_op jit(solution)/shard_map/ppermute | solution.py:480
  89.9 11.8 %collective-permute-start.23 = (bf16[8,32,512]{2,1,0:T(8,128)(2,1)S(1)}, bf16[8,32,512]{2,1,0:T(8,128)(2,1)S(1)}, u32[]{:S(2)}, u32[]{:S(2)}) collective-permute-start(bf16[8,32,512]{2,1,0:T(8,128)(2,1)S(1)} %get-tuple-element.148), channel_id=1, source_target_pairs={{0,4},{4,0},{8,12},{12,8},{16,20},{20,16},{24,28},{28,24},{1,5},{5... | collective-permute-start | bytes 786440 | tf_op jit(solution)/shard_map/ppermute | solution.py:480
  92.4 7.8 %collective-permute-start.22 = (bf16[1,4,32,512]{3,2,1,0:T(8,128)(2,1)S(1)}, bf16[1,4,32,512]{3,2,1,0:T(8,128)(2,1)S(1)}, u32[]{:S(2)}, u32[]{:S(2)}) collective-permute-start(bf16[1,4,32,512]{3,2,1,0:T(8,128)(2,1)S(1)} %get-tuple-element.146.held_ref), channel_id=1, source_target_pairs={{0,16},{4,20},{8,24},{12,28},{16,0},{20,4},{24,8},{28,12},{1,17},{... | collective-permute-start | bytes 393224 | tf_op jit(solution)/shard_map/ppermute | solution.py:480
  100.2 11.6 %collective-permute-start.27 = (bf16[2,4,32,512]{3,2,1,0:T(8,128)(2,1)S(1)}, bf16[2,4,32,512]{3,2,1,0:T(8,128)(2,1)S(1)}, u32[]{:S(2)}, u32[]{:S(2)}) collective-permute-start(bf16[2,4,32,512]{3,2,1,0:T(8,128)(2,1)S(1)} %get-tuple-element.155.held_ref.refs_4_), channel_id=1, source_target_pairs={{0,8},{4,12},{8,0},{12,4},{16,24},{20,28},{24,16},{28,20},{1,9},{5... | collective-permute-start | bytes 786440 | tf_op jit(solution)/shard_map/ppermute | solution.py:480
  102.8 14.8 %collective-permute-start.29 = (bf16[8,48,512]{2,1,0:T(8,128)(2,1)S(1)}, bf16[8,48,512]{2,1,0:T(8,128)(2,1)S(1)}, u32[]{:S(2)}, u32[]{:S(2)}) collective-permute-start(bf16[8,48,512]{2,1,0:T(8,128)(2,1)S(1)} %get-tuple-element.159), channel_id=1, source_target_pairs={{0,4},{4,0},{8,12},{12,8},{16,20},{20,16},{24,28},{28,24},{1,5},{5... | collective-permute-start | bytes 1179656 | tf_op jit(solution)/shard_map/ppermute | solution.py:480
  112.4 9.1 %collective-permute-start.30 = (bf16[8,32,512]{2,1,0:T(8,128)(2,1)S(1)}, bf16[8,32,512]{2,1,0:T(8,128)(2,1)S(1)}, u32[]{:S(2)}, u32[]{:S(2)}) collective-permute-start(bf16[8,32,512]{2,1,0:T(8,128)(2,1)S(1)} %get-tuple-element.160), channel_id=1, source_target_pairs={{0,4},{4,0},{8,12},{12,8},{16,20},{20,16},{24,28},{28,24},{1,5},{5... | collective-permute-start | bytes 786440 | tf_op jit(solution)/shard_map/ppermute | solution.py:480
  (16 other events, 104.9 us)

commit v12 on v11

--- a/solution.py
+++ b/solution.py
@@ -5,9 +5,10 @@
 from jax.experimental.pallas import tpu as pltpu
 from jax.sharding import PartitionSpec as P
 
-SHARES = (2, 3, 2, 1)
+SHARES = (2, 2, 2, 1, 1)
 ORDER = (
-    0, 1, 0, 2, 0, 1, 3, 2, 1, 0, 0, 2, 1, 1, 0, 3, 2, 1, 0, 2, 3, 3, 2, 0, 3, 1, 3, 2, 3, 1, 2, 3,
+    0, 1, 2, 0, 1, 4, 2, 3, 1, 0, 3, 2, 3, 0, 4, 1, 0, 2, 1, 4, 4, 0, 3, 1, 2, 0, 2, 3, 1, 3, 4, 0,
+    2, 4, 3, 1, 4, 2, 3, 4,
 )
 READ_CAP = 2
 VMEM_BYTES = 12 * 1024 * 1024

time: 126 us -> 119 us (0.944)
  waiting for transfers between devices: 62.1 us -> 41.1 us
  starting transfers between devices: 36.9 us -> 49.8 us
    ppermute x32 -> x40, waiting for transfers between devices: 62.1 us -> 41.1 us  [flip(): lax.ppermute(value, axis, [(d, d ^ bit) for d in range(lax.axis_size(axis...]
    ppermute x32 -> x40, starting transfers between devices: 36.9 us -> 49.8 us  [flip(): lax.ppermute(value, axis, [(d, d ^ bit) for d in range(lax.axis_size(axis...]
    pallas_call x37 -> x45, Pallas kernels: 22.8 us -> 23.7 us  [call(): pl.pallas_call(body, out_shape=out_shape, in_specs=in_specs, out_specs=ou...]
  transfers between devices with their start and end apart: 32 -> 40, of which waited for: 18 -> 16; matrix products, arithmetic and copies ran while one was open for 0% -> 0% of each run, Pallas kernels for 13% -> 15%
where the time goes in v12:
time: 119 us
  starting transfers between devices  49.8 us (42%)
  waiting for transfers between devices  41.1 us (35%)
  Pallas kernels  23.7 us (20%)
  local copies, waits for them, and re-layouts  3.14 us (3%)
    ppermute x40, starting transfers between devices, flip(): lax.ppermute(value, axis, [(d, d ^ bit) for d in range(lax.axis_size(axis...  49.8 us
    ppermute x40, waiting for transfers between devices, flip(): lax.ppermute(value, axis, [(d, d ^ bit) for d in range(lax.axis_size(axis...  41.1 us
    pallas_call x45, Pallas kernels, call(): pl.pallas_call(body, out_shape=out_shape, in_specs=in_specs, out_specs=ou...  23.7 us
    unnamed x16, local copies, waits for them, and re-layouts  3.14 us
  transfers between devices with their start and end apart: 40, of which 16 were waited for; matrix products, arithmetic and copies ran while one was open for 0% of the time, Pallas kernels for 15%

profile of v12, /device:TPU:0, one launch (start us, length us, event | category | flops | bytes accessed | tf_op | source)
XLA Modules:
  0.0 118.9 jit_solution(16196491531257285321)
XLA Ops:
  0.6 4.4 %shard_map.95 = (s32[256]{0:T(256)}, s32[16]{0:T(128)}, bf16[4,4,32,512]{3,2,1,0:T(8,128)(2,1)}, bf16[528,512]{1,0:T(8,128)(2,1)}, bf16[512,512]{1,0:T(8,128)(2,1)}) custom-call(s32[1]{0:T(128)} %bitcast.me_ref, s32[96]{0:T(128)} %slot_hbm.1, s32[96]{0:T(128)} %col_hbm.1, s32[96]{0:T(128)} %id_hbm.1, s32[8,4,8]{2,1,0:T(4,128)} %bitcast.22, s32[16]{0:T(128)} %readers_ref.3, ...), custom_call_target="tpu_custom_call" | custom-call | bytes 1 | tf_op jit(solution)/shard_map/pallas_call | solution.py:24
  5.1 3.0 %collective-permute-start.1 = (bf16[528,512]{1,0:T(8,128)(2,1)}, bf16[528,512]{1,0:T(8,128)(2,1)S(1)}, u32[]{:S(2)}, u32[]{:S(2)}) collective-permute-start(bf16[528,512]{1,0:T(8,128)(2,1)} %get-tuple-element.110), channel_id=1, source_target_pairs={{0,4},{4,0},{8,12},{12,8},{16,20},{20,16},{24,28},{28,24},{1,5},{5... | collective-permute-start | bytes 1622024 | tf_op jit(solution)/shard_map/ppermute | solution.py:481
  12.8 3.4 %shard_map.97 = (bf16[4,4,32,512]{3,2,1,0:T(8,128)(2,1)S(1)}, bf16[4,4,16,512]{3,2,1,0:T(8,128)(2,1)S(1)}, bf16[4,4,16,512]{3,2,1,0:T(8,128)(2,1)S(1)}, bf16[4,4,32,512]{3,2,1,0:T(8,128)(2,1)S(1)}, f32[8,128]{1,0:T(8,128)}) custom-call(s32[256]{0:T(256)S(1)} %copy-done.6, bf16[48,128,128]{2,1,0:T(8,128)(2,1)S(1)} %copy-done.1, bf16[512,512]{1,0:T(8,128)(2,1)S(1)} %copy-done.2), custom_call_target="tpu_custom_call" | custom-call | bytes 1 | tf_op jit(solution)/shard_map/pallas_call | solution.py:24
  16.7 2.3 %shard_map.96 = (bf16[4,4,32,512]{3,2,1,0:T(8,128)(2,1)S(1)}, bf16[4,4,32,512]{3,2,1,0:T(8,128)(2,1)S(1)}, bf16[4,4,16,512]{3,2,1,0:T(8,128)(2,1)S(1)}, bf16[4,4,16,512]{3,2,1,0:T(8,128)(2,1)S(1)}, f32[8,128]{1,0:T(8,128)S(1)}) custom-call(s32[256]{0:T(256)S(1)} %copy-done.6, bf16[48,128,128]{2,1,0:T(8,128)(2,1)S(1)} %copy-done.1, bf16[512,512]{1,0:T(8,128)(2,1)S(1)} %copy-done.2), custom_call_target="tpu_custom_call" | custom-call | bytes 1 | tf_op jit(solution)/shard_map/pallas_call | solution.py:24
  19.0 2.7 %collective-permute-done.got_ref = bf16[4,4,32,512]{3,2,1,0:T(8,128)(2,1)S(1)} collective-permute-done((bf16[4,4,32,512]{3,2,1,0:T(8,128)(2,1)}, bf16[4,4,32,512]{3,2,1,0:T(8,128)(2,1)S(1)}, u32[]{:S(2)}, u32[]{:S(2)}) %collective-permute-start) | collective-permute-done | bytes 524320 | tf_op jit(solution)/shard_map/ppermute | solution.py:481
  21.9 2.7 %collective-permute-start.3 = (bf16[2,4,32,512]{3,2,1,0:T(8,128)(2,1)S(1)}, bf16[2,4,32,512]{3,2,1,0:T(8,128)(2,1)S(1)}, u32[]{:S(2)}, u32[]{:S(2)}) collective-permute-start(bf16[2,4,32,512]{3,2,1,0:T(8,128)(2,1)S(1)} %get-tuple-element.117), channel_id=1, source_target_pairs={{0,16},{4,20},{8,24},{12,28},{16,0},{20,4},{24,8},{28,12},{1,17},{... | collective-permute-start | bytes 786440 | tf_op jit(solution)/shard_map/ppermute | solution.py:481
  27.8 4.9 %collective-permute-done.2.got_ref = bf16[4,4,32,512]{3,2,1,0:T(8,128)(2,1)S(1)} collective-permute-done((bf16[4,4,32,512]{3,2,1,0:T(8,128)(2,1)S(1)}, bf16[4,4,32,512]{3,2,1,0:T(8,128)(2,1)S(1)}, u32[]{:S(2)}, u32[]{:S(2)}) %collective-permute-start.2) | collective-permute-done | bytes 524320 | tf_op jit(solution)/shard_map/ppermute | solution.py:481
  32.9 2.2 %collective-permute-start.6 = (bf16[2,4,32,512]{3,2,1,0:T(8,128)(2,1)S(1)}, bf16[2,4,32,512]{3,2,1,0:T(8,128)(2,1)S(1)}, u32[]{:S(2)}, u32[]{:S(2)}) collective-permute-start(bf16[2,4,32,512]{3,2,1,0:T(8,128)(2,1)S(1)} %get-tuple-element.126), channel_id=1, source_target_pairs={{0,8},{4,12},{8,0},{12,4},{16,24},{20,28},{24,16},{28,20},{1,9},{5... | collective-permute-start | bytes 786440 | tf_op jit(solution)/shard_map/ppermute | solution.py:481
  36.8 2.6 %collective-permute-start.8 = (bf16[1,4,32,512]{3,2,1,0:T(8,128)(2,1)S(1)}, bf16[1,4,32,512]{3,2,1,0:T(8,128)(2,1)S(1)}, u32[]{:S(2)}, u32[]{:S(2)}) collective-permute-start(bf16[1,4,32,512]{3,2,1,0:T(8,128)(2,1)S(1)} %get-tuple-element.132), channel_id=1, source_target_pairs={{0,16},{4,20},{8,24},{12,28},{16,0},{20,4},{24,8},{28,12},{1,17},{... | collective-permute-start | bytes 393224 | tf_op jit(solution)/shard_map/ppermute | solution.py:481
  40.2 4.3 %collective-permute-done.6.got_ref = bf16[2,4,32,512]{3,2,1,0:T(8,128)(2,1)S(1)} collective-permute-done((bf16[2,4,32,512]{3,2,1,0:T(8,128)(2,1)S(1)}, bf16[2,4,32,512]{3,2,1,0:T(8,128)(2,1)S(1)}, u32[]{:S(2)}, u32[]{:S(2)}) %collective-permute-start.6) | collective-permute-done | bytes 262176 | tf_op jit(solution)/shard_map/ppermute | solution.py:481
  46.2 2.6 %collective-permute-start.11 = (bf16[1,4,32,512]{3,2,1,0:T(8,128)(2,1)S(1)}, bf16[1,4,32,512]{3,2,1,0:T(8,128)(2,1)S(1)}, u32[]{:S(2)}, u32[]{:S(2)}) collective-permute-start(bf16[1,4,32,512]{3,2,1,0:T(8,128)(2,1)S(1)} %get-tuple-element.141), channel_id=1, source_target_pairs={{0,16},{4,20},{8,24},{12,28},{16,0},{20,4},{24,8},{28,12},{1,17},{... | collective-permute-start | bytes 393224 | tf_op jit(solution)/shard_map/ppermute | solution.py:481
  54.4 4.6 %collective-permute-done.12.got_ref = bf16[1,4,16,512]{3,2,1,0:T(8,128)(2,1)S(1)} collective-permute-done((bf16[1,4,16,512]{3,2,1,0:T(8,128)(2,1)S(1)}, bf16[1,4,16,512]{3,2,1,0:T(8,128)(2,1)S(1)}, u32[]{:S(2)}, u32[]{:S(2)}) %collective-permute-start.12) | collective-permute-done | bytes 65568 | tf_op jit(solution)/shard_map/ppermute | solution.py:481
  63.3 2.2 %collective-permute-start.21 = (bf16[1,4,32,512]{3,2,1,0:T(8,128)(2,1)S(1)}, bf16[1,4,32,512]{3,2,1,0:T(8,128)(2,1)S(1)}, u32[]{:S(2)}, u32[]{:S(2)}) collective-permute-start(bf16[1,4,32,512]{3,2,1,0:T(8,128)(2,1)S(1)} %get-tuple-element.164.held_ref), channel_id=1, source_target_pairs={{0,16},{4,20},{8,24},{12,28},{16,0},{20,4},{24,8},{28,12},{1,17},{... | collective-permute-start | bytes 393224 | tf_op jit(solution)/shard_map/ppermute | solution.py:481
  66.5 5.2 %collective-permute-done.19.got_ref = bf16[1,4,16,512]{3,2,1,0:T(8,128)(2,1)} collective-permute-done((bf16[1,4,16,512]{3,2,1,0:T(8,128)(2,1)}, bf16[1,4,16,512]{3,2,1,0:T(8,128)(2,1)}, u32[]{:S(2)}, u32[]{:S(2)}) %collective-permute-start.19) | collective-permute-done | bytes 65568 | tf_op jit(solution)/shard_map/ppermute | solution.py:481
  72.9 4.3 %collective-permute-done.20.got_ref = bf16[1,4,16,512]{3,2,1,0:T(8,128)(2,1)S(1)} collective-permute-done((bf16[1,4,16,512]{3,2,1,0:T(8,128)(2,1)S(1)}, bf16[1,4,16,512]{3,2,1,0:T(8,128)(2,1)S(1)}, u32[]{:S(2)}, u32[]{:S(2)}) %collective-permute-start.20) | collective-permute-done | bytes 65568 | tf_op jit(solution)/shard_map/ppermute | solution.py:481
  77.4 4.2 %collective-permute-done.22.got_ref = bf16[1,4,16,512]{3,2,1,0:T(8,128)(2,1)S(1)} collective-permute-done((bf16[1,4,16,512]{3,2,1,0:T(8,128)(2,1)S(1)}, bf16[1,4,16,512]{3,2,1,0:T(8,128)(2,1)S(1)}, u32[]{:S(2)}, u32[]{:S(2)}) %collective-permute-start.22) | collective-permute-done | bytes 65568 | tf_op jit(solution)/shard_map/ppermute | solution.py:481
  82.1 2.4 %collective-permute-start.26 = (bf16[1,4,32,512]{3,2,1,0:T(8,128)(2,1)S(1)}, bf16[1,4,32,512]{3,2,1,0:T(8,128)(2,1)S(1)}, u32[]{:S(2)}, u32[]{:S(2)}) collective-permute-start(bf16[1,4,32,512]{3,2,1,0:T(8,128)(2,1)S(1)} %get-tuple-element.175.held_ref), channel_id=1, source_target_pairs={{0,16},{4,20},{8,24},{12,28},{16,0},{20,4},{24,8},{28,12},{1,17},{... | collective-permute-start | bytes 393224 | tf_op jit(solution)/shard_map/ppermute | solution.py:481
  88.2 2.0 %collective-permute-start.32 = (bf16[2,4,32,512]{3,2,1,0:T(8,128)(2,1)S(1)}, bf16[2,4,32,512]{3,2,1,0:T(8,128)(2,1)S(1)}, u32[]{:S(2)}, u32[]{:S(2)}) collective-permute-start(bf16[2,4,32,512]{3,2,1,0:T(8,128)(2,1)S(1)} %get-tuple-element.186.held_ref.refs_4_), channel_id=1, source_target_pairs={{0,8},{4,12},{8,0},{12,4},{16,24},{20,28},{24,16},{28,20},{1,9},{5... | collective-permute-start | bytes 786440 | tf_op jit(solution)/shard_map/ppermute | solution.py:481
  90.7 3.8 %collective-permute-start.29 = (bf16[1,4,16,512]{3,2,1,0:T(8,128)(2,1)S(1)}, bf16[1,4,16,512]{3,2,1,0:T(8,128)(2,1)S(1)}, u32[]{:S(2)}, u32[]{:S(2)}) collective-permute-start(bf16[1,4,16,512]{3,2,1,0:T(8,128)(2,1)S(1)} %get-tuple-element.181.held_ref), channel_id=1, source_target_pairs={{0,16},{4,20},{8,24},{12,28},{16,0},{20,4},{24,8},{28,12},{1,17},{... | collective-permute-start | bytes 196616 | tf_op jit(solution)/shard_map/ppermute | solution.py:481
  98.3 2.7 %collective-permute-start.33 = (bf16[1,4,16,512]{3,2,1,0:T(8,128)(2,1)S(1)}, bf16[1,4,16,512]{3,2,1,0:T(8,128)(2,1)S(1)}, u32[]{:S(2)}, u32[]{:S(2)}) collective-permute-start(bf16[1,4,16,512]{3,2,1,0:T(8,128)(2,1)S(1)} %get-tuple-element.188.held_ref), channel_id=1, source_target_pairs={{0,16},{4,20},{8,24},{12,28},{16,0},{20,4},{24,8},{28,12},{1,17},{... | collective-permute-start | bytes 196616 | tf_op jit(solution)/shard_map/ppermute | solution.py:481
  103.6 2.1 %collective-permute-start.36 = (bf16[2,4,16,512]{3,2,1,0:T(8,128)(2,1)S(1)}, bf16[2,4,16,512]{3,2,1,0:T(8,128)(2,1)S(1)}, u32[]{:S(2)}, u32[]{:S(2)}) collective-permute-start(bf16[2,4,16,512]{3,2,1,0:T(8,128)(2,1)S(1)} %get-tuple-element.193.held_ref.refs_8_), channel_id=1, source_target_pairs={{0,8},{4,12},{8,0},{12,4},{16,24},{20,28},{24,16},{28,20},{1,9},{5... | collective-permute-start | bytes 393224 | tf_op jit(solution)/shard_map/ppermute | solution.py:481
  110.9 3.3 %collective-permute-done.38.value_ref.refs_13_ = bf16[8,16,512]{2,1,0:T(8,128)(2,1)S(1)} collective-permute-done((bf16[8,16,512]{2,1,0:T(8,128)(2,1)S(1)}, bf16[8,16,512]{2,1,0:T(8,128)(2,1)S(1)}, u32[]{:S(2)}, u32[]{:S(2)}) %collective-permute-start.38) | collective-permute-done | bytes 131104 | tf_op jit(solution)/shard_map/ppermute | solution.py:481
  114.2 2.7 %shard_map.138 = (bf16[4,128,512]{2,1,0:T(8,128)(2,1)}, bf16[16,128,512]{2,1,0:T(8,128)(2,1)}, f32[8,128]{1,0:T(8,128)S(1)}) custom-call(f32[8,128]{1,0:T(8,128)S(1)} %shard_map.137.token_ref, s32[1]{0:T(128)} %bitcast.me_ref, s32[16]{0:T(128)S(1)} %copy-done.5, s32[16]{0:T(128)S(1)} %copy-done.7, ...), custom_call_target="tpu_custom_call" | custom-call | bytes 1 | tf_op jit(solution)/shard_map/pallas_call | solution.py:24
  116.9 1.9 %shard_map.139 = (bf16[4,128,512]{2,1,0:T(8,128)(2,1)}, bf16[16,128,512]{2,1,0:T(8,128)(2,1)}, f32[8,128]{1,0:T(8,128)}) custom-call(f32[8,128]{1,0:T(8,128)S(1)} %get-tuple-element.198.token_ref, s32[1]{0:T(128)} %bitcast.me_ref, s32[16]{0:T(128)S(1)} %copy-done.5, s32[16]{0:T(128)S(1)} %copy-done.7, ...), custom_call_target="tpu_custom_call", output_to_operand_aliasing={{0}: (5, {}), {1}: (6, {})} | custom-call | bytes 1 | tf_op jit(solution)/shard_map/pallas_call | solution.py:24
  (117 shorter events, 41.4 us)
Async XLA Ops:
  5.1 19.5 %collective-permute-start.1 = (bf16[528,512]{1,0:T(8,128)(2,1)}, bf16[528,512]{1,0:T(8,128)(2,1)S(1)}, u32[]{:S(2)}, u32[]{:S(2)}) collective-permute-start(bf16[528,512]{1,0:T(8,128)(2,1)} %get-tuple-element.110), channel_id=1, source_target_pairs={{0,4},{4,0},{8,12},{12,8},{16,20},{20,16},{24,28},{28,24},{1,5},{5... | collective-permute-start | bytes 1622024 | tf_op jit(solution)/shard_map/ppermute | solution.py:481
  8.1 13.6 %collective-permute-start = (bf16[4,4,32,512]{3,2,1,0:T(8,128)(2,1)}, bf16[4,4,32,512]{3,2,1,0:T(8,128)(2,1)S(1)}, u32[]{:S(2)}, u32[]{:S(2)}) collective-permute-start(bf16[4,4,32,512]{3,2,1,0:T(8,128)(2,1)} %get-tuple-element.107), channel_id=1, source_target_pairs={{0,8},{4,12},{8,0},{12,4},{16,24},{20,28},{24,16},{28,20},{1,9},{5... | collective-permute-start | bytes 1572872 | tf_op jit(solution)/shard_map/ppermute | solution.py:481
  16.2 16.5 %collective-permute-start.2 = (bf16[4,4,32,512]{3,2,1,0:T(8,128)(2,1)S(1)}, bf16[4,4,32,512]{3,2,1,0:T(8,128)(2,1)S(1)}, u32[]{:S(2)}, u32[]{:S(2)}) collective-permute-start(bf16[4,4,32,512]{3,2,1,0:T(8,128)(2,1)S(1)} %get-tuple-element.114), channel_id=1, source_target_pairs={{0,4},{4,0},{8,12},{12,8},{16,20},{20,16},{24,28},{28,24},{1,5},{5... | collective-permute-start | bytes 1572872 | tf_op jit(solution)/shard_map/ppermute | solution.py:481
  21.9 14.7 %collective-permute-start.3 = (bf16[2,4,32,512]{3,2,1,0:T(8,128)(2,1)S(1)}, bf16[2,4,32,512]{3,2,1,0:T(8,128)(2,1)S(1)}, u32[]{:S(2)}, u32[]{:S(2)}) collective-permute-start(bf16[2,4,32,512]{3,2,1,0:T(8,128)(2,1)S(1)} %get-tuple-element.117), channel_id=1, source_target_pairs={{0,16},{4,20},{8,24},{12,28},{16,0},{20,4},{24,8},{28,12},{1,17},{... | collective-permute-start | bytes 786440 | tf_op jit(solution)/shard_map/ppermute | solution.py:481
  24.9 11.9 %collective-permute-start.4 = (bf16[2,4,32,512]{3,2,1,0:T(8,128)(2,1)S(1)}, bf16[2,4,32,512]{3,2,1,0:T(8,128)(2,1)S(1)}, u32[]{:S(2)}, u32[]{:S(2)}) collective-permute-start(bf16[2,4,32,512]{3,2,1,0:T(8,128)(2,1)S(1)} %get-tuple-element.120), channel_id=1, source_target_pairs={{0,8},{4,12},{8,0},{12,4},{16,24},{20,28},{24,16},{28,20},{1,9},{5... | collective-permute-start | bytes 786440 | tf_op jit(solution)/shard_map/ppermute | solution.py:481
  26.5 13.5 %collective-permute-start.5 = (bf16[4,4,16,512]{3,2,1,0:T(8,128)(2,1)S(1)}, bf16[4,4,16,512]{3,2,1,0:T(8,128)(2,1)S(1)}, u32[]{:S(2)}, u32[]{:S(2)}) collective-permute-start(bf16[4,4,16,512]{3,2,1,0:T(8,128)(2,1)S(1)} %get-tuple-element.123), channel_id=1, source_target_pairs={{0,4},{4,0},{8,12},{12,8},{16,20},{20,16},{24,28},{28,24},{1,5},{5... | collective-permute-start | bytes 786440 | tf_op jit(solution)/shard_map/ppermute | solution.py:481
  32.9 11.5 %collective-permute-start.6 = (bf16[2,4,32,512]{3,2,1,0:T(8,128)(2,1)S(1)}, bf16[2,4,32,512]{3,2,1,0:T(8,128)(2,1)S(1)}, u32[]{:S(2)}, u32[]{:S(2)}) collective-permute-start(bf16[2,4,32,512]{3,2,1,0:T(8,128)(2,1)S(1)} %get-tuple-element.126), channel_id=1, source_target_pairs={{0,8},{4,12},{8,0},{12,4},{16,24},{20,28},{24,16},{28,20},{1,9},{5... | collective-permute-start | bytes 786440 | tf_op jit(solution)/shard_map/ppermute | solution.py:481
  35.1 9.4 %collective-permute-start.7 = (bf16[4,4,16,512]{3,2,1,0:T(8,128)(2,1)S(1)}, bf16[4,4,16,512]{3,2,1,0:T(8,128)(2,1)S(1)}, u32[]{:S(2)}, u32[]{:S(2)}) collective-permute-start(bf16[4,4,16,512]{3,2,1,0:T(8,128)(2,1)S(1)} %get-tuple-element.129), channel_id=1, source_target_pairs={{0,4},{4,0},{8,12},{12,8},{16,20},{20,16},{24,28},{28,24},{1,5},{5... | collective-permute-start | bytes 786440 | tf_op jit(solution)/shard_map/ppermute | solution.py:481
  36.8 12.0 %collective-permute-start.8 = (bf16[1,4,32,512]{3,2,1,0:T(8,128)(2,1)S(1)}, bf16[1,4,32,512]{3,2,1,0:T(8,128)(2,1)S(1)}, u32[]{:S(2)}, u32[]{:S(2)}) collective-permute-start(bf16[1,4,32,512]{3,2,1,0:T(8,128)(2,1)S(1)} %get-tuple-element.132), channel_id=1, source_target_pairs={{0,16},{4,20},{8,24},{12,28},{16,0},{20,4},{24,8},{28,12},{1,17},{... | collective-permute-start | bytes 393224 | tf_op jit(solution)/shard_map/ppermute | solution.py:481
  39.5 9.4 %collective-permute-start.9 = (bf16[1,4,32,512]{3,2,1,0:T(8,128)(2,1)S(1)}, bf16[1,4,32,512]{3,2,1,0:T(8,128)(2,1)S(1)}, u32[]{:S(2)}, u32[]{:S(2)}) collective-permute-start(bf16[1,4,32,512]{3,2,1,0:T(8,128)(2,1)S(1)} %get-tuple-element.135), channel_id=1, source_target_pairs={{0,4},{4,0},{8,12},{12,8},{16,20},{20,16},{24,28},{28,24},{1,5},{5... | collective-permute-start | bytes 393224 | tf_op jit(solution)/shard_map/ppermute | solution.py:481
  44.7 8.3 %collective-permute-start.10 = (bf16[2,4,16,512]{3,2,1,0:T(8,128)(2,1)S(1)}, bf16[2,4,16,512]{3,2,1,0:T(8,128)(2,1)S(1)}, u32[]{:S(2)}, u32[]{:S(2)}) collective-permute-start(bf16[2,4,16,512]{3,2,1,0:T(8,128)(2,1)S(1)} %get-tuple-element.138), channel_id=1, source_target_pairs={{0,8},{4,12},{8,0},{12,4},{16,24},{20,28},{24,16},{28,20},{1,9},{5... | collective-permute-start | bytes 393224 | tf_op jit(solution)/shard_map/ppermute | solution.py:481
  48.9 10.1 %collective-permute-start.13 = (bf16[1,4,32,512]{3,2,1,0:T(8,128)(2,1)S(1)}, bf16[1,4,32,512]{3,2,1,0:T(8,128)(2,1)S(1)}, u32[]{:S(2)}, u32[]{:S(2)}) collective-permute-start(bf16[1,4,32,512]{3,2,1,0:T(8,128)(2,1)S(1)} %bitcast.14), channel_id=1, source_target_pairs={{0,2},{1,3},{2,0},{3,1},{4,6},{5,7},{6,4},{7,5},{8,10},{9,11},{10,... | collective-permute-start | bytes 393224 | tf_op jit(solution)/shard_map/ppermute | solution.py:481
  50.5 8.7 %collective-permute-start.14 = (bf16[2,4,16,512]{3,2,1,0:T(8,128)(2,1)S(1)}, bf16[2,4,16,512]{3,2,1,0:T(8,128)(2,1)S(1)}, u32[]{:S(2)}, u32[]{:S(2)}) collective-permute-start(bf16[2,4,16,512]{3,2,1,0:T(8,128)(2,1)S(1)} %get-tuple-element.149), channel_id=1, source_target_pairs={{0,8},{4,12},{8,0},{12,4},{16,24},{20,28},{24,16},{28,20},{1,9},{5... | collective-permute-start | bytes 393224 | tf_op jit(solution)/shard_map/ppermute | solution.py:481
  50.9 8.9 %collective-permute-start.15 = (bf16[1,4,32,512]{3,2,1,0:T(8,128)(2,1)S(1)}, bf16[1,4,32,512]{3,2,1,0:T(8,128)(2,1)S(1)}, u32[]{:S(2)}, u32[]{:S(2)}) collective-permute-start(bf16[1,4,32,512]{3,2,1,0:T(8,128)(2,1)S(1)} %bitcast.10), channel_id=1, source_target_pairs={{0,2},{1,3},{2,0},{3,1},{4,6},{5,7},{6,4},{7,5},{8,10},{9,11},{10,... | collective-permute-start | bytes 393224 | tf_op jit(solution)/shard_map/ppermute | solution.py:481
  62.1 9.6 %collective-permute-start.19 = (bf16[1,4,16,512]{3,2,1,0:T(8,128)(2,1)}, bf16[1,4,16,512]{3,2,1,0:T(8,128)(2,1)}, u32[]{:S(2)}, u32[]{:S(2)}) collective-permute-start(bf16[1,4,16,512]{3,2,1,0:T(8,128)(2,1)} %get-tuple-element.160), channel_id=1, source_target_pairs={{0,16},{4,20},{8,24},{12,28},{16,0},{20,4},{24,8},{28,12},{1,17},{... | collective-permute-start | bytes 196616 | tf_op jit(solution)/shard_map/ppermute | solution.py:481
  63.3 13.8 %collective-permute-start.21 = (bf16[1,4,32,512]{3,2,1,0:T(8,128)(2,1)S(1)}, bf16[1,4,32,512]{3,2,1,0:T(8,128)(2,1)S(1)}, u32[]{:S(2)}, u32[]{:S(2)}) collective-permute-start(bf16[1,4,32,512]{3,2,1,0:T(8,128)(2,1)S(1)} %get-tuple-element.164.held_ref), channel_id=1, source_target_pairs={{0,16},{4,20},{8,24},{12,28},{16,0},{20,4},{24,8},{28,12},{1,17},{... | collective-permute-start | bytes 393224 | tf_op jit(solution)/shard_map/ppermute | solution.py:481
  65.9 15.8 %collective-permute-start.24 = (bf16[2,4,32,512]{3,2,1,0:T(8,128)(2,1)S(1)}, bf16[2,4,32,512]{3,2,1,0:T(8,128)(2,1)S(1)}, u32[]{:S(2)}, u32[]{:S(2)}) collective-permute-start(bf16[2,4,32,512]{3,2,1,0:T(8,128)(2,1)S(1)} %get-tuple-element.170.held_ref), channel_id=1, source_target_pairs={{0,1},{1,0},{2,3},{3,2},{4,5},{5,4},{6,7},{7,6},{8,9},{9,8},{10,11... | collective-permute-start | bytes 786440 | tf_op jit(solution)/shard_map/ppermute | solution.py:481
  72.9 8.8 %collective-permute-start.23 = (bf16[1,4,32,512]{3,2,1,0:T(8,128)(2,1)S(1)}, bf16[1,4,32,512]{3,2,1,0:T(8,128)(2,1)S(1)}, u32[]{:S(2)}, u32[]{:S(2)}) collective-permute-start(bf16[1,4,32,512]{3,2,1,0:T(8,128)(2,1)S(1)} %get-tuple-element.168.held_ref), channel_id=1, source_target_pairs={{0,16},{4,20},{8,24},{12,28},{16,0},{20,4},{24,8},{28,12},{1,17},{... | collective-permute-start | bytes 393224 | tf_op jit(solution)/shard_map/ppermute | solution.py:481
  77.2 8.7 %collective-permute-start.25 = (bf16[2,4,32,512]{3,2,1,0:T(8,128)(2,1)S(1)}, bf16[2,4,32,512]{3,2,1,0:T(8,128)(2,1)S(1)}, u32[]{:S(2)}, u32[]{:S(2)}) collective-permute-start(bf16[2,4,32,512]{3,2,1,0:T(8,128)(2,1)S(1)} %get-tuple-element.173.held_ref.refs_0_), channel_id=1, source_target_pairs={{0,8},{4,12},{8,0},{12,4},{16,24},{20,28},{24,16},{28,20},{1,9},{5... | collective-permute-start | bytes 786440 | tf_op jit(solution)/shard_map/ppermute | solution.py:481
  84.5 9.9 %collective-permute-start.28 = (bf16[2,4,32,512]{3,2,1,0:T(8,128)(2,1)S(1)}, bf16[2,4,32,512]{3,2,1,0:T(8,128)(2,1)S(1)}, u32[]{:S(2)}, u32[]{:S(2)}) collective-permute-start(bf16[2,4,32,512]{3,2,1,0:T(8,128)(2,1)S(1)} %get-tuple-element.179.held_ref.refs_2_), channel_id=1, source_target_pairs={{0,8},{4,12},{8,0},{12,4},{16,24},{20,28},{24,16},{28,20},{1,9},{5... | collective-permute-start | bytes 786440 | tf_op jit(solution)/shard_map/ppermute | solution.py:481
  86.4 14.6 %collective-permute-start.31 = (bf16[8,32,512]{2,1,0:T(8,128)(2,1)S(1)}, bf16[8,32,512]{2,1,0:T(8,128)(2,1)S(1)}, u32[]{:S(2)}, u32[]{:S(2)}) collective-permute-start(bf16[8,32,512]{2,1,0:T(8,128)(2,1)S(1)} %get-tuple-element.185), channel_id=1, source_target_pairs={{0,4},{4,0},{8,12},{12,8},{16,20},{20,16},{24,28},{28,24},{1,5},{5... | collective-permute-start | bytes 786440 | tf_op jit(solution)/shard_map/ppermute | solution.py:481
  88.2 12.8 %collective-permute-start.32 = (bf16[2,4,32,512]{3,2,1,0:T(8,128)(2,1)S(1)}, bf16[2,4,32,512]{3,2,1,0:T(8,128)(2,1)S(1)}, u32[]{:S(2)}, u32[]{:S(2)}) collective-permute-start(bf16[2,4,32,512]{3,2,1,0:T(8,128)(2,1)S(1)} %get-tuple-element.186.held_ref.refs_4_), channel_id=1, source_target_pairs={{0,8},{4,12},{8,0},{12,4},{16,24},{20,28},{24,16},{28,20},{1,9},{5... | collective-permute-start | bytes 786440 | tf_op jit(solution)/shard_map/ppermute | solution.py:481
  95.0 13.9 %collective-permute-start.35 = (bf16[8,32,512]{2,1,0:T(8,128)(2,1)S(1)}, bf16[8,32,512]{2,1,0:T(8,128)(2,1)S(1)}, u32[]{:S(2)}, u32[]{:S(2)}) collective-permute-start(bf16[8,32,512]{2,1,0:T(8,128)(2,1)S(1)} %get-tuple-element.192), channel_id=1, source_target_pairs={{0,4},{4,0},{8,12},{12,8},{16,20},{20,16},{24,28},{28,24},{1,5},{5... | collective-permute-start | bytes 786440 | tf_op jit(solution)/shard_map/ppermute | solution.py:481
  101.6 9.3 %collective-permute-start.37 = (bf16[8,32,512]{2,1,0:T(8,128)(2,1)S(1)}, bf16[8,32,512]{2,1,0:T(8,128)(2,1)S(1)}, u32[]{:S(2)}, u32[]{:S(2)}) collective-permute-start(bf16[8,32,512]{2,1,0:T(8,128)(2,1)S(1)} %get-tuple-element.195), channel_id=1, source_target_pairs={{0,4},{4,0},{8,12},{12,8},{16,20},{20,16},{24,28},{28,24},{1,5},{5... | collective-permute-start | bytes 786440 | tf_op jit(solution)/shard_map/ppermute | solution.py:481
  (24 other events, 153.1 us)

commit v13 on v12

--- a/solution.py
+++ b/solution.py
@@ -7,8 +7,8 @@
 
 SHARES = (2, 2, 2, 1, 1)
 ORDER = (
-    0, 1, 2, 0, 1, 4, 2, 3, 1, 0, 3, 2, 3, 0, 4, 1, 0, 2, 1, 4, 4, 0, 3, 1, 2, 0, 2, 3, 1, 3, 4, 0,
-    2, 4, 3, 1, 4, 2, 3, 4,
+    0, 1, 2, 0, 1, 2, 1, 3, 4, 0, 2, 1, 1, 4, 1, 2, 3, 4, 0, 2, 0, 3, 3, 2, 4, 1, 0, 4, 2, 4, 3, 1,
+    0, 3, 4, 2, 3, 0, 4, 3,
 )
 READ_CAP = 2
 VMEM_BYTES = 12 * 1024 * 1024
@@ -340,15 +340,16 @@
     return call(body, [both, TOKEN], [VMEM] * 3, [VMEM] * 2, (token, held, got))
 
 
-def mix(token, mine, offsets, held, got, weight):
+def mix(token, offsets, held, got, weight):
     _, blocks, rows, depth = held.shape
     width = weight.shape[1]
 
-    def body(token_ref, mine_ref, held_ref, got_ref, w_ref, out_ref, token_out):
+    def body(token_ref, held_ref, got_ref, w_ref, out_ref, token_out):
+        mine = lax.axis_index("feat")
         total = jnp.zeros((blocks * rows, width), jnp.float32)
         for n, offset in enumerate(offsets):
             piece = (held_ref if n < held.shape[0] else got_ref)[n % held.shape[0]]
-            at = pl.multiple_of((mine_ref[0] ^ offset) * depth, depth)
+            at = pl.multiple_of((mine ^ offset) * depth, depth)
             total += jnp.dot(
                 piece.reshape(blocks * rows, depth), w_ref[pl.ds(at, depth)], preferred_element_type=jnp.float32
             )
@@ -358,43 +359,36 @@
     return call(
         body,
         [jax.ShapeDtypeStruct((1, blocks, rows, width), jnp.bfloat16), TOKEN],
-        [VMEM, SMEM, VMEM, VMEM, VMEM],
+        [VMEM] * 4,
         [VMEM] * 2,
-        (token, mine, held, got, weight),
-    )
-
-
-def pick(token, choice, held, got):
+        (token, held, got, weight),
+    )
+
+
+def pick(token, wanted, held, got):
     count = 2 * held.shape[0] * READ_CAP
-
-    def body(token_ref, choice_ref, held_ref, got_ref, out, token_out):
+    extra = -(-count // 16) * 16
+    _, blocks, rows, width = held.shape
+
+    def body(token_ref, wanted_ref, held_ref, got_ref, out, token_out):
+        lines = wanted_ref[pl.ds(wanted.shape[0] - extra, extra)].astype(jnp.float32)
         for i in range(count):
             n = i // READ_CAP
             source = held_ref if n < held.shape[0] else got_ref
-            out[i] = source[n % held.shape[0], choice_ref[i]]
+            total = jnp.zeros((rows, width), jnp.bfloat16)
+            for b in range(blocks):
+                chosen = jnp.where(lines[i : i + 1] == b, 1.0, 0.0)
+                chosen = jnp.broadcast_to(chosen, (rows, width)).astype(jnp.bfloat16)
+                total += chosen * source[n % held.shape[0], b]
+            out[i] = total
         token_out[...] = token_ref[...]
 
     return call(
         body,
         [jax.ShapeDtypeStruct((count, *held.shape[2:]), held.dtype), TOKEN],
-        [VMEM, SMEM, VMEM, VMEM],
+        [VMEM] * 4,
         [VMEM] * 2,
-        (token, choice, held, got),
-    )
-
-
-def read_choice(token, got, count):
-    extra = -(-count // 16) * 16
-    first = got.shape[0] - extra
-
-    def body(token_ref, got_ref, choice, token_out):
-        lines = got_ref[pl.ds(first, extra)].astype(jnp.float32)
-        for i in range(count):
-            choice[i] = jnp.max(lines[i : i + 1]).astype(jnp.int32)
-        token_out[...] = token_ref[...]
-
-    return call(
-        body, [jax.ShapeDtypeStruct((count,), jnp.int32), TOKEN], [VMEM] * 2, [SMEM, VMEM], (token, got)
+        (token, wanted, held, got),
     )
 
 
@@ -470,7 +464,7 @@
 def local(features, tiles, tile_slot, tile_col, tile_id, touched, weight, readers):
     edges, feats = lax.axis_size("edge"), lax.axis_size("feat")
     half = edges // 2
-    me, mine = lax.axis_index("edge"), lax.axis_index("feat")
+    me = lax.axis_index("edge")
     block = tiles.shape[1]
     blocks = features.shape[0] // block
     width = features.shape[1]
@@ -481,7 +475,7 @@
         return lax.ppermute(value, axis, [(d, d ^ bit) for d in range(lax.axis_size(axis))])
 
     columns = offsets_of(edges, 2)
-    me, mine = me.reshape(1), mine.reshape(1)
+    me = me.reshape(1)
     column_bits = [1 << i for i in range(1, edges.bit_length() - 1)]
     orders = [[*column_bits, 1], [1, *column_bits]]
     table, entry, *early, inputs = first_part(
@@ -509,26 +503,26 @@
             (held,) = chained(join, held, got)
             bit //= 2
 
-    choice, nears, fars = None, [], []
+    wanted, nears, fars = None, [], []
     ended = object()
 
     def one_part(part):
-        nonlocal choice
+        nonlocal wanted
         first, *rest = orders[min(part, 1)]
         got = flip(away[part], first)
         yield
         total, sent = chained(combine, kept[part], got, weight)
         if part == 1:
-            (choice,) = chained(read_choice, got, half * READ_CAP)
+            wanted = got
         for bit in rest:
             got = flip(sent, bit)
             yield
             total, *sent = chained(combine, total, got, weight)
             sent = sent[0] if sent else None
         held, got = yield from spread(total[None], feats, 1, "feat")
-        (mixed,) = chained(mix, mine, offsets_of(feats, 1), held, got, weight)
+        (mixed,) = chained(mix, offsets_of(feats, 1), held, got, weight)
         held, got = yield from spread(mixed, edges, 2, "edge")
-        (picked,) = chained(pick, choice, held, got)
+        (picked,) = chained(pick, wanted, held, got)
         nears.append((held, got, spans[part]))
         far = flip(picked, 1)
         yield

time: 119 us -> 118 us (level)
  waiting for transfers between devices: 41.1 us -> 46 us
  Pallas kernels: 23.7 us -> 19.3 us
  local copies, waits for them, and re-layouts: 3.14 us -> 1.73 us
    ppermute x40, waiting for transfers between devices: 41.1 us -> 46 us  [flip(): lax.ppermute(value, axis, [(d, d ^ bit) for d in range(lax.axis_size(axis...]
    pallas_call x45 -> x44, Pallas kernels: 23.7 us -> 19.3 us  [call(): pl.pallas_call(body, out_shape=out_shape, in_specs=in_specs, out_specs=ou...]
    unnamed x16 -> x14, local copies, waits for them, and re-layouts: 3.14 us -> 1.73 us
  transfers between devices with their start and end apart: 40 -> 40, of which waited for: 16 -> 21; matrix products, arithmetic and copies ran while one was open for 0% -> 0% of each run, Pallas kernels for 15% -> 11%
where the time goes in v13:
time: 118 us
  starting transfers between devices  49.6 us (42%)
  waiting for transfers between devices  46 us (39%)
  Pallas kernels  19.3 us (16%)
  local copies, waits for them, and re-layouts  1.73 us (1%)
    ppermute x40, starting transfers between devices, flip(): lax.ppermute(value, axis, [(d, d ^ bit) for d in range(lax.axis_size(axis...  49.6 us
    ppermute x40, waiting for transfers between devices, flip(): lax.ppermute(value, axis, [(d, d ^ bit) for d in range(lax.axis_size(axis...  46 us
    pallas_call x44, Pallas kernels, call(): pl.pallas_call(body, out_shape=out_shape, in_specs=in_specs, out_specs=ou...  19.3 us
  transfers between devices with their start and end apart: 40, of which 21 were waited for; matrix products, arithmetic and copies ran while one was open for 0% of the time, Pallas kernels for 11%

profile of v13, /device:TPU:0, one launch (start us, length us, event | category | flops | bytes accessed | tf_op | source)
XLA Modules:
  0.0 117.7 jit_solution(2518477505280002797)
XLA Ops:
  0.6 4.6 %shard_map.95 = (s32[256]{0:T(256)}, s32[16]{0:T(128)}, bf16[4,4,32,512]{3,2,1,0:T(8,128)(2,1)}, bf16[528,512]{1,0:T(8,128)(2,1)}, bf16[512,512]{1,0:T(8,128)(2,1)}) custom-call(s32[1]{0:T(128)} %bitcast.me_ref, s32[96]{0:T(128)} %slot_hbm.1, s32[96]{0:T(128)} %col_hbm.1, s32[96]{0:T(128)} %id_hbm.1, s32[8,4,8]{2,1,0:T(4,128)} %bitcast.21, s32[16]{0:T(128)} %readers_ref.3, ...), custom_call_target="tpu_custom_call" | custom-call | bytes 1 | tf_op jit(solution)/shard_map/pallas_call | solution.py:24
  5.2 3.0 %collective-permute-start.1 = (bf16[528,512]{1,0:T(8,128)(2,1)}, bf16[528,512]{1,0:T(8,128)(2,1)S(1)}, u32[]{:S(2)}, u32[]{:S(2)}) collective-permute-start(bf16[528,512]{1,0:T(8,128)(2,1)} %get-tuple-element.108), channel_id=1, source_target_pairs={{0,4},{4,0},{8,12},{12,8},{16,20},{20,16},{24,28},{28,24},{1,5},{5... | collective-permute-start | bytes 1622024 | tf_op jit(solution)/shard_map/ppermute | solution.py:475
  11.5 3.4 %shard_map.97 = (bf16[4,4,32,512]{3,2,1,0:T(8,128)(2,1)S(1)}, bf16[4,4,16,512]{3,2,1,0:T(8,128)(2,1)S(1)}, bf16[4,4,16,512]{3,2,1,0:T(8,128)(2,1)S(1)}, bf16[4,4,32,512]{3,2,1,0:T(8,128)(2,1)S(1)}, f32[8,128]{1,0:T(8,128)}) custom-call(s32[256]{0:T(256)S(1)} %copy-done.4, bf16[48,128,128]{2,1,0:T(8,128)(2,1)S(1)} %copy-done.1, bf16[512,512]{1,0:T(8,128)(2,1)S(1)} %copy-done.2), custom_call_target="tpu_custom_call" | custom-call | bytes 1 | tf_op jit(solution)/shard_map/pallas_call | solution.py:24
  15.5 2.3 %shard_map.96 = (bf16[4,4,32,512]{3,2,1,0:T(8,128)(2,1)S(1)}, bf16[4,4,32,512]{3,2,1,0:T(8,128)(2,1)S(1)}, bf16[4,4,16,512]{3,2,1,0:T(8,128)(2,1)S(1)}, bf16[4,4,16,512]{3,2,1,0:T(8,128)(2,1)S(1)}, f32[8,128]{1,0:T(8,128)S(1)}) custom-call(s32[256]{0:T(256)S(1)} %copy-done.5, bf16[48,128,128]{2,1,0:T(8,128)(2,1)S(1)} %copy-done.1, bf16[512,512]{1,0:T(8,128)(2,1)S(1)} %copy-done.2), custom_call_target="tpu_custom_call" | custom-call | bytes 1 | tf_op jit(solution)/shard_map/pallas_call | solution.py:24
  17.7 4.1 %collective-permute-done.got_ref = bf16[4,4,32,512]{3,2,1,0:T(8,128)(2,1)S(1)} collective-permute-done((bf16[4,4,32,512]{3,2,1,0:T(8,128)(2,1)}, bf16[4,4,32,512]{3,2,1,0:T(8,128)(2,1)S(1)}, u32[]{:S(2)}, u32[]{:S(2)}) %collective-permute-start) | collective-permute-done | bytes 524320 | tf_op jit(solution)/shard_map/ppermute | solution.py:475
  22.1 2.7 %collective-permute-start.3 = (bf16[2,4,32,512]{3,2,1,0:T(8,128)(2,1)S(1)}, bf16[2,4,32,512]{3,2,1,0:T(8,128)(2,1)S(1)}, u32[]{:S(2)}, u32[]{:S(2)}) collective-permute-start(bf16[2,4,32,512]{3,2,1,0:T(8,128)(2,1)S(1)} %get-tuple-element.114), channel_id=1, source_target_pairs={{0,16},{4,20},{8,24},{12,28},{16,0},{20,4},{24,8},{28,12},{1,17},{... | collective-permute-start | bytes 786440 | tf_op jit(solution)/shard_map/ppermute | solution.py:475
  26.7 5.3 %collective-permute-done.2.got_ref = bf16[4,4,32,512]{3,2,1,0:T(8,128)(2,1)S(1)} collective-permute-done((bf16[4,4,32,512]{3,2,1,0:T(8,128)(2,1)S(1)}, bf16[4,4,32,512]{3,2,1,0:T(8,128)(2,1)S(1)}, u32[]{:S(2)}, u32[]{:S(2)}) %collective-permute-start.2) | collective-permute-done | bytes 524320 | tf_op jit(solution)/shard_map/ppermute | solution.py:475
  36.7 2.3 %collective-permute-start.6 = (bf16[1,4,32,512]{3,2,1,0:T(8,128)(2,1)S(1)}, bf16[1,4,32,512]{3,2,1,0:T(8,128)(2,1)S(1)}, u32[]{:S(2)}, u32[]{:S(2)}) collective-permute-start(bf16[1,4,32,512]{3,2,1,0:T(8,128)(2,1)S(1)} %get-tuple-element.123), channel_id=1, source_target_pairs={{0,16},{4,20},{8,24},{12,28},{16,0},{20,4},{24,8},{28,12},{1,17},{... | collective-permute-start | bytes 393224 | tf_op jit(solution)/shard_map/ppermute | solution.py:475
  40.5 4.1 %collective-permute-done.5.got_ref = bf16[2,4,32,512]{3,2,1,0:T(8,128)(2,1)S(1)} collective-permute-done((bf16[2,4,32,512]{3,2,1,0:T(8,128)(2,1)S(1)}, bf16[2,4,32,512]{3,2,1,0:T(8,128)(2,1)S(1)}, u32[]{:S(2)}, u32[]{:S(2)}) %collective-permute-start.5) | collective-permute-done | bytes 262176 | tf_op jit(solution)/shard_map/ppermute | solution.py:475
  49.5 2.6 %collective-permute-done.10.got_ref = bf16[1,4,32,512]{3,2,1,0:T(8,128)(2,1)S(1)} collective-permute-done((bf16[1,4,32,512]{3,2,1,0:T(8,128)(2,1)S(1)}, bf16[1,4,32,512]{3,2,1,0:T(8,128)(2,1)S(1)}, u32[]{:S(2)}, u32[]{:S(2)}) %collective-permute-start.10) | collective-permute-done | bytes 131104 | tf_op jit(solution)/shard_map/ppermute | solution.py:475
  59.9 4.4 %collective-permute-done.14.got_ref = bf16[1,4,32,512]{3,2,1,0:T(8,128)(2,1)S(1)} collective-permute-done((bf16[1,4,32,512]{3,2,1,0:T(8,128)(2,1)S(1)}, bf16[1,4,32,512]{3,2,1,0:T(8,128)(2,1)S(1)}, u32[]{:S(2)}, u32[]{:S(2)}) %collective-permute-start.14) | collective-permute-done | bytes 131104 | tf_op jit(solution)/shard_map/ppermute | solution.py:475
  67.0 2.7 %collective-permute-start.25 = (bf16[2,4,32,512]{3,2,1,0:T(8,128)(2,1)S(1)}, bf16[2,4,32,512]{3,2,1,0:T(8,128)(2,1)S(1)}, u32[]{:S(2)}, u32[]{:S(2)}) collective-permute-start(bf16[2,4,32,512]{3,2,1,0:T(8,128)(2,1)S(1)} %get-tuple-element.169.held_ref.refs_0_), channel_id=1, source_target_pairs={{0,8},{4,12},{8,0},{12,4},{16,24},{20,28},{24,16},{28,20},{1,9},{5... | collective-permute-start | bytes 786440 | tf_op jit(solution)/shard_map/ppermute | solution.py:475
  70.8 2.5 %collective-permute-done.21.got_ref = bf16[1,4,16,512]{3,2,1,0:T(8,128)(2,1)S(1)} collective-permute-done((bf16[1,4,16,512]{3,2,1,0:T(8,128)(2,1)S(1)}, bf16[1,4,16,512]{3,2,1,0:T(8,128)(2,1)S(1)}, u32[]{:S(2)}, u32[]{:S(2)}) %collective-permute-start.21) | collective-permute-done | bytes 65568 | tf_op jit(solution)/shard_map/ppermute | solution.py:475
  75.2 2.5 %collective-permute-done.22.got_ref = bf16[1,4,16,512]{3,2,1,0:T(8,128)(2,1)S(1)} collective-permute-done((bf16[1,4,16,512]{3,2,1,0:T(8,128)(2,1)S(1)}, bf16[1,4,16,512]{3,2,1,0:T(8,128)(2,1)S(1)}, u32[]{:S(2)}, u32[]{:S(2)}) %collective-permute-start.22) | collective-permute-done | bytes 65568 | tf_op jit(solution)/shard_map/ppermute | solution.py:475
  79.3 2.4 %collective-permute-start.28 = (bf16[2,4,32,512]{3,2,1,0:T(8,128)(2,1)S(1)}, bf16[2,4,32,512]{3,2,1,0:T(8,128)(2,1)S(1)}, u32[]{:S(2)}, u32[]{:S(2)}) collective-permute-start(bf16[2,4,32,512]{3,2,1,0:T(8,128)(2,1)S(1)} %get-tuple-element.175.held_ref.refs_2_), channel_id=1, source_target_pairs={{0,8},{4,12},{8,0},{12,4},{16,24},{20,28},{24,16},{28,20},{1,9},{5... | collective-permute-start | bytes 786440 | tf_op jit(solution)/shard_map/ppermute | solution.py:475
  83.2 2.8 %collective-permute-done.24.got_ref = bf16[1,4,16,512]{3,2,1,0:T(8,128)(2,1)S(1)} collective-permute-done((bf16[1,4,16,512]{3,2,1,0:T(8,128)(2,1)S(1)}, bf16[1,4,16,512]{3,2,1,0:T(8,128)(2,1)S(1)}, u32[]{:S(2)}, u32[]{:S(2)}) %collective-permute-start.24) | collective-permute-done | bytes 65568 | tf_op jit(solution)/shard_map/ppermute | solution.py:475
  86.2 2.8 %collective-permute-start.31 = (bf16[8,32,512]{2,1,0:T(8,128)(2,1)S(1)}, bf16[8,32,512]{2,1,0:T(8,128)(2,1)S(1)}, u32[]{:S(2)}, u32[]{:S(2)}) collective-permute-start(bf16[8,32,512]{2,1,0:T(8,128)(2,1)S(1)} %get-tuple-element.181), channel_id=1, source_target_pairs={{0,4},{4,0},{8,12},{12,8},{16,20},{20,16},{24,28},{28,24},{1,5},{5... | collective-permute-start | bytes 786440 | tf_op jit(solution)/shard_map/ppermute | solution.py:475
  89.9 3.1 %collective-permute-start.29 = (bf16[1,4,16,512]{3,2,1,0:T(8,128)(2,1)S(1)}, bf16[1,4,16,512]{3,2,1,0:T(8,128)(2,1)S(1)}, u32[]{:S(2)}, u32[]{:S(2)}) collective-permute-start(bf16[1,4,16,512]{3,2,1,0:T(8,128)(2,1)S(1)} %get-tuple-element.177.held_ref), channel_id=1, source_target_pairs={{0,16},{4,20},{8,24},{12,28},{16,0},{20,4},{24,8},{28,12},{1,17},{... | collective-permute-start | bytes 196616 | tf_op jit(solution)/shard_map/ppermute | solution.py:475
  93.3 3.4 %collective-permute-done.29.got_ref = bf16[1,4,16,512]{3,2,1,0:T(8,128)(2,1)S(1)} collective-permute-done((bf16[1,4,16,512]{3,2,1,0:T(8,128)(2,1)S(1)}, bf16[1,4,16,512]{3,2,1,0:T(8,128)(2,1)S(1)}, u32[]{:S(2)}, u32[]{:S(2)}) %collective-permute-start.29) | collective-permute-done | bytes 65568 | tf_op jit(solution)/shard_map/ppermute | solution.py:475
  97.3 3.4 %collective-permute-start.33 = (bf16[1,4,16,512]{3,2,1,0:T(8,128)(2,1)S(1)}, bf16[1,4,16,512]{3,2,1,0:T(8,128)(2,1)S(1)}, u32[]{:S(2)}, u32[]{:S(2)}) collective-permute-start(bf16[1,4,16,512]{3,2,1,0:T(8,128)(2,1)S(1)} %get-tuple-element.184.held_ref), channel_id=1, source_target_pairs={{0,16},{4,20},{8,24},{12,28},{16,0},{20,4},{24,8},{28,12},{1,17},{... | collective-permute-start | bytes 196616 | tf_op jit(solution)/shard_map/ppermute | solution.py:475
  103.2 3.8 %collective-permute-start.36 = (bf16[2,4,16,512]{3,2,1,0:T(8,128)(2,1)S(1)}, bf16[2,4,16,512]{3,2,1,0:T(8,128)(2,1)S(1)}, u32[]{:S(2)}, u32[]{:S(2)}) collective-permute-start(bf16[2,4,16,512]{3,2,1,0:T(8,128)(2,1)S(1)} %get-tuple-element.189.held_ref.refs_8_), channel_id=1, source_target_pairs={{0,8},{4,12},{8,0},{12,4},{16,24},{20,28},{24,16},{28,20},{1,9},{5... | collective-permute-start | bytes 393224 | tf_op jit(solution)/shard_map/ppermute | solution.py:475
  107.5 2.5 %collective-permute-done.36.got_ref.refs_9_ = bf16[2,4,16,512]{3,2,1,0:T(8,128)(2,1)S(1)} collective-permute-done((bf16[2,4,16,512]{3,2,1,0:T(8,128)(2,1)S(1)}, bf16[2,4,16,512]{3,2,1,0:T(8,128)(2,1)S(1)}, u32[]{:S(2)}, u32[]{:S(2)}) %collective-permute-start.36) | collective-permute-done | bytes 131104 | tf_op jit(solution)/shard_map/ppermute | solution.py:475
  110.5 2.6 %collective-permute-done.38.value_ref.refs_13_ = bf16[8,16,512]{2,1,0:T(8,128)(2,1)S(1)} collective-permute-done((bf16[8,16,512]{2,1,0:T(8,128)(2,1)S(1)}, bf16[8,16,512]{2,1,0:T(8,128)(2,1)S(1)}, u32[]{:S(2)}, u32[]{:S(2)}) %collective-permute-start.38) | collective-permute-done | bytes 131104 | tf_op jit(solution)/shard_map/ppermute | solution.py:475
  113.1 2.7 %shard_map.137 = (bf16[4,128,512]{2,1,0:T(8,128)(2,1)}, bf16[16,128,512]{2,1,0:T(8,128)(2,1)}, f32[8,128]{1,0:T(8,128)S(1)}) custom-call(f32[8,128]{1,0:T(8,128)S(1)} %shard_map.136.token_ref, s32[1]{0:T(128)} %bitcast.me_ref, s32[16]{0:T(128)S(1)} %copy-done.3, s32[16]{0:T(128)S(1)} %copy-done.6, ...), custom_call_target="tpu_custom_call" | custom-call | bytes 1 | tf_op jit(solution)/shard_map/pallas_call | solution.py:24
  (114 shorter events, 40.9 us)
Async XLA Ops:
  5.2 19.5 %collective-permute-start.1 = (bf16[528,512]{1,0:T(8,128)(2,1)}, bf16[528,512]{1,0:T(8,128)(2,1)S(1)}, u32[]{:S(2)}, u32[]{:S(2)}) collective-permute-start(bf16[528,512]{1,0:T(8,128)(2,1)} %get-tuple-element.108), channel_id=1, source_target_pairs={{0,4},{4,0},{8,12},{12,8},{16,20},{20,16},{24,28},{28,24},{1,5},{5... | collective-permute-start | bytes 1622024 | tf_op jit(solution)/shard_map/ppermute | solution.py:475
  8.2 13.6 %collective-permute-start = (bf16[4,4,32,512]{3,2,1,0:T(8,128)(2,1)}, bf16[4,4,32,512]{3,2,1,0:T(8,128)(2,1)S(1)}, u32[]{:S(2)}, u32[]{:S(2)}) collective-permute-start(bf16[4,4,32,512]{3,2,1,0:T(8,128)(2,1)} %get-tuple-element.105), channel_id=1, source_target_pairs={{0,8},{4,12},{8,0},{12,4},{16,24},{20,28},{24,16},{28,20},{1,9},{5... | collective-permute-start | bytes 1572872 | tf_op jit(solution)/shard_map/ppermute | solution.py:475
  14.9 17.1 %collective-permute-start.2 = (bf16[4,4,32,512]{3,2,1,0:T(8,128)(2,1)S(1)}, bf16[4,4,32,512]{3,2,1,0:T(8,128)(2,1)S(1)}, u32[]{:S(2)}, u32[]{:S(2)}) collective-permute-start(bf16[4,4,32,512]{3,2,1,0:T(8,128)(2,1)S(1)} %get-tuple-element.111), channel_id=1, source_target_pairs={{0,4},{4,0},{8,12},{12,8},{16,20},{20,16},{24,28},{28,24},{1,5},{5... | collective-permute-start | bytes 1572872 | tf_op jit(solution)/shard_map/ppermute | solution.py:475
  22.1 14.0 %collective-permute-start.3 = (bf16[2,4,32,512]{3,2,1,0:T(8,128)(2,1)S(1)}, bf16[2,4,32,512]{3,2,1,0:T(8,128)(2,1)S(1)}, u32[]{:S(2)}, u32[]{:S(2)}) collective-permute-start(bf16[2,4,32,512]{3,2,1,0:T(8,128)(2,1)S(1)} %get-tuple-element.114), channel_id=1, source_target_pairs={{0,16},{4,20},{8,24},{12,28},{16,0},{20,4},{24,8},{28,12},{1,17},{... | collective-permute-start | bytes 786440 | tf_op jit(solution)/shard_map/ppermute | solution.py:475
  25.0 11.6 %collective-permute-start.4 = (bf16[2,4,32,512]{3,2,1,0:T(8,128)(2,1)S(1)}, bf16[2,4,32,512]{3,2,1,0:T(8,128)(2,1)S(1)}, u32[]{:S(2)}, u32[]{:S(2)}) collective-permute-start(bf16[2,4,32,512]{3,2,1,0:T(8,128)(2,1)S(1)} %get-tuple-element.117), channel_id=1, source_target_pairs={{0,8},{4,12},{8,0},{12,4},{16,24},{20,28},{24,16},{28,20},{1,9},{5... | collective-permute-start | bytes 786440 | tf_op jit(solution)/shard_map/ppermute | solution.py:475
  32.2 12.3 %collective-permute-start.5 = (bf16[2,4,32,512]{3,2,1,0:T(8,128)(2,1)S(1)}, bf16[2,4,32,512]{3,2,1,0:T(8,128)(2,1)S(1)}, u32[]{:S(2)}, u32[]{:S(2)}) collective-permute-start(bf16[2,4,32,512]{3,2,1,0:T(8,128)(2,1)S(1)} %get-tuple-element.120), channel_id=1, source_target_pairs={{0,8},{4,12},{8,0},{12,4},{16,24},{20,28},{24,16},{28,20},{1,9},{5... | collective-permute-start | bytes 786440 | tf_op jit(solution)/shard_map/ppermute | solution.py:475
  34.1 12.7 %collective-permute-start.7 = (bf16[4,4,16,512]{3,2,1,0:T(8,128)(2,1)S(1)}, bf16[4,4,16,512]{3,2,1,0:T(8,128)(2,1)S(1)}, u32[]{:S(2)}, u32[]{:S(2)}) collective-permute-start(bf16[4,4,16,512]{3,2,1,0:T(8,128)(2,1)S(1)} %get-tuple-element.126), channel_id=1, source_target_pairs={{0,4},{4,0},{8,12},{12,8},{16,20},{20,16},{24,28},{28,24},{1,5},{5... | collective-permute-start | bytes 786440 | tf_op jit(solution)/shard_map/ppermute | solution.py:475
  35.6 12.4 %collective-permute-start.8 = (bf16[4,4,16,512]{3,2,1,0:T(8,128)(2,1)S(1)}, bf16[4,4,16,512]{3,2,1,0:T(8,128)(2,1)S(1)}, u32[]{:S(2)}, u32[]{:S(2)}) collective-permute-start(bf16[4,4,16,512]{3,2,1,0:T(8,128)(2,1)S(1)} %get-tuple-element.129), channel_id=1, source_target_pairs={{0,4},{4,0},{8,12},{12,8},{16,20},{20,16},{24,28},{28,24},{1,5},{5... | collective-permute-start | bytes 786440 | tf_op jit(solution)/shard_map/ppermute | solution.py:475
  36.7 8.4 %collective-permute-start.6 = (bf16[1,4,32,512]{3,2,1,0:T(8,128)(2,1)S(1)}, bf16[1,4,32,512]{3,2,1,0:T(8,128)(2,1)S(1)}, u32[]{:S(2)}, u32[]{:S(2)}) collective-permute-start(bf16[1,4,32,512]{3,2,1,0:T(8,128)(2,1)S(1)} %get-tuple-element.123), channel_id=1, source_target_pairs={{0,16},{4,20},{8,24},{12,28},{16,0},{20,4},{24,8},{28,12},{1,17},{... | collective-permute-start | bytes 393224 | tf_op jit(solution)/shard_map/ppermute | solution.py:475
  39.0 10.4 %collective-permute-start.9 = (bf16[1,4,32,512]{3,2,1,0:T(8,128)(2,1)S(1)}, bf16[1,4,32,512]{3,2,1,0:T(8,128)(2,1)S(1)}, u32[]{:S(2)}, u32[]{:S(2)}) collective-permute-start(bf16[1,4,32,512]{3,2,1,0:T(8,128)(2,1)S(1)} %get-tuple-element.132), channel_id=1, source_target_pairs={{0,4},{4,0},{8,12},{12,8},{16,20},{20,16},{24,28},{28,24},{1,5},{5... | collective-permute-start | bytes 393224 | tf_op jit(solution)/shard_map/ppermute | solution.py:475
  44.7 7.4 %collective-permute-start.10 = (bf16[1,4,32,512]{3,2,1,0:T(8,128)(2,1)S(1)}, bf16[1,4,32,512]{3,2,1,0:T(8,128)(2,1)S(1)}, u32[]{:S(2)}, u32[]{:S(2)}) collective-permute-start(bf16[1,4,32,512]{3,2,1,0:T(8,128)(2,1)S(1)} %get-tuple-element.135), channel_id=1, source_target_pairs={{0,16},{4,20},{8,24},{12,28},{16,0},{20,4},{24,8},{28,12},{1,17},{... | collective-permute-start | bytes 393224 | tf_op jit(solution)/shard_map/ppermute | solution.py:475
  54.2 10.1 %collective-permute-start.14 = (bf16[1,4,32,512]{3,2,1,0:T(8,128)(2,1)S(1)}, bf16[1,4,32,512]{3,2,1,0:T(8,128)(2,1)S(1)}, u32[]{:S(2)}, u32[]{:S(2)}) collective-permute-start(bf16[1,4,32,512]{3,2,1,0:T(8,128)(2,1)S(1)} %get-tuple-element.144.held_ref), channel_id=1, source_target_pairs={{0,16},{4,20},{8,24},{12,28},{16,0},{20,4},{24,8},{28,12},{1,17},{... | collective-permute-start | bytes 393224 | tf_op jit(solution)/shard_map/ppermute | solution.py:475
  56.0 8.4 %collective-permute-start.15 = (bf16[1,4,32,512]{3,2,1,0:T(8,128)(2,1)S(1)}, bf16[1,4,32,512]{3,2,1,0:T(8,128)(2,1)S(1)}, u32[]{:S(2)}, u32[]{:S(2)}) collective-permute-start(bf16[1,4,32,512]{3,2,1,0:T(8,128)(2,1)S(1)} %bitcast.11), channel_id=1, source_target_pairs={{0,2},{1,3},{2,0},{3,1},{4,6},{5,7},{6,4},{7,5},{8,10},{9,11},{10,... | collective-permute-start | bytes 393224 | tf_op jit(solution)/shard_map/ppermute | solution.py:475
  57.5 7.8 %collective-permute-start.16 = (bf16[2,4,16,512]{3,2,1,0:T(8,128)(2,1)S(1)}, bf16[2,4,16,512]{3,2,1,0:T(8,128)(2,1)S(1)}, u32[]{:S(2)}, u32[]{:S(2)}) collective-permute-start(bf16[2,4,16,512]{3,2,1,0:T(8,128)(2,1)S(1)} %get-tuple-element.149), channel_id=1, source_target_pairs={{0,8},{4,12},{8,0},{12,4},{16,24},{20,28},{24,16},{28,20},{1,9},{5... | collective-permute-start | bytes 393224 | tf_op jit(solution)/shard_map/ppermute | solution.py:475
  58.9 7.5 %collective-permute-start.18 = (bf16[1,4,32,512]{3,2,1,0:T(8,128)(2,1)S(1)}, bf16[1,4,32,512]{3,2,1,0:T(8,128)(2,1)S(1)}, u32[]{:S(2)}, u32[]{:S(2)}) collective-permute-start(bf16[1,4,32,512]{3,2,1,0:T(8,128)(2,1)S(1)} %bitcast.9), channel_id=1, source_target_pairs={{0,2},{1,3},{2,0},{3,1},{4,6},{5,7},{6,4},{7,5},{8,10},{9,11},{10,... | collective-permute-start | bytes 393224 | tf_op jit(solution)/shard_map/ppermute | solution.py:475
  67.0 19.0 %collective-permute-start.25 = (bf16[2,4,32,512]{3,2,1,0:T(8,128)(2,1)S(1)}, bf16[2,4,32,512]{3,2,1,0:T(8,128)(2,1)S(1)}, u32[]{:S(2)}, u32[]{:S(2)}) collective-permute-start(bf16[2,4,32,512]{3,2,1,0:T(8,128)(2,1)S(1)} %get-tuple-element.169.held_ref.refs_0_), channel_id=1, source_target_pairs={{0,8},{4,12},{8,0},{12,4},{16,24},{20,28},{24,16},{28,20},{1,9},{5... | collective-permute-start | bytes 786440 | tf_op jit(solution)/shard_map/ppermute | solution.py:475
  70.2 9.1 %collective-permute-start.23 = (bf16[1,4,32,512]{3,2,1,0:T(8,128)(2,1)S(1)}, bf16[1,4,32,512]{3,2,1,0:T(8,128)(2,1)S(1)}, u32[]{:S(2)}, u32[]{:S(2)}) collective-permute-start(bf16[1,4,32,512]{3,2,1,0:T(8,128)(2,1)S(1)} %get-tuple-element.165.held_ref), channel_id=1, source_target_pairs={{0,16},{4,20},{8,24},{12,28},{16,0},{20,4},{24,8},{28,12},{1,17},{... | collective-permute-start | bytes 393224 | tf_op jit(solution)/shard_map/ppermute | solution.py:475
  75.0 14.0 %collective-permute-start.26 = (bf16[1,4,32,512]{3,2,1,0:T(8,128)(2,1)S(1)}, bf16[1,4,32,512]{3,2,1,0:T(8,128)(2,1)S(1)}, u32[]{:S(2)}, u32[]{:S(2)}) collective-permute-start(bf16[1,4,32,512]{3,2,1,0:T(8,128)(2,1)S(1)} %get-tuple-element.171.held_ref), channel_id=1, source_target_pairs={{0,16},{4,20},{8,24},{12,28},{16,0},{20,4},{24,8},{28,12},{1,17},{... | collective-permute-start | bytes 393224 | tf_op jit(solution)/shard_map/ppermute | solution.py:475
  79.3 13.6 %collective-permute-start.28 = (bf16[2,4,32,512]{3,2,1,0:T(8,128)(2,1)S(1)}, bf16[2,4,32,512]{3,2,1,0:T(8,128)(2,1)S(1)}, u32[]{:S(2)}, u32[]{:S(2)}) collective-permute-start(bf16[2,4,32,512]{3,2,1,0:T(8,128)(2,1)S(1)} %get-tuple-element.175.held_ref.refs_2_), channel_id=1, source_target_pairs={{0,8},{4,12},{8,0},{12,4},{16,24},{20,28},{24,16},{28,20},{1,9},{5... | collective-permute-start | bytes 786440 | tf_op jit(solution)/shard_map/ppermute | solution.py:475
  86.2 15.0 %collective-permute-start.31 = (bf16[8,32,512]{2,1,0:T(8,128)(2,1)S(1)}, bf16[8,32,512]{2,1,0:T(8,128)(2,1)S(1)}, u32[]{:S(2)}, u32[]{:S(2)}) collective-permute-start(bf16[8,32,512]{2,1,0:T(8,128)(2,1)S(1)} %get-tuple-element.181), channel_id=1, source_target_pairs={{0,4},{4,0},{8,12},{12,8},{16,20},{20,16},{24,28},{28,24},{1,5},{5... | collective-permute-start | bytes 786440 | tf_op jit(solution)/shard_map/ppermute | solution.py:475
  89.0 12.1 %collective-permute-start.32 = (bf16[2,4,32,512]{3,2,1,0:T(8,128)(2,1)S(1)}, bf16[2,4,32,512]{3,2,1,0:T(8,128)(2,1)S(1)}, u32[]{:S(2)}, u32[]{:S(2)}) collective-permute-start(bf16[2,4,32,512]{3,2,1,0:T(8,128)(2,1)S(1)} %get-tuple-element.182.held_ref.refs_4_), channel_id=1, source_target_pairs={{0,8},{4,12},{8,0},{12,4},{16,24},{20,28},{24,16},{28,20},{1,9},{5... | collective-permute-start | bytes 786440 | tf_op jit(solution)/shard_map/ppermute | solution.py:475
  89.2 7.6 %collective-permute-start.30 = (bf16[2,4,16,512]{3,2,1,0:T(8,128)(2,1)S(1)}, bf16[2,4,16,512]{3,2,1,0:T(8,128)(2,1)S(1)}, u32[]{:S(2)}, u32[]{:S(2)}) collective-permute-start(bf16[2,4,16,512]{3,2,1,0:T(8,128)(2,1)S(1)} %get-tuple-element.179.held_ref), channel_id=1, source_target_pairs={{0,1},{1,0},{2,3},{3,2},{4,5},{5,4},{6,7},{7,6},{8,9},{9,8},{10,11... | collective-permute-start | bytes 393224 | tf_op jit(solution)/shard_map/ppermute | solution.py:475
  93.0 14.4 %collective-permute-start.35 = (bf16[8,32,512]{2,1,0:T(8,128)(2,1)S(1)}, bf16[8,32,512]{2,1,0:T(8,128)(2,1)S(1)}, u32[]{:S(2)}, u32[]{:S(2)}) collective-permute-start(bf16[8,32,512]{2,1,0:T(8,128)(2,1)S(1)} %get-tuple-element.188), channel_id=1, source_target_pairs={{0,4},{4,0},{8,12},{12,8},{16,20},{20,16},{24,28},{28,24},{1,5},{5... | collective-permute-start | bytes 786440 | tf_op jit(solution)/shard_map/ppermute | solution.py:475
  101.3 9.2 %collective-permute-start.37 = (bf16[8,32,512]{2,1,0:T(8,128)(2,1)S(1)}, bf16[8,32,512]{2,1,0:T(8,128)(2,1)S(1)}, u32[]{:S(2)}, u32[]{:S(2)}) collective-permute-start(bf16[8,32,512]{2,1,0:T(8,128)(2,1)S(1)} %get-tuple-element.191), channel_id=1, source_target_pairs={{0,4},{4,0},{8,12},{12,8},{16,20},{20,16},{24,28},{28,24},{1,5},{5... | collective-permute-start | bytes 786440 | tf_op jit(solution)/shard_map/ppermute | solution.py:475
  (23 other events, 151.5 us)

commit v14 on v13

--- a/solution.py
+++ b/solution.py
@@ -7,8 +7,8 @@
 
 SHARES = (2, 2, 2, 1, 1)
 ORDER = (
-    0, 1, 2, 0, 1, 2, 1, 3, 4, 0, 2, 1, 1, 4, 1, 2, 3, 4, 0, 2, 0, 3, 3, 2, 4, 1, 0, 4, 2, 4, 3, 1,
-    0, 3, 4, 2, 3, 0, 4, 3,
+    0, 1, 2, 0, 1, 4, 0, 2, 1, 0, 4, 2, 1, 3, 0, 4, 2, 1, 3, 4, 0, 1, 4, 2, 3, 0, 3, 2, 1, 4, 3, 0,
+    2, 3, 4, 1, 3, 2, 4, 3,
 )
 READ_CAP = 2
 VMEM_BYTES = 12 * 1024 * 1024

time: 118 us -> 111 us (0.941)
  waiting for transfers between devices: 46 us -> 35.7 us
  starting transfers between devices: 49.6 us -> 53.5 us
    ppermute x40, waiting for transfers between devices: 46 us -> 35.7 us  [flip(): lax.ppermute(value, axis, [(d, d ^ bit) for d in range(lax.axis_size(axis...]
    ppermute x40, starting transfers between devices: 49.6 us -> 53.5 us  [flip(): lax.ppermute(value, axis, [(d, d ^ bit) for d in range(lax.axis_size(axis...]
  transfers between devices with their start and end apart: 40 -> 40, of which waited for: 21 -> 19; matrix products, arithmetic and copies ran while one was open for 0% -> 0% of each run, Pallas kernels for 11% -> 11%
where the time goes in v14:
time: 111 us
  starting transfers between devices  53.5 us (48%)
  waiting for transfers between devices  35.7 us (32%)
  Pallas kernels  19.3 us (17%)
  local copies, waits for them, and re-layouts  1.73 us (2%)
    ppermute x40, starting transfers between devices, flip(): lax.ppermute(value, axis, [(d, d ^ bit) for d in range(lax.axis_size(axis...  53.5 us
    ppermute x40, waiting for transfers between devices, flip(): lax.ppermute(value, axis, [(d, d ^ bit) for d in range(lax.axis_size(axis...  35.7 us
    pallas_call x44, Pallas kernels, call(): pl.pallas_call(body, out_shape=out_shape, in_specs=in_specs, out_specs=ou...  19.3 us
  transfers between devices with their start and end apart: 40, of which 19 were waited for; matrix products, arithmetic and copies ran while one was open for 0% of the time, Pallas kernels for 11%

profile of v14, /device:TPU:0, one launch (start us, length us, event | category | flops | bytes accessed | tf_op | source)
XLA Modules:
  0.0 111.3 jit_solution(15256703834227753057)
XLA Ops:
  0.6 4.6 %shard_map.95 = (s32[256]{0:T(256)}, s32[16]{0:T(128)}, bf16[4,4,32,512]{3,2,1,0:T(8,128)(2,1)}, bf16[528,512]{1,0:T(8,128)(2,1)}, bf16[512,512]{1,0:T(8,128)(2,1)}) custom-call(s32[1]{0:T(128)} %bitcast.me_ref, s32[96]{0:T(128)} %slot_hbm.1, s32[96]{0:T(128)} %col_hbm.1, s32[96]{0:T(128)} %id_hbm.1, s32[8,4,8]{2,1,0:T(4,128)} %bitcast.21, s32[16]{0:T(128)} %readers_ref.3, ...), custom_call_target="tpu_custom_call" | custom-call | bytes 1 | tf_op jit(solution)/shard_map/pallas_call | solution.py:24
  5.2 3.1 %collective-permute-start = (bf16[4,4,32,512]{3,2,1,0:T(8,128)(2,1)}, bf16[4,4,32,512]{3,2,1,0:T(8,128)(2,1)S(1)}, u32[]{:S(2)}, u32[]{:S(2)}) collective-permute-start(bf16[4,4,32,512]{3,2,1,0:T(8,128)(2,1)} %get-tuple-element.105), channel_id=1, source_target_pairs={{0,8},{4,12},{8,0},{12,4},{16,24},{20,28},{24,16},{28,20},{1,9},{5... | collective-permute-start | bytes 1572872 | tf_op jit(solution)/shard_map/ppermute | solution.py:475
  11.5 3.4 %shard_map.97 = (bf16[4,4,32,512]{3,2,1,0:T(8,128)(2,1)S(1)}, bf16[4,4,16,512]{3,2,1,0:T(8,128)(2,1)S(1)}, bf16[4,4,16,512]{3,2,1,0:T(8,128)(2,1)S(1)}, bf16[4,4,32,512]{3,2,1,0:T(8,128)(2,1)S(1)}, f32[8,128]{1,0:T(8,128)}) custom-call(s32[256]{0:T(256)S(1)} %copy-done.4, bf16[48,128,128]{2,1,0:T(8,128)(2,1)S(1)} %copy-done.1, bf16[512,512]{1,0:T(8,128)(2,1)S(1)} %copy-done.2), custom_call_target="tpu_custom_call" | custom-call | bytes 1 | tf_op jit(solution)/shard_map/pallas_call | solution.py:24
  15.5 2.3 %shard_map.96 = (bf16[4,4,32,512]{3,2,1,0:T(8,128)(2,1)S(1)}, bf16[4,4,32,512]{3,2,1,0:T(8,128)(2,1)S(1)}, bf16[4,4,16,512]{3,2,1,0:T(8,128)(2,1)S(1)}, bf16[4,4,16,512]{3,2,1,0:T(8,128)(2,1)S(1)}, f32[8,128]{1,0:T(8,128)S(1)}) custom-call(s32[256]{0:T(256)S(1)} %copy-done.5, bf16[48,128,128]{2,1,0:T(8,128)(2,1)S(1)} %copy-done.1, bf16[512,512]{1,0:T(8,128)(2,1)S(1)} %copy-done.2), custom_call_target="tpu_custom_call" | custom-call | bytes 1 | tf_op jit(solution)/shard_map/pallas_call | solution.py:24
  17.7 2.7 %collective-permute-done.got_ref = bf16[4,4,32,512]{3,2,1,0:T(8,128)(2,1)S(1)} collective-permute-done((bf16[4,4,32,512]{3,2,1,0:T(8,128)(2,1)}, bf16[4,4,32,512]{3,2,1,0:T(8,128)(2,1)S(1)}, u32[]{:S(2)}, u32[]{:S(2)}) %collective-permute-start) | collective-permute-done | bytes 524320 | tf_op jit(solution)/shard_map/ppermute | solution.py:475
  20.7 2.8 %collective-permute-start.3 = (bf16[2,4,32,512]{3,2,1,0:T(8,128)(2,1)S(1)}, bf16[2,4,32,512]{3,2,1,0:T(8,128)(2,1)S(1)}, u32[]{:S(2)}, u32[]{:S(2)}) collective-permute-start(bf16[2,4,32,512]{3,2,1,0:T(8,128)(2,1)S(1)} %get-tuple-element.114), channel_id=1, source_target_pairs={{0,16},{4,20},{8,24},{12,28},{16,0},{20,4},{24,8},{28,12},{1,17},{... | collective-permute-start | bytes 786440 | tf_op jit(solution)/shard_map/ppermute | solution.py:475
  26.9 8.0 %collective-permute-done.2.got_ref = bf16[4,4,32,512]{3,2,1,0:T(8,128)(2,1)S(1)} collective-permute-done((bf16[4,4,32,512]{3,2,1,0:T(8,128)(2,1)S(1)}, bf16[4,4,32,512]{3,2,1,0:T(8,128)(2,1)S(1)}, u32[]{:S(2)}, u32[]{:S(2)}) %collective-permute-start.2) | collective-permute-done | bytes 524320 | tf_op jit(solution)/shard_map/ppermute | solution.py:475
  35.4 2.0 %collective-permute-start.6 = (bf16[1,4,32,512]{3,2,1,0:T(8,128)(2,1)S(1)}, bf16[1,4,32,512]{3,2,1,0:T(8,128)(2,1)S(1)}, u32[]{:S(2)}, u32[]{:S(2)}) collective-permute-start(bf16[1,4,32,512]{3,2,1,0:T(8,128)(2,1)S(1)} %get-tuple-element.123), channel_id=1, source_target_pairs={{0,4},{4,0},{8,12},{12,8},{16,20},{20,16},{24,28},{28,24},{1,5},{5... | collective-permute-start | bytes 393224 | tf_op jit(solution)/shard_map/ppermute | solution.py:475
  37.5 2.7 %collective-permute-start.8 = (bf16[1,4,32,512]{3,2,1,0:T(8,128)(2,1)S(1)}, bf16[1,4,32,512]{3,2,1,0:T(8,128)(2,1)S(1)}, u32[]{:S(2)}, u32[]{:S(2)}) collective-permute-start(bf16[1,4,32,512]{3,2,1,0:T(8,128)(2,1)S(1)} %get-tuple-element.129), channel_id=1, source_target_pairs={{0,16},{4,20},{8,24},{12,28},{16,0},{20,4},{24,8},{28,12},{1,17},{... | collective-permute-start | bytes 393224 | tf_op jit(solution)/shard_map/ppermute | solution.py:475
  44.4 2.5 %collective-permute-start.11 = (bf16[1,4,32,512]{3,2,1,0:T(8,128)(2,1)S(1)}, bf16[1,4,32,512]{3,2,1,0:T(8,128)(2,1)S(1)}, u32[]{:S(2)}, u32[]{:S(2)}) collective-permute-start(bf16[1,4,32,512]{3,2,1,0:T(8,128)(2,1)S(1)} %get-tuple-element.137), channel_id=1, source_target_pairs={{0,16},{4,20},{8,24},{12,28},{16,0},{20,4},{24,8},{28,12},{1,17},{... | collective-permute-start | bytes 393224 | tf_op jit(solution)/shard_map/ppermute | solution.py:475
  52.0 2.0 %collective-permute-start.16 = (bf16[1,4,32,512]{3,2,1,0:T(8,128)(2,1)S(1)}, bf16[1,4,32,512]{3,2,1,0:T(8,128)(2,1)S(1)}, u32[]{:S(2)}, u32[]{:S(2)}) collective-permute-start(bf16[1,4,32,512]{3,2,1,0:T(8,128)(2,1)S(1)} %bitcast.9), channel_id=1, source_target_pairs={{0,2},{1,3},{2,0},{3,1},{4,6},{5,7},{6,4},{7,5},{8,10},{9,11},{10,... | collective-permute-start | bytes 393224 | tf_op jit(solution)/shard_map/ppermute | solution.py:475
  54.4 2.1 %collective-permute-start.18 = (bf16[2,4,16,512]{3,2,1,0:T(8,128)(2,1)S(1)}, bf16[2,4,16,512]{3,2,1,0:T(8,128)(2,1)S(1)}, u32[]{:S(2)}, u32[]{:S(2)}) collective-permute-start(bf16[2,4,16,512]{3,2,1,0:T(8,128)(2,1)S(1)} %get-tuple-element.154), channel_id=1, source_target_pairs={{0,8},{4,12},{8,0},{12,4},{16,24},{20,28},{24,16},{28,20},{1,9},{5... | collective-permute-start | bytes 393224 | tf_op jit(solution)/shard_map/ppermute | solution.py:475
  57.9 2.4 %collective-permute-done.15.got_ref = bf16[1,4,16,512]{3,2,1,0:T(8,128)(2,1)S(1)} collective-permute-done((bf16[1,4,16,512]{3,2,1,0:T(8,128)(2,1)S(1)}, bf16[1,4,16,512]{3,2,1,0:T(8,128)(2,1)S(1)}, u32[]{:S(2)}, u32[]{:S(2)}) %collective-permute-start.15) | collective-permute-done | bytes 65568 | tf_op jit(solution)/shard_map/ppermute | solution.py:475
  64.9 4.6 %collective-permute-done.20.got_ref = bf16[1,4,32,512]{3,2,1,0:T(8,128)(2,1)S(1)} collective-permute-done((bf16[1,4,32,512]{3,2,1,0:T(8,128)(2,1)S(1)}, bf16[1,4,32,512]{3,2,1,0:T(8,128)(2,1)S(1)}, u32[]{:S(2)}, u32[]{:S(2)}) %collective-permute-start.20) | collective-permute-done | bytes 131104 | tf_op jit(solution)/shard_map/ppermute | solution.py:475
  69.6 2.5 %collective-permute-start.24 = (bf16[1,4,16,512]{3,2,1,0:T(8,128)(2,1)S(1)}, bf16[1,4,16,512]{3,2,1,0:T(8,128)(2,1)S(1)}, u32[]{:S(2)}, u32[]{:S(2)}) collective-permute-start(bf16[1,4,16,512]{3,2,1,0:T(8,128)(2,1)S(1)} %get-tuple-element.167), channel_id=1, source_target_pairs={{0,16},{4,20},{8,24},{12,28},{16,0},{20,4},{24,8},{28,12},{1,17},{... | collective-permute-start | bytes 196616 | tf_op jit(solution)/shard_map/ppermute | solution.py:475
  75.6 2.3 %collective-permute-start.26 = (bf16[1,4,16,512]{3,2,1,0:T(8,128)(2,1)S(1)}, bf16[1,4,16,512]{3,2,1,0:T(8,128)(2,1)S(1)}, u32[]{:S(2)}, u32[]{:S(2)}) collective-permute-start(bf16[1,4,16,512]{3,2,1,0:T(8,128)(2,1)S(1)} %bitcast.17), channel_id=1, source_target_pairs={{0,2},{1,3},{2,0},{3,1},{4,6},{5,7},{6,4},{7,5},{8,10},{9,11},{10,... | collective-permute-start | bytes 196616 | tf_op jit(solution)/shard_map/ppermute | solution.py:475
  79.2 2.3 %collective-permute-start.31 = (bf16[8,32,512]{2,1,0:T(8,128)(2,1)S(1)}, bf16[8,32,512]{2,1,0:T(8,128)(2,1)S(1)}, u32[]{:S(2)}, u32[]{:S(2)}) collective-permute-start(bf16[8,32,512]{2,1,0:T(8,128)(2,1)S(1)} %get-tuple-element.181), channel_id=1, source_target_pairs={{0,4},{4,0},{8,12},{12,8},{16,20},{20,16},{24,28},{28,24},{1,5},{5... | collective-permute-start | bytes 786440 | tf_op jit(solution)/shard_map/ppermute | solution.py:475
  83.7 2.1 %collective-permute-start.29 = (bf16[1,4,16,512]{3,2,1,0:T(8,128)(2,1)S(1)}, bf16[1,4,16,512]{3,2,1,0:T(8,128)(2,1)S(1)}, u32[]{:S(2)}, u32[]{:S(2)}) collective-permute-start(bf16[1,4,16,512]{3,2,1,0:T(8,128)(2,1)S(1)} %get-tuple-element.177.held_ref), channel_id=1, source_target_pairs={{0,16},{4,20},{8,24},{12,28},{16,0},{20,4},{24,8},{28,12},{1,17},{... | collective-permute-start | bytes 196616 | tf_op jit(solution)/shard_map/ppermute | solution.py:475
  86.9 2.1 %collective-permute-start.35 = (bf16[8,32,512]{2,1,0:T(8,128)(2,1)S(1)}, bf16[8,32,512]{2,1,0:T(8,128)(2,1)S(1)}, u32[]{:S(2)}, u32[]{:S(2)}) collective-permute-start(bf16[8,32,512]{2,1,0:T(8,128)(2,1)S(1)} %get-tuple-element.188), channel_id=1, source_target_pairs={{0,4},{4,0},{8,12},{12,8},{16,20},{20,16},{24,28},{28,24},{1,5},{5... | collective-permute-start | bytes 786440 | tf_op jit(solution)/shard_map/ppermute | solution.py:475
  91.2 3.4 %collective-permute-start.33 = (bf16[1,4,16,512]{3,2,1,0:T(8,128)(2,1)S(1)}, bf16[1,4,16,512]{3,2,1,0:T(8,128)(2,1)S(1)}, u32[]{:S(2)}, u32[]{:S(2)}) collective-permute-start(bf16[1,4,16,512]{3,2,1,0:T(8,128)(2,1)S(1)} %get-tuple-element.184.held_ref), channel_id=1, source_target_pairs={{0,16},{4,20},{8,24},{12,28},{16,0},{20,4},{24,8},{28,12},{1,17},{... | collective-permute-start | bytes 196616 | tf_op jit(solution)/shard_map/ppermute | solution.py:475
  97.0 3.5 %collective-permute-start.36 = (bf16[2,4,16,512]{3,2,1,0:T(8,128)(2,1)S(1)}, bf16[2,4,16,512]{3,2,1,0:T(8,128)(2,1)S(1)}, u32[]{:S(2)}, u32[]{:S(2)}) collective-permute-start(bf16[2,4,16,512]{3,2,1,0:T(8,128)(2,1)S(1)} %get-tuple-element.189.held_ref.refs_8_), channel_id=1, source_target_pairs={{0,8},{4,12},{8,0},{12,4},{16,24},{20,28},{24,16},{28,20},{1,9},{5... | collective-permute-start | bytes 393224 | tf_op jit(solution)/shard_map/ppermute | solution.py:475
  103.8 2.8 %collective-permute-done.38.value_ref.refs_13_ = bf16[8,16,512]{2,1,0:T(8,128)(2,1)S(1)} collective-permute-done((bf16[8,16,512]{2,1,0:T(8,128)(2,1)S(1)}, bf16[8,16,512]{2,1,0:T(8,128)(2,1)S(1)}, u32[]{:S(2)}, u32[]{:S(2)}) %collective-permute-start.38) | collective-permute-done | bytes 131104 | tf_op jit(solution)/shard_map/ppermute | solution.py:475
  106.7 2.7 %shard_map.137 = (bf16[4,128,512]{2,1,0:T(8,128)(2,1)}, bf16[16,128,512]{2,1,0:T(8,128)(2,1)}, f32[8,128]{1,0:T(8,128)S(1)}) custom-call(f32[8,128]{1,0:T(8,128)S(1)} %shard_map.136.token_ref, s32[1]{0:T(128)} %bitcast.me_ref, s32[16]{0:T(128)S(1)} %copy-done.3, s32[16]{0:T(128)S(1)} %copy-done.6, ...), custom_call_target="tpu_custom_call" | custom-call | bytes 1 | tf_op jit(solution)/shard_map/pallas_call | solution.py:24
  109.3 1.9 %shard_map.138 = (bf16[4,128,512]{2,1,0:T(8,128)(2,1)}, bf16[16,128,512]{2,1,0:T(8,128)(2,1)}, f32[8,128]{1,0:T(8,128)}) custom-call(f32[8,128]{1,0:T(8,128)S(1)} %get-tuple-element.194.token_ref, s32[1]{0:T(128)} %bitcast.me_ref, s32[16]{0:T(128)S(1)} %copy-done.3, s32[16]{0:T(128)S(1)} %copy-done.6, ...), custom_call_target="tpu_custom_call", output_to_operand_aliasing={{0}: (5, {}), {1}: (6, {})} | custom-call | bytes 1 | tf_op jit(solution)/shard_map/pallas_call | solution.py:24
  (114 shorter events, 39.6 us)
Async XLA Ops:
  5.2 15.2 %collective-permute-start = (bf16[4,4,32,512]{3,2,1,0:T(8,128)(2,1)}, bf16[4,4,32,512]{3,2,1,0:T(8,128)(2,1)S(1)}, u32[]{:S(2)}, u32[]{:S(2)}) collective-permute-start(bf16[4,4,32,512]{3,2,1,0:T(8,128)(2,1)} %get-tuple-element.105), channel_id=1, source_target_pairs={{0,8},{4,12},{8,0},{12,4},{16,24},{20,28},{24,16},{28,20},{1,9},{5... | collective-permute-start | bytes 1572872 | tf_op jit(solution)/shard_map/ppermute | solution.py:475
  8.3 15.4 %collective-permute-start.1 = (bf16[528,512]{1,0:T(8,128)(2,1)}, bf16[528,512]{1,0:T(8,128)(2,1)S(1)}, u32[]{:S(2)}, u32[]{:S(2)}) collective-permute-start(bf16[528,512]{1,0:T(8,128)(2,1)} %get-tuple-element.108), channel_id=1, source_target_pairs={{0,4},{4,0},{8,12},{12,8},{16,20},{20,16},{24,28},{28,24},{1,5},{5... | collective-permute-start | bytes 1622024 | tf_op jit(solution)/shard_map/ppermute | solution.py:475
  14.9 20.1 %collective-permute-start.2 = (bf16[4,4,32,512]{3,2,1,0:T(8,128)(2,1)S(1)}, bf16[4,4,32,512]{3,2,1,0:T(8,128)(2,1)S(1)}, u32[]{:S(2)}, u32[]{:S(2)}) collective-permute-start(bf16[4,4,32,512]{3,2,1,0:T(8,128)(2,1)S(1)} %get-tuple-element.111), channel_id=1, source_target_pairs={{0,4},{4,0},{8,12},{12,8},{16,20},{20,16},{24,28},{28,24},{1,5},{5... | collective-permute-start | bytes 1572872 | tf_op jit(solution)/shard_map/ppermute | solution.py:475
  20.7 14.6 %collective-permute-start.3 = (bf16[2,4,32,512]{3,2,1,0:T(8,128)(2,1)S(1)}, bf16[2,4,32,512]{3,2,1,0:T(8,128)(2,1)S(1)}, u32[]{:S(2)}, u32[]{:S(2)}) collective-permute-start(bf16[2,4,32,512]{3,2,1,0:T(8,128)(2,1)S(1)} %get-tuple-element.114), channel_id=1, source_target_pairs={{0,16},{4,20},{8,24},{12,28},{16,0},{20,4},{24,8},{28,12},{1,17},{... | collective-permute-start | bytes 786440 | tf_op jit(solution)/shard_map/ppermute | solution.py:475
  24.0 13.4 %collective-permute-start.4 = (bf16[2,4,32,512]{3,2,1,0:T(8,128)(2,1)S(1)}, bf16[2,4,32,512]{3,2,1,0:T(8,128)(2,1)S(1)}, u32[]{:S(2)}, u32[]{:S(2)}) collective-permute-start(bf16[2,4,32,512]{3,2,1,0:T(8,128)(2,1)S(1)} %get-tuple-element.117), channel_id=1, source_target_pairs={{0,8},{4,12},{8,0},{12,4},{16,24},{20,28},{24,16},{28,20},{1,9},{5... | collective-permute-start | bytes 786440 | tf_op jit(solution)/shard_map/ppermute | solution.py:475
  25.4 15.1 %collective-permute-start.5 = (bf16[4,4,16,512]{3,2,1,0:T(8,128)(2,1)S(1)}, bf16[4,4,16,512]{3,2,1,0:T(8,128)(2,1)S(1)}, u32[]{:S(2)}, u32[]{:S(2)}) collective-permute-start(bf16[4,4,16,512]{3,2,1,0:T(8,128)(2,1)S(1)} %get-tuple-element.120), channel_id=1, source_target_pairs={{0,4},{4,0},{8,12},{12,8},{16,20},{20,16},{24,28},{28,24},{1,5},{5... | collective-permute-start | bytes 786440 | tf_op jit(solution)/shard_map/ppermute | solution.py:475
  35.2 9.1 %collective-permute-start.7 = (bf16[2,4,32,512]{3,2,1,0:T(8,128)(2,1)S(1)}, bf16[2,4,32,512]{3,2,1,0:T(8,128)(2,1)S(1)}, u32[]{:S(2)}, u32[]{:S(2)}) collective-permute-start(bf16[2,4,32,512]{3,2,1,0:T(8,128)(2,1)S(1)} %get-tuple-element.126), channel_id=1, source_target_pairs={{0,8},{4,12},{8,0},{12,4},{16,24},{20,28},{24,16},{28,20},{1,9},{5... | collective-permute-start | bytes 786440 | tf_op jit(solution)/shard_map/ppermute | solution.py:475
  37.5 9.3 %collective-permute-start.8 = (bf16[1,4,32,512]{3,2,1,0:T(8,128)(2,1)S(1)}, bf16[1,4,32,512]{3,2,1,0:T(8,128)(2,1)S(1)}, u32[]{:S(2)}, u32[]{:S(2)}) collective-permute-start(bf16[1,4,32,512]{3,2,1,0:T(8,128)(2,1)S(1)} %get-tuple-element.129), channel_id=1, source_target_pairs={{0,16},{4,20},{8,24},{12,28},{16,0},{20,4},{24,8},{28,12},{1,17},{... | collective-permute-start | bytes 393224 | tf_op jit(solution)/shard_map/ppermute | solution.py:475
  42.0 7.0 %collective-permute-start.9 = (bf16[1,4,32,512]{3,2,1,0:T(8,128)(2,1)S(1)}, bf16[1,4,32,512]{3,2,1,0:T(8,128)(2,1)S(1)}, u32[]{:S(2)}, u32[]{:S(2)}) collective-permute-start(bf16[1,4,32,512]{3,2,1,0:T(8,128)(2,1)S(1)} %bitcast.13), channel_id=1, source_target_pairs={{0,2},{1,3},{2,0},{3,1},{4,6},{5,7},{6,4},{7,5},{8,10},{9,11},{10,... | collective-permute-start | bytes 393224 | tf_op jit(solution)/shard_map/ppermute | solution.py:475
  49.0 7.5 %collective-permute-start.14 = (bf16[2,4,32,512]{3,2,1,0:T(8,128)(2,1)S(1)}, bf16[2,4,32,512]{3,2,1,0:T(8,128)(2,1)S(1)}, u32[]{:S(2)}, u32[]{:S(2)}) collective-permute-start(bf16[2,4,32,512]{3,2,1,0:T(8,128)(2,1)S(1)} %get-tuple-element.144.held_ref), channel_id=1, source_target_pairs={{0,1},{1,0},{2,3},{3,2},{4,5},{5,4},{6,7},{7,6},{8,9},{9,8},{10,11... | collective-permute-start | bytes 786440 | tf_op jit(solution)/shard_map/ppermute | solution.py:475
  51.9 8.9 %collective-permute-start.17 = (bf16[2,4,32,512]{3,2,1,0:T(8,128)(2,1)S(1)}, bf16[2,4,32,512]{3,2,1,0:T(8,128)(2,1)S(1)}, u32[]{:S(2)}, u32[]{:S(2)}) collective-permute-start(bf16[2,4,32,512]{3,2,1,0:T(8,128)(2,1)S(1)} %get-tuple-element.151.held_ref), channel_id=1, source_target_pairs={{0,1},{1,0},{2,3},{3,2},{4,5},{5,4},{6,7},{7,6},{8,9},{9,8},{10,11... | collective-permute-start | bytes 786440 | tf_op jit(solution)/shard_map/ppermute | solution.py:475
  52.0 8.2 %collective-permute-start.16 = (bf16[1,4,32,512]{3,2,1,0:T(8,128)(2,1)S(1)}, bf16[1,4,32,512]{3,2,1,0:T(8,128)(2,1)S(1)}, u32[]{:S(2)}, u32[]{:S(2)}) collective-permute-start(bf16[1,4,32,512]{3,2,1,0:T(8,128)(2,1)S(1)} %bitcast.9), channel_id=1, source_target_pairs={{0,2},{1,3},{2,0},{3,1},{4,6},{5,7},{6,4},{7,5},{8,10},{9,11},{10,... | collective-permute-start | bytes 393224 | tf_op jit(solution)/shard_map/ppermute | solution.py:475
  54.4 8.8 %collective-permute-start.18 = (bf16[2,4,16,512]{3,2,1,0:T(8,128)(2,1)S(1)}, bf16[2,4,16,512]{3,2,1,0:T(8,128)(2,1)S(1)}, u32[]{:S(2)}, u32[]{:S(2)}) collective-permute-start(bf16[2,4,16,512]{3,2,1,0:T(8,128)(2,1)S(1)} %get-tuple-element.154), channel_id=1, source_target_pairs={{0,8},{4,12},{8,0},{12,4},{16,24},{20,28},{24,16},{28,20},{1,9},{5... | collective-permute-start | bytes 393224 | tf_op jit(solution)/shard_map/ppermute | solution.py:475
  56.9 12.5 %collective-permute-start.20 = (bf16[1,4,32,512]{3,2,1,0:T(8,128)(2,1)S(1)}, bf16[1,4,32,512]{3,2,1,0:T(8,128)(2,1)S(1)}, u32[]{:S(2)}, u32[]{:S(2)}) collective-permute-start(bf16[1,4,32,512]{3,2,1,0:T(8,128)(2,1)S(1)} %get-tuple-element.158.held_ref), channel_id=1, source_target_pairs={{0,16},{4,20},{8,24},{12,28},{16,0},{20,4},{24,8},{28,12},{1,17},{... | collective-permute-start | bytes 393224 | tf_op jit(solution)/shard_map/ppermute | solution.py:475
  60.3 12.4 %collective-permute-start.23 = (bf16[2,4,32,512]{3,2,1,0:T(8,128)(2,1)S(1)}, bf16[2,4,32,512]{3,2,1,0:T(8,128)(2,1)S(1)}, u32[]{:S(2)}, u32[]{:S(2)}) collective-permute-start(bf16[2,4,32,512]{3,2,1,0:T(8,128)(2,1)S(1)} %get-tuple-element.164.held_ref), channel_id=1, source_target_pairs={{0,1},{1,0},{2,3},{3,2},{4,5},{5,4},{6,7},{7,6},{8,9},{9,8},{10,11... | collective-permute-start | bytes 786440 | tf_op jit(solution)/shard_map/ppermute | solution.py:475
  61.2 10.9 %collective-permute-start.21 = (bf16[1,4,32,512]{3,2,1,0:T(8,128)(2,1)S(1)}, bf16[1,4,32,512]{3,2,1,0:T(8,128)(2,1)S(1)}, u32[]{:S(2)}, u32[]{:S(2)}) collective-permute-start(bf16[1,4,32,512]{3,2,1,0:T(8,128)(2,1)S(1)} %get-tuple-element.160.held_ref), channel_id=1, source_target_pairs={{0,16},{4,20},{8,24},{12,28},{16,0},{20,4},{24,8},{28,12},{1,17},{... | collective-permute-start | bytes 393224 | tf_op jit(solution)/shard_map/ppermute | solution.py:475
  69.5 9.5 %collective-permute-start.25 = (bf16[2,4,32,512]{3,2,1,0:T(8,128)(2,1)S(1)}, bf16[2,4,32,512]{3,2,1,0:T(8,128)(2,1)S(1)}, u32[]{:S(2)}, u32[]{:S(2)}) collective-permute-start(bf16[2,4,32,512]{3,2,1,0:T(8,128)(2,1)S(1)} %get-tuple-element.169.held_ref.refs_0_), channel_id=1, source_target_pairs={{0,8},{4,12},{8,0},{12,4},{16,24},{20,28},{24,16},{28,20},{1,9},{5... | collective-permute-start | bytes 786440 | tf_op jit(solution)/shard_map/ppermute | solution.py:475
  73.1 10.2 %collective-permute-start.27 = (bf16[1,4,32,512]{3,2,1,0:T(8,128)(2,1)S(1)}, bf16[1,4,32,512]{3,2,1,0:T(8,128)(2,1)S(1)}, u32[]{:S(2)}, u32[]{:S(2)}) collective-permute-start(bf16[1,4,32,512]{3,2,1,0:T(8,128)(2,1)S(1)} %get-tuple-element.173.held_ref), channel_id=1, source_target_pairs={{0,16},{4,20},{8,24},{12,28},{16,0},{20,4},{24,8},{28,12},{1,17},{... | collective-permute-start | bytes 393224 | tf_op jit(solution)/shard_map/ppermute | solution.py:475
  74.5 12.2 %collective-permute-start.28 = (bf16[2,4,32,512]{3,2,1,0:T(8,128)(2,1)S(1)}, bf16[2,4,32,512]{3,2,1,0:T(8,128)(2,1)S(1)}, u32[]{:S(2)}, u32[]{:S(2)}) collective-permute-start(bf16[2,4,32,512]{3,2,1,0:T(8,128)(2,1)S(1)} %get-tuple-element.175.held_ref.refs_2_), channel_id=1, source_target_pairs={{0,8},{4,12},{8,0},{12,4},{16,24},{20,28},{24,16},{28,20},{1,9},{5... | collective-permute-start | bytes 786440 | tf_op jit(solution)/shard_map/ppermute | solution.py:475
  79.2 15.5 %collective-permute-start.31 = (bf16[8,32,512]{2,1,0:T(8,128)(2,1)S(1)}, bf16[8,32,512]{2,1,0:T(8,128)(2,1)S(1)}, u32[]{:S(2)}, u32[]{:S(2)}) collective-permute-start(bf16[8,32,512]{2,1,0:T(8,128)(2,1)S(1)} %get-tuple-element.181), channel_id=1, source_target_pairs={{0,4},{4,0},{8,12},{12,8},{16,20},{20,16},{24,28},{28,24},{1,5},{5... | collective-permute-start | bytes 786440 | tf_op jit(solution)/shard_map/ppermute | solution.py:475
  83.4 11.2 %collective-permute-start.32 = (bf16[2,4,32,512]{3,2,1,0:T(8,128)(2,1)S(1)}, bf16[2,4,32,512]{3,2,1,0:T(8,128)(2,1)S(1)}, u32[]{:S(2)}, u32[]{:S(2)}) collective-permute-start(bf16[2,4,32,512]{3,2,1,0:T(8,128)(2,1)S(1)} %get-tuple-element.182.held_ref.refs_4_), channel_id=1, source_target_pairs={{0,8},{4,12},{8,0},{12,4},{16,24},{20,28},{24,16},{28,20},{1,9},{5... | collective-permute-start | bytes 786440 | tf_op jit(solution)/shard_map/ppermute | solution.py:475
  83.7 6.9 %collective-permute-start.30 = (bf16[2,4,16,512]{3,2,1,0:T(8,128)(2,1)S(1)}, bf16[2,4,16,512]{3,2,1,0:T(8,128)(2,1)S(1)}, u32[]{:S(2)}, u32[]{:S(2)}) collective-permute-start(bf16[2,4,16,512]{3,2,1,0:T(8,128)(2,1)S(1)} %get-tuple-element.179.held_ref), channel_id=1, source_target_pairs={{0,1},{1,0},{2,3},{3,2},{4,5},{5,4},{6,7},{7,6},{8,9},{9,8},{10,11... | collective-permute-start | bytes 393224 | tf_op jit(solution)/shard_map/ppermute | solution.py:475
  86.9 15.3 %collective-permute-start.35 = (bf16[8,32,512]{2,1,0:T(8,128)(2,1)S(1)}, bf16[8,32,512]{2,1,0:T(8,128)(2,1)S(1)}, u32[]{:S(2)}, u32[]{:S(2)}) collective-permute-start(bf16[8,32,512]{2,1,0:T(8,128)(2,1)S(1)} %get-tuple-element.188), channel_id=1, source_target_pairs={{0,4},{4,0},{8,12},{12,8},{16,20},{20,16},{24,28},{28,24},{1,5},{5... | collective-permute-start | bytes 786440 | tf_op jit(solution)/shard_map/ppermute | solution.py:475
  94.8 9.0 %collective-permute-start.37 = (bf16[8,32,512]{2,1,0:T(8,128)(2,1)S(1)}, bf16[8,32,512]{2,1,0:T(8,128)(2,1)S(1)}, u32[]{:S(2)}, u32[]{:S(2)}) collective-permute-start(bf16[8,32,512]{2,1,0:T(8,128)(2,1)S(1)} %get-tuple-element.191), channel_id=1, source_target_pairs={{0,4},{4,0},{8,12},{12,8},{16,20},{20,16},{24,28},{28,24},{1,5},{5... | collective-permute-start | bytes 786440 | tf_op jit(solution)/shard_map/ppermute | solution.py:475
  (23 other events, 153.3 us)

commit v15 on v14

--- a/solution.py
+++ b/solution.py
@@ -7,7 +7,7 @@
 
 SHARES = (2, 2, 2, 1, 1)
 ORDER = (
-    0, 1, 2, 0, 1, 4, 0, 2, 1, 0, 4, 2, 1, 3, 0, 4, 2, 1, 3, 4, 0, 1, 4, 2, 3, 0, 3, 2, 1, 4, 3, 0,
+    1, 0, 2, 4, 1, 0, 2, 3, 1, 0, 4, 2, 1, 0, 0, 2, 4, 1, 0, 3, 1, 4, 4, 2, 3, 0, 3, 2, 1, 4, 0, 3,
     2, 3, 4, 1, 3, 2, 4, 3,
 )
 READ_CAP = 2

time: 111 us -> 115 us (1.036)
  starting transfers between devices: 53.5 us -> 69.2 us
  waiting for transfers between devices: 35.7 us -> 23.8 us
    ppermute x40, starting transfers between devices: 53.5 us -> 69.2 us  [flip(): lax.ppermute(value, axis, [(d, d ^ bit) for d in range(lax.axis_size(axis...]
    ppermute x40, waiting for transfers between devices: 35.7 us -> 23.8 us  [flip(): lax.ppermute(value, axis, [(d, d ^ bit) for d in range(lax.axis_size(axis...]
  transfers between devices with their start and end apart: 40 -> 40, of which waited for: 19 -> 13; matrix products, arithmetic and copies ran while one was open for 0% -> 0% of each run, Pallas kernels for 11% -> 11%
where the time goes in v15:
time: 115 us
  starting transfers between devices  69.2 us (60%)
  waiting for transfers between devices  23.8 us (21%)
  Pallas kernels  19.3 us (17%)
  local copies, waits for them, and re-layouts  1.73 us (2%)
    ppermute x40, starting transfers between devices, flip(): lax.ppermute(value, axis, [(d, d ^ bit) for d in range(lax.axis_size(axis...  69.2 us
    ppermute x40, waiting for transfers between devices, flip(): lax.ppermute(value, axis, [(d, d ^ bit) for d in range(lax.axis_size(axis...  23.8 us
    pallas_call x44, Pallas kernels, call(): pl.pallas_call(body, out_shape=out_shape, in_specs=in_specs, out_specs=ou...  19.3 us
  transfers between devices with their start and end apart: 40, of which 13 were waited for; matrix products, arithmetic and copies ran while one was open for 0% of the time, Pallas kernels for 11%

profile of v15, /device:TPU:0, one launch (start us, length us, event | category | flops | bytes accessed | tf_op | source)
XLA Modules:
  0.0 115.0 jit_solution(17413633986163604535)
XLA Ops:
  0.6 4.6 %shard_map.95 = (s32[256]{0:T(256)}, s32[16]{0:T(128)}, bf16[4,4,32,512]{3,2,1,0:T(8,128)(2,1)}, bf16[528,512]{1,0:T(8,128)(2,1)}, bf16[512,512]{1,0:T(8,128)(2,1)}) custom-call(s32[1]{0:T(128)} %bitcast.me_ref, s32[96]{0:T(128)} %slot_hbm.1, s32[96]{0:T(128)} %col_hbm.1, s32[96]{0:T(128)} %id_hbm.1, s32[8,4,8]{2,1,0:T(4,128)} %bitcast.21, s32[16]{0:T(128)} %readers_ref.3, ...), custom_call_target="tpu_custom_call" | custom-call | bytes 1 | tf_op jit(solution)/shard_map/pallas_call | solution.py:24
  5.2 3.0 %collective-permute-start = (bf16[528,512]{1,0:T(8,128)(2,1)}, bf16[528,512]{1,0:T(8,128)(2,1)S(1)}, u32[]{:S(2)}, u32[]{:S(2)}) collective-permute-start(bf16[528,512]{1,0:T(8,128)(2,1)} %get-tuple-element.105), channel_id=1, source_target_pairs={{0,4},{4,0},{8,12},{12,8},{16,20},{20,16},{24,28},{28,24},{1,5},{5... | collective-permute-start | bytes 1622024 | tf_op jit(solution)/shard_map/ppermute | solution.py:475
  11.5 3.3 %shard_map.98 = (bf16[4,4,32,512]{3,2,1,0:T(8,128)(2,1)S(1)}, bf16[4,4,16,512]{3,2,1,0:T(8,128)(2,1)S(1)}, bf16[4,4,16,512]{3,2,1,0:T(8,128)(2,1)S(1)}, bf16[4,4,32,512]{3,2,1,0:T(8,128)(2,1)S(1)}, f32[8,128]{1,0:T(8,128)}) custom-call(s32[256]{0:T(256)S(1)} %copy-done.4, bf16[48,128,128]{2,1,0:T(8,128)(2,1)S(1)} %copy-done.1, bf16[512,512]{1,0:T(8,128)(2,1)S(1)} %copy-done.2), custom_call_target="tpu_custom_call" | custom-call | bytes 1 | tf_op jit(solution)/shard_map/pallas_call | solution.py:24
  17.0 2.3 %shard_map.96 = (bf16[4,4,32,512]{3,2,1,0:T(8,128)(2,1)S(1)}, bf16[4,4,32,512]{3,2,1,0:T(8,128)(2,1)S(1)}, bf16[4,4,16,512]{3,2,1,0:T(8,128)(2,1)S(1)}, bf16[4,4,16,512]{3,2,1,0:T(8,128)(2,1)S(1)}, f32[8,128]{1,0:T(8,128)S(1)}) custom-call(s32[256]{0:T(256)S(1)} %copy-done.4, bf16[48,128,128]{2,1,0:T(8,128)(2,1)S(1)} %copy-done.1, bf16[512,512]{1,0:T(8,128)(2,1)S(1)} %copy-done.2), custom_call_target="tpu_custom_call" | custom-call | bytes 1 | tf_op jit(solution)/shard_map/pallas_call | solution.py:24
  19.2 2.3 %collective-permute-done.got_ref.wanted_ref = bf16[528,512]{1,0:T(8,128)(2,1)S(1)} collective-permute-done((bf16[528,512]{1,0:T(8,128)(2,1)}, bf16[528,512]{1,0:T(8,128)(2,1)S(1)}, u32[]{:S(2)}, u32[]{:S(2)}) %collective-permute-start) | collective-permute-done | bytes 540704 | tf_op jit(solution)/shard_map/ppermute | solution.py:475
  21.8 2.2 %collective-permute-start.4 = (bf16[2,4,32,512]{3,2,1,0:T(8,128)(2,1)S(1)}, bf16[2,4,32,512]{3,2,1,0:T(8,128)(2,1)S(1)}, u32[]{:S(2)}, u32[]{:S(2)}) collective-permute-start(bf16[2,4,32,512]{3,2,1,0:T(8,128)(2,1)S(1)} %get-tuple-element.117), channel_id=1, source_target_pairs={{0,8},{4,12},{8,0},{12,4},{16,24},{20,28},{24,16},{28,20},{1,9},{5... | collective-permute-start | bytes 786440 | tf_op jit(solution)/shard_map/ppermute | solution.py:475
  24.3 2.7 %collective-permute-start.5 = (bf16[2,4,32,512]{3,2,1,0:T(8,128)(2,1)S(1)}, bf16[2,4,32,512]{3,2,1,0:T(8,128)(2,1)S(1)}, u32[]{:S(2)}, u32[]{:S(2)}) collective-permute-start(bf16[2,4,32,512]{3,2,1,0:T(8,128)(2,1)S(1)} %get-tuple-element.120), channel_id=1, source_target_pairs={{0,16},{4,20},{8,24},{12,28},{16,0},{20,4},{24,8},{28,12},{1,17},{... | collective-permute-start | bytes 786440 | tf_op jit(solution)/shard_map/ppermute | solution.py:475
  26.9 5.8 %collective-permute-done.2.got_ref = bf16[4,4,32,512]{3,2,1,0:T(8,128)(2,1)S(1)} collective-permute-done((bf16[4,4,32,512]{3,2,1,0:T(8,128)(2,1)S(1)}, bf16[4,4,32,512]{3,2,1,0:T(8,128)(2,1)S(1)}, u32[]{:S(2)}, u32[]{:S(2)}) %collective-permute-start.2) | collective-permute-done | bytes 524320 | tf_op jit(solution)/shard_map/ppermute | solution.py:475
  33.0 2.2 %collective-permute-start.6 = (bf16[2,4,32,512]{3,2,1,0:T(8,128)(2,1)S(1)}, bf16[2,4,32,512]{3,2,1,0:T(8,128)(2,1)S(1)}, u32[]{:S(2)}, u32[]{:S(2)}) collective-permute-start(bf16[2,4,32,512]{3,2,1,0:T(8,128)(2,1)S(1)} %get-tuple-element.123), channel_id=1, source_target_pairs={{0,8},{4,12},{8,0},{12,4},{16,24},{20,28},{24,16},{28,20},{1,9},{5... | collective-permute-start | bytes 786440 | tf_op jit(solution)/shard_map/ppermute | solution.py:475
  38.7 3.2 %collective-permute-start.8 = (bf16[1,4,32,512]{3,2,1,0:T(8,128)(2,1)S(1)}, bf16[1,4,32,512]{3,2,1,0:T(8,128)(2,1)S(1)}, u32[]{:S(2)}, u32[]{:S(2)}) collective-permute-start(bf16[1,4,32,512]{3,2,1,0:T(8,128)(2,1)S(1)} %get-tuple-element.129), channel_id=1, source_target_pairs={{0,16},{4,20},{8,24},{12,28},{16,0},{20,4},{24,8},{28,12},{1,17},{... | collective-permute-start | bytes 393224 | tf_op jit(solution)/shard_map/ppermute | solution.py:475
  45.8 3.6 %collective-permute-start.12 = (bf16[1,4,32,512]{3,2,1,0:T(8,128)(2,1)S(1)}, bf16[1,4,32,512]{3,2,1,0:T(8,128)(2,1)S(1)}, u32[]{:S(2)}, u32[]{:S(2)}) collective-permute-start(bf16[1,4,32,512]{3,2,1,0:T(8,128)(2,1)S(1)} %bitcast.11), channel_id=1, source_target_pairs={{0,2},{1,3},{2,0},{3,1},{4,6},{5,7},{6,4},{7,5},{8,10},{9,11},{10,... | collective-permute-start | bytes 393224 | tf_op jit(solution)/shard_map/ppermute | solution.py:475
  49.9 2.5 %collective-permute-done.11.got_ref = bf16[1,4,32,512]{3,2,1,0:T(8,128)(2,1)S(1)} collective-permute-done((bf16[1,4,32,512]{3,2,1,0:T(8,128)(2,1)S(1)}, bf16[1,4,32,512]{3,2,1,0:T(8,128)(2,1)S(1)}, u32[]{:S(2)}, u32[]{:S(2)}) %collective-permute-start.11) | collective-permute-done | bytes 131104 | tf_op jit(solution)/shard_map/ppermute | solution.py:475
  52.5 2.0 %collective-permute-done.13.got_ref = bf16[1,4,32,512]{3,2,1,0:T(8,128)(2,1)S(1)} collective-permute-done((bf16[1,4,32,512]{3,2,1,0:T(8,128)(2,1)S(1)}, bf16[1,4,32,512]{3,2,1,0:T(8,128)(2,1)S(1)}, u32[]{:S(2)}, u32[]{:S(2)}) %collective-permute-start.13) | collective-permute-done | bytes 131104 | tf_op jit(solution)/shard_map/ppermute | solution.py:475
  59.9 3.9 %collective-permute-start.19 = (bf16[2,4,16,512]{3,2,1,0:T(8,128)(2,1)S(1)}, bf16[2,4,16,512]{3,2,1,0:T(8,128)(2,1)S(1)}, u32[]{:S(2)}, u32[]{:S(2)}) collective-permute-start(bf16[2,4,16,512]{3,2,1,0:T(8,128)(2,1)S(1)} %get-tuple-element.156), channel_id=1, source_target_pairs={{0,8},{4,12},{8,0},{12,4},{16,24},{20,28},{24,16},{28,20},{1,9},{5... | collective-permute-start | bytes 393224 | tf_op jit(solution)/shard_map/ppermute | solution.py:475
  64.3 2.9 %collective-permute-start.20 = (bf16[1,4,32,512]{3,2,1,0:T(8,128)(2,1)S(1)}, bf16[1,4,32,512]{3,2,1,0:T(8,128)(2,1)S(1)}, u32[]{:S(2)}, u32[]{:S(2)}) collective-permute-start(bf16[1,4,32,512]{3,2,1,0:T(8,128)(2,1)S(1)} %get-tuple-element.158.held_ref), channel_id=1, source_target_pairs={{0,16},{4,20},{8,24},{12,28},{16,0},{20,4},{24,8},{28,12},{1,17},{... | collective-permute-start | bytes 393224 | tf_op jit(solution)/shard_map/ppermute | solution.py:475
  67.9 3.2 %collective-permute-start.25 = (bf16[2,4,32,512]{3,2,1,0:T(8,128)(2,1)S(1)}, bf16[2,4,32,512]{3,2,1,0:T(8,128)(2,1)S(1)}, u32[]{:S(2)}, u32[]{:S(2)}) collective-permute-start(bf16[2,4,32,512]{3,2,1,0:T(8,128)(2,1)S(1)} %get-tuple-element.169.held_ref.refs_0_), channel_id=1, source_target_pairs={{0,8},{4,12},{8,0},{12,4},{16,24},{20,28},{24,16},{28,20},{1,9},{5... | collective-permute-start | bytes 786440 | tf_op jit(solution)/shard_map/ppermute | solution.py:475
  71.1 2.0 %collective-permute-done.20.got_ref = bf16[1,4,32,512]{3,2,1,0:T(8,128)(2,1)S(1)} collective-permute-done((bf16[1,4,32,512]{3,2,1,0:T(8,128)(2,1)S(1)}, bf16[1,4,32,512]{3,2,1,0:T(8,128)(2,1)S(1)}, u32[]{:S(2)}, u32[]{:S(2)}) %collective-permute-start.20) | collective-permute-done | bytes 131104 | tf_op jit(solution)/shard_map/ppermute | solution.py:475
  77.3 3.5 %collective-permute-start.28 = (bf16[2,4,32,512]{3,2,1,0:T(8,128)(2,1)S(1)}, bf16[2,4,32,512]{3,2,1,0:T(8,128)(2,1)S(1)}, u32[]{:S(2)}, u32[]{:S(2)}) collective-permute-start(bf16[2,4,32,512]{3,2,1,0:T(8,128)(2,1)S(1)} %get-tuple-element.175.held_ref.refs_2_), channel_id=1, source_target_pairs={{0,8},{4,12},{8,0},{12,4},{16,24},{20,28},{24,16},{28,20},{1,9},{5... | collective-permute-start | bytes 786440 | tf_op jit(solution)/shard_map/ppermute | solution.py:475
  87.8 3.4 %collective-permute-start.29 = (bf16[1,4,16,512]{3,2,1,0:T(8,128)(2,1)S(1)}, bf16[1,4,16,512]{3,2,1,0:T(8,128)(2,1)S(1)}, u32[]{:S(2)}, u32[]{:S(2)}) collective-permute-start(bf16[1,4,16,512]{3,2,1,0:T(8,128)(2,1)S(1)} %get-tuple-element.177.held_ref), channel_id=1, source_target_pairs={{0,16},{4,20},{8,24},{12,28},{16,0},{20,4},{24,8},{28,12},{1,17},{... | collective-permute-start | bytes 196616 | tf_op jit(solution)/shard_map/ppermute | solution.py:475
  94.7 2.7 %collective-permute-start.33 = (bf16[1,4,16,512]{3,2,1,0:T(8,128)(2,1)S(1)}, bf16[1,4,16,512]{3,2,1,0:T(8,128)(2,1)S(1)}, u32[]{:S(2)}, u32[]{:S(2)}) collective-permute-start(bf16[1,4,16,512]{3,2,1,0:T(8,128)(2,1)S(1)} %get-tuple-element.184.held_ref), channel_id=1, source_target_pairs={{0,16},{4,20},{8,24},{12,28},{16,0},{20,4},{24,8},{28,12},{1,17},{... | collective-permute-start | bytes 196616 | tf_op jit(solution)/shard_map/ppermute | solution.py:475
  100.7 3.6 %collective-permute-start.36 = (bf16[2,4,16,512]{3,2,1,0:T(8,128)(2,1)S(1)}, bf16[2,4,16,512]{3,2,1,0:T(8,128)(2,1)S(1)}, u32[]{:S(2)}, u32[]{:S(2)}) collective-permute-start(bf16[2,4,16,512]{3,2,1,0:T(8,128)(2,1)S(1)} %get-tuple-element.189.held_ref.refs_8_), channel_id=1, source_target_pairs={{0,8},{4,12},{8,0},{12,4},{16,24},{20,28},{24,16},{28,20},{1,9},{5... | collective-permute-start | bytes 393224 | tf_op jit(solution)/shard_map/ppermute | solution.py:475
  104.4 2.3 %collective-permute-start.38 = (bf16[8,16,512]{2,1,0:T(8,128)(2,1)S(1)}, bf16[8,16,512]{2,1,0:T(8,128)(2,1)S(1)}, u32[]{:S(2)}, u32[]{:S(2)}) collective-permute-start(bf16[8,16,512]{2,1,0:T(8,128)(2,1)S(1)} %get-tuple-element.192), channel_id=1, source_target_pairs={{0,4},{4,0},{8,12},{12,8},{16,20},{20,16},{24,28},{28,24},{1,5},{5... | collective-permute-start | bytes 393224 | tf_op jit(solution)/shard_map/ppermute | solution.py:475
  110.4 2.7 %shard_map.137 = (bf16[4,128,512]{2,1,0:T(8,128)(2,1)}, bf16[16,128,512]{2,1,0:T(8,128)(2,1)}, f32[8,128]{1,0:T(8,128)S(1)}) custom-call(f32[8,128]{1,0:T(8,128)S(1)} %shard_map.136.token_ref, s32[1]{0:T(128)} %bitcast.me_ref, s32[16]{0:T(128)S(1)} %copy-done.3, s32[16]{0:T(128)S(1)} %copy-done.5, ...), custom_call_target="tpu_custom_call" | custom-call | bytes 1 | tf_op jit(solution)/shard_map/pallas_call | solution.py:24
  113.1 1.9 %shard_map.138 = (bf16[4,128,512]{2,1,0:T(8,128)(2,1)}, bf16[16,128,512]{2,1,0:T(8,128)(2,1)}, f32[8,128]{1,0:T(8,128)}) custom-call(f32[8,128]{1,0:T(8,128)S(1)} %get-tuple-element.194.token_ref, s32[1]{0:T(128)} %bitcast.me_ref, s32[16]{0:T(128)S(1)} %copy-done.3, s32[16]{0:T(128)S(1)} %copy-done.5, ...), custom_call_target="tpu_custom_call", output_to_operand_aliasing={{0}: (5, {}), {1}: (6, {})} | custom-call | bytes 1 | tf_op jit(solution)/shard_map/pallas_call | solution.py:24
  (112 shorter events, 42.1 us)
Async XLA Ops:
  5.2 16.3 %collective-permute-start = (bf16[528,512]{1,0:T(8,128)(2,1)}, bf16[528,512]{1,0:T(8,128)(2,1)S(1)}, u32[]{:S(2)}, u32[]{:S(2)}) collective-permute-start(bf16[528,512]{1,0:T(8,128)(2,1)} %get-tuple-element.105), channel_id=1, source_target_pairs={{0,4},{4,0},{8,12},{12,8},{16,20},{20,16},{24,28},{28,24},{1,5},{5... | collective-permute-start | bytes 1622024 | tf_op jit(solution)/shard_map/ppermute | solution.py:475
  8.2 15.8 %collective-permute-start.1 = (bf16[4,4,32,512]{3,2,1,0:T(8,128)(2,1)}, bf16[4,4,32,512]{3,2,1,0:T(8,128)(2,1)S(1)}, u32[]{:S(2)}, u32[]{:S(2)}) collective-permute-start(bf16[4,4,32,512]{3,2,1,0:T(8,128)(2,1)} %get-tuple-element.108), channel_id=1, source_target_pairs={{0,8},{4,12},{8,0},{12,4},{16,24},{20,28},{24,16},{28,20},{1,9},{5... | collective-permute-start | bytes 1572872 | tf_op jit(solution)/shard_map/ppermute | solution.py:475
  14.9 17.9 %collective-permute-start.2 = (bf16[4,4,32,512]{3,2,1,0:T(8,128)(2,1)S(1)}, bf16[4,4,32,512]{3,2,1,0:T(8,128)(2,1)S(1)}, u32[]{:S(2)}, u32[]{:S(2)}) collective-permute-start(bf16[4,4,32,512]{3,2,1,0:T(8,128)(2,1)S(1)} %get-tuple-element.111), channel_id=1, source_target_pairs={{0,4},{4,0},{8,12},{12,8},{16,20},{20,16},{24,28},{28,24},{1,5},{5... | collective-permute-start | bytes 1572872 | tf_op jit(solution)/shard_map/ppermute | solution.py:475
  15.5 22.9 %collective-permute-start.3 = (bf16[4,4,16,512]{3,2,1,0:T(8,128)(2,1)S(1)}, bf16[4,4,16,512]{3,2,1,0:T(8,128)(2,1)S(1)}, u32[]{:S(2)}, u32[]{:S(2)}) collective-permute-start(bf16[4,4,16,512]{3,2,1,0:T(8,128)(2,1)S(1)} %get-tuple-element.114), channel_id=1, source_target_pairs={{0,4},{4,0},{8,12},{12,8},{16,20},{20,16},{24,28},{28,24},{1,5},{5... | collective-permute-start | bytes 786440 | tf_op jit(solution)/shard_map/ppermute | solution.py:475
  21.8 16.7 %collective-permute-start.4 = (bf16[2,4,32,512]{3,2,1,0:T(8,128)(2,1)S(1)}, bf16[2,4,32,512]{3,2,1,0:T(8,128)(2,1)S(1)}, u32[]{:S(2)}, u32[]{:S(2)}) collective-permute-start(bf16[2,4,32,512]{3,2,1,0:T(8,128)(2,1)S(1)} %get-tuple-element.117), channel_id=1, source_target_pairs={{0,8},{4,12},{8,0},{12,4},{16,24},{20,28},{24,16},{28,20},{1,9},{5... | collective-permute-start | bytes 786440 | tf_op jit(solution)/shard_map/ppermute | solution.py:475
  24.3 17.6 %collective-permute-start.5 = (bf16[2,4,32,512]{3,2,1,0:T(8,128)(2,1)S(1)}, bf16[2,4,32,512]{3,2,1,0:T(8,128)(2,1)S(1)}, u32[]{:S(2)}, u32[]{:S(2)}) collective-permute-start(bf16[2,4,32,512]{3,2,1,0:T(8,128)(2,1)S(1)} %get-tuple-element.120), channel_id=1, source_target_pairs={{0,16},{4,20},{8,24},{12,28},{16,0},{20,4},{24,8},{28,12},{1,17},{... | collective-permute-start | bytes 786440 | tf_op jit(solution)/shard_map/ppermute | solution.py:475
  33.0 12.1 %collective-permute-start.6 = (bf16[2,4,32,512]{3,2,1,0:T(8,128)(2,1)S(1)}, bf16[2,4,32,512]{3,2,1,0:T(8,128)(2,1)S(1)}, u32[]{:S(2)}, u32[]{:S(2)}) collective-permute-start(bf16[2,4,32,512]{3,2,1,0:T(8,128)(2,1)S(1)} %get-tuple-element.123), channel_id=1, source_target_pairs={{0,8},{4,12},{8,0},{12,4},{16,24},{20,28},{24,16},{28,20},{1,9},{5... | collective-permute-start | bytes 786440 | tf_op jit(solution)/shard_map/ppermute | solution.py:475
  35.3 10.4 %collective-permute-start.7 = (bf16[4,4,16,512]{3,2,1,0:T(8,128)(2,1)S(1)}, bf16[4,4,16,512]{3,2,1,0:T(8,128)(2,1)S(1)}, u32[]{:S(2)}, u32[]{:S(2)}) collective-permute-start(bf16[4,4,16,512]{3,2,1,0:T(8,128)(2,1)S(1)} %get-tuple-element.126), channel_id=1, source_target_pairs={{0,4},{4,0},{8,12},{12,8},{16,20},{20,16},{24,28},{28,24},{1,5},{5... | collective-permute-start | bytes 786440 | tf_op jit(solution)/shard_map/ppermute | solution.py:475
  42.0 7.5 %collective-permute-start.9 = (bf16[1,4,32,512]{3,2,1,0:T(8,128)(2,1)S(1)}, bf16[1,4,32,512]{3,2,1,0:T(8,128)(2,1)S(1)}, u32[]{:S(2)}, u32[]{:S(2)}) collective-permute-start(bf16[1,4,32,512]{3,2,1,0:T(8,128)(2,1)S(1)} %get-tuple-element.132), channel_id=1, source_target_pairs={{0,4},{4,0},{8,12},{12,8},{16,20},{20,16},{24,28},{28,24},{1,5},{5... | collective-permute-start | bytes 393224 | tf_op jit(solution)/shard_map/ppermute | solution.py:475
  54.6 9.2 %collective-permute-start.17 = (bf16[2,4,32,512]{3,2,1,0:T(8,128)(2,1)S(1)}, bf16[2,4,32,512]{3,2,1,0:T(8,128)(2,1)S(1)}, u32[]{:S(2)}, u32[]{:S(2)}) collective-permute-start(bf16[2,4,32,512]{3,2,1,0:T(8,128)(2,1)S(1)} %get-tuple-element.151.held_ref), channel_id=1, source_target_pairs={{0,1},{1,0},{2,3},{3,2},{4,5},{5,4},{6,7},{7,6},{8,9},{9,8},{10,11... | collective-permute-start | bytes 786440 | tf_op jit(solution)/shard_map/ppermute | solution.py:475
  55.1 8.6 %collective-permute-start.15 = (bf16[1,4,32,512]{3,2,1,0:T(8,128)(2,1)S(1)}, bf16[1,4,32,512]{3,2,1,0:T(8,128)(2,1)S(1)}, u32[]{:S(2)}, u32[]{:S(2)}) collective-permute-start(bf16[1,4,32,512]{3,2,1,0:T(8,128)(2,1)S(1)} %bitcast.9), channel_id=1, source_target_pairs={{0,2},{1,3},{2,0},{3,1},{4,6},{5,7},{6,4},{7,5},{8,10},{9,11},{10,... | collective-permute-start | bytes 393224 | tf_op jit(solution)/shard_map/ppermute | solution.py:475
  56.4 7.3 %collective-permute-start.16 = (bf16[1,4,16,512]{3,2,1,0:T(8,128)(2,1)S(1)}, bf16[1,4,16,512]{3,2,1,0:T(8,128)(2,1)S(1)}, u32[]{:S(2)}, u32[]{:S(2)}) collective-permute-start(bf16[1,4,16,512]{3,2,1,0:T(8,128)(2,1)S(1)} %get-tuple-element.149), channel_id=1, source_target_pairs={{0,16},{4,20},{8,24},{12,28},{16,0},{20,4},{24,8},{28,12},{1,17},{... | collective-permute-start | bytes 196616 | tf_op jit(solution)/shard_map/ppermute | solution.py:475
  58.1 9.8 %collective-permute-start.18 = (bf16[1,4,32,512]{3,2,1,0:T(8,128)(2,1)S(1)}, bf16[1,4,32,512]{3,2,1,0:T(8,128)(2,1)S(1)}, u32[]{:S(2)}, u32[]{:S(2)}) collective-permute-start(bf16[1,4,32,512]{3,2,1,0:T(8,128)(2,1)S(1)} %get-tuple-element.153.held_ref), channel_id=1, source_target_pairs={{0,16},{4,20},{8,24},{12,28},{16,0},{20,4},{24,8},{28,12},{1,17},{... | collective-permute-start | bytes 393224 | tf_op jit(solution)/shard_map/ppermute | solution.py:475
  59.9 11.2 %collective-permute-start.19 = (bf16[2,4,16,512]{3,2,1,0:T(8,128)(2,1)S(1)}, bf16[2,4,16,512]{3,2,1,0:T(8,128)(2,1)S(1)}, u32[]{:S(2)}, u32[]{:S(2)}) collective-permute-start(bf16[2,4,16,512]{3,2,1,0:T(8,128)(2,1)S(1)} %get-tuple-element.156), channel_id=1, source_target_pairs={{0,8},{4,12},{8,0},{12,4},{16,24},{20,28},{24,16},{28,20},{1,9},{5... | collective-permute-start | bytes 393224 | tf_op jit(solution)/shard_map/ppermute | solution.py:475
  64.3 8.9 %collective-permute-start.20 = (bf16[1,4,32,512]{3,2,1,0:T(8,128)(2,1)S(1)}, bf16[1,4,32,512]{3,2,1,0:T(8,128)(2,1)S(1)}, u32[]{:S(2)}, u32[]{:S(2)}) collective-permute-start(bf16[1,4,32,512]{3,2,1,0:T(8,128)(2,1)S(1)} %get-tuple-element.158.held_ref), channel_id=1, source_target_pairs={{0,16},{4,20},{8,24},{12,28},{16,0},{20,4},{24,8},{28,12},{1,17},{... | collective-permute-start | bytes 393224 | tf_op jit(solution)/shard_map/ppermute | solution.py:475
  67.2 7.9 %collective-permute-start.23 = (bf16[2,4,32,512]{3,2,1,0:T(8,128)(2,1)S(1)}, bf16[2,4,32,512]{3,2,1,0:T(8,128)(2,1)S(1)}, u32[]{:S(2)}, u32[]{:S(2)}) collective-permute-start(bf16[2,4,32,512]{3,2,1,0:T(8,128)(2,1)S(1)} %get-tuple-element.164.held_ref), channel_id=1, source_target_pairs={{0,1},{1,0},{2,3},{3,2},{4,5},{5,4},{6,7},{7,6},{8,9},{9,8},{10,11... | collective-permute-start | bytes 786440 | tf_op jit(solution)/shard_map/ppermute | solution.py:475
  67.9 13.6 %collective-permute-start.25 = (bf16[2,4,32,512]{3,2,1,0:T(8,128)(2,1)S(1)}, bf16[2,4,32,512]{3,2,1,0:T(8,128)(2,1)S(1)}, u32[]{:S(2)}, u32[]{:S(2)}) collective-permute-start(bf16[2,4,32,512]{3,2,1,0:T(8,128)(2,1)S(1)} %get-tuple-element.169.held_ref.refs_0_), channel_id=1, source_target_pairs={{0,8},{4,12},{8,0},{12,4},{16,24},{20,28},{24,16},{28,20},{1,9},{5... | collective-permute-start | bytes 786440 | tf_op jit(solution)/shard_map/ppermute | solution.py:475
  73.3 7.5 %collective-permute-start.24 = (bf16[1,4,16,512]{3,2,1,0:T(8,128)(2,1)S(1)}, bf16[1,4,16,512]{3,2,1,0:T(8,128)(2,1)S(1)}, u32[]{:S(2)}, u32[]{:S(2)}) collective-permute-start(bf16[1,4,16,512]{3,2,1,0:T(8,128)(2,1)S(1)} %get-tuple-element.167), channel_id=1, source_target_pairs={{0,16},{4,20},{8,24},{12,28},{16,0},{20,4},{24,8},{28,12},{1,17},{... | collective-permute-start | bytes 196616 | tf_op jit(solution)/shard_map/ppermute | solution.py:475
  75.6 10.8 %collective-permute-start.27 = (bf16[1,4,32,512]{3,2,1,0:T(8,128)(2,1)S(1)}, bf16[1,4,32,512]{3,2,1,0:T(8,128)(2,1)S(1)}, u32[]{:S(2)}, u32[]{:S(2)}) collective-permute-start(bf16[1,4,32,512]{3,2,1,0:T(8,128)(2,1)S(1)} %get-tuple-element.173.held_ref), channel_id=1, source_target_pairs={{0,16},{4,20},{8,24},{12,28},{16,0},{20,4},{24,8},{28,12},{1,17},{... | collective-permute-start | bytes 393224 | tf_op jit(solution)/shard_map/ppermute | solution.py:475
  77.3 14.0 %collective-permute-start.28 = (bf16[2,4,32,512]{3,2,1,0:T(8,128)(2,1)S(1)}, bf16[2,4,32,512]{3,2,1,0:T(8,128)(2,1)S(1)}, u32[]{:S(2)}, u32[]{:S(2)}) collective-permute-start(bf16[2,4,32,512]{3,2,1,0:T(8,128)(2,1)S(1)} %get-tuple-element.175.held_ref.refs_2_), channel_id=1, source_target_pairs={{0,8},{4,12},{8,0},{12,4},{16,24},{20,28},{24,16},{28,20},{1,9},{5... | collective-permute-start | bytes 786440 | tf_op jit(solution)/shard_map/ppermute | solution.py:475
  81.7 12.5 %collective-permute-start.30 = (bf16[8,32,512]{2,1,0:T(8,128)(2,1)S(1)}, bf16[8,32,512]{2,1,0:T(8,128)(2,1)S(1)}, u32[]{:S(2)}, u32[]{:S(2)}) collective-permute-start(bf16[8,32,512]{2,1,0:T(8,128)(2,1)S(1)} %get-tuple-element.179), channel_id=1, source_target_pairs={{0,4},{4,0},{8,12},{12,8},{16,20},{20,16},{24,28},{28,24},{1,5},{5... | collective-permute-start | bytes 786440 | tf_op jit(solution)/shard_map/ppermute | solution.py:475
  86.4 12.5 %collective-permute-start.32 = (bf16[2,4,32,512]{3,2,1,0:T(8,128)(2,1)S(1)}, bf16[2,4,32,512]{3,2,1,0:T(8,128)(2,1)S(1)}, u32[]{:S(2)}, u32[]{:S(2)}) collective-permute-start(bf16[2,4,32,512]{3,2,1,0:T(8,128)(2,1)S(1)} %get-tuple-element.182.held_ref.refs_4_), channel_id=1, source_target_pairs={{0,8},{4,12},{8,0},{12,4},{16,24},{20,28},{24,16},{28,20},{1,9},{5... | collective-permute-start | bytes 786440 | tf_op jit(solution)/shard_map/ppermute | solution.py:475
  91.4 15.4 %collective-permute-start.35 = (bf16[8,32,512]{2,1,0:T(8,128)(2,1)S(1)}, bf16[8,32,512]{2,1,0:T(8,128)(2,1)S(1)}, u32[]{:S(2)}, u32[]{:S(2)}) collective-permute-start(bf16[8,32,512]{2,1,0:T(8,128)(2,1)S(1)} %get-tuple-element.188), channel_id=1, source_target_pairs={{0,4},{4,0},{8,12},{12,8},{16,20},{20,16},{24,28},{28,24},{1,5},{5... | collective-permute-start | bytes 786440 | tf_op jit(solution)/shard_map/ppermute | solution.py:475
  99.1 9.7 %collective-permute-start.37 = (bf16[8,32,512]{2,1,0:T(8,128)(2,1)S(1)}, bf16[8,32,512]{2,1,0:T(8,128)(2,1)S(1)}, u32[]{:S(2)}, u32[]{:S(2)}) collective-permute-start(bf16[8,32,512]{2,1,0:T(8,128)(2,1)S(1)} %get-tuple-element.191), channel_id=1, source_target_pairs={{0,4},{4,0},{8,12},{12,8},{16,20},{20,16},{24,28},{28,24},{1,5},{5... | collective-permute-start | bytes 786440 | tf_op jit(solution)/shard_map/ppermute | solution.py:475
  (22 other events, 143.4 us)

commit v16 on v15

--- a/solution.py
+++ b/solution.py
@@ -7,8 +7,8 @@
 
 SHARES = (2, 2, 2, 1, 1)
 ORDER = (
-    1, 0, 2, 4, 1, 0, 2, 3, 1, 0, 4, 2, 1, 0, 0, 2, 4, 1, 0, 3, 1, 4, 4, 2, 3, 0, 3, 2, 1, 4, 0, 3,
-    2, 3, 4, 1, 3, 2, 4, 3,
+    1, 0, 2, 3, 1, 0, 2, 4, 1, 0, 4, 2, 1, 0, 0, 4, 4, 3, 1, 0, 2, 1, 4, 0, 2, 3, 1, 3, 2, 4, 3, 1,
+    2, 3, 4, 0, 3, 2, 4, 3,
 )
 READ_CAP = 2
 VMEM_BYTES = 12 * 1024 * 1024

time: 115 us -> 118 us (1.026)
  waiting for transfers between devices: 23.8 us -> 41.4 us
  starting transfers between devices: 69.2 us -> 54.3 us
    ppermute x40, waiting for transfers between devices: 23.8 us -> 41.4 us  [flip(): lax.ppermute(value, axis, [(d, d ^ bit) for d in range(lax.axis_size(axis...]
    ppermute x40, starting transfers between devices: 69.2 us -> 54.3 us  [flip(): lax.ppermute(value, axis, [(d, d ^ bit) for d in range(lax.axis_size(axis...]
  transfers between devices with their start and end apart: 40 -> 40, of which waited for: 13 -> 19; matrix products, arithmetic and copies ran while one was open for 0% -> 0% of each run, Pallas kernels for 11% -> 11%
where the time goes in v16:
time: 118 us
  starting transfers between devices  54.3 us (46%)
  waiting for transfers between devices  41.4 us (35%)
  Pallas kernels  19.3 us (16%)
  local copies, waits for them, and re-layouts  1.73 us (1%)
    ppermute x40, starting transfers between devices, flip(): lax.ppermute(value, axis, [(d, d ^ bit) for d in range(lax.axis_size(axis...  54.3 us
    ppermute x40, waiting for transfers between devices, flip(): lax.ppermute(value, axis, [(d, d ^ bit) for d in range(lax.axis_size(axis...  41.4 us
    pallas_call x44, Pallas kernels, call(): pl.pallas_call(body, out_shape=out_shape, in_specs=in_specs, out_specs=ou...  19.3 us
  transfers between devices with their start and end apart: 40, of which 19 were waited for; matrix products, arithmetic and copies ran while one was open for 0% of the time, Pallas kernels for 11%

profile of v16, /device:TPU:0, one launch (start us, length us, event | category | flops | bytes accessed | tf_op | source)
XLA Modules:
  0.0 117.8 jit_solution(18354811919192181376)
XLA Ops:
  0.6 4.6 %shard_map.95 = (s32[256]{0:T(256)}, s32[16]{0:T(128)}, bf16[4,4,32,512]{3,2,1,0:T(8,128)(2,1)}, bf16[528,512]{1,0:T(8,128)(2,1)}, bf16[512,512]{1,0:T(8,128)(2,1)}) custom-call(s32[1]{0:T(128)} %bitcast.me_ref, s32[96]{0:T(128)} %slot_hbm.1, s32[96]{0:T(128)} %col_hbm.1, s32[96]{0:T(128)} %id_hbm.1, s32[8,4,8]{2,1,0:T(4,128)} %bitcast.21, s32[16]{0:T(128)} %readers_ref.3, ...), custom_call_target="tpu_custom_call" | custom-call | bytes 1 | tf_op jit(solution)/shard_map/pallas_call | solution.py:24
  5.2 3.0 %collective-permute-start = (bf16[528,512]{1,0:T(8,128)(2,1)}, bf16[528,512]{1,0:T(8,128)(2,1)S(1)}, u32[]{:S(2)}, u32[]{:S(2)}) collective-permute-start(bf16[528,512]{1,0:T(8,128)(2,1)} %get-tuple-element.105), channel_id=1, source_target_pairs={{0,4},{4,0},{8,12},{12,8},{16,20},{20,16},{24,28},{28,24},{1,5},{5... | collective-permute-start | bytes 1622024 | tf_op jit(solution)/shard_map/ppermute | solution.py:475
  11.5 3.3 %shard_map.98 = (bf16[4,4,32,512]{3,2,1,0:T(8,128)(2,1)S(1)}, bf16[4,4,16,512]{3,2,1,0:T(8,128)(2,1)S(1)}, bf16[4,4,16,512]{3,2,1,0:T(8,128)(2,1)S(1)}, bf16[4,4,32,512]{3,2,1,0:T(8,128)(2,1)S(1)}, f32[8,128]{1,0:T(8,128)}) custom-call(s32[256]{0:T(256)S(1)} %copy-done.4, bf16[48,128,128]{2,1,0:T(8,128)(2,1)S(1)} %copy-done.1, bf16[512,512]{1,0:T(8,128)(2,1)S(1)} %copy-done.2), custom_call_target="tpu_custom_call" | custom-call | bytes 1 | tf_op jit(solution)/shard_map/pallas_call | solution.py:24
  17.0 2.3 %shard_map.96 = (bf16[4,4,32,512]{3,2,1,0:T(8,128)(2,1)S(1)}, bf16[4,4,32,512]{3,2,1,0:T(8,128)(2,1)S(1)}, bf16[4,4,16,512]{3,2,1,0:T(8,128)(2,1)S(1)}, bf16[4,4,16,512]{3,2,1,0:T(8,128)(2,1)S(1)}, f32[8,128]{1,0:T(8,128)S(1)}) custom-call(s32[256]{0:T(256)S(1)} %copy-done.4, bf16[48,128,128]{2,1,0:T(8,128)(2,1)S(1)} %copy-done.1, bf16[512,512]{1,0:T(8,128)(2,1)S(1)} %copy-done.2), custom_call_target="tpu_custom_call" | custom-call | bytes 1 | tf_op jit(solution)/shard_map/pallas_call | solution.py:24
  19.2 2.3 %collective-permute-done.got_ref.wanted_ref = bf16[528,512]{1,0:T(8,128)(2,1)S(1)} collective-permute-done((bf16[528,512]{1,0:T(8,128)(2,1)}, bf16[528,512]{1,0:T(8,128)(2,1)S(1)}, u32[]{:S(2)}, u32[]{:S(2)}) %collective-permute-start) | collective-permute-done | bytes 540704 | tf_op jit(solution)/shard_map/ppermute | solution.py:475
  21.8 2.2 %collective-permute-start.4 = (bf16[2,4,32,512]{3,2,1,0:T(8,128)(2,1)S(1)}, bf16[2,4,32,512]{3,2,1,0:T(8,128)(2,1)S(1)}, u32[]{:S(2)}, u32[]{:S(2)}) collective-permute-start(bf16[2,4,32,512]{3,2,1,0:T(8,128)(2,1)S(1)} %get-tuple-element.117), channel_id=1, source_target_pairs={{0,8},{4,12},{8,0},{12,4},{16,24},{20,28},{24,16},{28,20},{1,9},{5... | collective-permute-start | bytes 786440 | tf_op jit(solution)/shard_map/ppermute | solution.py:475
  24.3 2.7 %collective-permute-start.5 = (bf16[2,4,32,512]{3,2,1,0:T(8,128)(2,1)S(1)}, bf16[2,4,32,512]{3,2,1,0:T(8,128)(2,1)S(1)}, u32[]{:S(2)}, u32[]{:S(2)}) collective-permute-start(bf16[2,4,32,512]{3,2,1,0:T(8,128)(2,1)S(1)} %get-tuple-element.120), channel_id=1, source_target_pairs={{0,16},{4,20},{8,24},{12,28},{16,0},{20,4},{24,8},{28,12},{1,17},{... | collective-permute-start | bytes 786440 | tf_op jit(solution)/shard_map/ppermute | solution.py:475
  26.9 5.8 %collective-permute-done.2.got_ref = bf16[4,4,32,512]{3,2,1,0:T(8,128)(2,1)S(1)} collective-permute-done((bf16[4,4,32,512]{3,2,1,0:T(8,128)(2,1)S(1)}, bf16[4,4,32,512]{3,2,1,0:T(8,128)(2,1)S(1)}, u32[]{:S(2)}, u32[]{:S(2)}) %collective-permute-start.2) | collective-permute-done | bytes 524320 | tf_op jit(solution)/shard_map/ppermute | solution.py:475
  33.0 2.2 %collective-permute-start.6 = (bf16[2,4,32,512]{3,2,1,0:T(8,128)(2,1)S(1)}, bf16[2,4,32,512]{3,2,1,0:T(8,128)(2,1)S(1)}, u32[]{:S(2)}, u32[]{:S(2)}) collective-permute-start(bf16[2,4,32,512]{3,2,1,0:T(8,128)(2,1)S(1)} %get-tuple-element.123), channel_id=1, source_target_pairs={{0,8},{4,12},{8,0},{12,4},{16,24},{20,28},{24,16},{28,20},{1,9},{5... | collective-permute-start | bytes 786440 | tf_op jit(solution)/shard_map/ppermute | solution.py:475
  38.7 3.2 %collective-permute-start.8 = (bf16[1,4,32,512]{3,2,1,0:T(8,128)(2,1)S(1)}, bf16[1,4,32,512]{3,2,1,0:T(8,128)(2,1)S(1)}, u32[]{:S(2)}, u32[]{:S(2)}) collective-permute-start(bf16[1,4,32,512]{3,2,1,0:T(8,128)(2,1)S(1)} %get-tuple-element.129), channel_id=1, source_target_pairs={{0,16},{4,20},{8,24},{12,28},{16,0},{20,4},{24,8},{28,12},{1,17},{... | collective-permute-start | bytes 393224 | tf_op jit(solution)/shard_map/ppermute | solution.py:475
  44.3 2.1 %collective-permute-start.10 = (bf16[2,4,16,512]{3,2,1,0:T(8,128)(2,1)S(1)}, bf16[2,4,16,512]{3,2,1,0:T(8,128)(2,1)S(1)}, u32[]{:S(2)}, u32[]{:S(2)}) collective-permute-start(bf16[2,4,16,512]{3,2,1,0:T(8,128)(2,1)S(1)} %get-tuple-element.135), channel_id=1, source_target_pairs={{0,8},{4,12},{8,0},{12,4},{16,24},{20,28},{24,16},{28,20},{1,9},{5... | collective-permute-start | bytes 393224 | tf_op jit(solution)/shard_map/ppermute | solution.py:475
  46.4 2.6 %collective-permute-start.11 = (bf16[1,4,32,512]{3,2,1,0:T(8,128)(2,1)S(1)}, bf16[1,4,32,512]{3,2,1,0:T(8,128)(2,1)S(1)}, u32[]{:S(2)}, u32[]{:S(2)}) collective-permute-start(bf16[1,4,32,512]{3,2,1,0:T(8,128)(2,1)S(1)} %get-tuple-element.138), channel_id=1, source_target_pairs={{0,16},{4,20},{8,24},{12,28},{16,0},{20,4},{24,8},{28,12},{1,17},{... | collective-permute-start | bytes 393224 | tf_op jit(solution)/shard_map/ppermute | solution.py:475
  51.3 2.4 %collective-permute-done.11.got_ref = bf16[1,4,32,512]{3,2,1,0:T(8,128)(2,1)S(1)} collective-permute-done((bf16[1,4,32,512]{3,2,1,0:T(8,128)(2,1)S(1)}, bf16[1,4,32,512]{3,2,1,0:T(8,128)(2,1)S(1)}, u32[]{:S(2)}, u32[]{:S(2)}) %collective-permute-start.11) | collective-permute-done | bytes 131104 | tf_op jit(solution)/shard_map/ppermute | solution.py:475
  64.1 3.0 %collective-permute-done.16.got_ref = bf16[1,4,16,512]{3,2,1,0:T(8,128)(2,1)S(1)} collective-permute-done((bf16[1,4,16,512]{3,2,1,0:T(8,128)(2,1)S(1)}, bf16[1,4,16,512]{3,2,1,0:T(8,128)(2,1)S(1)}, u32[]{:S(2)}, u32[]{:S(2)}) %collective-permute-start.16) | collective-permute-done | bytes 65568 | tf_op jit(solution)/shard_map/ppermute | solution.py:475
  70.2 5.2 %collective-permute-done.21.got_ref = bf16[1,4,32,512]{3,2,1,0:T(8,128)(2,1)S(1)} collective-permute-done((bf16[1,4,32,512]{3,2,1,0:T(8,128)(2,1)S(1)}, bf16[1,4,32,512]{3,2,1,0:T(8,128)(2,1)S(1)}, u32[]{:S(2)}, u32[]{:S(2)}) %collective-permute-start.21) | collective-permute-done | bytes 131104 | tf_op jit(solution)/shard_map/ppermute | solution.py:475
  78.1 3.0 %collective-permute-done.23.got_ref.refs_1_ = bf16[2,4,32,512]{3,2,1,0:T(8,128)(2,1)S(1)} collective-permute-done((bf16[2,4,32,512]{3,2,1,0:T(8,128)(2,1)S(1)}, bf16[2,4,32,512]{3,2,1,0:T(8,128)(2,1)S(1)}, u32[]{:S(2)}, u32[]{:S(2)}) %collective-permute-start.23) | collective-permute-done | bytes 262176 | tf_op jit(solution)/shard_map/ppermute | solution.py:475
  81.7 2.1 %collective-permute-done.25.got_ref = bf16[1,4,16,512]{3,2,1,0:T(8,128)(2,1)S(1)} collective-permute-done((bf16[1,4,16,512]{3,2,1,0:T(8,128)(2,1)S(1)}, bf16[1,4,16,512]{3,2,1,0:T(8,128)(2,1)S(1)}, u32[]{:S(2)}, u32[]{:S(2)}) %collective-permute-start.25) | collective-permute-done | bytes 65568 | tf_op jit(solution)/shard_map/ppermute | solution.py:475
  85.2 1.9 %collective-permute-done.26.got_ref.refs_3_ = bf16[2,4,32,512]{3,2,1,0:T(8,128)(2,1)S(1)} collective-permute-done((bf16[2,4,32,512]{3,2,1,0:T(8,128)(2,1)S(1)}, bf16[2,4,32,512]{3,2,1,0:T(8,128)(2,1)S(1)}, u32[]{:S(2)}, u32[]{:S(2)}) %collective-permute-start.26) | collective-permute-done | bytes 262176 | tf_op jit(solution)/shard_map/ppermute | solution.py:475
  89.6 2.3 %collective-permute-start.32 = (bf16[2,4,32,512]{3,2,1,0:T(8,128)(2,1)S(1)}, bf16[2,4,32,512]{3,2,1,0:T(8,128)(2,1)S(1)}, u32[]{:S(2)}, u32[]{:S(2)}) collective-permute-start(bf16[2,4,32,512]{3,2,1,0:T(8,128)(2,1)S(1)} %get-tuple-element.182.held_ref.refs_4_), channel_id=1, source_target_pairs={{0,8},{4,12},{8,0},{12,4},{16,24},{20,28},{24,16},{28,20},{1,9},{5... | collective-permute-start | bytes 786440 | tf_op jit(solution)/shard_map/ppermute | solution.py:475
  93.4 4.4 %collective-permute-done.29.got_ref = bf16[1,4,16,512]{3,2,1,0:T(8,128)(2,1)S(1)} collective-permute-done((bf16[1,4,16,512]{3,2,1,0:T(8,128)(2,1)S(1)}, bf16[1,4,16,512]{3,2,1,0:T(8,128)(2,1)S(1)}, u32[]{:S(2)}, u32[]{:S(2)}) %collective-permute-start.29) | collective-permute-done | bytes 65568 | tf_op jit(solution)/shard_map/ppermute | solution.py:475
  98.3 2.7 %collective-permute-start.33 = (bf16[1,4,16,512]{3,2,1,0:T(8,128)(2,1)S(1)}, bf16[1,4,16,512]{3,2,1,0:T(8,128)(2,1)S(1)}, u32[]{:S(2)}, u32[]{:S(2)}) collective-permute-start(bf16[1,4,16,512]{3,2,1,0:T(8,128)(2,1)S(1)} %get-tuple-element.184.held_ref), channel_id=1, source_target_pairs={{0,16},{4,20},{8,24},{12,28},{16,0},{20,4},{24,8},{28,12},{1,17},{... | collective-permute-start | bytes 196616 | tf_op jit(solution)/shard_map/ppermute | solution.py:475
  103.6 2.1 %collective-permute-start.36 = (bf16[2,4,16,512]{3,2,1,0:T(8,128)(2,1)S(1)}, bf16[2,4,16,512]{3,2,1,0:T(8,128)(2,1)S(1)}, u32[]{:S(2)}, u32[]{:S(2)}) collective-permute-start(bf16[2,4,16,512]{3,2,1,0:T(8,128)(2,1)S(1)} %get-tuple-element.189.held_ref.refs_8_), channel_id=1, source_target_pairs={{0,8},{4,12},{8,0},{12,4},{16,24},{20,28},{24,16},{28,20},{1,9},{5... | collective-permute-start | bytes 393224 | tf_op jit(solution)/shard_map/ppermute | solution.py:475
  110.4 2.7 %collective-permute-done.38.value_ref.refs_13_ = bf16[8,16,512]{2,1,0:T(8,128)(2,1)S(1)} collective-permute-done((bf16[8,16,512]{2,1,0:T(8,128)(2,1)S(1)}, bf16[8,16,512]{2,1,0:T(8,128)(2,1)S(1)}, u32[]{:S(2)}, u32[]{:S(2)}) %collective-permute-start.38) | collective-permute-done | bytes 131104 | tf_op jit(solution)/shard_map/ppermute | solution.py:475
  113.1 2.7 %shard_map.137 = (bf16[4,128,512]{2,1,0:T(8,128)(2,1)}, bf16[16,128,512]{2,1,0:T(8,128)(2,1)}, f32[8,128]{1,0:T(8,128)S(1)}) custom-call(f32[8,128]{1,0:T(8,128)S(1)} %shard_map.136.token_ref, s32[1]{0:T(128)} %bitcast.me_ref, s32[16]{0:T(128)S(1)} %copy-done.3, s32[16]{0:T(128)S(1)} %copy-done.5, ...), custom_call_target="tpu_custom_call" | custom-call | bytes 1 | tf_op jit(solution)/shard_map/pallas_call | solution.py:24
  (112 shorter events, 46.1 us)
Async XLA Ops:
  5.2 16.3 %collective-permute-start = (bf16[528,512]{1,0:T(8,128)(2,1)}, bf16[528,512]{1,0:T(8,128)(2,1)S(1)}, u32[]{:S(2)}, u32[]{:S(2)}) collective-permute-start(bf16[528,512]{1,0:T(8,128)(2,1)} %get-tuple-element.105), channel_id=1, source_target_pairs={{0,4},{4,0},{8,12},{12,8},{16,20},{20,16},{24,28},{28,24},{1,5},{5... | collective-permute-start | bytes 1622024 | tf_op jit(solution)/shard_map/ppermute | solution.py:475
  8.2 15.8 %collective-permute-start.1 = (bf16[4,4,32,512]{3,2,1,0:T(8,128)(2,1)}, bf16[4,4,32,512]{3,2,1,0:T(8,128)(2,1)S(1)}, u32[]{:S(2)}, u32[]{:S(2)}) collective-permute-start(bf16[4,4,32,512]{3,2,1,0:T(8,128)(2,1)} %get-tuple-element.108), channel_id=1, source_target_pairs={{0,8},{4,12},{8,0},{12,4},{16,24},{20,28},{24,16},{28,20},{1,9},{5... | collective-permute-start | bytes 1572872 | tf_op jit(solution)/shard_map/ppermute | solution.py:475
  14.9 17.9 %collective-permute-start.2 = (bf16[4,4,32,512]{3,2,1,0:T(8,128)(2,1)S(1)}, bf16[4,4,32,512]{3,2,1,0:T(8,128)(2,1)S(1)}, u32[]{:S(2)}, u32[]{:S(2)}) collective-permute-start(bf16[4,4,32,512]{3,2,1,0:T(8,128)(2,1)S(1)} %get-tuple-element.111), channel_id=1, source_target_pairs={{0,4},{4,0},{8,12},{12,8},{16,20},{20,16},{24,28},{28,24},{1,5},{5... | collective-permute-start | bytes 1572872 | tf_op jit(solution)/shard_map/ppermute | solution.py:475
  15.5 22.9 %collective-permute-start.3 = (bf16[4,4,16,512]{3,2,1,0:T(8,128)(2,1)S(1)}, bf16[4,4,16,512]{3,2,1,0:T(8,128)(2,1)S(1)}, u32[]{:S(2)}, u32[]{:S(2)}) collective-permute-start(bf16[4,4,16,512]{3,2,1,0:T(8,128)(2,1)S(1)} %get-tuple-element.114), channel_id=1, source_target_pairs={{0,4},{4,0},{8,12},{12,8},{16,20},{20,16},{24,28},{28,24},{1,5},{5... | collective-permute-start | bytes 786440 | tf_op jit(solution)/shard_map/ppermute | solution.py:475
  21.8 16.7 %collective-permute-start.4 = (bf16[2,4,32,512]{3,2,1,0:T(8,128)(2,1)S(1)}, bf16[2,4,32,512]{3,2,1,0:T(8,128)(2,1)S(1)}, u32[]{:S(2)}, u32[]{:S(2)}) collective-permute-start(bf16[2,4,32,512]{3,2,1,0:T(8,128)(2,1)S(1)} %get-tuple-element.117), channel_id=1, source_target_pairs={{0,8},{4,12},{8,0},{12,4},{16,24},{20,28},{24,16},{28,20},{1,9},{5... | collective-permute-start | bytes 786440 | tf_op jit(solution)/shard_map/ppermute | solution.py:475
  24.3 17.6 %collective-permute-start.5 = (bf16[2,4,32,512]{3,2,1,0:T(8,128)(2,1)S(1)}, bf16[2,4,32,512]{3,2,1,0:T(8,128)(2,1)S(1)}, u32[]{:S(2)}, u32[]{:S(2)}) collective-permute-start(bf16[2,4,32,512]{3,2,1,0:T(8,128)(2,1)S(1)} %get-tuple-element.120), channel_id=1, source_target_pairs={{0,16},{4,20},{8,24},{12,28},{16,0},{20,4},{24,8},{28,12},{1,17},{... | collective-permute-start | bytes 786440 | tf_op jit(solution)/shard_map/ppermute | solution.py:475
  33.0 10.5 %collective-permute-start.6 = (bf16[2,4,32,512]{3,2,1,0:T(8,128)(2,1)S(1)}, bf16[2,4,32,512]{3,2,1,0:T(8,128)(2,1)S(1)}, u32[]{:S(2)}, u32[]{:S(2)}) collective-permute-start(bf16[2,4,32,512]{3,2,1,0:T(8,128)(2,1)S(1)} %get-tuple-element.123), channel_id=1, source_target_pairs={{0,8},{4,12},{8,0},{12,4},{16,24},{20,28},{24,16},{28,20},{1,9},{5... | collective-permute-start | bytes 786440 | tf_op jit(solution)/shard_map/ppermute | solution.py:475
  35.3 8.9 %collective-permute-start.7 = (bf16[4,4,16,512]{3,2,1,0:T(8,128)(2,1)S(1)}, bf16[4,4,16,512]{3,2,1,0:T(8,128)(2,1)S(1)}, u32[]{:S(2)}, u32[]{:S(2)}) collective-permute-start(bf16[4,4,16,512]{3,2,1,0:T(8,128)(2,1)S(1)} %get-tuple-element.126), channel_id=1, source_target_pairs={{0,4},{4,0},{8,12},{12,8},{16,20},{20,16},{24,28},{28,24},{1,5},{5... | collective-permute-start | bytes 786440 | tf_op jit(solution)/shard_map/ppermute | solution.py:475
  38.7 10.3 %collective-permute-start.8 = (bf16[1,4,32,512]{3,2,1,0:T(8,128)(2,1)S(1)}, bf16[1,4,32,512]{3,2,1,0:T(8,128)(2,1)S(1)}, u32[]{:S(2)}, u32[]{:S(2)}) collective-permute-start(bf16[1,4,32,512]{3,2,1,0:T(8,128)(2,1)S(1)} %get-tuple-element.129), channel_id=1, source_target_pairs={{0,16},{4,20},{8,24},{12,28},{16,0},{20,4},{24,8},{28,12},{1,17},{... | collective-permute-start | bytes 393224 | tf_op jit(solution)/shard_map/ppermute | solution.py:475
  42.0 8.6 %collective-permute-start.9 = (bf16[1,4,32,512]{3,2,1,0:T(8,128)(2,1)S(1)}, bf16[1,4,32,512]{3,2,1,0:T(8,128)(2,1)S(1)}, u32[]{:S(2)}, u32[]{:S(2)}) collective-permute-start(bf16[1,4,32,512]{3,2,1,0:T(8,128)(2,1)S(1)} %get-tuple-element.132), channel_id=1, source_target_pairs={{0,4},{4,0},{8,12},{12,8},{16,20},{20,16},{24,28},{28,24},{1,5},{5... | collective-permute-start | bytes 393224 | tf_op jit(solution)/shard_map/ppermute | solution.py:475
  55.8 11.4 %collective-permute-start.18 = (bf16[2,4,32,512]{3,2,1,0:T(8,128)(2,1)S(1)}, bf16[2,4,32,512]{3,2,1,0:T(8,128)(2,1)S(1)}, u32[]{:S(2)}, u32[]{:S(2)}) collective-permute-start(bf16[2,4,32,512]{3,2,1,0:T(8,128)(2,1)S(1)} %get-tuple-element.154.held_ref), channel_id=1, source_target_pairs={{0,1},{1,0},{2,3},{3,2},{4,5},{5,4},{6,7},{7,6},{8,9},{9,8},{10,11... | collective-permute-start | bytes 786440 | tf_op jit(solution)/shard_map/ppermute | solution.py:475
  56.6 10.5 %collective-permute-start.17 = (bf16[2,4,16,512]{3,2,1,0:T(8,128)(2,1)S(1)}, bf16[2,4,16,512]{3,2,1,0:T(8,128)(2,1)S(1)}, u32[]{:S(2)}, u32[]{:S(2)}) collective-permute-start(bf16[2,4,16,512]{3,2,1,0:T(8,128)(2,1)S(1)} %get-tuple-element.152), channel_id=1, source_target_pairs={{0,8},{4,12},{8,0},{12,4},{16,24},{20,28},{24,16},{28,20},{1,9},{5... | collective-permute-start | bytes 393224 | tf_op jit(solution)/shard_map/ppermute | solution.py:475
  58.6 9.7 %collective-permute-start.19 = (bf16[1,4,32,512]{3,2,1,0:T(8,128)(2,1)S(1)}, bf16[1,4,32,512]{3,2,1,0:T(8,128)(2,1)S(1)}, u32[]{:S(2)}, u32[]{:S(2)}) collective-permute-start(bf16[1,4,32,512]{3,2,1,0:T(8,128)(2,1)S(1)} %get-tuple-element.156.held_ref), channel_id=1, source_target_pairs={{0,16},{4,20},{8,24},{12,28},{16,0},{20,4},{24,8},{28,12},{1,17},{... | collective-permute-start | bytes 393224 | tf_op jit(solution)/shard_map/ppermute | solution.py:475
  60.2 9.4 %collective-permute-start.20 = (bf16[1,4,32,512]{3,2,1,0:T(8,128)(2,1)S(1)}, bf16[1,4,32,512]{3,2,1,0:T(8,128)(2,1)S(1)}, u32[]{:S(2)}, u32[]{:S(2)}) collective-permute-start(bf16[1,4,32,512]{3,2,1,0:T(8,128)(2,1)S(1)} %bitcast.9), channel_id=1, source_target_pairs={{0,2},{1,3},{2,0},{3,1},{4,6},{5,7},{6,4},{7,5},{8,10},{9,11},{10,... | collective-permute-start | bytes 393224 | tf_op jit(solution)/shard_map/ppermute | solution.py:475
  68.3 12.8 %collective-permute-start.23 = (bf16[2,4,32,512]{3,2,1,0:T(8,128)(2,1)S(1)}, bf16[2,4,32,512]{3,2,1,0:T(8,128)(2,1)S(1)}, u32[]{:S(2)}, u32[]{:S(2)}) collective-permute-start(bf16[2,4,32,512]{3,2,1,0:T(8,128)(2,1)S(1)} %get-tuple-element.164.held_ref.refs_0_), channel_id=1, source_target_pairs={{0,8},{4,12},{8,0},{12,4},{16,24},{20,28},{24,16},{28,20},{1,9},{5... | collective-permute-start | bytes 786440 | tf_op jit(solution)/shard_map/ppermute | solution.py:475
  69.6 11.6 %collective-permute-start.24 = (bf16[2,4,32,512]{3,2,1,0:T(8,128)(2,1)S(1)}, bf16[2,4,32,512]{3,2,1,0:T(8,128)(2,1)S(1)}, u32[]{:S(2)}, u32[]{:S(2)}) collective-permute-start(bf16[2,4,32,512]{3,2,1,0:T(8,128)(2,1)S(1)} %get-tuple-element.166.held_ref), channel_id=1, source_target_pairs={{0,1},{1,0},{2,3},{3,2},{4,5},{5,4},{6,7},{7,6},{8,9},{9,8},{10,11... | collective-permute-start | bytes 786440 | tf_op jit(solution)/shard_map/ppermute | solution.py:475
  69.7 7.9 %collective-permute-start.22 = (bf16[2,4,16,512]{3,2,1,0:T(8,128)(2,1)S(1)}, bf16[2,4,16,512]{3,2,1,0:T(8,128)(2,1)S(1)}, u32[]{:S(2)}, u32[]{:S(2)}) collective-permute-start(bf16[2,4,16,512]{3,2,1,0:T(8,128)(2,1)S(1)} %get-tuple-element.162.held_ref), channel_id=1, source_target_pairs={{0,1},{1,0},{2,3},{3,2},{4,5},{5,4},{6,7},{7,6},{8,9},{9,8},{10,11... | collective-permute-start | bytes 393224 | tf_op jit(solution)/shard_map/ppermute | solution.py:475
  75.3 11.8 %collective-permute-start.26 = (bf16[2,4,32,512]{3,2,1,0:T(8,128)(2,1)S(1)}, bf16[2,4,32,512]{3,2,1,0:T(8,128)(2,1)S(1)}, u32[]{:S(2)}, u32[]{:S(2)}) collective-permute-start(bf16[2,4,32,512]{3,2,1,0:T(8,128)(2,1)S(1)} %get-tuple-element.171.held_ref.refs_2_), channel_id=1, source_target_pairs={{0,8},{4,12},{8,0},{12,4},{16,24},{20,28},{24,16},{28,20},{1,9},{5... | collective-permute-start | bytes 786440 | tf_op jit(solution)/shard_map/ppermute | solution.py:475
  75.7 8.1 %collective-permute-start.25 = (bf16[1,4,16,512]{3,2,1,0:T(8,128)(2,1)S(1)}, bf16[1,4,16,512]{3,2,1,0:T(8,128)(2,1)S(1)}, u32[]{:S(2)}, u32[]{:S(2)}) collective-permute-start(bf16[1,4,16,512]{3,2,1,0:T(8,128)(2,1)S(1)} %get-tuple-element.169), channel_id=1, source_target_pairs={{0,16},{4,20},{8,24},{12,28},{16,0},{20,4},{24,8},{28,12},{1,17},{... | collective-permute-start | bytes 196616 | tf_op jit(solution)/shard_map/ppermute | solution.py:475
  81.6 8.0 %collective-permute-start.28 = (bf16[1,4,32,512]{3,2,1,0:T(8,128)(2,1)S(1)}, bf16[1,4,32,512]{3,2,1,0:T(8,128)(2,1)S(1)}, u32[]{:S(2)}, u32[]{:S(2)}) collective-permute-start(bf16[1,4,32,512]{3,2,1,0:T(8,128)(2,1)S(1)} %get-tuple-element.175.held_ref), channel_id=1, source_target_pairs={{0,16},{4,20},{8,24},{12,28},{16,0},{20,4},{24,8},{28,12},{1,17},{... | collective-permute-start | bytes 393224 | tf_op jit(solution)/shard_map/ppermute | solution.py:475
  87.3 13.7 %collective-permute-start.31 = (bf16[8,32,512]{2,1,0:T(8,128)(2,1)S(1)}, bf16[8,32,512]{2,1,0:T(8,128)(2,1)S(1)}, u32[]{:S(2)}, u32[]{:S(2)}) collective-permute-start(bf16[8,32,512]{2,1,0:T(8,128)(2,1)S(1)} %get-tuple-element.181), channel_id=1, source_target_pairs={{0,4},{4,0},{8,12},{12,8},{16,20},{20,16},{24,28},{28,24},{1,5},{5... | collective-permute-start | bytes 786440 | tf_op jit(solution)/shard_map/ppermute | solution.py:475
  89.6 11.4 %collective-permute-start.32 = (bf16[2,4,32,512]{3,2,1,0:T(8,128)(2,1)S(1)}, bf16[2,4,32,512]{3,2,1,0:T(8,128)(2,1)S(1)}, u32[]{:S(2)}, u32[]{:S(2)}) collective-permute-start(bf16[2,4,32,512]{3,2,1,0:T(8,128)(2,1)S(1)} %get-tuple-element.182.held_ref.refs_4_), channel_id=1, source_target_pairs={{0,8},{4,12},{8,0},{12,4},{16,24},{20,28},{24,16},{28,20},{1,9},{5... | collective-permute-start | bytes 786440 | tf_op jit(solution)/shard_map/ppermute | solution.py:475
  91.9 16.7 %collective-permute-start.35 = (bf16[8,32,512]{2,1,0:T(8,128)(2,1)S(1)}, bf16[8,32,512]{2,1,0:T(8,128)(2,1)S(1)}, u32[]{:S(2)}, u32[]{:S(2)}) collective-permute-start(bf16[8,32,512]{2,1,0:T(8,128)(2,1)S(1)} %get-tuple-element.188), channel_id=1, source_target_pairs={{0,4},{4,0},{8,12},{12,8},{16,20},{20,16},{24,28},{28,24},{1,5},{5... | collective-permute-start | bytes 786440 | tf_op jit(solution)/shard_map/ppermute | solution.py:475
  101.2 9.3 %collective-permute-start.37 = (bf16[8,32,512]{2,1,0:T(8,128)(2,1)S(1)}, bf16[8,32,512]{2,1,0:T(8,128)(2,1)S(1)}, u32[]{:S(2)}, u32[]{:S(2)}) collective-permute-start(bf16[8,32,512]{2,1,0:T(8,128)(2,1)S(1)} %get-tuple-element.191), channel_id=1, source_target_pairs={{0,4},{4,0},{8,12},{12,8},{16,20},{20,16},{24,28},{28,24},{1,5},{5... | collective-permute-start | bytes 786440 | tf_op jit(solution)/shard_map/ppermute | solution.py:475
  (22 other events, 142.0 us)

commit v17 on v13

--- a/solution.py
+++ b/solution.py
@@ -7,7 +7,7 @@
 
 SHARES = (2, 2, 2, 1, 1)
 ORDER = (
-    0, 1, 2, 0, 1, 2, 1, 3, 4, 0, 2, 1, 1, 4, 1, 2, 3, 4, 0, 2, 0, 3, 3, 2, 4, 1, 0, 4, 2, 4, 3, 1,
+    1, 0, 2, 4, 1, 0, 2, 3, 1, 0, 4, 2, 3, 1, 1, 4, 0, 4, 1, 2, 2, 3, 3, 0, 2, 1, 0, 4, 2, 4, 3, 1,
     0, 3, 4, 2, 3, 0, 4, 3,
 )
 READ_CAP = 2

time: 118 us -> 116 us (0.983)
  waiting for transfers between devices: 46 us -> 31 us
  starting transfers between devices: 49.6 us -> 63 us
    ppermute x40, waiting for transfers between devices: 46 us -> 31 us  [flip(): lax.ppermute(value, axis, [(d, d ^ bit) for d in range(lax.axis_size(axis...]
    ppermute x40, starting transfers between devices: 49.6 us -> 63 us  [flip(): lax.ppermute(value, axis, [(d, d ^ bit) for d in range(lax.axis_size(axis...]
  transfers between devices with their start and end apart: 40 -> 40, of which waited for: 21 -> 18; matrix products, arithmetic and copies ran while one was open for 0% -> 0% of each run, Pallas kernels for 11% -> 11%
where the time goes in v17:
time: 116 us
  starting transfers between devices  63 us (54%)
  waiting for transfers between devices  31 us (27%)
  Pallas kernels  19.3 us (17%)
  local copies, waits for them, and re-layouts  1.73 us (1%)
    ppermute x40, starting transfers between devices, flip(): lax.ppermute(value, axis, [(d, d ^ bit) for d in range(lax.axis_size(axis...  63 us
    ppermute x40, waiting for transfers between devices, flip(): lax.ppermute(value, axis, [(d, d ^ bit) for d in range(lax.axis_size(axis...  31 us
    pallas_call x44, Pallas kernels, call(): pl.pallas_call(body, out_shape=out_shape, in_specs=in_specs, out_specs=ou...  19.3 us
  transfers between devices with their start and end apart: 40, of which 18 were waited for; matrix products, arithmetic and copies ran while one was open for 0% of the time, Pallas kernels for 11%

profile of v17, /device:TPU:0, one launch (start us, length us, event | category | flops | bytes accessed | tf_op | source)
XLA Modules:
  0.0 116.0 jit_solution(18374189728307027360)
XLA Ops:
  0.6 4.6 %shard_map.95 = (s32[256]{0:T(256)}, s32[16]{0:T(128)}, bf16[4,4,32,512]{3,2,1,0:T(8,128)(2,1)}, bf16[528,512]{1,0:T(8,128)(2,1)}, bf16[512,512]{1,0:T(8,128)(2,1)}) custom-call(s32[1]{0:T(128)} %bitcast.me_ref, s32[96]{0:T(128)} %slot_hbm.1, s32[96]{0:T(128)} %col_hbm.1, s32[96]{0:T(128)} %id_hbm.1, s32[8,4,8]{2,1,0:T(4,128)} %bitcast.21, s32[16]{0:T(128)} %readers_ref.3, ...), custom_call_target="tpu_custom_call" | custom-call | bytes 1 | tf_op jit(solution)/shard_map/pallas_call | solution.py:24
  5.2 3.0 %collective-permute-start = (bf16[528,512]{1,0:T(8,128)(2,1)}, bf16[528,512]{1,0:T(8,128)(2,1)S(1)}, u32[]{:S(2)}, u32[]{:S(2)}) collective-permute-start(bf16[528,512]{1,0:T(8,128)(2,1)} %get-tuple-element.105), channel_id=1, source_target_pairs={{0,4},{4,0},{8,12},{12,8},{16,20},{20,16},{24,28},{28,24},{1,5},{5... | collective-permute-start | bytes 1622024 | tf_op jit(solution)/shard_map/ppermute | solution.py:475
  11.5 3.3 %shard_map.98 = (bf16[4,4,32,512]{3,2,1,0:T(8,128)(2,1)S(1)}, bf16[4,4,16,512]{3,2,1,0:T(8,128)(2,1)S(1)}, bf16[4,4,16,512]{3,2,1,0:T(8,128)(2,1)S(1)}, bf16[4,4,32,512]{3,2,1,0:T(8,128)(2,1)S(1)}, f32[8,128]{1,0:T(8,128)}) custom-call(s32[256]{0:T(256)S(1)} %copy-done.4, bf16[48,128,128]{2,1,0:T(8,128)(2,1)S(1)} %copy-done.1, bf16[512,512]{1,0:T(8,128)(2,1)S(1)} %copy-done.2), custom_call_target="tpu_custom_call" | custom-call | bytes 1 | tf_op jit(solution)/shard_map/pallas_call | solution.py:24
  17.0 2.3 %shard_map.96 = (bf16[4,4,32,512]{3,2,1,0:T(8,128)(2,1)S(1)}, bf16[4,4,32,512]{3,2,1,0:T(8,128)(2,1)S(1)}, bf16[4,4,16,512]{3,2,1,0:T(8,128)(2,1)S(1)}, bf16[4,4,16,512]{3,2,1,0:T(8,128)(2,1)S(1)}, f32[8,128]{1,0:T(8,128)S(1)}) custom-call(s32[256]{0:T(256)S(1)} %copy-done.4, bf16[48,128,128]{2,1,0:T(8,128)(2,1)S(1)} %copy-done.1, bf16[512,512]{1,0:T(8,128)(2,1)S(1)} %copy-done.2), custom_call_target="tpu_custom_call" | custom-call | bytes 1 | tf_op jit(solution)/shard_map/pallas_call | solution.py:24
  19.2 2.3 %collective-permute-done.got_ref.wanted_ref = bf16[528,512]{1,0:T(8,128)(2,1)S(1)} collective-permute-done((bf16[528,512]{1,0:T(8,128)(2,1)}, bf16[528,512]{1,0:T(8,128)(2,1)S(1)}, u32[]{:S(2)}, u32[]{:S(2)}) %collective-permute-start) | collective-permute-done | bytes 540704 | tf_op jit(solution)/shard_map/ppermute | solution.py:475
  21.8 2.2 %collective-permute-start.4 = (bf16[2,4,32,512]{3,2,1,0:T(8,128)(2,1)S(1)}, bf16[2,4,32,512]{3,2,1,0:T(8,128)(2,1)S(1)}, u32[]{:S(2)}, u32[]{:S(2)}) collective-permute-start(bf16[2,4,32,512]{3,2,1,0:T(8,128)(2,1)S(1)} %get-tuple-element.117), channel_id=1, source_target_pairs={{0,8},{4,12},{8,0},{12,4},{16,24},{20,28},{24,16},{28,20},{1,9},{5... | collective-permute-start | bytes 786440 | tf_op jit(solution)/shard_map/ppermute | solution.py:475
  24.3 2.7 %collective-permute-start.5 = (bf16[2,4,32,512]{3,2,1,0:T(8,128)(2,1)S(1)}, bf16[2,4,32,512]{3,2,1,0:T(8,128)(2,1)S(1)}, u32[]{:S(2)}, u32[]{:S(2)}) collective-permute-start(bf16[2,4,32,512]{3,2,1,0:T(8,128)(2,1)S(1)} %get-tuple-element.120), channel_id=1, source_target_pairs={{0,16},{4,20},{8,24},{12,28},{16,0},{20,4},{24,8},{28,12},{1,17},{... | collective-permute-start | bytes 786440 | tf_op jit(solution)/shard_map/ppermute | solution.py:475
  26.9 5.8 %collective-permute-done.2.got_ref = bf16[4,4,32,512]{3,2,1,0:T(8,128)(2,1)S(1)} collective-permute-done((bf16[4,4,32,512]{3,2,1,0:T(8,128)(2,1)S(1)}, bf16[4,4,32,512]{3,2,1,0:T(8,128)(2,1)S(1)}, u32[]{:S(2)}, u32[]{:S(2)}) %collective-permute-start.2) | collective-permute-done | bytes 524320 | tf_op jit(solution)/shard_map/ppermute | solution.py:475
  33.0 2.2 %collective-permute-start.6 = (bf16[2,4,32,512]{3,2,1,0:T(8,128)(2,1)S(1)}, bf16[2,4,32,512]{3,2,1,0:T(8,128)(2,1)S(1)}, u32[]{:S(2)}, u32[]{:S(2)}) collective-permute-start(bf16[2,4,32,512]{3,2,1,0:T(8,128)(2,1)S(1)} %get-tuple-element.123), channel_id=1, source_target_pairs={{0,8},{4,12},{8,0},{12,4},{16,24},{20,28},{24,16},{28,20},{1,9},{5... | collective-permute-start | bytes 786440 | tf_op jit(solution)/shard_map/ppermute | solution.py:475
  38.7 3.2 %collective-permute-start.8 = (bf16[1,4,32,512]{3,2,1,0:T(8,128)(2,1)S(1)}, bf16[1,4,32,512]{3,2,1,0:T(8,128)(2,1)S(1)}, u32[]{:S(2)}, u32[]{:S(2)}) collective-permute-start(bf16[1,4,32,512]{3,2,1,0:T(8,128)(2,1)S(1)} %get-tuple-element.129), channel_id=1, source_target_pairs={{0,16},{4,20},{8,24},{12,28},{16,0},{20,4},{24,8},{28,12},{1,17},{... | collective-permute-start | bytes 393224 | tf_op jit(solution)/shard_map/ppermute | solution.py:475
  46.0 2.7 %collective-permute-start.12 = (bf16[2,4,16,512]{3,2,1,0:T(8,128)(2,1)S(1)}, bf16[2,4,16,512]{3,2,1,0:T(8,128)(2,1)S(1)}, u32[]{:S(2)}, u32[]{:S(2)}) collective-permute-start(bf16[2,4,16,512]{3,2,1,0:T(8,128)(2,1)S(1)} %get-tuple-element.141), channel_id=1, source_target_pairs={{0,8},{4,12},{8,0},{12,4},{16,24},{20,28},{24,16},{28,20},{1,9},{5... | collective-permute-start | bytes 393224 | tf_op jit(solution)/shard_map/ppermute | solution.py:475
  50.4 2.3 %collective-permute-done.11.got_ref = bf16[1,4,32,512]{3,2,1,0:T(8,128)(2,1)S(1)} collective-permute-done((bf16[1,4,32,512]{3,2,1,0:T(8,128)(2,1)S(1)}, bf16[1,4,32,512]{3,2,1,0:T(8,128)(2,1)S(1)}, u32[]{:S(2)}, u32[]{:S(2)}) %collective-permute-start.11) | collective-permute-done | bytes 131104 | tf_op jit(solution)/shard_map/ppermute | solution.py:475
  56.4 2.5 %collective-permute-start.18 = (bf16[1,4,32,512]{3,2,1,0:T(8,128)(2,1)S(1)}, bf16[1,4,32,512]{3,2,1,0:T(8,128)(2,1)S(1)}, u32[]{:S(2)}, u32[]{:S(2)}) collective-permute-start(bf16[1,4,32,512]{3,2,1,0:T(8,128)(2,1)S(1)} %get-tuple-element.154.held_ref), channel_id=1, source_target_pairs={{0,16},{4,20},{8,24},{12,28},{16,0},{20,4},{24,8},{28,12},{1,17},{... | collective-permute-start | bytes 393224 | tf_op jit(solution)/shard_map/ppermute | solution.py:475
  61.0 4.3 %collective-permute-done.17.got_ref = bf16[1,4,16,512]{3,2,1,0:T(8,128)(2,1)S(1)} collective-permute-done((bf16[1,4,16,512]{3,2,1,0:T(8,128)(2,1)S(1)}, bf16[1,4,16,512]{3,2,1,0:T(8,128)(2,1)S(1)}, u32[]{:S(2)}, u32[]{:S(2)}) %collective-permute-start.17) | collective-permute-done | bytes 65568 | tf_op jit(solution)/shard_map/ppermute | solution.py:475
  67.3 4.2 %collective-permute-start.25 = (bf16[2,4,32,512]{3,2,1,0:T(8,128)(2,1)S(1)}, bf16[2,4,32,512]{3,2,1,0:T(8,128)(2,1)S(1)}, u32[]{:S(2)}, u32[]{:S(2)}) collective-permute-start(bf16[2,4,32,512]{3,2,1,0:T(8,128)(2,1)S(1)} %get-tuple-element.169.held_ref.refs_0_), channel_id=1, source_target_pairs={{0,8},{4,12},{8,0},{12,4},{16,24},{20,28},{24,16},{28,20},{1,9},{5... | collective-permute-start | bytes 786440 | tf_op jit(solution)/shard_map/ppermute | solution.py:475
  74.1 3.1 %collective-permute-done.22.got_ref = bf16[1,4,16,512]{3,2,1,0:T(8,128)(2,1)S(1)} collective-permute-done((bf16[1,4,16,512]{3,2,1,0:T(8,128)(2,1)S(1)}, bf16[1,4,16,512]{3,2,1,0:T(8,128)(2,1)S(1)}, u32[]{:S(2)}, u32[]{:S(2)}) %collective-permute-start.22) | collective-permute-done | bytes 65568 | tf_op jit(solution)/shard_map/ppermute | solution.py:475
  77.7 2.1 %collective-permute-start.26 = (bf16[1,4,32,512]{3,2,1,0:T(8,128)(2,1)S(1)}, bf16[1,4,32,512]{3,2,1,0:T(8,128)(2,1)S(1)}, u32[]{:S(2)}, u32[]{:S(2)}) collective-permute-start(bf16[1,4,32,512]{3,2,1,0:T(8,128)(2,1)S(1)} %get-tuple-element.171.held_ref), channel_id=1, source_target_pairs={{0,16},{4,20},{8,24},{12,28},{16,0},{20,4},{24,8},{28,12},{1,17},{... | collective-permute-start | bytes 393224 | tf_op jit(solution)/shard_map/ppermute | solution.py:475
  81.0 2.3 %collective-permute-start.28 = (bf16[2,4,32,512]{3,2,1,0:T(8,128)(2,1)S(1)}, bf16[2,4,32,512]{3,2,1,0:T(8,128)(2,1)S(1)}, u32[]{:S(2)}, u32[]{:S(2)}) collective-permute-start(bf16[2,4,32,512]{3,2,1,0:T(8,128)(2,1)S(1)} %get-tuple-element.175.held_ref.refs_2_), channel_id=1, source_target_pairs={{0,8},{4,12},{8,0},{12,4},{16,24},{20,28},{24,16},{28,20},{1,9},{5... | collective-permute-start | bytes 786440 | tf_op jit(solution)/shard_map/ppermute | solution.py:475
  85.0 2.1 %collective-permute-done.26.got_ref = bf16[1,4,32,512]{3,2,1,0:T(8,128)(2,1)S(1)} collective-permute-done((bf16[1,4,32,512]{3,2,1,0:T(8,128)(2,1)S(1)}, bf16[1,4,32,512]{3,2,1,0:T(8,128)(2,1)S(1)}, u32[]{:S(2)}, u32[]{:S(2)}) %collective-permute-start.26) | collective-permute-done | bytes 131104 | tf_op jit(solution)/shard_map/ppermute | solution.py:475
  87.9 3.1 %collective-permute-start.29 = (bf16[1,4,16,512]{3,2,1,0:T(8,128)(2,1)S(1)}, bf16[1,4,16,512]{3,2,1,0:T(8,128)(2,1)S(1)}, u32[]{:S(2)}, u32[]{:S(2)}) collective-permute-start(bf16[1,4,16,512]{3,2,1,0:T(8,128)(2,1)S(1)} %get-tuple-element.177.held_ref), channel_id=1, source_target_pairs={{0,16},{4,20},{8,24},{12,28},{16,0},{20,4},{24,8},{28,12},{1,17},{... | collective-permute-start | bytes 196616 | tf_op jit(solution)/shard_map/ppermute | solution.py:475
  91.7 2.3 %collective-permute-start.35 = (bf16[8,32,512]{2,1,0:T(8,128)(2,1)S(1)}, bf16[8,32,512]{2,1,0:T(8,128)(2,1)S(1)}, u32[]{:S(2)}, u32[]{:S(2)}) collective-permute-start(bf16[8,32,512]{2,1,0:T(8,128)(2,1)S(1)} %get-tuple-element.188), channel_id=1, source_target_pairs={{0,4},{4,0},{8,12},{12,8},{16,20},{20,16},{24,28},{28,24},{1,5},{5... | collective-permute-start | bytes 786440 | tf_op jit(solution)/shard_map/ppermute | solution.py:475
  95.8 3.4 %collective-permute-start.33 = (bf16[1,4,16,512]{3,2,1,0:T(8,128)(2,1)S(1)}, bf16[1,4,16,512]{3,2,1,0:T(8,128)(2,1)S(1)}, u32[]{:S(2)}, u32[]{:S(2)}) collective-permute-start(bf16[1,4,16,512]{3,2,1,0:T(8,128)(2,1)S(1)} %get-tuple-element.184.held_ref), channel_id=1, source_target_pairs={{0,16},{4,20},{8,24},{12,28},{16,0},{20,4},{24,8},{28,12},{1,17},{... | collective-permute-start | bytes 196616 | tf_op jit(solution)/shard_map/ppermute | solution.py:475
  102.3 2.3 %collective-permute-start.36 = (bf16[2,4,16,512]{3,2,1,0:T(8,128)(2,1)S(1)}, bf16[2,4,16,512]{3,2,1,0:T(8,128)(2,1)S(1)}, u32[]{:S(2)}, u32[]{:S(2)}) collective-permute-start(bf16[2,4,16,512]{3,2,1,0:T(8,128)(2,1)S(1)} %get-tuple-element.189.held_ref.refs_8_), channel_id=1, source_target_pairs={{0,8},{4,12},{8,0},{12,4},{16,24},{20,28},{24,16},{28,20},{1,9},{5... | collective-permute-start | bytes 393224 | tf_op jit(solution)/shard_map/ppermute | solution.py:475
  111.4 2.7 %shard_map.137 = (bf16[4,128,512]{2,1,0:T(8,128)(2,1)}, bf16[16,128,512]{2,1,0:T(8,128)(2,1)}, f32[8,128]{1,0:T(8,128)S(1)}) custom-call(f32[8,128]{1,0:T(8,128)S(1)} %shard_map.136.token_ref, s32[1]{0:T(128)} %bitcast.me_ref, s32[16]{0:T(128)S(1)} %copy-done.3, s32[16]{0:T(128)S(1)} %copy-done.5, ...), custom_call_target="tpu_custom_call" | custom-call | bytes 1 | tf_op jit(solution)/shard_map/pallas_call | solution.py:24
  (112 shorter events, 43.9 us)
Async XLA Ops:
  5.2 16.3 %collective-permute-start = (bf16[528,512]{1,0:T(8,128)(2,1)}, bf16[528,512]{1,0:T(8,128)(2,1)S(1)}, u32[]{:S(2)}, u32[]{:S(2)}) collective-permute-start(bf16[528,512]{1,0:T(8,128)(2,1)} %get-tuple-element.105), channel_id=1, source_target_pairs={{0,4},{4,0},{8,12},{12,8},{16,20},{20,16},{24,28},{28,24},{1,5},{5... | collective-permute-start | bytes 1622024 | tf_op jit(solution)/shard_map/ppermute | solution.py:475
  8.2 15.8 %collective-permute-start.1 = (bf16[4,4,32,512]{3,2,1,0:T(8,128)(2,1)}, bf16[4,4,32,512]{3,2,1,0:T(8,128)(2,1)S(1)}, u32[]{:S(2)}, u32[]{:S(2)}) collective-permute-start(bf16[4,4,32,512]{3,2,1,0:T(8,128)(2,1)} %get-tuple-element.108), channel_id=1, source_target_pairs={{0,8},{4,12},{8,0},{12,4},{16,24},{20,28},{24,16},{28,20},{1,9},{5... | collective-permute-start | bytes 1572872 | tf_op jit(solution)/shard_map/ppermute | solution.py:475
  14.9 17.9 %collective-permute-start.2 = (bf16[4,4,32,512]{3,2,1,0:T(8,128)(2,1)S(1)}, bf16[4,4,32,512]{3,2,1,0:T(8,128)(2,1)S(1)}, u32[]{:S(2)}, u32[]{:S(2)}) collective-permute-start(bf16[4,4,32,512]{3,2,1,0:T(8,128)(2,1)S(1)} %get-tuple-element.111), channel_id=1, source_target_pairs={{0,4},{4,0},{8,12},{12,8},{16,20},{20,16},{24,28},{28,24},{1,5},{5... | collective-permute-start | bytes 1572872 | tf_op jit(solution)/shard_map/ppermute | solution.py:475
  15.5 22.9 %collective-permute-start.3 = (bf16[4,4,16,512]{3,2,1,0:T(8,128)(2,1)S(1)}, bf16[4,4,16,512]{3,2,1,0:T(8,128)(2,1)S(1)}, u32[]{:S(2)}, u32[]{:S(2)}) collective-permute-start(bf16[4,4,16,512]{3,2,1,0:T(8,128)(2,1)S(1)} %get-tuple-element.114), channel_id=1, source_target_pairs={{0,4},{4,0},{8,12},{12,8},{16,20},{20,16},{24,28},{28,24},{1,5},{5... | collective-permute-start | bytes 786440 | tf_op jit(solution)/shard_map/ppermute | solution.py:475
  21.8 16.7 %collective-permute-start.4 = (bf16[2,4,32,512]{3,2,1,0:T(8,128)(2,1)S(1)}, bf16[2,4,32,512]{3,2,1,0:T(8,128)(2,1)S(1)}, u32[]{:S(2)}, u32[]{:S(2)}) collective-permute-start(bf16[2,4,32,512]{3,2,1,0:T(8,128)(2,1)S(1)} %get-tuple-element.117), channel_id=1, source_target_pairs={{0,8},{4,12},{8,0},{12,4},{16,24},{20,28},{24,16},{28,20},{1,9},{5... | collective-permute-start | bytes 786440 | tf_op jit(solution)/shard_map/ppermute | solution.py:475
  24.3 19.2 %collective-permute-start.5 = (bf16[2,4,32,512]{3,2,1,0:T(8,128)(2,1)S(1)}, bf16[2,4,32,512]{3,2,1,0:T(8,128)(2,1)S(1)}, u32[]{:S(2)}, u32[]{:S(2)}) collective-permute-start(bf16[2,4,32,512]{3,2,1,0:T(8,128)(2,1)S(1)} %get-tuple-element.120), channel_id=1, source_target_pairs={{0,16},{4,20},{8,24},{12,28},{16,0},{20,4},{24,8},{28,12},{1,17},{... | collective-permute-start | bytes 786440 | tf_op jit(solution)/shard_map/ppermute | solution.py:475
  33.0 12.1 %collective-permute-start.6 = (bf16[2,4,32,512]{3,2,1,0:T(8,128)(2,1)S(1)}, bf16[2,4,32,512]{3,2,1,0:T(8,128)(2,1)S(1)}, u32[]{:S(2)}, u32[]{:S(2)}) collective-permute-start(bf16[2,4,32,512]{3,2,1,0:T(8,128)(2,1)S(1)} %get-tuple-element.123), channel_id=1, source_target_pairs={{0,8},{4,12},{8,0},{12,4},{16,24},{20,28},{24,16},{28,20},{1,9},{5... | collective-permute-start | bytes 786440 | tf_op jit(solution)/shard_map/ppermute | solution.py:475
  35.3 10.6 %collective-permute-start.7 = (bf16[4,4,16,512]{3,2,1,0:T(8,128)(2,1)S(1)}, bf16[4,4,16,512]{3,2,1,0:T(8,128)(2,1)S(1)}, u32[]{:S(2)}, u32[]{:S(2)}) collective-permute-start(bf16[4,4,16,512]{3,2,1,0:T(8,128)(2,1)S(1)} %get-tuple-element.126), channel_id=1, source_target_pairs={{0,4},{4,0},{8,12},{12,8},{16,20},{20,16},{24,28},{28,24},{1,5},{5... | collective-permute-start | bytes 786440 | tf_op jit(solution)/shard_map/ppermute | solution.py:475
  38.7 10.0 %collective-permute-start.8 = (bf16[1,4,32,512]{3,2,1,0:T(8,128)(2,1)S(1)}, bf16[1,4,32,512]{3,2,1,0:T(8,128)(2,1)S(1)}, u32[]{:S(2)}, u32[]{:S(2)}) collective-permute-start(bf16[1,4,32,512]{3,2,1,0:T(8,128)(2,1)S(1)} %get-tuple-element.129), channel_id=1, source_target_pairs={{0,16},{4,20},{8,24},{12,28},{16,0},{20,4},{24,8},{28,12},{1,17},{... | collective-permute-start | bytes 393224 | tf_op jit(solution)/shard_map/ppermute | solution.py:475
  41.9 8.4 %collective-permute-start.10 = (bf16[2,4,16,512]{3,2,1,0:T(8,128)(2,1)S(1)}, bf16[2,4,16,512]{3,2,1,0:T(8,128)(2,1)S(1)}, u32[]{:S(2)}, u32[]{:S(2)}) collective-permute-start(bf16[2,4,16,512]{3,2,1,0:T(8,128)(2,1)S(1)} %get-tuple-element.135), channel_id=1, source_target_pairs={{0,8},{4,12},{8,0},{12,4},{16,24},{20,28},{24,16},{28,20},{1,9},{5... | collective-permute-start | bytes 393224 | tf_op jit(solution)/shard_map/ppermute | solution.py:475
  45.2 7.4 %collective-permute-start.11 = (bf16[1,4,32,512]{3,2,1,0:T(8,128)(2,1)S(1)}, bf16[1,4,32,512]{3,2,1,0:T(8,128)(2,1)S(1)}, u32[]{:S(2)}, u32[]{:S(2)}) collective-permute-start(bf16[1,4,32,512]{3,2,1,0:T(8,128)(2,1)S(1)} %get-tuple-element.138), channel_id=1, source_target_pairs={{0,16},{4,20},{8,24},{12,28},{16,0},{20,4},{24,8},{28,12},{1,17},{... | collective-permute-start | bytes 393224 | tf_op jit(solution)/shard_map/ppermute | solution.py:475
  56.4 9.9 %collective-permute-start.18 = (bf16[1,4,32,512]{3,2,1,0:T(8,128)(2,1)S(1)}, bf16[1,4,32,512]{3,2,1,0:T(8,128)(2,1)S(1)}, u32[]{:S(2)}, u32[]{:S(2)}) collective-permute-start(bf16[1,4,32,512]{3,2,1,0:T(8,128)(2,1)S(1)} %get-tuple-element.154.held_ref), channel_id=1, source_target_pairs={{0,16},{4,20},{8,24},{12,28},{16,0},{20,4},{24,8},{28,12},{1,17},{... | collective-permute-start | bytes 393224 | tf_op jit(solution)/shard_map/ppermute | solution.py:475
  58.9 7.4 %collective-permute-start.19 = (bf16[1,4,32,512]{3,2,1,0:T(8,128)(2,1)S(1)}, bf16[1,4,32,512]{3,2,1,0:T(8,128)(2,1)S(1)}, u32[]{:S(2)}, u32[]{:S(2)}) collective-permute-start(bf16[1,4,32,512]{3,2,1,0:T(8,128)(2,1)S(1)} %bitcast.9), channel_id=1, source_target_pairs={{0,2},{1,3},{2,0},{3,1},{4,6},{5,7},{6,4},{7,5},{8,10},{9,11},{10,... | collective-permute-start | bytes 393224 | tf_op jit(solution)/shard_map/ppermute | solution.py:475
  66.4 10.8 %collective-permute-start.23 = (bf16[2,4,32,512]{3,2,1,0:T(8,128)(2,1)S(1)}, bf16[2,4,32,512]{3,2,1,0:T(8,128)(2,1)S(1)}, u32[]{:S(2)}, u32[]{:S(2)}) collective-permute-start(bf16[2,4,32,512]{3,2,1,0:T(8,128)(2,1)S(1)} %get-tuple-element.165.held_ref), channel_id=1, source_target_pairs={{0,1},{1,0},{2,3},{3,2},{4,5},{5,4},{6,7},{7,6},{8,9},{9,8},{10,11... | collective-permute-start | bytes 786440 | tf_op jit(solution)/shard_map/ppermute | solution.py:475
  67.3 16.1 %collective-permute-start.25 = (bf16[2,4,32,512]{3,2,1,0:T(8,128)(2,1)S(1)}, bf16[2,4,32,512]{3,2,1,0:T(8,128)(2,1)S(1)}, u32[]{:S(2)}, u32[]{:S(2)}) collective-permute-start(bf16[2,4,32,512]{3,2,1,0:T(8,128)(2,1)S(1)} %get-tuple-element.169.held_ref.refs_0_), channel_id=1, source_target_pairs={{0,8},{4,12},{8,0},{12,4},{16,24},{20,28},{24,16},{28,20},{1,9},{5... | collective-permute-start | bytes 786440 | tf_op jit(solution)/shard_map/ppermute | solution.py:475
  71.9 9.1 %collective-permute-start.24 = (bf16[1,4,32,512]{3,2,1,0:T(8,128)(2,1)S(1)}, bf16[1,4,32,512]{3,2,1,0:T(8,128)(2,1)S(1)}, u32[]{:S(2)}, u32[]{:S(2)}) collective-permute-start(bf16[1,4,32,512]{3,2,1,0:T(8,128)(2,1)S(1)} %get-tuple-element.167.held_ref), channel_id=1, source_target_pairs={{0,16},{4,20},{8,24},{12,28},{16,0},{20,4},{24,8},{28,12},{1,17},{... | collective-permute-start | bytes 393224 | tf_op jit(solution)/shard_map/ppermute | solution.py:475
  77.7 9.5 %collective-permute-start.26 = (bf16[1,4,32,512]{3,2,1,0:T(8,128)(2,1)S(1)}, bf16[1,4,32,512]{3,2,1,0:T(8,128)(2,1)S(1)}, u32[]{:S(2)}, u32[]{:S(2)}) collective-permute-start(bf16[1,4,32,512]{3,2,1,0:T(8,128)(2,1)S(1)} %get-tuple-element.171.held_ref), channel_id=1, source_target_pairs={{0,16},{4,20},{8,24},{12,28},{16,0},{20,4},{24,8},{28,12},{1,17},{... | collective-permute-start | bytes 393224 | tf_op jit(solution)/shard_map/ppermute | solution.py:475
  81.0 10.5 %collective-permute-start.28 = (bf16[2,4,32,512]{3,2,1,0:T(8,128)(2,1)S(1)}, bf16[2,4,32,512]{3,2,1,0:T(8,128)(2,1)S(1)}, u32[]{:S(2)}, u32[]{:S(2)}) collective-permute-start(bf16[2,4,32,512]{3,2,1,0:T(8,128)(2,1)S(1)} %get-tuple-element.175.held_ref.refs_2_), channel_id=1, source_target_pairs={{0,8},{4,12},{8,0},{12,4},{16,24},{20,28},{24,16},{28,20},{1,9},{5... | collective-permute-start | bytes 786440 | tf_op jit(solution)/shard_map/ppermute | solution.py:475
  83.5 15.8 %collective-permute-start.31 = (bf16[8,32,512]{2,1,0:T(8,128)(2,1)S(1)}, bf16[8,32,512]{2,1,0:T(8,128)(2,1)S(1)}, u32[]{:S(2)}, u32[]{:S(2)}) collective-permute-start(bf16[8,32,512]{2,1,0:T(8,128)(2,1)S(1)} %get-tuple-element.181), channel_id=1, source_target_pairs={{0,4},{4,0},{8,12},{12,8},{16,20},{20,16},{24,28},{28,24},{1,5},{5... | collective-permute-start | bytes 786440 | tf_op jit(solution)/shard_map/ppermute | solution.py:475
  87.2 12.1 %collective-permute-start.32 = (bf16[2,4,32,512]{3,2,1,0:T(8,128)(2,1)S(1)}, bf16[2,4,32,512]{3,2,1,0:T(8,128)(2,1)S(1)}, u32[]{:S(2)}, u32[]{:S(2)}) collective-permute-start(bf16[2,4,32,512]{3,2,1,0:T(8,128)(2,1)S(1)} %get-tuple-element.182.held_ref.refs_4_), channel_id=1, source_target_pairs={{0,8},{4,12},{8,0},{12,4},{16,24},{20,28},{24,16},{28,20},{1,9},{5... | collective-permute-start | bytes 786440 | tf_op jit(solution)/shard_map/ppermute | solution.py:475
  87.3 8.0 %collective-permute-start.30 = (bf16[2,4,16,512]{3,2,1,0:T(8,128)(2,1)S(1)}, bf16[2,4,16,512]{3,2,1,0:T(8,128)(2,1)S(1)}, u32[]{:S(2)}, u32[]{:S(2)}) collective-permute-start(bf16[2,4,16,512]{3,2,1,0:T(8,128)(2,1)S(1)} %get-tuple-element.179.held_ref), channel_id=1, source_target_pairs={{0,1},{1,0},{2,3},{3,2},{4,5},{5,4},{6,7},{7,6},{8,9},{9,8},{10,11... | collective-permute-start | bytes 393224 | tf_op jit(solution)/shard_map/ppermute | solution.py:475
  87.9 7.4 %collective-permute-start.29 = (bf16[1,4,16,512]{3,2,1,0:T(8,128)(2,1)S(1)}, bf16[1,4,16,512]{3,2,1,0:T(8,128)(2,1)S(1)}, u32[]{:S(2)}, u32[]{:S(2)}) collective-permute-start(bf16[1,4,16,512]{3,2,1,0:T(8,128)(2,1)S(1)} %get-tuple-element.177.held_ref), channel_id=1, source_target_pairs={{0,16},{4,20},{8,24},{12,28},{16,0},{20,4},{24,8},{28,12},{1,17},{... | collective-permute-start | bytes 196616 | tf_op jit(solution)/shard_map/ppermute | solution.py:475
  91.7 15.5 %collective-permute-start.35 = (bf16[8,32,512]{2,1,0:T(8,128)(2,1)S(1)}, bf16[8,32,512]{2,1,0:T(8,128)(2,1)S(1)}, u32[]{:S(2)}, u32[]{:S(2)}) collective-permute-start(bf16[8,32,512]{2,1,0:T(8,128)(2,1)S(1)} %get-tuple-element.188), channel_id=1, source_target_pairs={{0,4},{4,0},{8,12},{12,8},{16,20},{20,16},{24,28},{28,24},{1,5},{5... | collective-permute-start | bytes 786440 | tf_op jit(solution)/shard_map/ppermute | solution.py:475
  99.4 10.2 %collective-permute-start.37 = (bf16[8,32,512]{2,1,0:T(8,128)(2,1)S(1)}, bf16[8,32,512]{2,1,0:T(8,128)(2,1)S(1)}, u32[]{:S(2)}, u32[]{:S(2)}) collective-permute-start(bf16[8,32,512]{2,1,0:T(8,128)(2,1)S(1)} %get-tuple-element.191), channel_id=1, source_target_pairs={{0,4},{4,0},{8,12},{12,8},{16,20},{20,16},{24,28},{28,24},{1,5},{5... | collective-permute-start | bytes 786440 | tf_op jit(solution)/shard_map/ppermute | solution.py:475
  (22 other events, 140.5 us)
